TPU v7x, 32 devices: a whole 2x2x4 slice. The times are simulated.
32 devices in a mesh: row: 4 (over y, x), col: 8 (over z, core).
Axes of the slice: x: 2, y: 2, z: 4, core: 2. Of those that a mesh axis runs over, the one named last changes fastest.
Arguments:
- embed: float32 [8192, 128], P(('row', 'col')), may hold values from -6 to 6
- cotangent: float32 [8192, 128], P(('col', 'row')), may hold values from -6 to 6
- tile_values: float32 [8, 4, 128, 128, 128], P('col', 'row'), may hold values from 0 to 1
- tile_coords: int32 [2, 8, 4, 128], P(None, 'col', 'row'), may hold values from 0 to 15, as said below
- tile_count: int32 [8, 4], P('col', 'row'), may hold values from 1 to 128, as said below
- row_degree: int32 [8192], P(('col', 'row')), may hold values from 16 to 511
- col_degree: int32 [8192], P(('row', 'col')), may hold values from 16 to 511
Outputs:
- propagated: float32 [8192, 128], P(('col', 'row'))
- embed_grad: float32 [8192, 128], P(('row', 'col'))
Inputs may be any that keep to these rules, and one draw needn't show every extreme that they name: `tile_coords`: within one device block the slots hold distinct tile positions; the first component is below 8 and the second below 16. `tile_count`: some device block has all 128 slots live.
All inputs are finite; a program needn't handle non-finite values.
Results may differ from a plain program's by a relative error of at most 0.0003.
Values sent between devices are 32-bit elements; how exact they have to be, the bound alone decides.
No kernel may reach another device: no remote copies, remote signals or barrier semaphores. Data moves between devices by JAX's collectives and lax.ppermute only.
A program may use at most 128 MiB of HBM per device.

v0:
```python
import math

import jax
import jax.numpy as jnp
from jax import lax
from jax.sharding import PartitionSpec as P


def tile_terms(values, rows_at, cols_at, live_mask, panel_tiles, grad_tiles):
    picked = jnp.take(panel_tiles, cols_at, axis=0)
    forward_each = jnp.einsum("tij,tjd->tid", values, picked, precision=lax.Precision.HIGHEST)
    row_hot = (
        (rows_at[None, :] == jnp.arange(grad_tiles.shape[0], dtype=jnp.int32)[:, None])
        & live_mask[None, :]
    ).astype(jnp.float32)
    forward = jnp.einsum("at,tid->aid", row_hot, forward_each, precision=lax.Precision.HIGHEST)
    grad_picked = jnp.take(grad_tiles, rows_at, axis=0)
    backward_each = jnp.einsum("tij,tid->tjd", values, grad_picked, precision=lax.Precision.HIGHEST)
    col_hot = (
        (cols_at[None, :] == jnp.arange(panel_tiles.shape[0], dtype=jnp.int32)[:, None])
        & live_mask[None, :]
    ).astype(jnp.float32)
    backward = jnp.einsum("bt,tjd->bjd", col_hot, backward_each, precision=lax.Precision.HIGHEST)
    return (forward, backward)


def per_device(embed, cotangent, tile_values, tile_coords, tile_count, row_degree, col_degree):
    tile_size = tile_values.shape[-1]
    feature_width = embed.shape[1]
    capacity = tile_values.shape[2]
    values = tile_values[0, 0]
    rows_at = tile_coords[0, 0, 0]
    cols_at = tile_coords[1, 0, 0]
    live_count = tile_count[0, 0]
    scaled = embed * lax.rsqrt(col_degree.astype(jnp.float32))[:, None]
    grad_scaled = cotangent * lax.rsqrt(row_degree.astype(jnp.float32))[:, None]
    embed_panel = lax.all_gather(scaled, "col", axis=0, tiled=True)
    grad_panel = lax.all_gather(grad_scaled, "row", axis=0, tiled=True)
    panel_tiles = embed_panel.reshape(-1, tile_size, feature_width)
    grad_tiles = grad_panel.reshape(-1, tile_size, feature_width)
    group_size = math.gcd(capacity, 32)

    def visit(turn_index, totals):
        first_slot = turn_index * group_size
        group_values = lax.dynamic_slice_in_dim(values, first_slot, group_size, 0)
        group_rows = lax.dynamic_slice_in_dim(rows_at, first_slot, group_size, 0)
        group_cols = lax.dynamic_slice_in_dim(cols_at, first_slot, group_size, 0)
        live_mask = first_slot + jnp.arange(group_size, dtype=jnp.int32) < live_count
        forward_part, backward_part = tile_terms(
            group_values, group_rows, group_cols, live_mask, panel_tiles, grad_tiles
        )
        return (totals[0] + forward_part, totals[1] + backward_part)

    empty_forward = jnp.zeros(grad_tiles.shape, jnp.float32)
    empty_backward = jnp.zeros(panel_tiles.shape, jnp.float32)
    turns = (live_count + group_size - 1) // group_size
    forward, backward = lax.fori_loop(0, turns, visit, (empty_forward, empty_backward))
    summed = lax.psum_scatter(
        forward.reshape(-1, feature_width), "row", scatter_dimension=0, tiled=True
    )
    propagated = summed * lax.rsqrt(row_degree.astype(jnp.float32))[:, None]
    grad_summed = lax.psum_scatter(
        backward.reshape(-1, feature_width), "col", scatter_dimension=0, tiled=True
    )
    embed_grad = grad_summed * lax.rsqrt(col_degree.astype(jnp.float32))[:, None]
    return (propagated, embed_grad)


def solution(mesh):
    return jax.shard_map(
        per_device,
        mesh=mesh,
        in_specs=(
            P(("row", "col"), None),
            P(("col", "row"), None),
            P("col", "row", None, None, None),
            P(None, "col", "row", None),
            P("col", "row"),
            P(("col", "row")),
            P(("row", "col")),
        ),
        out_specs=(P(("col", "row"), None), P(("row", "col"), None)),
        check_vma=False,
    )
```

profile of v0, /device:TPU:0, one launch (start us, length us, event | category | flops | bytes accessed | tf_op | source)
XLA Modules:
  0.0 175.2 jit_solution(15441616350559565096)
XLA Ops:
  7.2 0.0 all-gather.2.cloned.1.call-start
  7.2 0.7 convert_rsqrt_fusion.1
  7.9 1.7 broadcast_multiply_fusion.3
  9.6 0.0 all-gather.2.cloned.1.call-update
  9.6 0.0 reduce-scatter.3.cloned.1.call-start
  10.3 0.7 convert_rsqrt_fusion
  11.0 1.0 broadcast_multiply_fusion.1
  12.0 11.5 %all_gather.7 = f32[1024,128]{1,0:T(8,128)S(1)} all-gather(f32[256,128]{1,0:T(8,128)S(1)} %broadcast_multiply_fusion.1), channel_id=1, replica_groups=mesh['row'=4,'col'=8] {'row'}, dimensions={0}, use_global_device_ids=true | all-gather | bytes 655360 | tf_op jit(solution)/shard_map/all_gather | solution.py:38
  23.5 0.7 slice_bitcast_fusion
  24.2 10.8 %all-gather.2.cloned.1.call-done = f32[2048,128]{1,0:T(8,128)} async-done(((f32[256,128]{1,0:T(8,128)}), f32[2048,128]{1,0:T(8,128)}) %all-gather.2.cloned.1.call-update) | async-done | bytes 1048592 | tf_op jit(solution)/shard_map/all_gather | solution.py:37
  35.0 1.0 broadcast_in_dim.39
  36.1 35.4 %while.12 = (s32[]{:T(128)}, f32[8,128,128]{2,0,1:T(8,128)S(1)}, f32[16,128,128]{2,0,1:T(8,128)}, s32[]{:T(128)}, s32[128]{0:T(128)S(1)}, /*index=5*/s32[]{:T(12...) while((s32[]{:T(128)}, f32[8,128,128]{2,0,1:T(8,128)S(1)}, ...), condition=%wide.region_1.2_spmd, body=%wide.region_0.1_spmd.sunk | while | flops 1763053696 | bytes 36710624 | solution.py:57
  36.1 0.1 compare_and_fusion.3
  36.2 0.7 gather_fusion.1
  36.9 0.0 copy-start
  36.9 5.2 %fusion.56 = f32[32,128,128]{2,1,0:T(8,128)S(1)} fusion(f32[32,128,128]{2,1,0:T(8,128)S(1)} %gather_fusion.1, f32[128,128,128]{2,1,0:T(8,128)} %get-tuple-element.190, s32[]{:T(128)S(6)} %select_n.49, pred[32]{0:T(512)(128)(4,1)S(1)} %get-tuple-element.155), kind=kOutput, calls=%fused_computation.6.clone.1 | convolution fusion | flops 805830656 | bytes 6291492 | tf_op jit(solution)/shard_map/while/body/tij,tid->tjd/dot_general | solution.py:18
  42.1 0.7 add_compare_fusion.2
  42.8 0.0 copy-done
  42.8 2.3 %fusion.57 = f32[16,128,128]{2,0,1:T(8,128)S(1)} fusion(f32[16,128,128]{2,0,1:T(8,128)S(1)} %copy-done, f32[32,128,128]{2,1,0:T(8,128)S(1)} %fusion.56, s32[32]{0:T(128)S(1)} %get-tuple-element.152, pred[32]{0:T(512)(128)(4,1)S(1)} %add_compare_fusion.2), kind=kOutput, calls=%fused_computation.12.clone.1 | convolution fusion | flops 100926464 | bytes 4194464 | tf_op jit(solution)/shard_map/while/body/bt,tjd->bjd/dot_general | solution.py:23
  45.1 0.0 copy-start.1
  45.1 0.9 copy-done.1
  46.0 1.9 %gather_fusion = f32[32,128,128]{2,1,0:T(8,128)S(1)} fusion(f32[16,128,128]{2,1,0:T(8,128)} %get-tuple-element.192, s32[1024]{0:T(1024)S(1)} %pad_clamp_fusion.4), kind=kCustom, calls=%fused_computation.clone.1 | custom fusion | bytes 4194432 | tf_op jit(solution)/shard_map/while/body/jit(_take)/gather | solution.py:10
  47.9 3.8 %fusion.54 = f32[32,128,128]{2,1,0:T(8,128)S(1)} fusion(f32[32,128,128]{2,1,0:T(8,128)S(1)} %gather_fusion, f32[128,128,128]{2,1,0:T(8,128)} %get-tuple-element.190, s32[]{:T(128)S(6)} %select_n.49, pred[32]{0:T(512)(128)(4,1)S(1)} %get-tuple-element.153), kind=kOutput, calls=%fused_computation.8.clone.1 | convolution fusion | flops 805830656 | bytes 6291492 | tf_op jit(solution)/shard_map/while/body/tij,tjd->tid/dot_general | solution.py:11
  51.8 2.0 %fusion.55 = f32[8,128,128]{2,0,1:T(8,128)S(1)} fusion(f32[8,128,128]{2,0,1:T(8,128)S(1)} %get-tuple-element.171, f32[32,128,128]{2,1,0:T(8,128)S(1)} %fusion.54, s32[32]{0:T(128)S(1)} %get-tuple-element.154, pred[32]{0:T(512)(128)(4,1)S(1)} %add_compare_fusion.2), kind=kOutput, calls=%fused_computation.13.clone.1 | convolution fusion | flops 50463232 | bytes 3145888 | tf_op jit(solution)/shard_map/while/body/at,tid->aid/dot_general | solution.py:16
  53.8 0.1 compare_and_fusion.3
  53.9 0.7 gather_fusion.1
  54.6 0.0 copy-start
  54.6 5.2 %fusion.56 = f32[32,128,128]{2,1,0:T(8,128)S(1)} fusion(f32[32,128,128]{2,1,0:T(8,128)S(1)} %gather_fusion.1, f32[128,128,128]{2,1,0:T(8,128)} %get-tuple-element.190, s32[]{:T(128)S(6)} %select_n.49, pred[32]{0:T(512)(128)(4,1)S(1)} %get-tuple-element.155), kind=kOutput, calls=%fused_computation.6.clone.1 | convolution fusion | flops 805830656 | bytes 6291492 | tf_op jit(solution)/shard_map/while/body/tij,tid->tjd/dot_general | solution.py:18
  59.8 0.7 add_compare_fusion.2
  60.5 0.0 copy-done
  60.5 2.3 %fusion.57 = f32[16,128,128]{2,0,1:T(8,128)S(1)} fusion(f32[16,128,128]{2,0,1:T(8,128)S(1)} %copy-done, f32[32,128,128]{2,1,0:T(8,128)S(1)} %fusion.56, s32[32]{0:T(128)S(1)} %get-tuple-element.152, pred[32]{0:T(512)(128)(4,1)S(1)} %add_compare_fusion.2), kind=kOutput, calls=%fused_computation.12.clone.1 | convolution fusion | flops 100926464 | bytes 4194464 | tf_op jit(solution)/shard_map/while/body/bt,tjd->bjd/dot_general | solution.py:23
  62.8 0.0 copy-start.1
  62.8 0.9 copy-done.1
  63.7 1.9 %gather_fusion = f32[32,128,128]{2,1,0:T(8,128)S(1)} fusion(f32[16,128,128]{2,1,0:T(8,128)} %get-tuple-element.192, s32[1024]{0:T(1024)S(1)} %pad_clamp_fusion.4), kind=kCustom, calls=%fused_computation.clone.1 | custom fusion | bytes 4194432 | tf_op jit(solution)/shard_map/while/body/jit(_take)/gather | solution.py:10
  65.7 3.8 %fusion.54 = f32[32,128,128]{2,1,0:T(8,128)S(1)} fusion(f32[32,128,128]{2,1,0:T(8,128)S(1)} %gather_fusion, f32[128,128,128]{2,1,0:T(8,128)} %get-tuple-element.190, s32[]{:T(128)S(6)} %select_n.49, pred[32]{0:T(512)(128)(4,1)S(1)} %get-tuple-element.153), kind=kOutput, calls=%fused_computation.8.clone.1 | convolution fusion | flops 805830656 | bytes 6291492 | tf_op jit(solution)/shard_map/while/body/tij,tjd->tid/dot_general | solution.py:11
  69.5 2.0 %fusion.55 = f32[8,128,128]{2,0,1:T(8,128)S(1)} fusion(f32[8,128,128]{2,0,1:T(8,128)S(1)} %get-tuple-element.171, f32[32,128,128]{2,1,0:T(8,128)S(1)} %fusion.54, s32[32]{0:T(128)S(1)} %get-tuple-element.154, pred[32]{0:T(512)(128)(4,1)S(1)} %add_compare_fusion.2), kind=kOutput, calls=%fused_computation.13.clone.1 | convolution fusion | flops 50463232 | bytes 3145888 | tf_op jit(solution)/shard_map/while/body/at,tid->aid/dot_general | solution.py:16
  71.5 0.0 copy-start.2
  71.5 0.9 copy.9
  72.4 0.0 reduce-scatter.3.cloned.1.call-update
  72.5 0.0 reduce-scatter.5.cloned.1.call-start
  72.5 0.4 copy-done.2
  72.9 1.3 copy.10
  74.2 0.0 reduce-scatter.5.cloned.1.call-update
  74.2 58.0 %reduce-scatter.3.cloned.1.call-done = f32[256,128]{1,0:T(8,128)} async-done(((f32[1024,128]{1,0:T(8,128)}), f32[256,128]{1,0:T(8,128)}) %reduce-scatter.3.cloned.1.call-update) | async-done | bytes 131088 | tf_op jit(solution)/shard_map/reduce_scatter | solution.py:58
  132.3 1.7 broadcast_multiply_fusion
  133.9 33.1 %reduce-scatter.5.cloned.1.call-done = f32[256,128]{1,0:T(8,128)} async-done(((f32[2048,128]{1,0:T(8,128)}), f32[256,128]{1,0:T(8,128)}) %reduce-scatter.5.cloned.1.call-update) | async-done | bytes 131088 | tf_op jit(solution)/shard_map/reduce_scatter | solution.py:62
  167.0 1.7 broadcast_multiply_fusion.2
  (9 shorter events, 0.1 us)
Async XLA Ops:
  7.2 27.8 %all-gather.2.cloned.1.call-start = ((), (), s32[]{:S(2)}) async-start(), calls=%async_computation.2 | async-start | bytes 1179648 | tf_op jit(solution)/shard_map/all_gather | solution.py:37
  9.6 122.7 %reduce-scatter.3.cloned.1.call-start = ((), (), s32[]{:S(2)}) async-start(), calls=%async_computation.3 | async-start | bytes 655360 | tf_op jit(solution)/shard_map/reduce_scatter | solution.py:58
  36.9 5.9 %copy-start = (f32[16,128,128]{2,0,1:T(8,128)S(1)}, f32[16,128,128]{2,0,1:T(8,128)}, u32[]{:S(2)}) copy-start(f32[16,128,128]{2,0,1:T(8,128)} %get-tuple-element.172) | copy-start | bytes 3145732 | tf_op jit(solution)/shard_map/while
  45.1 1.0 copy-start.1
  54.6 5.9 %copy-start = (f32[16,128,128]{2,0,1:T(8,128)S(1)}, f32[16,128,128]{2,0,1:T(8,128)}, u32[]{:S(2)}) copy-start(f32[16,128,128]{2,0,1:T(8,128)} %get-tuple-element.172) | copy-start | bytes 3145732 | tf_op jit(solution)/shard_map/while
  62.8 1.0 copy-start.1
  71.5 1.4 copy-start.2
  72.5 94.5 %reduce-scatter.5.cloned.1.call-start = ((), (), s32[]{:S(2)}) async-start(), calls=%async_computation.4 | async-start | bytes 1179648 | tf_op jit(solution)/shard_map/reduce_scatter | solution.py:62
Sparse Core Ops, SparseCore 0:
  10.2 24.7 all-gather.1
  72.6 59.6 reduce-scatter.2
  134.6 32.2 reduce-scatter.4
where the time goes:
time: 176 us; the launch traced here: 175 us
  waiting for transfers between devices  102 us (58%)
  matrix products  26.6 us (15%)
  between operations  14.4 us (8%)
  blocking collectives  11.5 us (7%)
  local copies, waits for them, and re-layouts  11.4 us (6%)
  other arithmetic  8.86 us (5%)
    reduce_scatter x1, waiting for transfers between devices, per_device(): lax.psum_scatter(forward.reshape(-1, feature_width), 'row', scatter_dimen...  58 us
    reduce_scatter x1, waiting for transfers between devices, per_device(): lax.psum_scatter(backward.reshape(-1, feature_width), 'col', scatter_dime...  33.1 us
    all_gather x1, blocking collectives, per_device(): grad_panel = lax.all_gather(grad_scaled, 'row', axis=0, tiled=True)  11.5 us
    all_gather x1, waiting for transfers between devices, per_device(): embed_panel = lax.all_gather(scaled, 'col', axis=0, tiled=True)  10.8 us
    dot_general x2, matrix products, tile_terms(): jnp.einsum('tij,tid->tjd', values, grad_picked, precision=lax.Precision.H...  10.4 us
    dot_general x2, matrix products, tile_terms(): jnp.einsum('tij,tjd->tid', values, picked, precision=lax.Precision.HIGHEST)  7.67 us
    dot_general x2, matrix products, tile_terms(): jnp.einsum('bt,tjd->bjd', col_hot, backward_each, precision=lax.Precision...  4.53 us
    dot_general x2, matrix products, tile_terms(): jnp.einsum('at,tid->aid', row_hot, forward_each, precision=lax.Precision....  3.97 us
  transfers between devices with their start and end apart: 3, of which 3 were waited for; matrix products, arithmetic and copies ran while one was open for 3% of the time, Pallas kernels for 0%

commit v1 on v0

v1 whole, which is shorter than its diff:
```python
import functools

import jax
import jax.numpy as jnp
from jax import lax
from jax.experimental import pallas as pl
from jax.experimental.pallas import tpu as pltpu
from jax.sharding import PartitionSpec as P

F32 = jnp.float32
BF16 = jnp.bfloat16
WHOLE = pl.BlockSpec(memory_space=pltpu.VMEM)
SCALARS = pl.BlockSpec(memory_space=pltpu.SMEM)


def params(mebibytes):
    return pltpu.CompilerParams(vmem_limit_bytes=mebibytes * 2**20)


def cost(flops, moved):
    return pl.CostEstimate(flops=flops, bytes_accessed=moved, transcendentals=0)


def halves(x):
    high = x.astype(BF16)
    return high, (x - high.astype(F32)).astype(BF16)


def product(left, right):
    return jnp.dot(left, right, preferred_element_type=F32)


def row_factors(degree_ref, at, width):
    factors = lax.rsqrt(degree_ref[at : at + 1, :].astype(F32))
    return jnp.broadcast_to(factors, (width, factors.shape[1])).T


def scale_kernel(embed_ref, col_degree_ref, cotangent_ref, row_degree_ref, scaled_ref, grad_ref):
    tile = col_degree_ref.shape[1]
    for x_ref, degree_ref, out_ref in (
        (cotangent_ref, row_degree_ref, grad_ref),
        (embed_ref, col_degree_ref, scaled_ref),
    ):
        for at in range(degree_ref.shape[0]):
            rows = pl.ds(at * tile, tile)
            out_ref[rows, :] = x_ref[rows, :] * row_factors(degree_ref, at, x_ref.shape[1])


def finish_kernel(*refs):
    *part_refs, degree_ref, out_ref = refs
    tile = degree_ref.shape[1]
    for at in range(degree_ref.shape[0]):
        rows = pl.ds(at * tile, tile)
        total = part_refs[0][rows, :]
        for part_ref in part_refs[1:]:
            total = total + part_ref[rows, :]
        out_ref[rows, :] = total * row_factors(degree_ref, at, out_ref.shape[1])


def pair_kernel(kept_ref, got_ref, *out_refs):
    for at, out_ref in enumerate(out_refs):
        out_ref[...] = kept_ref[at] + got_ref[at]


def place(tile_at, shard, tiles):
    return ((tile_at // tiles) ^ shard) * tiles + tile_at % tiles


def split_kernel(tiles, coords_ref, count_ref, values_ref, high_ref, low_ref):
    group, tile, _ = values_ref.shape
    first = pl.program_id(0) * group
    my_row, my_col = lax.axis_index("row"), lax.axis_index("col")
    for slot in range(group):
        row_at = place(coords_ref[0, 0, 0, first + slot], my_row, tiles)
        col_at = place(coords_ref[1, 0, 0, first + slot], my_col, tiles)
        live = first + slot < count_ref[0, 0]
        high, low = halves(jnp.where(live, values_ref[slot], 0.0))
        rows = pl.ds(pl.multiple_of(row_at * tile, tile), tile)
        cols = pl.ds(pl.multiple_of(col_at * tile, tile), tile)
        high_ref[rows, cols] = high
        low_ref[rows, cols] = low


def backward_kernel(tile, *refs):
    *grad_refs, high_ref, low_ref, kept_ref, sent_ref, grads = refs
    width = grad_refs[0].shape[1]
    shard = grad_refs[0].shape[0]

    @pl.when(pl.program_id(0) == 0)
    def _():
        for at, grad_ref in enumerate(grad_refs):
            for first in range(0, shard, tile):
                high, low = halves(grad_ref[pl.ds(first, tile), :].T)
                cols = pl.ds(at * shard + first, tile)
                grads[:width, cols] = high
                grads[width:, cols] = low

    both = product(grads[...], high_ref[...])
    total = both[:width] + both[width:] + product(grads[:width, :], low_ref[...])
    for first in range(0, shard, tile):
        rows = pl.ds(first, tile)
        kept_ref[0, rows, :] = total[:, first : first + tile].T
        sent_ref[0, rows, :] = total[:, shard + first : shard + first + tile].T


def forward_kernel(count, *refs):
    embed_refs, (high_ref, low_ref), out_refs, panel = refs[:count], refs[count : count + 2], refs[count + 2 : -1], refs[-1]
    shard, width = embed_refs[0].shape

    @pl.when(pl.program_id(0) == 0)
    def _():
        for at, embed_ref in enumerate(embed_refs):
            high, low = halves(embed_ref[...])
            panel[pl.ds(at * shard, shard), :width] = high
            panel[pl.ds(at * shard, shard), width:] = low

    both = product(high_ref[...], panel[...])
    total = both[:, :width] + both[:, width:] + product(low_ref[...], panel[:, :width])
    for at, out_ref in enumerate(out_refs):

        @pl.when(pl.program_id(0) == at)
        def _():
            out_ref[...] = total


def slots_kernel(tiles, coords_ref, count_ref, values_ref, embed_ref, grad_ref, forward_ref, backward_ref):
    group, tile, _ = values_ref.shape
    first = pl.program_id(0) * group
    my_row, my_col = lax.axis_index("row"), lax.axis_index("col")

    @pl.when(pl.program_id(0) == 0)
    def _():
        forward_ref[...] = jnp.zeros_like(forward_ref)
        backward_ref[...] = jnp.zeros_like(backward_ref)

    for slot in range(group):

        @pl.when(first + slot < count_ref[0, 0])
        def _():
            row_at = place(coords_ref[0, 0, 0, first + slot], my_row, tiles)
            col_at = place(coords_ref[1, 0, 0, first + slot], my_col, tiles)
            rows = pl.ds(pl.multiple_of(row_at * tile, tile), tile)
            cols = pl.ds(pl.multiple_of(col_at * tile, tile), tile)
            high, low = halves(values_ref[slot])
            embed_high, embed_low = halves(embed_ref[cols, :])
            forward_ref[rows, :] += product(high, embed_high) + product(high, embed_low) + product(low, embed_high)
            high, low = halves(values_ref[slot].T)
            grad_high, grad_low = halves(grad_ref[rows, :])
            backward_ref[cols, :] += product(high, grad_high) + product(high, grad_low) + product(low, grad_high)


def swap(x, axis, mask):
    size = lax.axis_size(axis)
    return lax.ppermute(x, axis, [(at, at ^ mask) for at in range(size)])


def per_device(embed, cotangent, tile_values, tile_coords, tile_count, row_degree, col_degree):
    shard, width = embed.shape
    capacity, tile = tile_values.shape[2:4]
    n_row, n_col = lax.axis_size("row"), lax.axis_size("col")
    pairs = n_col // 2
    tiles = shard // tile
    n_rows, n_cols = shard * n_row, shard * n_col
    values = tile_values.reshape(tile_values.shape[2:])
    row_degree = row_degree.reshape(-1, tile)
    col_degree = col_degree.reshape(-1, tile)
    block = jax.ShapeDtypeStruct((shard, width), F32)
    group = 8
    slot_specs = [SCALARS, SCALARS, pl.BlockSpec((group, tile, tile), lambda at: (at, 0, 0))]

    with jax.named_scope("scale"):
        scaled, grad_scaled = pl.pallas_call(
            scale_kernel,
            out_shape=(block, block),
            in_specs=[WHOLE] * 4,
            out_specs=(WHOLE, WHOLE),
            cost_estimate=cost(0, 4 * shard * width * 4),
        )(embed, col_degree, cotangent, row_degree)

    with jax.named_scope("gather"):
        grads = [grad_scaled] + [swap(grad_scaled, "row", k) for k in range(1, n_row)]
        own = [scaled] + [swap(scaled, "col", 2 * k) for k in range(1, pairs)]
        embeds = [x for mine in own for x in (mine, swap(mine, "col", 1))]

    dense = (n_rows // tile) * (n_cols // tile) <= capacity
    if dense:
        with jax.named_scope("split"):
            table = jax.ShapeDtypeStruct((n_rows, n_cols), BF16)
            table_spec = pl.BlockSpec((n_rows, n_cols), lambda at: (0, 0), pipeline_mode=pl.Buffered(1))
            high, low = pl.pallas_call(
                functools.partial(split_kernel, tiles),
                out_shape=(table, table),
                grid=(capacity // group,),
                in_specs=slot_specs,
                out_specs=(table_spec, table_spec),
                compiler_params=params(24),
                cost_estimate=cost(0, 2 * values.size * 4),
            )(tile_coords, tile_count, values)
        flops = 6 * n_rows * n_cols * width
        with jax.named_scope("backward"):
            halved = jax.ShapeDtypeStruct((pairs, shard, width), F32)
            strip = pl.BlockSpec((n_rows, 2 * shard), lambda at: (0, at))
            halved_spec = pl.BlockSpec((1, shard, width), lambda at: (at, 0, 0))
            kept, sent = pl.pallas_call(
                functools.partial(backward_kernel, tile),
                out_shape=(halved, halved),
                grid=(pairs,),
                in_specs=[WHOLE] * n_row + [strip, strip],
                out_specs=(halved_spec, halved_spec),
                scratch_shapes=[pltpu.VMEM((2 * width, n_rows), BF16)],
                compiler_params=params(24),
                cost_estimate=cost(flops, values.size * 4),
            )(*grads, high, low)
        with jax.named_scope("forward"):
            band = pl.BlockSpec((shard, n_cols), lambda at: (at, 0))
            forwards = pl.pallas_call(
                functools.partial(forward_kernel, n_col),
                out_shape=(block,) * n_row,
                grid=(n_row,),
                in_specs=[WHOLE] * n_col + [band, band],
                out_specs=(WHOLE,) * n_row,
                scratch_shapes=[pltpu.VMEM((n_cols, 2 * width), BF16)],
                compiler_params=params(24),
                cost_estimate=cost(flops, values.size * 4),
            )(*embeds, high, low)
    else:
        with jax.named_scope("slots"):
            forward, backward = pl.pallas_call(
                functools.partial(slots_kernel, tiles),
                out_shape=(
                    jax.ShapeDtypeStruct((n_rows, width), F32),
                    jax.ShapeDtypeStruct((n_cols, width), F32),
                ),
                grid=(capacity // group,),
                in_specs=slot_specs + [WHOLE, WHOLE],
                out_specs=(WHOLE, WHOLE),
                compiler_params=params(40),
                cost_estimate=cost(12 * values.size * width, values.size * 4),
            )(tile_coords, tile_count, values, jnp.concatenate(embeds), jnp.concatenate(grads))
            forwards = list(forward.reshape(n_row, shard, width))
            backward = backward.reshape(pairs, 2, shard, width)
            kept, sent = backward[:, 0], backward[:, 1]

    with jax.named_scope("reduce"):
        paired = pl.pallas_call(
            pair_kernel,
            out_shape=(block,) * pairs,
            in_specs=[WHOLE] * 2,
            out_specs=(WHOLE,) * pairs,
            compiler_params=params(16),
            cost_estimate=cost(0, 3 * pairs * shard * width * 4),
        )(kept, swap(sent, "col", 1))
        grad_parts = [paired[0]] + [swap(paired[k], "col", 2 * k) for k in range(1, pairs)]
        row_parts = [forwards[0]] + [swap(forwards[k], "row", k) for k in range(1, n_row)]

    def finish(parts, degree):
        return pl.pallas_call(
            finish_kernel,
            out_shape=block,
            in_specs=[WHOLE] * (len(parts) + 1),
            out_specs=WHOLE,
            cost_estimate=cost(0, (len(parts) + 1) * shard * width * 4),
        )(*parts, degree)

    with jax.named_scope("finish"):
        return finish(row_parts, row_degree), finish(grad_parts, col_degree)


def solution(mesh):
    return jax.shard_map(
        per_device,
        mesh=mesh,
        in_specs=(
            P(("row", "col"), None),
            P(("col", "row"), None),
            P("col", "row", None, None, None),
            P(None, "col", "row", None),
            P("col", "row"),
            P(("col", "row")),
            P(("row", "col")),
        ),
        out_specs=(P(("col", "row"), None), P(("row", "col"), None)),
        check_vma=False,
    )
```

time: 176 us -> 52.4 us (0.30)
  waiting for transfers between devices: 102 us -> 9.55 us
  matrix products: 26.6 us -> 0 us
  starting transfers between devices: 0.12 us -> 18.2 us
  Pallas kernels: 0 us -> 16.9 us
  between operations: 14.4 us -> 1.44 us
  blocking collectives: 11.5 us -> 0 us
  other arithmetic: 8.86 us -> 0 us
  local copies, waits for them, and re-layouts: 11.4 us -> 6.1 us
    reduce_scatter x2 -> x0, waiting for transfers between devices: 91.1 us -> none  [the longest x1 58 us: per_device(): lax.psum_scatter(forward.reshape(-1, feature_width), 'row', scatter_dimen...]
    dot_general x8 -> x0, matrix products: 26.6 us -> none  [the longest x2 10.4 us: tile_terms(): jnp.einsum('tij,tid->tjd', values, grad_picked, precision=lax.Precision.H...]
    ppermute x0 -> x17, starting transfers between devices: none -> 18.2 us  [swap(): return lax.ppermute(x, axis, [(at, at ^ mask) for at in range(size)])]
    pallas_call x0 -> x7, Pallas kernels: none -> 16.9 us  [the longest x1 4.61 us: per_device(): pl.pallas_call(functools.partial(split_kernel, tiles), out_shape=(table,...]
    all_gather x1 -> x0, blocking collectives: 11.5 us -> none  [per_device(): grad_panel = lax.all_gather(grad_scaled, 'row', axis=0, tiled=True)]
    all_gather x1 -> x0, waiting for transfers between devices: 10.8 us -> none  [per_device(): embed_panel = lax.all_gather(scaled, 'col', axis=0, tiled=True)]
    ppermute x0 -> x17, waiting for transfers between devices: none -> 9.55 us  [swap(): return lax.ppermute(x, axis, [(at, at ^ mask) for at in range(size)])]
    mul x4 -> x0, other arithmetic: 5.98 us -> none  [the longest x1 1.66 us: per_device(): scaled = embed * lax.rsqrt(col_degree.astype(jnp.float32))[:, None]]
  transfers between devices with their start and end apart: 3 -> 17, of which waited for: 3 -> 4; matrix products, arithmetic and copies ran while one was open for 3% -> 0% of each run, Pallas kernels for 0% -> 25%
where the time goes in v1:
time: 52.4 us; the launch traced here: 52.2 us
  starting transfers between devices  18.2 us (35%)
  Pallas kernels  16.9 us (32%)
  waiting for transfers between devices  9.55 us (18%)
  local copies, waits for them, and re-layouts  6.1 us (12%)
  between operations  1.44 us (3%)
    ppermute x17, starting transfers between devices, swap(): return lax.ppermute(x, axis, [(at, at ^ mask) for at in range(size)])  18.2 us
    ppermute x17, waiting for transfers between devices, swap(): return lax.ppermute(x, axis, [(at, at ^ mask) for at in range(size)])  9.55 us
    unnamed x24, local copies, waits for them, and re-layouts  6.1 us
    pallas_call x1, Pallas kernels, per_device(): pl.pallas_call(functools.partial(split_kernel, tiles), out_shape=(table,...  4.61 us
    pallas_call x2, Pallas kernels, finish(): pl.pallas_call(finish_kernel, out_shape=block, in_specs=[WHOLE] * (len(pa...  3.72 us
    pallas_call x1, Pallas kernels, per_device(): pl.pallas_call(functools.partial(backward_kernel, tile), out_shape=(halve...  3.6 us
    pallas_call x1, Pallas kernels, per_device(): pl.pallas_call(functools.partial(forward_kernel, n_col), out_shape=(block...  3.14 us
    pallas_call x1, Pallas kernels, per_device(): pl.pallas_call(scale_kernel, out_shape=(block, block), in_specs=[WHOLE] *...  1.8 us
  transfers between devices with their start and end apart: 17, of which 4 were waited for; matrix products, arithmetic and copies ran while one was open for 0% of the time, Pallas kernels for 25%

profile of v1, /device:TPU:0, one launch (start us, length us, event | category | flops | bytes accessed | tf_op | source)
XLA Modules:
  0.0 52.2 jit_solution(13527567998328472273)
XLA Ops:
  0.6 1.8 %scale.1 = (f32[256,128]{1,0:T(8,128)}, f32[256,128]{1,0:T(8,128)}) custom-call(f32[256,128]{1,0:T(8,128)} %embed_ref.1, s32[2,128]{1,0:T(2,128)} %bitcast.6, f32[256,128]{1,0:T(8,128)} %cotangent_ref.1, s32[2,128]{1,0:T(2,128)} %bitcast.4), custom_call_target="tpu_custom_call" | custom-call | bytes 524288 | tf_op jit(solution)/shard_map/scale/pallas_call | solution.py:172
  2.4 2.9 %collective-permute-start.10 = (f32[256,128]{1,0:T(8,128)}, f32[256,128]{1,0:T(8,128)S(1)}, u32[]{:S(2)}, u32[]{:S(2)}) collective-permute-start(f32[256,128]{1,0:T(8,128)} %get-tuple-element.23.refs_0_), channel_id=1, source_target_pairs={{0,8},{8,0},{16,24},{24,16},{1,9},{9,1},{17,25},{25,17},{2,10},{10... | collective-permute-start | bytes 393224 | tf_op jit(solution)/shard_map/gather/ppermute | solution.py:154
  5.4 1.5 %collective-permute-start.11 = (f32[256,128]{1,0:T(8,128)}, f32[256,128]{1,0:T(8,128)S(1)}, u32[]{:S(2)}, u32[]{:S(2)}) collective-permute-start(f32[256,128]{1,0:T(8,128)} %get-tuple-element.23.refs_0_), channel_id=1, source_target_pairs={{0,16},{8,24},{16,0},{24,8},{1,17},{9,25},{17,1},{25,9},{2,18},{10... | collective-permute-start | bytes 393224 | tf_op jit(solution)/shard_map/gather/ppermute | solution.py:154
  6.9 0.0 collective-permute-start.12
  6.9 2.1 %collective-permute-start.1 = (f32[256,128]{1,0:T(8,128)}, f32[256,128]{1,0:T(8,128)S(1)}, u32[]{:S(2)}, u32[]{:S(2)}) collective-permute-start(f32[256,128]{1,0:T(8,128)} %get-tuple-element.16.refs_0_), channel_id=1, source_target_pairs={{0,2},{1,3},{2,0},{3,1},{4,6},{5,7},{6,4},{7,5},{8,10},{9,11},{10,... | collective-permute-start | bytes 393224 | tf_op jit(solution)/shard_map/gather/ppermute | solution.py:154
  8.9 2.6 %collective-permute-start.3 = (f32[256,128]{1,0:T(8,128)}, f32[256,128]{1,0:T(8,128)S(1)}, u32[]{:S(2)}, u32[]{:S(2)}) collective-permute-start(f32[256,128]{1,0:T(8,128)} %get-tuple-element.16.refs_0_), channel_id=1, source_target_pairs={{0,4},{1,5},{2,6},{3,7},{4,0},{5,1},{6,2},{7,3},{8,12},{9,13},{10,... | collective-permute-start | bytes 393224 | tf_op jit(solution)/shard_map/gather/ppermute | solution.py:154
  12.2 0.0 copy-start
  12.2 3.4 %copy-done = f32[1,1,128,128,128]{4,3,2,1,0:T(8,128)S(1)} copy-done((f32[1,1,128,128,128]{4,3,2,1,0:T(8,128)S(1)}, f32[1,1,128,128,128]{4,3,2,1,0:T(8,128)}, u32[]{:S(2)}) %copy-start) | copy-done | bytes 8388632
  15.6 0.7 %copy-done.5 = s32[2,1,1,128]{3,2,1,0:T(1,128)S(1)} copy-done((s32[2,1,1,128]{3,2,1,0:T(1,128)S(1)}, s32[2,1,1,128]{3,2,1,0:T(1,128)}, u32[]{:S(2)}) %copy-start.5) | copy-done | bytes 1048
  16.2 4.6 %split.1 = (bf16[1024,2048]{1,0:T(8,128)(2,1)S(1)}, bf16[1024,2048]{1,0:T(8,128)(2,1)S(1)}) custom-call(s32[2,1,1,128]{3,2,1,0:T(1,128)S(1)} %copy-done.5, s32[1,1]{1,0:T(1,128)S(6)} %copy.9.count_ref, f32[128,128,128]{2,1,0:T(8,128)S(1)} %bitcast.3), custom_call_target="tpu_custom_call" | custom-call | bytes 16777216 | tf_op jit(solution)/shard_map/split/pallas_call | solution.py:190
  20.9 0.0 collective-permute-done.10.refs_1_
  20.9 0.1 collective-permute-start.5
  21.0 0.0 collective-permute-done.11.refs_2_
  21.0 0.0 collective-permute-done.12.refs_3_
  21.0 3.6 %backward.1 = (f32[4,256,128]{2,1,0:T(8,128)S(1)}, f32[4,256,128]{2,1,0:T(8,128)S(1)}) custom-call(f32[256,128]{1,0:T(8,128)S(1)} %copy-done.2, f32[256,128]{1,0:T(8,128)S(1)} %collective-permute-done.10.refs_1_, f32[256,128]{1,0:T(8,128)S(1)} %collective-permute-done.11.refs_2_, f32[256,128]{1,0:T(8,128)S(1)} %collective-permute-done.12.refs_3_, ...), custom_call_target="tpu_custom_call" | custom-call | flops 1610612736 | bytes 8388608 | tf_op jit(solution)/shard_map/backward/pallas_call | solution.py:204
  24.6 0.1 collective-permute-start.13
  24.7 0.5 collective-permute-start
  25.2 0.0 collective-permute-done.1.refs_2_
  25.2 0.1 collective-permute-start.2
  25.3 0.0 collective-permute-done.3.refs_4_
  25.3 0.4 collective-permute-start.4
  25.7 2.1 %collective-permute-done.5.refs_6_ = f32[256,128]{1,0:T(8,128)S(1)} collective-permute-done((f32[256,128]{1,0:T(8,128)S(1)}, f32[256,128]{1,0:T(8,128)S(1)}, u32[]{:S(2)}, u32[]{:S(2)}) %collective-permute-start.5) | collective-permute-done | bytes 131104 | tf_op jit(solution)/shard_map/gather/ppermute | solution.py:154
  27.8 0.0 collective-permute-start.6
  27.8 0.0 collective-permute-done.refs_1_
  27.8 0.0 collective-permute-done.2.refs_3_
  27.8 0.0 collective-permute-done.4.refs_5_
  27.9 1.3 %collective-permute-done.6.refs_7_ = f32[256,128]{1,0:T(8,128)S(1)} collective-permute-done((f32[256,128]{1,0:T(8,128)S(1)}, f32[256,128]{1,0:T(8,128)S(1)}, u32[]{:S(2)}, u32[]{:S(2)}) %collective-permute-start.6) | collective-permute-done | bytes 131104 | tf_op jit(solution)/shard_map/gather/ppermute | solution.py:154
  29.2 3.1 %forward.1 = (f32[256,128]{1,0:T(8,128)S(1)}, f32[256,128]{1,0:T(8,128)S(1)}, f32[256,128]{1,0:T(8,128)S(1)}, f32[256,128]{1,0:T(8,128)S(1)}) custom-call(f32[256,128]{1,0:T(8,128)S(1)} %copy-done.1, f32[256,128]{1,0:T(8,128)S(1)} %collective-permute-done.refs_1_, f32[256,128]{1,0:T(8,128)S(1)} %collective-permute-done.1.refs_2_, ...), custom_call_target="tpu_custom_call" | custom-call | flops 1610612736 | bytes 8388608 | tf_op jit(solution)/shard_map/forward/pallas_call | solution.py:216
  32.3 0.0 copy-start.3
  32.3 1.5 %collective-permute-start.7 = (f32[256,128]{1,0:T(8,128)S(1)}, f32[256,128]{1,0:T(8,128)S(1)}, u32[]{:S(2)}, u32[]{:S(2)}) collective-permute-start(f32[256,128]{1,0:T(8,128)S(1)} %get-tuple-element.20), channel_id=1, source_target_pairs={{0,8},{8,0},{16,24},{24,16},{1,9},{9,1},{17,25},{25,17},{2,10},{10... | collective-permute-start | bytes 393224 | tf_op jit(solution)/shard_map/reduce/ppermute | solution.py:154
  33.8 1.5 %collective-permute-start.8 = (f32[256,128]{1,0:T(8,128)S(1)}, f32[256,128]{1,0:T(8,128)S(1)}, u32[]{:S(2)}, u32[]{:S(2)}) collective-permute-start(f32[256,128]{1,0:T(8,128)S(1)} %get-tuple-element.21), channel_id=1, source_target_pairs={{0,16},{8,24},{16,0},{24,8},{1,17},{9,25},{17,1},{25,9},{2,18},{10... | collective-permute-start | bytes 393224 | tf_op jit(solution)/shard_map/reduce/ppermute | solution.py:154
  35.4 0.5 collective-permute-start.9
  35.9 0.0 collective-permute-done.13.got_ref
  35.9 0.1 reduce.1
  36.0 0.6 %copy-done.4 = f32[256,128]{1,0:T(8,128)} copy-done((f32[256,128]{1,0:T(8,128)}, f32[256,128]{1,0:T(8,128)S(1)}, u32[]{:S(2)}) %copy-start.4) | copy-done | bytes 131096
  36.6 0.7 %collective-permute-start.14 = (f32[256,128]{1,0:T(8,128)S(1)}, f32[256,128]{1,0:T(8,128)S(1)}, u32[]{:S(2)}, u32[]{:S(2)}) collective-permute-start(f32[256,128]{1,0:T(8,128)S(1)} %get-tuple-element.27), channel_id=1, source_target_pairs={{0,2},{1,3},{2,0},{3,1},{4,6},{5,7},{6,4},{7,5},{8,10},{9,11},{10,... | collective-permute-start | bytes 393224 | tf_op jit(solution)/shard_map/reduce/ppermute | solution.py:154
  37.3 1.8 %collective-permute-start.15 = (f32[256,128]{1,0:T(8,128)S(1)}, f32[256,128]{1,0:T(8,128)S(1)}, u32[]{:S(2)}, u32[]{:S(2)}) collective-permute-start(f32[256,128]{1,0:T(8,128)S(1)} %get-tuple-element.28), channel_id=1, source_target_pairs={{0,4},{1,5},{2,6},{3,7},{4,0},{5,1},{6,2},{7,3},{8,12},{9,13},{10,... | collective-permute-start | bytes 393224 | tf_op jit(solution)/shard_map/reduce/ppermute | solution.py:154
  39.1 0.0 collective-permute-done.7.refs_1_
  39.1 1.9 %collective-permute-start.16 = (f32[256,128]{1,0:T(8,128)S(1)}, f32[256,128]{1,0:T(8,128)S(1)}, u32[]{:S(2)}, u32[]{:S(2)}) collective-permute-start(f32[256,128]{1,0:T(8,128)S(1)} %get-tuple-element.29), channel_id=1, source_target_pairs={{0,6},{1,7},{2,4},{3,5},{4,2},{5,3},{6,0},{7,1},{8,14},{9,15},{10,... | collective-permute-start | bytes 393224 | tf_op jit(solution)/shard_map/reduce/ppermute | solution.py:154
  41.0 0.9 %collective-permute-done.8.refs_2_ = f32[256,128]{1,0:T(8,128)S(1)} collective-permute-done((f32[256,128]{1,0:T(8,128)S(1)}, f32[256,128]{1,0:T(8,128)S(1)}, u32[]{:S(2)}, u32[]{:S(2)}) %collective-permute-start.8) | collective-permute-done | bytes 131104 | tf_op jit(solution)/shard_map/reduce/ppermute | solution.py:154
  41.9 0.0 collective-permute-done.9.refs_3_
  41.9 0.6 %copy-done.7 = f32[256,128]{1,0:T(8,128)} copy-done((f32[256,128]{1,0:T(8,128)}, f32[256,128]{1,0:T(8,128)S(1)}, u32[]{:S(2)}) %copy-start.7) | copy-done | bytes 131096
  42.6 0.1 copy-done.8
  42.6 1.9 %finish.2 = f32[256,128]{1,0:T(8,128)} custom-call(f32[256,128]{1,0:T(8,128)} %copy-done.3, f32[256,128]{1,0:T(8,128)} %copy-done.6, f32[256,128]{1,0:T(8,128)} %copy-done.7, f32[256,128]{1,0:T(8,128)} %copy-done.8, s32[2,128]{1,0:T(2,128)} %bitcast.5), custom_call_target="tpu_custom_call" | custom-call | bytes 655360 | tf_op jit(solution)/shard_map/finish/pallas_call | solution.py:257
  44.5 5.2 %collective-permute-done.15.refs_2_ = f32[256,128]{1,0:T(8,128)S(1)} collective-permute-done((f32[256,128]{1,0:T(8,128)S(1)}, f32[256,128]{1,0:T(8,128)S(1)}, u32[]{:S(2)}, u32[]{:S(2)}) %collective-permute-start.15) | collective-permute-done | bytes 131104 | tf_op jit(solution)/shard_map/reduce/ppermute | solution.py:154
  49.7 0.6 %copy-done.10 = f32[256,128]{1,0:T(8,128)} copy-done((f32[256,128]{1,0:T(8,128)}, f32[256,128]{1,0:T(8,128)S(1)}, u32[]{:S(2)}) %copy-start.10) | copy-done | bytes 131096
  50.3 0.1 copy-done.11
  50.3 1.9 %finish.3 = f32[256,128]{1,0:T(8,128)} custom-call(f32[256,128]{1,0:T(8,128)} %copy-done.4, f32[256,128]{1,0:T(8,128)} %copy-done.9, f32[256,128]{1,0:T(8,128)} %copy-done.10, f32[256,128]{1,0:T(8,128)} %copy-done.11, s32[2,128]{1,0:T(2,128)} %bitcast.7), custom_call_target="tpu_custom_call" | custom-call | bytes 655360 | tf_op jit(solution)/shard_map/finish/pallas_call | solution.py:257
  (17 shorter events, 0.0 us)
Async XLA Ops:
  2.4 18.4 %collective-permute-start.10 = (f32[256,128]{1,0:T(8,128)}, f32[256,128]{1,0:T(8,128)S(1)}, u32[]{:S(2)}, u32[]{:S(2)}) collective-permute-start(f32[256,128]{1,0:T(8,128)} %get-tuple-element.23.refs_0_), channel_id=1, source_target_pairs={{0,8},{8,0},{16,24},{24,16},{1,9},{9,1},{17,25},{25,17},{2,10},{10... | collective-permute-start | bytes 393224 | tf_op jit(solution)/shard_map/gather/ppermute | solution.py:154
  5.4 15.6 %collective-permute-start.11 = (f32[256,128]{1,0:T(8,128)}, f32[256,128]{1,0:T(8,128)S(1)}, u32[]{:S(2)}, u32[]{:S(2)}) collective-permute-start(f32[256,128]{1,0:T(8,128)} %get-tuple-element.23.refs_0_), channel_id=1, source_target_pairs={{0,16},{8,24},{16,0},{24,8},{1,17},{9,25},{17,1},{25,9},{2,18},{10... | collective-permute-start | bytes 393224 | tf_op jit(solution)/shard_map/gather/ppermute | solution.py:154
  6.9 14.1 %collective-permute-start.12 = (f32[256,128]{1,0:T(8,128)}, f32[256,128]{1,0:T(8,128)S(1)}, u32[]{:S(2)}, u32[]{:S(2)}) collective-permute-start(f32[256,128]{1,0:T(8,128)} %get-tuple-element.23.refs_0_), channel_id=1, source_target_pairs={{0,24},{8,16},{16,8},{24,0},{1,25},{9,17},{17,9},{25,1},{2,26},{10... | collective-permute-start | bytes 393224 | tf_op jit(solution)/shard_map/gather/ppermute | solution.py:154
  6.9 18.3 %collective-permute-start.1 = (f32[256,128]{1,0:T(8,128)}, f32[256,128]{1,0:T(8,128)S(1)}, u32[]{:S(2)}, u32[]{:S(2)}) collective-permute-start(f32[256,128]{1,0:T(8,128)} %get-tuple-element.16.refs_0_), channel_id=1, source_target_pairs={{0,2},{1,3},{2,0},{3,1},{4,6},{5,7},{6,4},{7,5},{8,10},{9,11},{10,... | collective-permute-start | bytes 393224 | tf_op jit(solution)/shard_map/gather/ppermute | solution.py:154
  8.9 16.3 %collective-permute-start.3 = (f32[256,128]{1,0:T(8,128)}, f32[256,128]{1,0:T(8,128)S(1)}, u32[]{:S(2)}, u32[]{:S(2)}) collective-permute-start(f32[256,128]{1,0:T(8,128)} %get-tuple-element.16.refs_0_), channel_id=1, source_target_pairs={{0,4},{1,5},{2,6},{3,7},{4,0},{5,1},{6,2},{7,3},{8,12},{9,13},{10,... | collective-permute-start | bytes 393224 | tf_op jit(solution)/shard_map/gather/ppermute | solution.py:154
  12.2 3.4 %copy-start = (f32[1,1,128,128,128]{4,3,2,1,0:T(8,128)S(1)}, f32[1,1,128,128,128]{4,3,2,1,0:T(8,128)}, u32[]{:S(2)}) copy-start(f32[1,1,128,128,128]{4,3,2,1,0:T(8,128)} %param.9) | copy-start | bytes 25165828
  15.6 0.7 %copy-start.5 = (s32[2,1,1,128]{3,2,1,0:T(1,128)S(1)}, s32[2,1,1,128]{3,2,1,0:T(1,128)}, u32[]{:S(2)}) copy-start(s32[2,1,1,128]{3,2,1,0:T(1,128)} %coords_ref.1) | copy-start | bytes 3076
  16.2 4.6 %copy-start.1 = (f32[256,128]{1,0:T(8,128)S(1)}, f32[256,128]{1,0:T(8,128)}, u32[]{:S(2)}) copy-start(f32[256,128]{1,0:T(8,128)} %get-tuple-element.16.refs_0_) | copy-start | bytes 393220
  16.2 4.7 %copy-start.2 = (f32[256,128]{1,0:T(8,128)S(1)}, f32[256,128]{1,0:T(8,128)}, u32[]{:S(2)}) copy-start(f32[256,128]{1,0:T(8,128)} %get-tuple-element.23.refs_0_) | copy-start | bytes 393220
  20.9 6.9 %collective-permute-start.5 = (f32[256,128]{1,0:T(8,128)S(1)}, f32[256,128]{1,0:T(8,128)S(1)}, u32[]{:S(2)}, u32[]{:S(2)}) collective-permute-start(f32[256,128]{1,0:T(8,128)S(1)} %copy-done.1), channel_id=1, source_target_pairs={{0,6},{1,7},{2,4},{3,5},{4,2},{5,3},{6,0},{7,1},{8,14},{9,15},{10,... | collective-permute-start | bytes 393224 | tf_op jit(solution)/shard_map/gather/ppermute | solution.py:154
  24.6 11.3 %collective-permute-start.13 = (f32[4,256,128]{2,1,0:T(8,128)S(1)}, f32[4,256,128]{2,1,0:T(8,128)S(1)}, u32[]{:S(2)}, u32[]{:S(2)}) collective-permute-start(f32[4,256,128]{2,1,0:T(8,128)S(1)} %get-tuple-element.25), channel_id=1, source_target_pairs={{0,1},{1,0},{2,3},{3,2},{4,5},{5,4},{6,7},{7,6},{8,9},{9,8},{10,11... | collective-permute-start | bytes 1572872 | tf_op jit(solution)/shard_map/reduce/ppermute | solution.py:154
  24.7 3.1 %collective-permute-start = (f32[256,128]{1,0:T(8,128)S(1)}, f32[256,128]{1,0:T(8,128)S(1)}, u32[]{:S(2)}, u32[]{:S(2)}) collective-permute-start(f32[256,128]{1,0:T(8,128)S(1)} %copy-done.1), channel_id=1, source_target_pairs={{0,1},{1,0},{2,3},{3,2},{4,5},{5,4},{6,7},{7,6},{8,9},{9,8},{10,11... | collective-permute-start | bytes 393224 | tf_op jit(solution)/shard_map/gather/ppermute | solution.py:154
  25.2 2.7 %collective-permute-start.2 = (f32[256,128]{1,0:T(8,128)S(1)}, f32[256,128]{1,0:T(8,128)S(1)}, u32[]{:S(2)}, u32[]{:S(2)}) collective-permute-start(f32[256,128]{1,0:T(8,128)S(1)} %collective-permute-done.1.refs_2_), channel_id=1, source_target_pairs={{0,1},{1,0},{2,3},{3,2},{4,5},{5,4},{6,7},{7,6},{8,9},{9,8},{10,11... | collective-permute-start | bytes 393224 | tf_op jit(solution)/shard_map/gather/ppermute | solution.py:154
  25.3 2.6 %collective-permute-start.4 = (f32[256,128]{1,0:T(8,128)S(1)}, f32[256,128]{1,0:T(8,128)S(1)}, u32[]{:S(2)}, u32[]{:S(2)}) collective-permute-start(f32[256,128]{1,0:T(8,128)S(1)} %collective-permute-done.3.refs_4_), channel_id=1, source_target_pairs={{0,1},{1,0},{2,3},{3,2},{4,5},{5,4},{6,7},{7,6},{8,9},{9,8},{10,11... | collective-permute-start | bytes 393224 | tf_op jit(solution)/shard_map/gather/ppermute | solution.py:154
  27.8 1.3 %collective-permute-start.6 = (f32[256,128]{1,0:T(8,128)S(1)}, f32[256,128]{1,0:T(8,128)S(1)}, u32[]{:S(2)}, u32[]{:S(2)}) collective-permute-start(f32[256,128]{1,0:T(8,128)S(1)} %collective-permute-done.5.refs_6_), channel_id=1, source_target_pairs={{0,1},{1,0},{2,3},{3,2},{4,5},{5,4},{6,7},{7,6},{8,9},{9,8},{10,11... | collective-permute-start | bytes 393224 | tf_op jit(solution)/shard_map/gather/ppermute | solution.py:154
  32.3 3.6 %copy-start.3 = (f32[256,128]{1,0:T(8,128)}, f32[256,128]{1,0:T(8,128)S(1)}, u32[]{:S(2)}) copy-start(f32[256,128]{1,0:T(8,128)S(1)} %get-tuple-element.19.refs_0_) | copy-start | bytes 393220
  32.3 6.8 %collective-permute-start.7 = (f32[256,128]{1,0:T(8,128)S(1)}, f32[256,128]{1,0:T(8,128)S(1)}, u32[]{:S(2)}, u32[]{:S(2)}) collective-permute-start(f32[256,128]{1,0:T(8,128)S(1)} %get-tuple-element.20), channel_id=1, source_target_pairs={{0,8},{8,0},{16,24},{24,16},{1,9},{9,1},{17,25},{25,17},{2,10},{10... | collective-permute-start | bytes 393224 | tf_op jit(solution)/shard_map/reduce/ppermute | solution.py:154
  33.8 8.1 %collective-permute-start.8 = (f32[256,128]{1,0:T(8,128)S(1)}, f32[256,128]{1,0:T(8,128)S(1)}, u32[]{:S(2)}, u32[]{:S(2)}) collective-permute-start(f32[256,128]{1,0:T(8,128)S(1)} %get-tuple-element.21), channel_id=1, source_target_pairs={{0,16},{8,24},{16,0},{24,8},{1,17},{9,25},{17,1},{25,9},{2,18},{10... | collective-permute-start | bytes 393224 | tf_op jit(solution)/shard_map/reduce/ppermute | solution.py:154
  35.4 6.5 %collective-permute-start.9 = (f32[256,128]{1,0:T(8,128)S(1)}, f32[256,128]{1,0:T(8,128)S(1)}, u32[]{:S(2)}, u32[]{:S(2)}) collective-permute-start(f32[256,128]{1,0:T(8,128)S(1)} %get-tuple-element.22), channel_id=1, source_target_pairs={{0,24},{8,16},{16,8},{24,0},{1,25},{9,17},{17,9},{25,1},{2,26},{10... | collective-permute-start | bytes 393224 | tf_op jit(solution)/shard_map/reduce/ppermute | solution.py:154
  36.0 0.7 %copy-start.4 = (f32[256,128]{1,0:T(8,128)}, f32[256,128]{1,0:T(8,128)S(1)}, u32[]{:S(2)}) copy-start(f32[256,128]{1,0:T(8,128)S(1)} %get-tuple-element.26.refs_0_) | copy-start | bytes 393220
  36.6 7.9 %collective-permute-start.14 = (f32[256,128]{1,0:T(8,128)S(1)}, f32[256,128]{1,0:T(8,128)S(1)}, u32[]{:S(2)}, u32[]{:S(2)}) collective-permute-start(f32[256,128]{1,0:T(8,128)S(1)} %get-tuple-element.27), channel_id=1, source_target_pairs={{0,2},{1,3},{2,0},{3,1},{4,6},{5,7},{6,4},{7,5},{8,10},{9,11},{10,... | collective-permute-start | bytes 393224 | tf_op jit(solution)/shard_map/reduce/ppermute | solution.py:154
  37.3 12.3 %collective-permute-start.15 = (f32[256,128]{1,0:T(8,128)S(1)}, f32[256,128]{1,0:T(8,128)S(1)}, u32[]{:S(2)}, u32[]{:S(2)}) collective-permute-start(f32[256,128]{1,0:T(8,128)S(1)} %get-tuple-element.28), channel_id=1, source_target_pairs={{0,4},{1,5},{2,6},{3,7},{4,0},{5,1},{6,2},{7,3},{8,12},{9,13},{10,... | collective-permute-start | bytes 393224 | tf_op jit(solution)/shard_map/reduce/ppermute | solution.py:154
  39.1 2.8 %copy-start.6 = (f32[256,128]{1,0:T(8,128)}, f32[256,128]{1,0:T(8,128)S(1)}, u32[]{:S(2)}) copy-start(f32[256,128]{1,0:T(8,128)S(1)} %collective-permute-done.7.refs_1_) | copy-start | bytes 393220
  39.1 10.5 %collective-permute-start.16 = (f32[256,128]{1,0:T(8,128)S(1)}, f32[256,128]{1,0:T(8,128)S(1)}, u32[]{:S(2)}, u32[]{:S(2)}) collective-permute-start(f32[256,128]{1,0:T(8,128)S(1)} %get-tuple-element.29), channel_id=1, source_target_pairs={{0,6},{1,7},{2,4},{3,5},{4,2},{5,3},{6,0},{7,1},{8,14},{9,15},{10,... | collective-permute-start | bytes 393224 | tf_op jit(solution)/shard_map/reduce/ppermute | solution.py:154
  41.9 0.7 %copy-start.7 = (f32[256,128]{1,0:T(8,128)}, f32[256,128]{1,0:T(8,128)S(1)}, u32[]{:S(2)}) copy-start(f32[256,128]{1,0:T(8,128)S(1)} %collective-permute-done.8.refs_2_) | copy-start | bytes 393220
  41.9 0.7 %copy-start.8 = (f32[256,128]{1,0:T(8,128)}, f32[256,128]{1,0:T(8,128)S(1)}, u32[]{:S(2)}) copy-start(f32[256,128]{1,0:T(8,128)S(1)} %collective-permute-done.9.refs_3_) | copy-start | bytes 393220
  44.5 5.2 %copy-start.9 = (f32[256,128]{1,0:T(8,128)}, f32[256,128]{1,0:T(8,128)S(1)}, u32[]{:S(2)}) copy-start(f32[256,128]{1,0:T(8,128)S(1)} %collective-permute-done.14.refs_1_) | copy-start | bytes 393220
  49.6 0.7 %copy-start.10 = (f32[256,128]{1,0:T(8,128)}, f32[256,128]{1,0:T(8,128)S(1)}, u32[]{:S(2)}) copy-start(f32[256,128]{1,0:T(8,128)S(1)} %collective-permute-done.15.refs_2_) | copy-start | bytes 393220
  49.6 0.7 %copy-start.11 = (f32[256,128]{1,0:T(8,128)}, f32[256,128]{1,0:T(8,128)S(1)}, u32[]{:S(2)}) copy-start(f32[256,128]{1,0:T(8,128)S(1)} %collective-permute-done.16.refs_3_) | copy-start | bytes 393220

commit v2 on v1

v2 whole, which is shorter than its diff:
```python
import functools

import jax
import jax.numpy as jnp
from jax import lax
from jax.experimental import pallas as pl
from jax.experimental.pallas import tpu as pltpu
from jax.sharding import PartitionSpec as P

F32 = jnp.float32
BF16 = jnp.bfloat16
WHOLE = pl.BlockSpec(memory_space=pltpu.VMEM)
SCALARS = pl.BlockSpec(memory_space=pltpu.SMEM)


def params(mebibytes):
    return pltpu.CompilerParams(vmem_limit_bytes=mebibytes * 2**20)


def cost(flops, moved):
    return pl.CostEstimate(flops=flops, bytes_accessed=moved, transcendentals=0)


def halves(x):
    high = x.astype(BF16)
    return high, (x - high.astype(F32)).astype(BF16)


def product(left, right):
    return jnp.dot(left, right, preferred_element_type=F32)


def row_factors(degree_ref, at, width):
    factors = lax.rsqrt(degree_ref[at : at + 1, :].astype(F32))
    return jnp.broadcast_to(factors, (width, factors.shape[1])).T


def scale_kernel(embed_ref, col_degree_ref, cotangent_ref, row_degree_ref, scaled_ref, grad_ref):
    tile = col_degree_ref.shape[1]
    for x_ref, degree_ref, out_ref in (
        (cotangent_ref, row_degree_ref, grad_ref),
        (embed_ref, col_degree_ref, scaled_ref),
    ):
        for at in range(degree_ref.shape[0]):
            rows = pl.ds(at * tile, tile)
            scaled = x_ref[rows, :] * row_factors(degree_ref, at, x_ref.shape[1])
            for copy in range(out_ref.shape[0]):
                out_ref[copy, rows, :] = scaled


def finish_kernel(parts_ref, degree_ref, out_ref):
    tile = degree_ref.shape[1]
    for at in range(degree_ref.shape[0]):
        rows = pl.ds(at * tile, tile)
        total = parts_ref[0, rows, :]
        for part in range(1, parts_ref.shape[0]):
            total = total + parts_ref[part, rows, :]
        out_ref[rows, :] = total * row_factors(degree_ref, at, out_ref.shape[1])


def pair_kernel(kept_ref, got_ref, out_ref):
    out_ref[...] = kept_ref[...] + got_ref[...]


def col_place(tile_at, tiles, my_core, pairs):
    shard = tile_at // tiles
    return (((shard % 2) ^ my_core) * pairs + shard // 2) * tiles + tile_at % tiles


def split_kernel(tiles, pairs, coords_ref, count_ref, values_ref, high_ref, low_ref):
    group, tile, _ = values_ref.shape
    first = pl.program_id(0) * group
    my_core = lax.axis_index("col") % 2
    for slot in range(group):
        row_at = coords_ref[0, 0, 0, first + slot]
        col_at = col_place(coords_ref[1, 0, 0, first + slot], tiles, my_core, pairs)
        live = first + slot < count_ref[0, 0]
        high, low = halves(jnp.where(live, values_ref[slot], 0.0))
        rows = pl.ds(pl.multiple_of(row_at * tile, tile), tile)
        cols = pl.ds(pl.multiple_of(col_at * tile, tile), tile)
        high_ref[rows, cols] = high
        low_ref[rows, cols] = low


def backward_kernel(tile, grads_ref, high_ref, low_ref, out_ref, grads):
    n_row, shard, width = grads_ref.shape

    @pl.when(pl.program_id(0) == 0)
    def _():
        for at in range(n_row):
            for first in range(0, shard, tile):
                high, low = halves(grads_ref[at, pl.ds(first, tile), :].T)
                cols = pl.ds(at * shard + first, tile)
                grads[:width, cols] = high
                grads[width:, cols] = low

    both = product(grads[...], high_ref[...])
    total = both[:width] + both[width:] + product(grads[:width, :], low_ref[...])
    for first in range(0, shard, tile):
        out_ref[0, pl.ds(first, tile), :] = total[:, first : first + tile].T


def forward_kernel(embeds_ref, high_ref, low_ref, *refs):
    before_refs, out_ref, panel = refs[:-2], refs[-2], refs[-1]
    count, shard, width = embeds_ref.shape

    @pl.when(pl.program_id(0) == 0)
    def _():
        for at in range(count):
            high, low = halves(embeds_ref[at])
            panel[pl.ds(at * shard, shard), :width] = high
            panel[pl.ds(at * shard, shard), width:] = low

    both = product(high_ref[...], panel[...])
    total = both[:, :width] + both[:, width:] + product(low_ref[...], panel[:, :width])
    for before_ref in before_refs:
        total = total + before_ref[0]
    out_ref[0] = total


def slots_kernel(tiles, pairs, coords_ref, count_ref, values_ref, embed_ref, grad_ref, forward_ref, backward_ref):
    group, tile, _ = values_ref.shape
    first = pl.program_id(0) * group
    my_core = lax.axis_index("col") % 2

    @pl.when(pl.program_id(0) == 0)
    def _():
        forward_ref[...] = jnp.zeros_like(forward_ref)
        backward_ref[...] = jnp.zeros_like(backward_ref)

    for slot in range(group):

        @pl.when(first + slot < count_ref[0, 0])
        def _():
            row_at = coords_ref[0, 0, 0, first + slot]
            col_at = col_place(coords_ref[1, 0, 0, first + slot], tiles, my_core, pairs)
            rows = pl.ds(pl.multiple_of(row_at * tile, tile), tile)
            cols = pl.ds(pl.multiple_of(col_at * tile, tile), tile)
            high, low = halves(values_ref[slot])
            embed_high, embed_low = halves(embed_ref[cols, :])
            forward_ref[rows, :] += product(high, embed_high) + product(high, embed_low) + product(low, embed_high)
            high, low = halves(values_ref[slot].T)
            grad_high, grad_low = halves(grad_ref[rows, :])
            backward_ref[cols, :] += product(high, grad_high) + product(high, grad_low) + product(low, grad_high)


def exchange(x, axis, groups=None):
    return lax.all_to_all(x, axis, split_axis=0, concat_axis=0, axis_index_groups=groups, tiled=True)


def per_device(embed, cotangent, tile_values, tile_coords, tile_count, row_degree, col_degree):
    shard, width = embed.shape
    capacity, tile = tile_values.shape[2:4]
    n_row, n_col = lax.axis_size("row"), lax.axis_size("col")
    pairs = n_col // 2
    same_core = [list(range(core, n_col, 2)) for core in range(2)]
    tiles = shard // tile
    n_rows, n_cols = shard * n_row, shard * n_col
    values = tile_values.reshape(tile_values.shape[2:])
    row_degree = row_degree.reshape(-1, tile)
    col_degree = col_degree.reshape(-1, tile)
    in_row = jax.ShapeDtypeStruct((n_row, shard, width), F32)
    in_col = jax.ShapeDtypeStruct((pairs, shard, width), F32)
    group = 8
    slot_specs = [SCALARS, SCALARS, pl.BlockSpec((group, tile, tile), lambda at: (at, 0, 0))]
    one_block = pl.BlockSpec((1, shard, width), lambda at: (at, 0, 0))

    def swap_cores(x):
        return lax.ppermute(x, "col", [(at, at ^ 1) for at in range(n_col)])

    with jax.named_scope("scale"):
        scaled, grad_scaled = pl.pallas_call(
            scale_kernel,
            out_shape=(in_col, in_row),
            in_specs=[WHOLE] * 4,
            out_specs=(WHOLE, WHOLE),
            compiler_params=params(8),
            cost_estimate=cost(0, 2 * (n_row + pairs) * shard * width * 4),
        )(embed, col_degree, cotangent, row_degree)

    with jax.named_scope("gather"):
        grads = exchange(grad_scaled, "row")
        own = exchange(scaled, "col", same_core)
        other = swap_cores(own)

    dense = (n_rows // tile) * (n_cols // tile) <= capacity
    if dense:
        with jax.named_scope("split"):
            table = jax.ShapeDtypeStruct((n_rows, n_cols), BF16)
            table_spec = pl.BlockSpec((n_rows, n_cols), lambda at: (0, 0), pipeline_mode=pl.Buffered(1))
            high, low = pl.pallas_call(
                functools.partial(split_kernel, tiles, pairs),
                out_shape=(table, table),
                grid=(capacity // group,),
                in_specs=slot_specs,
                out_specs=(table_spec, table_spec),
                compiler_params=params(24),
                cost_estimate=cost(0, 2 * values.size * 4),
            )(tile_coords, tile_count, pltpu.with_memory_space_constraint(values, pltpu.HBM))
        flops = 3 * n_rows * n_cols * width

        def backward_half(first):
            strip = pl.BlockSpec((n_rows, shard), lambda at: (0, first + at))
            return pl.pallas_call(
                functools.partial(backward_kernel, tile),
                out_shape=in_col,
                grid=(pairs,),
                in_specs=[WHOLE, strip, strip],
                out_specs=one_block,
                scratch_shapes=[pltpu.VMEM((2 * width, n_rows), BF16)],
                compiler_params=params(16),
                cost_estimate=cost(flops, values.size * 2),
            )(grads, high, low)

        def forward_half(embeds, half, before):
            band = pl.BlockSpec((shard, n_cols // 2), lambda at: (at, half))
            return pl.pallas_call(
                forward_kernel,
                out_shape=in_row,
                grid=(n_row,),
                in_specs=[WHOLE, band, band] + [one_block] * len(before),
                out_specs=one_block,
                scratch_shapes=[pltpu.VMEM((n_cols // 2, 2 * width), BF16)],
                compiler_params=params(16),
                cost_estimate=cost(flops, values.size * 2),
            )(embeds, high, low, *before)

        with jax.named_scope("backward"):
            sent = backward_half(pairs)
            kept = backward_half(0)
        with jax.named_scope("forward"):
            forward = forward_half(other, 1, [forward_half(own, 0, [])])
    else:
        with jax.named_scope("slots"):
            forward, backward = pl.pallas_call(
                functools.partial(slots_kernel, tiles, pairs),
                out_shape=(
                    jax.ShapeDtypeStruct((n_rows, width), F32),
                    jax.ShapeDtypeStruct((n_cols, width), F32),
                ),
                grid=(capacity // group,),
                in_specs=slot_specs + [WHOLE, WHOLE],
                out_specs=(WHOLE, WHOLE),
                compiler_params=params(40),
                cost_estimate=cost(12 * values.size * width, values.size * 4),
            )(tile_coords, tile_count, values, jnp.concatenate([own, other]).reshape(n_cols, width), grads.reshape(n_rows, width))
            forward = forward.reshape(n_row, shard, width)
            kept, sent = backward.reshape(2, pairs, shard, width)

    with jax.named_scope("reduce"):
        paired = pl.pallas_call(
            pair_kernel,
            out_shape=in_col,
            in_specs=[WHOLE] * 2,
            out_specs=WHOLE,
            compiler_params=params(16),
            cost_estimate=cost(0, 3 * pairs * shard * width * 4),
        )(kept, swap_cores(sent))
        grad_parts = exchange(paired, "col", same_core)
        row_parts = exchange(forward, "row")

    def finish(parts, degree):
        return pl.pallas_call(
            finish_kernel,
            out_shape=jax.ShapeDtypeStruct((shard, width), F32),
            in_specs=[WHOLE] * 2,
            out_specs=WHOLE,
            compiler_params=params(8),
            cost_estimate=cost(0, parts.size * 4),
        )(parts, degree)

    with jax.named_scope("finish"):
        return finish(row_parts, row_degree), finish(grad_parts, col_degree)


def solution(mesh):
    return jax.shard_map(
        per_device,
        mesh=mesh,
        in_specs=(
            P(("row", "col"), None),
            P(("col", "row"), None),
            P("col", "row", None, None, None),
            P(None, "col", "row", None),
            P("col", "row"),
            P(("col", "row")),
            P(("row", "col")),
        ),
        out_specs=(P(("col", "row"), None), P(("row", "col"), None)),
        check_vma=False,
    )
```

time: 52.4 us -> 90.1 us (1.72)
  blocking collectives: 0 us -> 20.6 us
  local copies, waits for them, and re-layouts: 6.1 us -> 16.5 us
  Pallas kernels: 16.9 us -> 24.9 us
  starting transfers between devices: 18.2 us -> 12 us
  waiting for transfers between devices: 9.55 us -> 13.9 us
    all_to_all x0 -> x1, blocking collectives: none -> 20.6 us  [exchange(): lax.all_to_all(x, axis, split_axis=0, concat_axis=0, axis_index_groups=gr...]
    ppermute x17 -> x2, starting transfers between devices: 18.2 us -> 0.57 us  [swap_cores(): return lax.ppermute(x, 'col', [(at, at ^ 1) for at in range(n_col)])]
    all_to_all x0 -> x3, waiting for transfers between devices: none -> 13.9 us  [exchange(): lax.all_to_all(x, axis, split_axis=0, concat_axis=0, axis_index_groups=gr...]
    all_to_all x0 -> x3, starting transfers between devices: none -> 11.4 us  [exchange(): lax.all_to_all(x, axis, split_axis=0, concat_axis=0, axis_index_groups=gr...]
    unnamed x24 -> x26, local copies, waits for them, and re-layouts: 6.1 us -> 16.5 us
    ppermute x17 -> x2, waiting for transfers between devices: 9.55 us -> 0.01 us  [swap_cores(): return lax.ppermute(x, 'col', [(at, at ^ 1) for at in range(n_col)])]
    pallas_call x7 -> x9, Pallas kernels: 16.9 us -> 24.9 us  [the longest x1 11.2 us: per_device(): pl.pallas_call(functools.partial(split_kernel, tiles, pairs), out_shape=(...]
  transfers between devices with their start and end apart: 17 -> 5, of which waited for: 4 -> 2; matrix products, arithmetic and copies ran while one was open for 0% -> 0% of each run, Pallas kernels for 25% -> 26%
where the time goes in v2:
time: 90.1 us; the launch traced here: 89.3 us
  Pallas kernels  24.9 us (28%)
  blocking collectives  20.6 us (23%)
  local copies, waits for them, and re-layouts  16.5 us (18%)
  waiting for transfers between devices  13.9 us (15%)
  starting transfers between devices  12 us (13%)
  between operations  1.39 us (2%)
    all_to_all x1, blocking collectives, exchange(): lax.all_to_all(x, axis, split_axis=0, concat_axis=0, axis_index_groups=gr...  20.6 us
    unnamed x26, local copies, waits for them, and re-layouts  16.5 us
    all_to_all x3, waiting for transfers between devices, exchange(): lax.all_to_all(x, axis, split_axis=0, concat_axis=0, axis_index_groups=gr...  13.9 us
    all_to_all x3, starting transfers between devices, exchange(): lax.all_to_all(x, axis, split_axis=0, concat_axis=0, axis_index_groups=gr...  11.4 us
    pallas_call x1, Pallas kernels, per_device(): pl.pallas_call(functools.partial(split_kernel, tiles, pairs), out_shape=(...  11.2 us
    pallas_call x2, Pallas kernels, backward_half(): pl.pallas_call(functools.partial(backward_kernel, tile), out_shape=in_col...  5.23 us
    pallas_call x2, Pallas kernels, forward_half(): pl.pallas_call(forward_kernel, out_shape=in_row, grid=(n_row,), in_specs=...  5.17 us
  transfers between devices with their start and end apart: 5, of which 2 were waited for; matrix products, arithmetic and copies ran while one was open for 0% of the time, Pallas kernels for 26%

profile of v2, /device:TPU:0, one launch (start us, length us, event | category | flops | bytes accessed | tf_op | source)
XLA Modules:
  0.0 89.3 jit_solution(14289224059138526015)
XLA Ops:
  0.6 0.0 copy-start.6
  0.6 0.9 %copy-done.6 = f32[256,128]{1,0:T(8,128)S(1)} copy-done((f32[256,128]{1,0:T(8,128)S(1)}, f32[256,128]{1,0:T(8,128)}, u32[]{:S(2)}) %copy-start.6) | copy-done | bytes 131096
  1.5 0.0 copy-start.7
  1.5 0.9 %copy-done.7 = f32[256,128]{1,0:T(8,128)S(1)} copy-done((f32[256,128]{1,0:T(8,128)S(1)}, f32[256,128]{1,0:T(8,128)}, u32[]{:S(2)}) %copy-start.7) | copy-done | bytes 131096
  2.4 0.0 copy-start.8
  2.4 0.7 copy-done.8
  3.1 0.0 copy-start.10
  3.1 0.7 copy-done.10
  3.8 1.0 %scale.1 = (f32[4,256,128]{2,1,0:T(8,128)S(1)}, f32[4,256,128]{2,1,0:T(8,128)}) custom-call(f32[256,128]{1,0:T(8,128)S(1)} %copy-done.6, s32[2,128]{1,0:T(2,128)S(1)} %bitcast.5, f32[256,128]{1,0:T(8,128)S(1)} %copy-done.7, s32[2,128]{1,0:T(2,128)S(1)} %bitcast.3), custom_call_target="tpu_custom_call" | custom-call | bytes 2097152 | tf_op jit(solution)/shard_map/scale/pallas_call | solution.py:172
  4.8 20.6 %all_to_all.20.embeds_ref = f32[4,256,128]{2,1,0:T(8,128)S(1)} all-to-all(f32[4,256,128]{2,1,0:T(8,128)S(1)} %get-tuple-element.6), channel_id=1, replica_groups={{0,2,4,6},{1,3,5,7},{8,10,12,14},{9,11,13,15},{16,18,20,22},{17,19,21,2..., dimensions={0} | all-to-all | bytes 1048576 | tf_op jit(solution)/shard_map/gather/all_to_all | solution.py:148
  25.4 3.7 %all-to-all-start.2 = ((f32[4,256,128]{2,1,0:T(8,128)}), f32[4,256,128]{2,1,0:T(8,128)S(1)}, u32[]{:S(2)}, u32[]{:S(2)}) async-start(f32[4,256,128]{2,1,0:T(8,128)} %get-tuple-element.9), calls=%async_computation.2 | async-start | bytes 1048576 | tf_op jit(solution)/shard_map/gather/all_to_all | solution.py:148
  29.1 0.0 collective-permute-start
  29.7 0.0 copy-start.12
  29.7 0.7 copy-done.12
  30.4 11.2 %split.1 = (bf16[1024,2048]{1,0:T(8,128)(2,1)S(1)}, bf16[1024,2048]{1,0:T(8,128)(2,1)S(1)}) custom-call(s32[2,1,1,128]{3,2,1,0:T(1,128)S(1)} %copy-done.12, s32[1,1]{1,0:T(1,128)S(6)} %copy.9.count_ref, f32[128,128,128]{2,1,0:T(8,128)} %bitcast.7), custom_call_target="tpu_custom_call" | custom-call | bytes 16777216 | tf_op jit(solution)/shard_map/split/pallas_call | solution.py:191
  41.6 0.0 copy-start
  41.6 1.9 %copy-done = bf16[1024,2048]{1,0:T(8,128)(2,1)} copy-done((bf16[1024,2048]{1,0:T(8,128)(2,1)}, bf16[1024,2048]{1,0:T(8,128)(2,1)S(1)}, u32[]{:S(2)}) %copy-start) | copy-done | bytes 4194328
  43.5 0.0 copy-start.3
  43.5 2.0 %copy-done.3 = bf16[1024,2048]{1,0:T(8,128)(2,1)} copy-done((bf16[1024,2048]{1,0:T(8,128)(2,1)}, bf16[1024,2048]{1,0:T(8,128)(2,1)S(1)}, u32[]{:S(2)}) %copy-start.3) | copy-done | bytes 4194328
  45.5 0.0 all-to-all-done.2.grads_ref
  45.5 0.0 copy-start.1
  45.5 2.2 %copy-done.1 = bf16[1024,2048]{1,0:T(8,128)(2,1)S(1)} copy-done((bf16[1024,2048]{1,0:T(8,128)(2,1)S(1)}, bf16[1024,2048]{1,0:T(8,128)(2,1)}, u32[]{:S(2)}) %copy-start.1) | copy-done | bytes 4194328
  47.7 0.0 copy-start.4
  47.7 2.2 %copy-done.4 = bf16[1024,2048]{1,0:T(8,128)(2,1)S(1)} copy-done((bf16[1024,2048]{1,0:T(8,128)(2,1)S(1)}, bf16[1024,2048]{1,0:T(8,128)(2,1)}, u32[]{:S(2)}) %copy-start.4) | copy-done | bytes 4194328
  49.9 2.6 %backward.3 = f32[4,256,128]{2,1,0:T(8,128)S(1)} custom-call(f32[4,256,128]{2,1,0:T(8,128)S(1)} %all-to-all-done.2.grads_ref, bf16[1024,2048]{1,0:T(8,128)(2,1)S(1)} %copy-done.1, bf16[1024,2048]{1,0:T(8,128)(2,1)S(1)} %copy-done.4), custom_call_target="tpu_custom_call" | custom-call | flops 805306368 | bytes 4194304 | tf_op jit(solution)/shard_map/backward/pallas_call | solution.py:204
  52.6 0.6 collective-permute-start.1
  53.1 2.2 %forward.2.refs_0_ = f32[4,256,128]{2,1,0:T(8,128)S(1)} custom-call(f32[4,256,128]{2,1,0:T(8,128)S(1)} %all_to_all.20.embeds_ref, bf16[1024,2048]{1,0:T(8,128)(2,1)S(1)} %copy-done.1, bf16[1024,2048]{1,0:T(8,128)(2,1)S(1)} %copy-done.4), custom_call_target="tpu_custom_call" | custom-call | flops 805306368 | bytes 4194304 | tf_op jit(solution)/shard_map/forward/pallas_call | solution.py:217
  55.3 0.0 collective-permute-done.embeds_ref
  55.3 3.0 %forward.3 = f32[4,256,128]{2,1,0:T(8,128)} custom-call(f32[4,256,128]{2,1,0:T(8,128)S(1)} %collective-permute-done.embeds_ref, bf16[1024,2048]{1,0:T(8,128)(2,1)S(1)} %copy-done.1, bf16[1024,2048]{1,0:T(8,128)(2,1)S(1)} %copy-done.4, f32[4,256,128]{2,1,0:T(8,128)S(1)} %forward.2.refs_0_), custom_call_target="tpu_custom_call" | custom-call | flops 805306368 | bytes 4194304 | tf_op jit(solution)/shard_map/forward/pallas_call | solution.py:217
  58.3 4.2 %all-to-all-start.1 = ((f32[4,256,128]{2,1,0:T(8,128)}), f32[4,256,128]{2,1,0:T(8,128)S(1)}, u32[]{:S(2)}, u32[]{:S(2)}) async-start(f32[4,256,128]{2,1,0:T(8,128)} %forward.3), calls=%async_computation.1 | async-start | bytes 1048576 | tf_op jit(solution)/shard_map/reduce/all_to_all | solution.py:148
  62.5 0.0 copy-start.2
  62.5 2.2 %copy-done.2 = bf16[1024,2048]{1,0:T(8,128)(2,1)S(1)} copy-done((bf16[1024,2048]{1,0:T(8,128)(2,1)S(1)}, bf16[1024,2048]{1,0:T(8,128)(2,1)}, u32[]{:S(2)}) %copy-start.2) | copy-done | bytes 4194328
  64.7 0.0 copy-start.5
  64.7 2.2 %copy-done.5 = bf16[1024,2048]{1,0:T(8,128)(2,1)S(1)} copy-done((bf16[1024,2048]{1,0:T(8,128)(2,1)S(1)}, bf16[1024,2048]{1,0:T(8,128)(2,1)}, u32[]{:S(2)}) %copy-start.5) | copy-done | bytes 4194328
  66.9 0.0 copy-start.9
  66.9 0.0 copy-start.11
  66.9 2.6 %backward.2.kept_ref = f32[4,256,128]{2,1,0:T(8,128)S(1)} custom-call(f32[4,256,128]{2,1,0:T(8,128)S(1)} %all-to-all-done.2.grads_ref, bf16[1024,2048]{1,0:T(8,128)(2,1)S(1)} %copy-done.2, bf16[1024,2048]{1,0:T(8,128)(2,1)S(1)} %copy-done.5), custom_call_target="tpu_custom_call" | custom-call | flops 805306368 | bytes 4194304 | tf_op jit(solution)/shard_map/backward/pallas_call | solution.py:204
  69.5 0.0 collective-permute-done.1.got_ref
  69.5 0.9 reduce.1
  70.4 0.3 all-to-all-done.1.parts_ref
  70.7 3.5 %all-to-all-start.3 = ((f32[4,256,128]{2,1,0:T(8,128)}), f32[4,256,128]{2,1,0:T(8,128)S(1)}, u32[]{:S(2)}, u32[]{:S(2)}) async-start(f32[4,256,128]{2,1,0:T(8,128)} %reduce.1), calls=%async_computation.3 | async-start | bytes 1048576 | tf_op jit(solution)/shard_map/reduce/all_to_all | solution.py:148
  74.2 0.0 copy-done.9
  74.2 0.8 finish.2
  75.0 13.5 %all-to-all-done.3.parts_ref = f32[4,256,128]{2,1,0:T(8,128)S(1)} async-done(((f32[4,256,128]{2,1,0:T(8,128)}), f32[4,256,128]{2,1,0:T(8,128)S(1)}, u32[]{:S(2)}, u32[]{:S(2)}) %all-to-all-start.3) | async-done | bytes 524320 | tf_op jit(solution)/shard_map/reduce/all_to_all | solution.py:148
  88.5 0.0 copy-done.11
  88.5 0.8 finish.3
Async XLA Ops:
  0.6 0.9 %copy-start.6 = (f32[256,128]{1,0:T(8,128)S(1)}, f32[256,128]{1,0:T(8,128)}, u32[]{:S(2)}) copy-start(f32[256,128]{1,0:T(8,128)} %embed_ref.1) | copy-start | bytes 393220
  1.5 0.9 %copy-start.7 = (f32[256,128]{1,0:T(8,128)S(1)}, f32[256,128]{1,0:T(8,128)}, u32[]{:S(2)}) copy-start(f32[256,128]{1,0:T(8,128)} %cotangent_ref.1) | copy-start | bytes 393220
  2.4 0.7 copy-start.8
  3.1 0.7 copy-start.10
  25.4 20.2 %all-to-all-start.2 = ((f32[4,256,128]{2,1,0:T(8,128)}), f32[4,256,128]{2,1,0:T(8,128)S(1)}, u32[]{:S(2)}, u32[]{:S(2)}) async-start(f32[4,256,128]{2,1,0:T(8,128)} %get-tuple-element.9), calls=%async_computation.2 | async-start | bytes 1048576 | tf_op jit(solution)/shard_map/gather/all_to_all | solution.py:148
  29.1 26.2 %collective-permute-start = (f32[4,256,128]{2,1,0:T(8,128)S(1)}, f32[4,256,128]{2,1,0:T(8,128)S(1)}, u32[]{:S(2)}, u32[]{:S(2)}) collective-permute-start(f32[4,256,128]{2,1,0:T(8,128)S(1)} %all_to_all.20.embeds_ref), channel_id=1, source_target_pairs={{0,1},{1,0},{2,3},{3,2},{4,5},{5,4},{6,7},{7,6},{8,9},{9,8},{10,11... | collective-permute-start | bytes 1572872 | tf_op jit(solution)/shard_map/gather/ppermute | solution.py:169
  29.7 0.7 copy-start.12
  41.6 1.9 %copy-start = (bf16[1024,2048]{1,0:T(8,128)(2,1)}, bf16[1024,2048]{1,0:T(8,128)(2,1)S(1)}, u32[]{:S(2)}) copy-start(bf16[1024,2048]{1,0:T(8,128)(2,1)S(1)} %get-tuple-element.7.high_ref) | copy-start | bytes 12582916
  43.5 2.0 %copy-start.3 = (bf16[1024,2048]{1,0:T(8,128)(2,1)}, bf16[1024,2048]{1,0:T(8,128)(2,1)S(1)}, u32[]{:S(2)}) copy-start(bf16[1024,2048]{1,0:T(8,128)(2,1)S(1)} %get-tuple-element.8.low_ref) | copy-start | bytes 12582916
  45.5 2.2 %copy-start.1 = (bf16[1024,2048]{1,0:T(8,128)(2,1)S(1)}, bf16[1024,2048]{1,0:T(8,128)(2,1)}, u32[]{:S(2)}) copy-start(bf16[1024,2048]{1,0:T(8,128)(2,1)} %copy-done) | copy-start | bytes 12582916
  47.7 2.2 %copy-start.4 = (bf16[1024,2048]{1,0:T(8,128)(2,1)S(1)}, bf16[1024,2048]{1,0:T(8,128)(2,1)}, u32[]{:S(2)}) copy-start(bf16[1024,2048]{1,0:T(8,128)(2,1)} %copy-done.3) | copy-start | bytes 12582916
  52.6 17.0 %collective-permute-start.1 = (f32[4,256,128]{2,1,0:T(8,128)S(1)}, f32[4,256,128]{2,1,0:T(8,128)S(1)}, u32[]{:S(2)}, u32[]{:S(2)}) collective-permute-start(f32[4,256,128]{2,1,0:T(8,128)S(1)} %backward.3), channel_id=1, source_target_pairs={{0,1},{1,0},{2,3},{3,2},{4,5},{5,4},{6,7},{7,6},{8,9},{9,8},{10,11... | collective-permute-start | bytes 1572872 | tf_op jit(solution)/shard_map/reduce/ppermute | solution.py:169
  58.3 12.4 %all-to-all-start.1 = ((f32[4,256,128]{2,1,0:T(8,128)}), f32[4,256,128]{2,1,0:T(8,128)S(1)}, u32[]{:S(2)}, u32[]{:S(2)}) async-start(f32[4,256,128]{2,1,0:T(8,128)} %forward.3), calls=%async_computation.1 | async-start | bytes 1048576 | tf_op jit(solution)/shard_map/reduce/all_to_all | solution.py:148
  62.5 2.2 %copy-start.2 = (bf16[1024,2048]{1,0:T(8,128)(2,1)S(1)}, bf16[1024,2048]{1,0:T(8,128)(2,1)}, u32[]{:S(2)}) copy-start(bf16[1024,2048]{1,0:T(8,128)(2,1)} %copy-done) | copy-start | bytes 12582916
  64.7 2.2 %copy-start.5 = (bf16[1024,2048]{1,0:T(8,128)(2,1)S(1)}, bf16[1024,2048]{1,0:T(8,128)(2,1)}, u32[]{:S(2)}) copy-start(bf16[1024,2048]{1,0:T(8,128)(2,1)} %copy-done.3) | copy-start | bytes 12582916
  66.9 7.3 %copy-start.9 = (s32[256]{0:T(256)S(1)}, s32[256]{0:T(256)}, u32[]{:S(2)}) copy-start(s32[256]{0:T(256)} %param.12) | copy-start | bytes 3076
  66.9 21.6 %copy-start.11 = (s32[256]{0:T(256)S(1)}, s32[256]{0:T(256)}, u32[]{:S(2)}) copy-start(s32[256]{0:T(256)} %param.13) | copy-start | bytes 3076
  70.7 17.8 %all-to-all-start.3 = ((f32[4,256,128]{2,1,0:T(8,128)}), f32[4,256,128]{2,1,0:T(8,128)S(1)}, u32[]{:S(2)}, u32[]{:S(2)}) async-start(f32[4,256,128]{2,1,0:T(8,128)} %reduce.1), calls=%async_computation.3 | async-start | bytes 1048576 | tf_op jit(solution)/shard_map/reduce/all_to_all | solution.py:148

commit v3 on v0

v3 whole, which is shorter than its diff:
```python
import functools
import math

import jax
import jax.numpy as jnp
from jax import lax
from jax.experimental import pallas as pl
from jax.experimental.pallas import tpu as pltpu
from jax.sharding import PartitionSpec as P

F32 = jnp.float32
BF16 = jnp.bfloat16
WHOLE = pl.BlockSpec(memory_space=pltpu.VMEM)
ANYWHERE = pl.BlockSpec(memory_space=pl.ANY)
SCALARS = pl.BlockSpec(memory_space=pltpu.SMEM)


def params(mebibytes):
    return pltpu.CompilerParams(vmem_limit_bytes=mebibytes * 2**20)


def cost(flops, moved):
    return pl.CostEstimate(flops=flops, bytes_accessed=moved, transcendentals=0)


def halves(x):
    high = x.astype(BF16)
    return high, (x - high.astype(F32)).astype(BF16)


def product(left, right):
    return jnp.dot(left, right, preferred_element_type=F32)


def row_factors(degree_ref, at, width):
    factors = lax.rsqrt(degree_ref[at : at + 1, :].astype(F32))
    return jnp.broadcast_to(factors, (width, factors.shape[1])).T


def scale_kernel(tiles, pairs, *refs):
    count_ref, in_refs, (grad_ref, scaled_ref, row_factor_ref, col_factor_ref, plan_ref) = refs[0], refs[1:6], refs[6:11]
    bufs, sems = refs[11:16], refs[16]
    copies = [pltpu.make_async_copy(*pair, sems.at[at]) for at, pair in enumerate(zip(in_refs, bufs))]
    for copy in copies:
        copy.start()
    for copy in copies:
        copy.wait()
    cotangent, embed, row_degree, col_degree, coords = bufs
    for x_buf, degree_buf, out_ref, factor_ref in (
        (embed, col_degree, scaled_ref, col_factor_ref),
        (cotangent, row_degree, grad_ref, row_factor_ref),
    ):
        tile = degree_buf.shape[1]
        for at in range(degree_buf.shape[0]):
            rows = pl.ds(at * tile, tile)
            factors = row_factors(degree_buf, at, x_buf.shape[1])
            factor_ref[rows, :] = factors
            out_ref[rows, :] = x_buf[rows, :] * factors
    capacity = coords.shape[-1]
    plan_ref[0:1, :] = row_place(coords[0, 0], tiles) * tile
    plan_ref[1:2, :] = col_place(coords[1, 0], tiles, pairs) * tile
    live = lax.broadcasted_iota(jnp.int32, (1, capacity), 1) < count_ref[0, 0]
    plan_ref[2:3, :] = live.astype(jnp.int32)


def finish_kernel(*refs):
    *part_refs, factor_ref, out_ref = refs
    total = part_refs[0][...]
    for part_ref in part_refs[1:]:
        total = total + part_ref[...]
    out_ref[...] = total * factor_ref[...]


def add_kernel(x_ref, y_ref, out_ref):
    out_ref[...] = x_ref[...] + y_ref[...]


def pair_kernel(kept_ref, got_ref, *out_refs):
    for at, out_ref in enumerate(out_refs):
        out_ref[...] = kept_ref[at] + got_ref[at]


def stack_kernel(*refs):
    *part_refs, out_ref = refs
    for at, part_ref in enumerate(part_refs):
        out_ref[at] = part_ref[...]


def row_place(tile_at, tiles):
    return tile_at ^ (lax.axis_index("row") * tiles)


def col_place(tile_at, tiles, pairs):
    tile_at = tile_at ^ (lax.axis_index("col") * tiles)
    shard = lax.shift_right_logical(tile_at, tiles.bit_length() - 1)
    return ((shard & 1) * pairs + lax.shift_right_logical(shard, 1)) * tiles + (tile_at & (tiles - 1))


def split_kernel(plan_ref, values_ref, high_ref, low_ref, buf, sems):
    capacity, tile, _ = values_ref.shape
    groups = sems.shape[0]
    group = capacity // groups
    copies = []
    for at in range(groups):
        slots = pl.ds(at * group, group)
        copies.append(pltpu.make_async_copy(values_ref.at[slots], buf.at[slots], sems.at[at]))
        copies[-1].start()
    for at, copy in enumerate(copies):
        copy.wait()

        @pl.loop(at * group, (at + 1) * group, unroll=2)
        def _(slot):
            rows = pl.ds(pl.multiple_of(plan_ref[0, slot], tile), tile)
            cols = pl.ds(pl.multiple_of(plan_ref[1, slot], tile), tile)
            high, low = halves(jnp.where(plan_ref[2, slot] > 0, buf[slot], 0.0))
            high_ref[rows, cols] = high
            low_ref[rows, cols] = low


def flip_kernel(tile, *refs):
    *grad_refs, block_ref, out_ref, copy_ref = refs
    copy_ref[...] = block_ref[...]
    shard, width = grad_refs[0].shape
    for at, grad_ref in enumerate(grad_refs):
        for first in range(0, shard, tile):
            high, low = halves(grad_ref[pl.ds(first, tile), :].T)
            cols = pl.ds(at * shard + first, tile)
            out_ref[:width, cols] = high
            out_ref[width:, cols] = low


def backward_kernel(first, tile, grads_ref, high_ref, low_ref, out_ref):
    count, shard, width = out_ref.shape
    for at in range(count):
        cols = pl.ds((first + at) * shard, shard)
        both = product(grads_ref[...], high_ref[:, cols])
        total = both[:width] + both[width:] + product(grads_ref[:width, :], low_ref[:, cols])
        for row in range(0, shard, tile):
            out_ref[at, pl.ds(row, tile), :] = total[:, row : row + tile].T


def forward_kernel(first, bands, embeds_ref, high_ref, low_ref, *refs):
    before_refs, out_refs, panel = refs[: -1 - bands], refs[-1 - bands : -1], refs[-1]
    count, shard, width = embeds_ref.shape
    for at in range(count):
        high, low = halves(embeds_ref[at])
        panel[pl.ds(at * shard, shard), :width] = high
        panel[pl.ds(at * shard, shard), width:] = low
    cols = pl.ds(first * shard, count * shard)
    for at, out_ref in enumerate(out_refs):
        rows = pl.ds(at * shard, shard)
        both = product(high_ref[rows, cols], panel[...])
        total = both[:, :width] + both[:, width:] + product(low_ref[rows, cols], panel[:, :width])
        if before_refs:
            total = total + before_refs[at][...]
        out_ref[...] = total


def slots_kernel(tiles, pairs, coords_ref, count_ref, values_ref, embed_ref, grad_ref, forward_ref, backward_ref):
    group, tile, _ = values_ref.shape
    first = pl.program_id(0) * group

    @pl.when(pl.program_id(0) == 0)
    def _():
        forward_ref[...] = jnp.zeros_like(forward_ref)
        backward_ref[...] = jnp.zeros_like(backward_ref)

    for slot in range(group):

        @pl.when(first + slot < count_ref[0, 0])
        def _():
            row_at = row_place(coords_ref[0, 0, 0, first + slot], tiles)
            col_at = col_place(coords_ref[1, 0, 0, first + slot], tiles, pairs)
            rows = pl.ds(pl.multiple_of(row_at * tile, tile), tile)
            cols = pl.ds(pl.multiple_of(col_at * tile, tile), tile)
            high, low = halves(values_ref[slot])
            embed_high, embed_low = halves(embed_ref[cols, :])
            forward_ref[rows, :] += product(high, embed_high) + product(high, embed_low) + product(low, embed_high)
            high, low = halves(values_ref[slot].T)
            grad_high, grad_low = halves(grad_ref[rows, :])
            backward_ref[cols, :] += product(high, grad_high) + product(high, grad_low) + product(low, grad_high)


def swap(x, axis, mask):
    return lax.ppermute(x, axis, [(at, at ^ mask) for at in range(lax.axis_size(axis))])


def call(kernel, out_shape, args, mebibytes=16, flops=0, scratch=(), specs=None, after=None):
    outs = out_shape if isinstance(out_shape, tuple) else (out_shape,)
    moved = sum(x.size * x.dtype.itemsize for x in (*args, *outs))
    specs = specs or [WHOLE] * len(args)
    body = kernel
    if after is not None:
        args, specs = (after, *args), [ANYWHERE, *specs]

        def body(_, *refs):
            kernel(*refs)

    return pl.pallas_call(
        body,
        out_shape=out_shape,
        in_specs=specs,
        out_specs=tuple(WHOLE for _ in outs) if isinstance(out_shape, tuple) else WHOLE,
        scratch_shapes=scratch,
        compiler_params=params(mebibytes),
        cost_estimate=cost(20 * flops, 20 * moved),
    )(*args)


def per_device(embed, cotangent, tile_values, tile_coords, tile_count, row_degree, col_degree):
    shard, width = embed.shape
    capacity, tile = tile_values.shape[2:4]
    n_row, n_col = lax.axis_size("row"), lax.axis_size("col")
    pairs = n_col // 2
    tiles = shard // tile
    n_rows, n_cols = shard * n_row, shard * n_col
    values = tile_values.reshape(tile_values.shape[2:])
    block = jax.ShapeDtypeStruct((shard, width), F32)

    def blocks(count):
        return jax.ShapeDtypeStruct((count, shard, width), F32)

    with jax.named_scope("scale"):
        args = (cotangent, embed, row_degree.reshape(-1, tile), col_degree.reshape(-1, tile), tile_coords)
        grad_scaled, scaled, row_factor, col_factor, plan = call(
            functools.partial(scale_kernel, tiles, pairs),
            (block,) * 4 + (jax.ShapeDtypeStruct((3, capacity), jnp.int32),),
            (tile_count, *(pltpu.with_memory_space_constraint(x, pltpu.HBM) for x in args)),
            mebibytes=4,
            specs=[SCALARS] + [pl.BlockSpec(memory_space=pltpu.HBM)] * len(args),
            scratch=[pltpu.VMEM(x.shape, x.dtype) for x in args] + [pltpu.SemaphoreType.DMA((len(args),))],
        )

    far = pairs // 2
    with jax.named_scope("gather"):
        crossed = swap(scaled, "col", 2 * far)
        grads = [grad_scaled] + [swap(grad_scaled, "row", k) for k in range(1, n_row)]
    dense = (n_rows // tile) * (n_cols // tile) <= capacity
    if dense:
        table = jax.ShapeDtypeStruct((n_rows, n_cols), BF16)
        groups = math.gcd(capacity, 8)
        with jax.named_scope("split"):
            high, low = call(
                split_kernel,
                (table, table),
                (plan, pltpu.with_memory_space_constraint(values, pltpu.HBM)),
                mebibytes=32,
                specs=[SCALARS, pl.BlockSpec(memory_space=pltpu.HBM)],
                scratch=[pltpu.VMEM(values.shape, F32), pltpu.SemaphoreType.DMA((groups,))],
            )
        with jax.named_scope("flip"):
            flipped, crossed = call(
                functools.partial(flip_kernel, tile),
                (jax.ShapeDtypeStruct((2 * width, n_rows), BF16), block),
                (*grads, crossed),
                after=low,
            )
    with jax.named_scope("gather"):
        own = {0: scaled, far: crossed}
        mask = far // 2
        while mask:
            own.update({at | mask: swap(x, "col", 2 * mask) for at, x in own.items()})
            mask //= 2
        own = [own[at] for at in range(pairs)]

    def stacked(after):
        return call(stack_kernel, blocks(pairs), own, after=after)

    def reduced(parts, after):
        mask, got = 1, []
        while mask < pairs:
            for at in reversed(range(0, pairs, 2 * mask)):
                arrived = swap(parts.pop(at + mask), "col", 2 * mask)
                if at:
                    after = parts[at] = call(add_kernel, block, (parts[at], arrived), after=after)
                else:
                    got.append(arrived)
            mask *= 2
        return parts[0], got, after

    def paired(kept, sent):
        return call(pair_kernel, (block,) * kept.shape[0], (kept, swap(sent, "col", 1)))

    if dense:

        def backward_part(first, count, after):
            return call(
                functools.partial(backward_kernel, first, tile),
                blocks(count),
                (flipped, high, low),
                mebibytes=24,
                after=after,
                flops=6 * n_rows * count * shard * width,
            )

        def forward_half(embeds, first, before=(), after=None):
            return call(
                functools.partial(forward_kernel, first, n_row),
                (block,) * n_row,
                (embeds, high, low, *before),
                mebibytes=24,
                flops=3 * n_rows * n_cols * width,
                scratch=[pltpu.VMEM((pairs * shard, 2 * width), BF16)],
                after=after,
            )

        with jax.named_scope("backward"):
            parts = {}
            after = plan
            for first, count in ((far, pairs - far), (0, far)):
                sent = backward_part(pairs + first, count, after)
                kept = backward_part(first, count, sent)
                added = paired(kept, sent)
                parts.update({first + at: x for at, x in enumerate(added)})
                after = added[0]
        with jax.named_scope("gather"):
            own = stacked(after)
            other = swap(own, "col", 1)
        with jax.named_scope("forward"):
            forwards = forward_half(own, 0)
        with jax.named_scope("reduce"):
            *parts, after = reduced(parts, forwards[0])
        with jax.named_scope("forward"):
            forwards = forward_half(other, pairs, forwards, after)
    else:
        group = 8
        with jax.named_scope("gather"):
            own = stacked(plan)
            other = swap(own, "col", 1)
        with jax.named_scope("slots"):
            forward, backward = pl.pallas_call(
                functools.partial(slots_kernel, tiles, pairs),
                out_shape=(
                    jax.ShapeDtypeStruct((n_rows, width), F32),
                    jax.ShapeDtypeStruct((n_cols, width), F32),
                ),
                grid=(capacity // group,),
                in_specs=[SCALARS, SCALARS, pl.BlockSpec((group, tile, tile), lambda at: (at, 0, 0)), WHOLE, WHOLE],
                out_specs=(WHOLE, WHOLE),
                compiler_params=params(40),
                cost_estimate=cost(12 * values.size * width, values.size * 4),
            )(tile_coords, tile_count, values, jnp.concatenate([own, other]).reshape(-1, width), jnp.concatenate(grads))
            forwards = list(forward.reshape(n_row, shard, width))
            *parts, _ = reduced(dict(enumerate(paired(*backward.reshape(2, pairs, shard, width)))), forward)

    with jax.named_scope("reduce"):
        row_parts = [forwards[0]] + [swap(forwards[k], "row", k) for k in range(1, n_row)]

    with jax.named_scope("finish"):
        propagated = call(finish_kernel, block, (*row_parts, row_factor), mebibytes=4)
        embed_grad = call(finish_kernel, block, (parts[0], *parts[1], col_factor), mebibytes=4)
    return propagated, embed_grad


def solution(mesh):
    return jax.shard_map(
        per_device,
        mesh=mesh,
        in_specs=(
            P(("row", "col"), None),
            P(("col", "row"), None),
            P("col", "row", None, None, None),
            P(None, "col", "row", None),
            P("col", "row"),
            P(("col", "row")),
            P(("row", "col")),
        ),
        out_specs=(P(("col", "row"), None), P(("row", "col"), None)),
        check_vma=False,
    )
```

time: 176 us -> 41.7 us (0.24)
  waiting for transfers between devices: 102 us -> 8.81 us
  matrix products: 26.6 us -> 0 us
  starting transfers between devices: 0.12 us -> 18.7 us
  between operations: 14.4 us -> 1.43 us
  Pallas kernels: 0 us -> 12.6 us
  blocking collectives: 11.5 us -> 0 us
  local copies, waits for them, and re-layouts: 11.4 us -> 0 us
  other arithmetic: 8.86 us -> 0 us
    reduce_scatter x2 -> x0, waiting for transfers between devices: 91.1 us -> none  [the longest x1 58 us: per_device(): lax.psum_scatter(forward.reshape(-1, feature_width), 'row', scatter_dimen...]
    dot_general x8 -> x0, matrix products: 26.6 us -> none  [the longest x2 10.4 us: tile_terms(): jnp.einsum('tij,tid->tjd', values, grad_picked, precision=lax.Precision.H...]
    ppermute x0 -> x15, starting transfers between devices: none -> 18.7 us  [swap(): lax.ppermute(x, axis, [(at, at ^ mask) for at in range(lax.axis_size(axis...]
    pallas_call x0 -> x15, Pallas kernels: none -> 12.6 us  [call(): pl.pallas_call(body, out_shape=out_shape, in_specs=specs, out_specs=tuple...]
    all_gather x1 -> x0, blocking collectives: 11.5 us -> none  [per_device(): grad_panel = lax.all_gather(grad_scaled, 'row', axis=0, tiled=True)]
    all_gather x1 -> x0, waiting for transfers between devices: 10.8 us -> none  [per_device(): embed_panel = lax.all_gather(scaled, 'col', axis=0, tiled=True)]
    ppermute x0 -> x15, waiting for transfers between devices: none -> 8.81 us  [swap(): lax.ppermute(x, axis, [(at, at ^ mask) for at in range(lax.axis_size(axis...]
    mul x4 -> x0, other arithmetic: 5.98 us -> none  [the longest x1 1.66 us: per_device(): scaled = embed * lax.rsqrt(col_degree.astype(jnp.float32))[:, None]]
  transfers between devices with their start and end apart: 3 -> 15, of which waited for: 3 -> 7; matrix products, arithmetic and copies ran while one was open for 3% -> 0% of each run, Pallas kernels for 0% -> 26%
where the time goes in v3:
time: 41.7 us; the launch traced here: 41.5 us
  starting transfers between devices  18.7 us (45%)
  Pallas kernels  12.6 us (30%)
  waiting for transfers between devices  8.81 us (21%)
  between operations  1.43 us (3%)
    ppermute x15, starting transfers between devices, swap(): lax.ppermute(x, axis, [(at, at ^ mask) for at in range(lax.axis_size(axis...  18.7 us
    pallas_call x15, Pallas kernels, call(): pl.pallas_call(body, out_shape=out_shape, in_specs=specs, out_specs=tuple...  12.6 us
    ppermute x15, waiting for transfers between devices, swap(): lax.ppermute(x, axis, [(at, at ^ mask) for at in range(lax.axis_size(axis...  8.81 us
  transfers between devices with their start and end apart: 15, of which 7 were waited for; matrix products, arithmetic and copies ran while one was open for 0% of the time, Pallas kernels for 26%

profile of v3, /device:TPU:0, one launch (start us, length us, event | category | flops | bytes accessed | tf_op | source)
XLA Modules:
  0.0 41.5 jit_solution(3005980725322588547)
XLA Ops:
  1.3 1.2 %scale.1 = (f32[256,128]{1,0:T(8,128)S(1)}, f32[256,128]{1,0:T(8,128)S(1)}, f32[256,128]{1,0:T(8,128)S(1)}, f32[256,128]{1,0:T(8,128)S(1)}, s32[3,128]{1,0:T(4,128)S(1)}) custom-call(s32[1,1]{1,0:T(1,128)S(6)} %copy.9.refs_0_, f32[256,128]{1,0:T(8,128)} %refs_1_.1, f32[256,128]{1,0:T(8,128)} %refs_2_.1, s32[2,128]{1,0:T(2,128)} %bitcast.4, ...), custom_call_target="tpu_custom_call" | custom-call | bytes 15820880 | tf_op jit(solution)/shard_map/scale/pallas_call | solution.py:199
  2.4 3.0 %collective-permute-start = (f32[256,128]{1,0:T(8,128)S(1)}, f32[256,128]{1,0:T(8,128)S(1)}, u32[]{:S(2)}, u32[]{:S(2)}) collective-permute-start(f32[256,128]{1,0:T(8,128)S(1)} %get-tuple-element.25.refs_0_), channel_id=1, source_target_pairs={{0,8},{8,0},{16,24},{24,16},{1,9},{9,1},{17,25},{25,17},{2,10},{10... | collective-permute-start | bytes 393224 | tf_op jit(solution)/shard_map/gather/ppermute | solution.py:185
  5.4 1.5 %collective-permute-start.1 = (f32[256,128]{1,0:T(8,128)S(1)}, f32[256,128]{1,0:T(8,128)S(1)}, u32[]{:S(2)}, u32[]{:S(2)}) collective-permute-start(f32[256,128]{1,0:T(8,128)S(1)} %get-tuple-element.25.refs_0_), channel_id=1, source_target_pairs={{0,16},{8,24},{16,0},{24,8},{1,17},{9,25},{17,1},{25,9},{2,18},{10... | collective-permute-start | bytes 393224 | tf_op jit(solution)/shard_map/gather/ppermute | solution.py:185
  7.0 0.0 collective-permute-start.2
  7.0 3.0 %collective-permute-start.3 = (f32[256,128]{1,0:T(8,128)S(1)}, f32[256,128]{1,0:T(8,128)S(1)}, u32[]{:S(2)}, u32[]{:S(2)}) collective-permute-start(f32[256,128]{1,0:T(8,128)S(1)} %get-tuple-element.26.refs_0_), channel_id=1, source_target_pairs={{0,4},{1,5},{2,6},{3,7},{4,0},{5,1},{6,2},{7,3},{8,12},{9,13},{10,... | collective-permute-start | bytes 393224 | tf_op jit(solution)/shard_map/gather/ppermute | solution.py:185
  10.0 1.6 %collective-permute-start.6 = (f32[256,128]{1,0:T(8,128)S(1)}, f32[256,128]{1,0:T(8,128)S(1)}, u32[]{:S(2)}, u32[]{:S(2)}) collective-permute-start(f32[256,128]{1,0:T(8,128)S(1)} %get-tuple-element.26.refs_0_), channel_id=1, source_target_pairs={{0,2},{1,3},{2,0},{3,1},{4,6},{5,7},{6,4},{7,5},{8,10},{9,11},{10,... | collective-permute-start | bytes 393224 | tf_op jit(solution)/shard_map/gather/ppermute | solution.py:185
  11.6 4.4 %split.1 = (bf16[1024,2048]{1,0:T(8,128)(2,1)S(1)}, bf16[1024,2048]{1,0:T(8,128)(2,1)S(1)}) custom-call(s32[3,128]{1,0:T(4,128)S(1)} %get-tuple-element.23.plan_ref._, f32[128,128,128]{2,1,0:T(8,128)} %bitcast.3), custom_call_target="tpu_custom_call" | custom-call | bytes 335575040 | tf_op jit(solution)/shard_map/split/pallas_call | solution.py:199
  16.0 0.0 collective-permute-done.refs_1_
  16.0 0.0 collective-permute-done.1.refs_2_
  16.0 0.0 collective-permute-done.2.refs_3_
  16.0 0.0 collective-permute-done.3.refs_4_
  16.0 0.2 flip.1
  16.2 0.7 %backward.6._ = f32[2,256,128]{2,1,0:T(8,128)S(1)} custom-call(s32[3,128]{1,0:T(4,128)S(1)} %get-tuple-element.23.plan_ref._, bf16[256,1024]{1,0:T(8,128)(2,1)S(1)} %get-tuple-element.27.refs_0_, bf16[1024,2048]{1,0:T(8,128)(2,1)S(1)} %get-tuple-element.28.refs_1_.high_ref, bf16[1024,2048]{1,0:T(8,128)(2,1)S(1)} %get-tuple-element.24._.refs_2_.low_ref), custom_call_target="tpu_custom_call" | custom-call | flops 8053063680 | bytes 183500800 | tf_op jit(solution)/shard_map/backward/pallas_call | solution.py:199
  16.9 0.1 collective-permute-start.4
  17.0 0.7 %backward.7.kept_ref = f32[2,256,128]{2,1,0:T(8,128)S(1)} custom-call(f32[2,256,128]{2,1,0:T(8,128)S(1)} %backward.6._, bf16[256,1024]{1,0:T(8,128)(2,1)S(1)} %get-tuple-element.27.refs_0_, bf16[1024,2048]{1,0:T(8,128)(2,1)S(1)} %get-tuple-element.28.refs_1_.high_ref, bf16[1024,2048]{1,0:T(8,128)(2,1)S(1)} %get-tuple-element.24._.refs_2_.low_ref), custom_call_target="tpu_custom_call" | custom-call | flops 8053063680 | bytes 183500800 | tf_op jit(solution)/shard_map/backward/pallas_call | solution.py:199
  17.7 0.5 %collective-permute-start.7 = (f32[256,128]{1,0:T(8,128)S(1)}, f32[256,128]{1,0:T(8,128)S(1)}, u32[]{:S(2)}, u32[]{:S(2)}) collective-permute-start(f32[256,128]{1,0:T(8,128)S(1)} %get-tuple-element.31.refs_2_), channel_id=1, source_target_pairs={{0,2},{1,3},{2,0},{3,1},{4,6},{5,7},{6,4},{7,5},{8,10},{9,11},{10,... | collective-permute-start | bytes 393224 | tf_op jit(solution)/shard_map/gather/ppermute | solution.py:185
  18.3 0.3 collective-permute-done.4.got_ref
  18.6 0.7 %backward.9._ = f32[2,256,128]{2,1,0:T(8,128)S(1)} custom-call(f32[256,128]{1,0:T(8,128)S(1)} %get-tuple-element.29._.refs_0_, bf16[256,1024]{1,0:T(8,128)(2,1)S(1)} %get-tuple-element.27.refs_0_, bf16[1024,2048]{1,0:T(8,128)(2,1)S(1)} %get-tuple-element.28.refs_1_.high_ref, bf16[1024,2048]{1,0:T(8,128)(2,1)S(1)} %get-tuple-element.24._.refs_2_.low_ref), custom_call_target="tpu_custom_call" | custom-call | flops 8053063680 | bytes 183500800 | tf_op jit(solution)/shard_map/backward/pallas_call | solution.py:199
  19.3 0.2 collective-permute-start.5
  19.5 0.7 %backward.10.kept_ref = f32[2,256,128]{2,1,0:T(8,128)S(1)} custom-call(f32[2,256,128]{2,1,0:T(8,128)S(1)} %backward.9._, bf16[256,1024]{1,0:T(8,128)(2,1)S(1)} %get-tuple-element.27.refs_0_, bf16[1024,2048]{1,0:T(8,128)(2,1)S(1)} %get-tuple-element.28.refs_1_.high_ref, bf16[1024,2048]{1,0:T(8,128)(2,1)S(1)} %get-tuple-element.24._.refs_2_.low_ref), custom_call_target="tpu_custom_call" | custom-call | flops 8053063680 | bytes 183500800 | tf_op jit(solution)/shard_map/backward/pallas_call | solution.py:199
  20.2 1.4 %collective-permute-start.8 = (f32[256,128]{1,0:T(8,128)S(1)}, f32[256,128]{1,0:T(8,128)S(1)}, u32[]{:S(2)}, u32[]{:S(2)}) collective-permute-start(f32[256,128]{1,0:T(8,128)S(1)} %get-tuple-element.33), channel_id=1, source_target_pairs={{0,2},{1,3},{2,0},{3,1},{4,6},{5,7},{6,4},{7,5},{8,10},{9,11},{10,... | collective-permute-start | bytes 393224 | tf_op jit(solution)/shard_map/reduce/ppermute | solution.py:185
  21.6 0.0 collective-permute-done.5.got_ref
  21.6 0.0 collective-permute-done.6.refs_1_
  21.6 2.4 %collective-permute-done.7.refs_3_ = f32[256,128]{1,0:T(8,128)S(1)} collective-permute-done((f32[256,128]{1,0:T(8,128)S(1)}, f32[256,128]{1,0:T(8,128)S(1)}, u32[]{:S(2)}, u32[]{:S(2)}) %collective-permute-start.7) | collective-permute-done | bytes 131104 | tf_op jit(solution)/shard_map/gather/ppermute | solution.py:185
  24.1 0.1 collective-permute-start.9
  24.2 1.3 %forward.2 = (f32[256,128]{1,0:T(8,128)S(1)}, f32[256,128]{1,0:T(8,128)S(1)}, f32[256,128]{1,0:T(8,128)S(1)}, f32[256,128]{1,0:T(8,128)S(1)}) custom-call(f32[4,256,128]{2,1,0:T(8,128)S(1)} %gather.1.embeds_ref, bf16[1024,2048]{1,0:T(8,128)(2,1)S(1)} %get-tuple-element.28.refs_1_.high_ref, bf16[1024,2048]{1,0:T(8,128)(2,1)S(1)} %get-tuple-element.24._.refs_2_.low_ref), custom_call_target="tpu_custom_call" | custom-call | flops 16106127360 | bytes 188743680 | tf_op jit(solution)/shard_map/forward/pallas_call | solution.py:199
  25.5 1.0 %collective-permute-done.8.refs_1_ = f32[256,128]{1,0:T(8,128)S(1)} collective-permute-done((f32[256,128]{1,0:T(8,128)S(1)}, f32[256,128]{1,0:T(8,128)S(1)}, u32[]{:S(2)}, u32[]{:S(2)}) %collective-permute-start.8) | collective-permute-done | bytes 131104 | tf_op jit(solution)/shard_map/reduce/ppermute | solution.py:185
  26.5 2.4 %collective-permute-start.14 = (f32[256,128]{1,0:T(8,128)S(1)}, f32[256,128]{1,0:T(8,128)S(1)}, u32[]{:S(2)}, u32[]{:S(2)}) collective-permute-start(f32[256,128]{1,0:T(8,128)S(1)} %reduce.1._), channel_id=1, source_target_pairs={{0,4},{1,5},{2,6},{3,7},{4,0},{5,1},{6,2},{7,3},{8,12},{9,13},{10,... | collective-permute-start | bytes 393224 | tf_op jit(solution)/shard_map/reduce/ppermute | solution.py:185
  28.9 1.2 %collective-permute-start.13 = (f32[256,128]{1,0:T(8,128)S(1)}, f32[256,128]{1,0:T(8,128)S(1)}, u32[]{:S(2)}, u32[]{:S(2)}) collective-permute-start(f32[256,128]{1,0:T(8,128)S(1)} %get-tuple-element.42), channel_id=1, source_target_pairs={{0,2},{1,3},{2,0},{3,1},{4,6},{5,7},{6,4},{7,5},{8,10},{9,11},{10,... | collective-permute-start | bytes 393224 | tf_op jit(solution)/shard_map/reduce/ppermute | solution.py:185
  30.1 0.0 collective-permute-done.9.refs_0_
  30.1 1.3 %forward.3 = (f32[256,128]{1,0:T(8,128)S(1)}, f32[256,128]{1,0:T(8,128)S(1)}, f32[256,128]{1,0:T(8,128)S(1)}, f32[256,128]{1,0:T(8,128)S(1)}) custom-call(f32[256,128]{1,0:T(8,128)S(1)} %reduce.1._, f32[4,256,128]{2,1,0:T(8,128)S(1)} %collective-permute-done.9.refs_0_, bf16[1024,2048]{1,0:T(8,128)(2,1)S(1)} %get-tuple-element.28.refs_1_.high_ref, ...), custom_call_target="tpu_custom_call" | custom-call | flops 16106127360 | bytes 199229440 | tf_op jit(solution)/shard_map/forward/pallas_call | solution.py:199
  31.5 1.6 %collective-permute-start.10 = (f32[256,128]{1,0:T(8,128)S(1)}, f32[256,128]{1,0:T(8,128)S(1)}, u32[]{:S(2)}, u32[]{:S(2)}) collective-permute-start(f32[256,128]{1,0:T(8,128)S(1)} %get-tuple-element.38), channel_id=1, source_target_pairs={{0,8},{8,0},{16,24},{24,16},{1,9},{9,1},{17,25},{25,17},{2,10},{10... | collective-permute-start | bytes 393224 | tf_op jit(solution)/shard_map/reduce/ppermute | solution.py:185
  33.0 1.5 %collective-permute-start.11 = (f32[256,128]{1,0:T(8,128)S(1)}, f32[256,128]{1,0:T(8,128)S(1)}, u32[]{:S(2)}, u32[]{:S(2)}) collective-permute-start(f32[256,128]{1,0:T(8,128)S(1)} %get-tuple-element.39), channel_id=1, source_target_pairs={{0,16},{8,24},{16,0},{24,8},{1,17},{9,25},{17,1},{25,9},{2,18},{10... | collective-permute-start | bytes 393224 | tf_op jit(solution)/shard_map/reduce/ppermute | solution.py:185
  34.5 0.5 %collective-permute-start.12 = (f32[256,128]{1,0:T(8,128)S(1)}, f32[256,128]{1,0:T(8,128)S(1)}, u32[]{:S(2)}, u32[]{:S(2)}) collective-permute-start(f32[256,128]{1,0:T(8,128)S(1)} %get-tuple-element.40), channel_id=1, source_target_pairs={{0,24},{8,16},{16,8},{24,0},{1,25},{9,17},{17,9},{25,1},{2,26},{10... | collective-permute-start | bytes 393224 | tf_op jit(solution)/shard_map/reduce/ppermute | solution.py:185
  35.0 0.5 %collective-permute-done.14.refs_2_ = f32[256,128]{1,0:T(8,128)S(1)} collective-permute-done((f32[256,128]{1,0:T(8,128)S(1)}, f32[256,128]{1,0:T(8,128)S(1)}, u32[]{:S(2)}, u32[]{:S(2)}) %collective-permute-start.14) | collective-permute-done | bytes 131104 | tf_op jit(solution)/shard_map/reduce/ppermute | solution.py:185
  35.5 0.5 %collective-permute-done.13.refs_1_ = f32[256,128]{1,0:T(8,128)S(1)} collective-permute-done((f32[256,128]{1,0:T(8,128)S(1)}, f32[256,128]{1,0:T(8,128)S(1)}, u32[]{:S(2)}, u32[]{:S(2)}) %collective-permute-start.13) | collective-permute-done | bytes 131104 | tf_op jit(solution)/shard_map/reduce/ppermute | solution.py:185
  36.0 0.7 %finish.3 = f32[256,128]{1,0:T(8,128)} custom-call(f32[256,128]{1,0:T(8,128)S(1)} %get-tuple-element.30._.refs_0_, f32[256,128]{1,0:T(8,128)S(1)} %collective-permute-done.13.refs_1_, f32[256,128]{1,0:T(8,128)S(1)} %collective-permute-done.14.refs_2_, f32[256,128]{1,0:T(8,128)S(1)} %get-tuple-element.43.refs_3_), custom_call_target="tpu_custom_call" | custom-call | bytes 13107200 | tf_op jit(solution)/shard_map/finish/pallas_call | solution.py:199
  36.7 0.7 %collective-permute-done.10.refs_1_ = f32[256,128]{1,0:T(8,128)S(1)} collective-permute-done((f32[256,128]{1,0:T(8,128)S(1)}, f32[256,128]{1,0:T(8,128)S(1)}, u32[]{:S(2)}, u32[]{:S(2)}) %collective-permute-start.10) | collective-permute-done | bytes 131104 | tf_op jit(solution)/shard_map/reduce/ppermute | solution.py:185
  37.4 3.4 %collective-permute-done.11.refs_2_ = f32[256,128]{1,0:T(8,128)S(1)} collective-permute-done((f32[256,128]{1,0:T(8,128)S(1)}, f32[256,128]{1,0:T(8,128)S(1)}, u32[]{:S(2)}, u32[]{:S(2)}) %collective-permute-start.11) | collective-permute-done | bytes 131104 | tf_op jit(solution)/shard_map/reduce/ppermute | solution.py:185
  40.8 0.0 collective-permute-done.12.refs_3_
  40.8 0.7 %finish.2 = f32[256,128]{1,0:T(8,128)} custom-call(f32[256,128]{1,0:T(8,128)S(1)} %get-tuple-element.37.refs_0_, f32[256,128]{1,0:T(8,128)S(1)} %collective-permute-done.10.refs_1_, f32[256,128]{1,0:T(8,128)S(1)} %collective-permute-done.11.refs_2_, f32[256,128]{1,0:T(8,128)S(1)} %collective-permute-done.12.refs_3_, f32[256,128]{1,0:T(8,128)S(1)} %get-tuple-element.41.refs_4_), custom_call_target="tpu_custom_call" | custom-call | bytes 15728640 | tf_op jit(solution)/shard_map/finish/pallas_call | solution.py:199
  (4 shorter events, 0.1 us)
Async XLA Ops:
  2.4 13.5 %collective-permute-start = (f32[256,128]{1,0:T(8,128)S(1)}, f32[256,128]{1,0:T(8,128)S(1)}, u32[]{:S(2)}, u32[]{:S(2)}) collective-permute-start(f32[256,128]{1,0:T(8,128)S(1)} %get-tuple-element.25.refs_0_), channel_id=1, source_target_pairs={{0,8},{8,0},{16,24},{24,16},{1,9},{9,1},{17,25},{25,17},{2,10},{10... | collective-permute-start | bytes 393224 | tf_op jit(solution)/shard_map/gather/ppermute | solution.py:185
  5.4 10.5 %collective-permute-start.1 = (f32[256,128]{1,0:T(8,128)S(1)}, f32[256,128]{1,0:T(8,128)S(1)}, u32[]{:S(2)}, u32[]{:S(2)}) collective-permute-start(f32[256,128]{1,0:T(8,128)S(1)} %get-tuple-element.25.refs_0_), channel_id=1, source_target_pairs={{0,16},{8,24},{16,0},{24,8},{1,17},{9,25},{17,1},{25,9},{2,18},{10... | collective-permute-start | bytes 393224 | tf_op jit(solution)/shard_map/gather/ppermute | solution.py:185
  7.0 9.0 %collective-permute-start.2 = (f32[256,128]{1,0:T(8,128)S(1)}, f32[256,128]{1,0:T(8,128)S(1)}, u32[]{:S(2)}, u32[]{:S(2)}) collective-permute-start(f32[256,128]{1,0:T(8,128)S(1)} %get-tuple-element.25.refs_0_), channel_id=1, source_target_pairs={{0,24},{8,16},{16,8},{24,0},{1,25},{9,17},{17,9},{25,1},{2,26},{10... | collective-permute-start | bytes 393224 | tf_op jit(solution)/shard_map/gather/ppermute | solution.py:185
  7.0 9.0 %collective-permute-start.3 = (f32[256,128]{1,0:T(8,128)S(1)}, f32[256,128]{1,0:T(8,128)S(1)}, u32[]{:S(2)}, u32[]{:S(2)}) collective-permute-start(f32[256,128]{1,0:T(8,128)S(1)} %get-tuple-element.26.refs_0_), channel_id=1, source_target_pairs={{0,4},{1,5},{2,6},{3,7},{4,0},{5,1},{6,2},{7,3},{8,12},{9,13},{10,... | collective-permute-start | bytes 393224 | tf_op jit(solution)/shard_map/gather/ppermute | solution.py:185
  10.0 11.6 %collective-permute-start.6 = (f32[256,128]{1,0:T(8,128)S(1)}, f32[256,128]{1,0:T(8,128)S(1)}, u32[]{:S(2)}, u32[]{:S(2)}) collective-permute-start(f32[256,128]{1,0:T(8,128)S(1)} %get-tuple-element.26.refs_0_), channel_id=1, source_target_pairs={{0,2},{1,3},{2,0},{3,1},{4,6},{5,7},{6,4},{7,5},{8,10},{9,11},{10,... | collective-permute-start | bytes 393224 | tf_op jit(solution)/shard_map/gather/ppermute | solution.py:185
  16.9 1.6 %collective-permute-start.4 = (f32[2,256,128]{2,1,0:T(8,128)S(1)}, f32[2,256,128]{2,1,0:T(8,128)S(1)}, u32[]{:S(2)}, u32[]{:S(2)}) collective-permute-start(f32[2,256,128]{2,1,0:T(8,128)S(1)} %backward.6._), channel_id=1, source_target_pairs={{0,1},{1,0},{2,3},{3,2},{4,5},{5,4},{6,7},{7,6},{8,9},{9,8},{10,11... | collective-permute-start | bytes 786440 | tf_op jit(solution)/shard_map/backward/ppermute | solution.py:185
  17.7 6.4 %collective-permute-start.7 = (f32[256,128]{1,0:T(8,128)S(1)}, f32[256,128]{1,0:T(8,128)S(1)}, u32[]{:S(2)}, u32[]{:S(2)}) collective-permute-start(f32[256,128]{1,0:T(8,128)S(1)} %get-tuple-element.31.refs_2_), channel_id=1, source_target_pairs={{0,2},{1,3},{2,0},{3,1},{4,6},{5,7},{6,4},{7,5},{8,10},{9,11},{10,... | collective-permute-start | bytes 393224 | tf_op jit(solution)/shard_map/gather/ppermute | solution.py:185
  19.3 2.3 %collective-permute-start.5 = (f32[2,256,128]{2,1,0:T(8,128)S(1)}, f32[2,256,128]{2,1,0:T(8,128)S(1)}, u32[]{:S(2)}, u32[]{:S(2)}) collective-permute-start(f32[2,256,128]{2,1,0:T(8,128)S(1)} %backward.9._), channel_id=1, source_target_pairs={{0,1},{1,0},{2,3},{3,2},{4,5},{5,4},{6,7},{7,6},{8,9},{9,8},{10,11... | collective-permute-start | bytes 786440 | tf_op jit(solution)/shard_map/backward/ppermute | solution.py:185
  20.2 6.3 %collective-permute-start.8 = (f32[256,128]{1,0:T(8,128)S(1)}, f32[256,128]{1,0:T(8,128)S(1)}, u32[]{:S(2)}, u32[]{:S(2)}) collective-permute-start(f32[256,128]{1,0:T(8,128)S(1)} %get-tuple-element.33), channel_id=1, source_target_pairs={{0,2},{1,3},{2,0},{3,1},{4,6},{5,7},{6,4},{7,5},{8,10},{9,11},{10,... | collective-permute-start | bytes 393224 | tf_op jit(solution)/shard_map/reduce/ppermute | solution.py:185
  24.1 6.0 %collective-permute-start.9 = (f32[4,256,128]{2,1,0:T(8,128)S(1)}, f32[4,256,128]{2,1,0:T(8,128)S(1)}, u32[]{:S(2)}, u32[]{:S(2)}) collective-permute-start(f32[4,256,128]{2,1,0:T(8,128)S(1)} %gather.1.embeds_ref), channel_id=1, source_target_pairs={{0,1},{1,0},{2,3},{3,2},{4,5},{5,4},{6,7},{7,6},{8,9},{9,8},{10,11... | collective-permute-start | bytes 1572872 | tf_op jit(solution)/shard_map/gather/ppermute | solution.py:185
  26.5 9.0 %collective-permute-start.14 = (f32[256,128]{1,0:T(8,128)S(1)}, f32[256,128]{1,0:T(8,128)S(1)}, u32[]{:S(2)}, u32[]{:S(2)}) collective-permute-start(f32[256,128]{1,0:T(8,128)S(1)} %reduce.1._), channel_id=1, source_target_pairs={{0,4},{1,5},{2,6},{3,7},{4,0},{5,1},{6,2},{7,3},{8,12},{9,13},{10,... | collective-permute-start | bytes 393224 | tf_op jit(solution)/shard_map/reduce/ppermute | solution.py:185
  28.9 7.1 %collective-permute-start.13 = (f32[256,128]{1,0:T(8,128)S(1)}, f32[256,128]{1,0:T(8,128)S(1)}, u32[]{:S(2)}, u32[]{:S(2)}) collective-permute-start(f32[256,128]{1,0:T(8,128)S(1)} %get-tuple-element.42), channel_id=1, source_target_pairs={{0,2},{1,3},{2,0},{3,1},{4,6},{5,7},{6,4},{7,5},{8,10},{9,11},{10,... | collective-permute-start | bytes 393224 | tf_op jit(solution)/shard_map/reduce/ppermute | solution.py:185
  31.5 5.9 %collective-permute-start.10 = (f32[256,128]{1,0:T(8,128)S(1)}, f32[256,128]{1,0:T(8,128)S(1)}, u32[]{:S(2)}, u32[]{:S(2)}) collective-permute-start(f32[256,128]{1,0:T(8,128)S(1)} %get-tuple-element.38), channel_id=1, source_target_pairs={{0,8},{8,0},{16,24},{24,16},{1,9},{9,1},{17,25},{25,17},{2,10},{10... | collective-permute-start | bytes 393224 | tf_op jit(solution)/shard_map/reduce/ppermute | solution.py:185
  33.0 7.8 %collective-permute-start.11 = (f32[256,128]{1,0:T(8,128)S(1)}, f32[256,128]{1,0:T(8,128)S(1)}, u32[]{:S(2)}, u32[]{:S(2)}) collective-permute-start(f32[256,128]{1,0:T(8,128)S(1)} %get-tuple-element.39), channel_id=1, source_target_pairs={{0,16},{8,24},{16,0},{24,8},{1,17},{9,25},{17,1},{25,9},{2,18},{10... | collective-permute-start | bytes 393224 | tf_op jit(solution)/shard_map/reduce/ppermute | solution.py:185
  34.5 6.3 %collective-permute-start.12 = (f32[256,128]{1,0:T(8,128)S(1)}, f32[256,128]{1,0:T(8,128)S(1)}, u32[]{:S(2)}, u32[]{:S(2)}) collective-permute-start(f32[256,128]{1,0:T(8,128)S(1)} %get-tuple-element.40), channel_id=1, source_target_pairs={{0,24},{8,16},{16,8},{24,0},{1,25},{9,17},{17,9},{25,1},{2,26},{10... | collective-permute-start | bytes 393224 | tf_op jit(solution)/shard_map/reduce/ppermute | solution.py:185

commit v4 on v3

v4 whole, which is shorter than its diff:
```python
import functools

import jax
import jax.numpy as jnp
from jax import lax
from jax.experimental import pallas as pl
from jax.experimental.pallas import tpu as pltpu
from jax.sharding import PartitionSpec as P

F32 = jnp.float32
BF16 = jnp.bfloat16
WHOLE = pl.BlockSpec(memory_space=pltpu.VMEM)
ANYWHERE = pl.BlockSpec(memory_space=pl.ANY)
SCALARS = pl.BlockSpec(memory_space=pltpu.SMEM)


def params(mebibytes):
    return pltpu.CompilerParams(vmem_limit_bytes=mebibytes * 2**20)


def cost(flops, moved):
    return pl.CostEstimate(flops=flops, bytes_accessed=moved, transcendentals=0)


def halves(x):
    high = x.astype(BF16)
    return high, (x - high.astype(F32)).astype(BF16)


def product(left, right):
    return jnp.dot(left, right, preferred_element_type=F32)


def row_factors(degree_ref, at, width):
    factors = lax.rsqrt(degree_ref[at : at + 1, :].astype(F32))
    return jnp.broadcast_to(factors, (width, factors.shape[1])).T


def scale_kernel(tiles, n_row, pairs, *refs):
    in_refs, (grad_ref, scaled_ref, row_factor_ref, col_factor_ref, plan_ref) = refs[:5], refs[5:10]
    bufs, sems = refs[10:15], refs[15]
    copies = [pltpu.make_async_copy(*pair, sems.at[at]) for at, pair in enumerate(zip(in_refs, bufs))]
    for copy in copies:
        copy.start()
    for copy in copies:
        copy.wait()
    cotangent, embed, row_degree, col_degree, coords = bufs
    for x_buf, degree_buf, out_ref, factor_ref in (
        (embed, col_degree, scaled_ref, col_factor_ref),
        (cotangent, row_degree, grad_ref, row_factor_ref),
    ):
        tile = degree_buf.shape[1]
        for at in range(degree_buf.shape[0]):
            rows = pl.ds(at * tile, tile)
            factors = row_factors(degree_buf, at, x_buf.shape[1])
            factor_ref[rows, :] = factors
            out_ref[0, rows, :] = x_buf[rows, :] * factors
    plan_ref[0:1, :] = row_place(coords[0, 0], tiles, n_row) * tile
    plan_ref[1:2, :] = col_place(coords[1, 0], tiles, pairs) * tile


def finish_kernel(*refs):
    *part_refs, factor_ref, out_ref = refs
    total = part_refs[0][0]
    for part_ref in part_refs[1:]:
        total = total + part_ref[0]
    out_ref[...] = total * factor_ref[...]


def add_kernel(x_ref, y_ref, *out_refs):
    count = out_refs[0].shape[0]
    for at, out_ref in enumerate(out_refs):
        part = pl.ds(at * count, count)
        out_ref[...] = x_ref[part] + y_ref[part]


def copy_kernel(x_ref, out_ref):
    out_ref[...] = x_ref[...]


def join_kernel(x_ref, y_ref, out_ref):
    count = x_ref.shape[0]
    out_ref[:count] = x_ref[...]
    out_ref[count:] = y_ref[...]


def bits_of(count):
    return count.bit_length() - 1


def reversed_bits(x, bits):
    out = jnp.zeros_like(x)
    for bit in range(bits):
        out = out | ((lax.shift_right_logical(x, bit) & 1) << (bits - 1 - bit))
    return out


def row_place(tile_at, tiles, n_row):
    tile_at = tile_at ^ (lax.axis_index("row") * tiles)
    shard = lax.shift_right_logical(tile_at, bits_of(tiles))
    order = jnp.where(lax.axis_index("col") % 2 == 0, reversed_bits(shard, bits_of(n_row)), shard)
    return order * tiles + (tile_at & (tiles - 1))


def col_place(tile_at, tiles, pairs):
    tile_at = tile_at ^ (lax.axis_index("col") * tiles)
    shard = lax.shift_right_logical(tile_at, bits_of(tiles))
    order = reversed_bits(lax.shift_right_logical(shard, 1), bits_of(pairs))
    half = pairs // 2
    second = (order >= half).astype(jnp.int32)
    order = second * pairs + (shard & 1) * half + (order & (half - 1))
    return order * tiles + (tile_at & (tiles - 1))


def split_kernel(plan_ref, count_ref, values_ref, high_ref, low_ref):
    capacity, tile, _ = values_ref.shape

    @pl.loop(0, capacity, unroll=4)
    def _(slot):
        rows = pl.ds(pl.multiple_of(plan_ref[0, slot], tile), tile)
        cols = pl.ds(pl.multiple_of(plan_ref[1, slot], tile), tile)
        high, low = halves(jnp.where(slot < count_ref[0, 0], values_ref[slot], 0.0))
        high_ref[rows, cols] = high
        low_ref[rows, cols] = low


def flip_kernel(tile, *refs):
    *grad_refs, out_ref = refs
    _, shard, width = grad_refs[0].shape
    done = 0
    for grad_ref in grad_refs:
        for at in range(grad_ref.shape[0]):
            for first in range(0, shard, tile):
                high, low = halves(grad_ref[at, pl.ds(first, tile), :].T)
                out_ref[:width, pl.ds(done + first, tile)] = high
                out_ref[width:, pl.ds(done + first, tile)] = low
            done += shard


def backward_kernel(firsts, tile, grads_ref, high_ref, low_ref, out_ref):
    _, shard, width = out_ref.shape
    for at, first in enumerate(firsts):
        cols = pl.ds(first * shard, shard)
        both = product(grads_ref[...], high_ref[:, cols])
        total = both[:width] + both[width:] + product(grads_ref[:width, :], low_ref[:, cols])
        for row in range(0, shard, tile):
            out_ref[at, pl.ds(row, tile), :] = total[:, row : row + tile].T


def forward_kernel(first, count, *refs):
    embed_refs, (high_ref, low_ref) = refs[:count], refs[count : count + 2]
    before_refs, out_refs, panel = refs[count + 2 : -3], refs[-3:-1], refs[-1]
    bands, shard, width = out_refs[0].shape
    done = 0
    for embeds_ref in embed_refs:
        for at in range(embeds_ref.shape[0]):
            high, low = halves(embeds_ref[at])
            panel[pl.ds(done, shard), :width] = high
            panel[pl.ds(done, shard), width:] = low
            done += shard
    cols = pl.ds(first * shard, done)
    for part, out_ref in enumerate(out_refs):
        for at in range(bands):
            rows = pl.ds((part * bands + at) * shard, shard)
            both = product(high_ref[rows, cols], panel[...])
            total = both[:, :width] + both[:, width:] + product(low_ref[rows, cols], panel[:, :width])
            if before_refs:
                total = total + before_refs[part][at]
            out_ref[at] = total


def slots_kernel(tiles, n_row, pairs, coords_ref, count_ref, values_ref, embed_ref, grad_ref, forward_ref, backward_ref):
    group, tile, _ = values_ref.shape
    first = pl.program_id(0) * group

    @pl.when(pl.program_id(0) == 0)
    def _():
        forward_ref[...] = jnp.zeros_like(forward_ref)
        backward_ref[...] = jnp.zeros_like(backward_ref)

    for slot in range(group):

        @pl.when(first + slot < count_ref[0, 0])
        def _():
            row_at = row_place(coords_ref[0, 0, 0, first + slot], tiles, n_row)
            col_at = col_place(coords_ref[1, 0, 0, first + slot], tiles, pairs)
            rows = pl.ds(pl.multiple_of(row_at * tile, tile), tile)
            cols = pl.ds(pl.multiple_of(col_at * tile, tile), tile)
            high, low = halves(values_ref[slot])
            embed_high, embed_low = halves(embed_ref[cols, :])
            forward_ref[rows, :] += product(high, embed_high) + product(high, embed_low) + product(low, embed_high)
            high, low = halves(values_ref[slot].T)
            grad_high, grad_low = halves(grad_ref[rows, :])
            backward_ref[cols, :] += product(high, grad_high) + product(high, grad_low) + product(low, grad_high)


def swap(x, axis, mask):
    return lax.ppermute(x, axis, [(at, at ^ mask) for at in range(lax.axis_size(axis))])


def call(kernel, out_shape, args, mebibytes=16, flops=0, scratch=(), specs=None, after=None):
    outs = out_shape if isinstance(out_shape, tuple) else (out_shape,)
    moved = sum(x.size * x.dtype.itemsize for x in (*args, *outs))
    specs = specs or [WHOLE] * len(args)
    body = kernel
    if after is not None:
        args, specs = (after, *args), [ANYWHERE, *specs]

        def body(_, *refs):
            kernel(*refs)

    return pl.pallas_call(
        body,
        out_shape=out_shape,
        in_specs=specs,
        out_specs=tuple(WHOLE for _ in outs) if isinstance(out_shape, tuple) else WHOLE,
        scratch_shapes=scratch,
        compiler_params=params(mebibytes),
        cost_estimate=cost(20 * flops, 20 * moved),
    )(*args)


def per_device(embed, cotangent, tile_values, tile_coords, tile_count, row_degree, col_degree):
    shard, width = embed.shape
    capacity, tile = tile_values.shape[2:4]
    n_row, n_col = lax.axis_size("row"), lax.axis_size("col")
    pairs = n_col // 2
    half = pairs // 2
    tiles = shard // tile
    n_rows, n_cols = shard * n_row, shard * n_col
    dense = (n_rows // tile) * (n_cols // tile) <= capacity
    block = jax.ShapeDtypeStruct((shard, width), F32)

    def blocks(count):
        return jax.ShapeDtypeStruct((count, shard, width), F32)

    def joined(x, y, after=None):
        flops = n_rows * n_cols * width
        return call(join_kernel, blocks(x.shape[0] + y.shape[0]), (x, y), after=after, flops=flops)

    values = tile_values.reshape(tile_values.shape[2:])
    if dense:
        with jax.named_scope("fetch"):
            values = swap(values, "col", 0)

    with jax.named_scope("scale"):
        args = (cotangent, embed, row_degree.reshape(-1, tile), col_degree.reshape(-1, tile), tile_coords)
        grad_scaled, scaled, row_factor, col_factor, plan = call(
            functools.partial(scale_kernel, tiles, n_row, pairs),
            (blocks(1), blocks(1), block, block, jax.ShapeDtypeStruct((2, capacity), jnp.int32)),
            [pltpu.with_memory_space_constraint(x, pltpu.HBM) for x in args],
            mebibytes=4,
            specs=[pl.BlockSpec(memory_space=pltpu.HBM)] * len(args),
            scratch=[pltpu.VMEM(x.shape, x.dtype) for x in args] + [pltpu.SemaphoreType.DMA((len(args),))],
        )

    def cross(x, mask, mirrored):
        masks = (mask, mirrored)
        at = [(row, col) for row in range(n_row) for col in range(n_col)]
        return lax.ppermute(
            x, ("row", "col"), [(row * n_col + col, (row ^ masks[col % 2]) * n_col + col) for row, col in at]
        )

    def row_steps():
        return [(1 << bit, n_row >> (bit + 1)) for bit in range(bits_of(n_row))]

    crossed = swap(scaled, "col", 2 * half)

    def gathered_grads(after):
        grads = [grad_scaled]
        for step, masks in enumerate(reversed(row_steps())):
            if step:
                grads = [joined(*grads, after=after)]
            grads.append(cross(grads[0], *masks))
        return grads

    def gathered_embeds(after):
        own, got, mask = scaled, crossed, half
        while mask > 1:
            own, mask = joined(own, got, after), mask // 2
            got = swap(own, "col", 2 * mask)
        return own, got

    def chip_sums(kept, sent, after=None):
        count = kept.shape[0] // 2
        return call(add_kernel, (blocks(count), blocks(count)), (kept, swap(sent, "col", 1)), after=after)

    def halved(kept, sent, after):
        mask = 1
        while kept.shape[0] > 1:
            count = kept.shape[0] // 2
            kept, sent = call(
                add_kernel, (blocks(count), blocks(count)), (kept, swap(sent, "col", 2 * mask)), after=after
            )
            mask *= 2
        return kept, swap(sent, "col", 2 * mask)

    def reduced_rows(kept, sent, after):
        for step, masks in enumerate(row_steps()):
            got = cross(sent, *masks)
            if kept.shape[0] == 1:
                return kept, got
            count = kept.shape[0] // 2
            kept, sent = call(add_kernel, (blocks(count), blocks(count)), (kept, got), after=after)

    far, near = range(1, pairs, 2), range(0, pairs, 2)
    if dense:
        table = jax.ShapeDtypeStruct((n_rows, n_cols), BF16)
        with jax.named_scope("split"):
            high, low = call(
                split_kernel,
                (table, table),
                (plan, tile_count, values),
                mebibytes=24,
                specs=[SCALARS, SCALARS, WHOLE],
            )
        with jax.named_scope("gather"):
            grads = gathered_grads(high)
            embeds, last_embeds = gathered_embeds(grads[0])
            other_embeds = swap(embeds, "col", 1)
        with jax.named_scope("flip"):
            flipped = call(
                functools.partial(flip_kernel, tile),
                jax.ShapeDtypeStruct((2 * width, n_rows), BF16),
                grads,
                after=embeds,
            )

        def backward_part(orders, core, after):
            shards = [order // half * pairs + core * half + order % half for order in orders]
            return call(
                functools.partial(backward_kernel, shards, tile),
                blocks(len(shards)),
                (flipped, high, low),
                mebibytes=24,
                after=after,
                flops=6 * n_rows * len(shards) * shard * width,
            )

        def forward_part(embeds, first, before=(), after=None):
            count = sum(x.shape[0] for x in embeds)
            return call(
                functools.partial(forward_kernel, first, len(embeds)),
                (blocks(n_row // 2), blocks(n_row // 2)),
                (*embeds, high, low, *before),
                mebibytes=24,
                flops=6 * n_rows * count * shard * width,
                scratch=[pltpu.VMEM((count * shard, 2 * width), BF16)],
                after=after,
            )

        with jax.named_scope("backward"):
            sent = backward_part(far, 1, plan)
            far_sums = chip_sums(backward_part(far, 0, sent), sent)
            sent = backward_part(near, 1, far_sums[0])
            kept = backward_part(near, 0, sent)
        with jax.named_scope("forward"):
            passed = call(copy_kernel, blocks(half), [last_embeds], after=kept)
            forwards = forward_part([embeds, other_embeds], 0, after=passed)
        with jax.named_scope("reduce"):
            crossing = call(add_kernel, (blocks(1),), halved(*far_sums, passed), after=forwards[0])[0]
        with jax.named_scope("forward"):
            forwards = forward_part([passed, swap(passed, "col", 1)], pairs, forwards, after=crossing)
        with jax.named_scope("reduce"):
            near_sums = chip_sums(kept, sent, after=forwards[0])
            after = near_sums[0]
    else:
        group = 8
        with jax.named_scope("gather"):
            grads = gathered_grads(plan)
            embeds, last_embeds = gathered_embeds(plan)
            panel = joined(joined(embeds, swap(embeds, "col", 1)), joined(last_embeds, swap(last_embeds, "col", 1)))
        with jax.named_scope("slots"):
            forward, backward = pl.pallas_call(
                functools.partial(slots_kernel, tiles, n_row, pairs),
                out_shape=(
                    jax.ShapeDtypeStruct((n_rows, width), F32),
                    jax.ShapeDtypeStruct((n_cols, width), F32),
                ),
                grid=(capacity // group,),
                in_specs=[SCALARS, SCALARS, pl.BlockSpec((group, tile, tile), lambda at: (at, 0, 0)), WHOLE, WHOLE],
                out_specs=(WHOLE, WHOLE),
                compiler_params=params(40),
                cost_estimate=cost(12 * values.size * width, values.size * 4),
            )(tile_coords, tile_count, values, panel.reshape(-1, width), joined(*grads).reshape(-1, width))
            forwards = forward.reshape(2, n_row // 2, shard, width)
            backward = backward.reshape(2, 2, half, shard, width)
            kept, sent = (backward[:, at].reshape(pairs, shard, width) for at in range(2))
        with jax.named_scope("reduce"):
            far_sums, near_sums = (chip_sums(kept[at::2], sent[at::2]) for at in (1, 0))
            crossing = call(add_kernel, (blocks(1),), halved(*far_sums, forward))[0]
            after = forward

    with jax.named_scope("reduce"):
        grad_parts = (*halved(*near_sums, after), swap(crossing, "col", 2 * half))
        row_parts = reduced_rows(*forwards, after)

    with jax.named_scope("finish"):
        propagated = call(finish_kernel, block, (*row_parts, row_factor), mebibytes=4)
        embed_grad = call(finish_kernel, block, (*grad_parts, col_factor), mebibytes=4)
    return propagated, embed_grad


def solution(mesh):
    return jax.shard_map(
        per_device,
        mesh=mesh,
        in_specs=(
            P(("row", "col"), None),
            P(("col", "row"), None),
            P("col", "row", None, None, None),
            P(None, "col", "row", None),
            P("col", "row"),
            P(("col", "row")),
            P(("row", "col")),
        ),
        out_specs=(P(("col", "row"), None), P(("row", "col"), None)),
        check_vma=False,
    )
```

time: 41.7 us -> 44.5 us (1.067)
  waiting for transfers between devices: 8.81 us -> 14.1 us
  Pallas kernels: 12.6 us -> 11.2 us
  starting transfers between devices: 18.7 us -> 17.6 us
    ppermute x15 -> x10, starting transfers between devices: 18.7 us -> 10.8 us  [swap(): lax.ppermute(x, axis, [(at, at ^ mask) for at in range(lax.axis_size(axis...]
    ppermute x0 -> x4, waiting for transfers between devices: none -> 7.77 us  [cross(): lax.ppermute(x, ('row', 'col'), [(row * n_col + col, (row ^ masks[col % 2...]
    ppermute x0 -> x4, starting transfers between devices: none -> 6.81 us  [cross(): lax.ppermute(x, ('row', 'col'), [(row * n_col + col, (row ^ masks[col % 2...]
    ppermute x15 -> x10, waiting for transfers between devices: 8.81 us -> 6.38 us  [swap(): lax.ppermute(x, axis, [(at, at ^ mask) for at in range(lax.axis_size(axis...]
    pallas_call x15 -> x18, Pallas kernels: 12.6 us -> 11.2 us  [call(): pl.pallas_call(body, out_shape=out_shape, in_specs=specs, out_specs=tuple...]
  transfers between devices with their start and end apart: 15 -> 14, of which waited for: 7 -> 7; matrix products, arithmetic and copies ran while one was open for 0% -> 0% of each run, Pallas kernels for 26% -> 24%
where the time goes in v4:
time: 44.5 us; the launch traced here: 44.3 us
  starting transfers between devices  17.6 us (40%)
  waiting for transfers between devices  14.1 us (32%)
  Pallas kernels  11.2 us (25%)
  between operations  1.43 us (3%)
    pallas_call x18, Pallas kernels, call(): pl.pallas_call(body, out_shape=out_shape, in_specs=specs, out_specs=tuple...  11.2 us
    ppermute x10, starting transfers between devices, swap(): lax.ppermute(x, axis, [(at, at ^ mask) for at in range(lax.axis_size(axis...  10.8 us
    ppermute x4, waiting for transfers between devices, cross(): lax.ppermute(x, ('row', 'col'), [(row * n_col + col, (row ^ masks[col % 2...  7.77 us
    ppermute x4, starting transfers between devices, cross(): lax.ppermute(x, ('row', 'col'), [(row * n_col + col, (row ^ masks[col % 2...  6.81 us
    ppermute x10, waiting for transfers between devices, swap(): lax.ppermute(x, axis, [(at, at ^ mask) for at in range(lax.axis_size(axis...  6.38 us
  transfers between devices with their start and end apart: 14, of which 7 were waited for; matrix products, arithmetic and copies ran while one was open for 0% of the time, Pallas kernels for 24%

profile of v4, /device:TPU:0, one launch (start us, length us, event | category | flops | bytes accessed | tf_op | source)
XLA Modules:
  0.0 44.3 jit_solution(17704990951323276465)
XLA Ops:
  0.6 3.4 %collective-permute-start = (f32[128,128,128]{2,1,0:T(8,128)}, f32[128,128,128]{2,1,0:T(8,128)S(1)}, u32[]{:S(2)}, u32[]{:S(2)}) collective-permute-start(f32[128,128,128]{2,1,0:T(8,128)} %bitcast.5), channel_id=1, source_target_pairs={{0,0},{1,1},{2,2},{3,3},{4,4},{5,5},{6,6},{7,7},{8,8},{9,9},{10,10... | collective-permute-start | bytes 25165832 | tf_op jit(solution)/shard_map/fetch/ppermute | solution.py:198
  4.0 1.2 %scale.1 = (f32[1,256,128]{2,1,0:T(8,128)S(1)}, f32[1,256,128]{2,1,0:T(8,128)S(1)}, f32[256,128]{1,0:T(8,128)S(1)}, f32[256,128]{1,0:T(8,128)S(1)}, s32[2,128]{1,0:T(2,128)S(1)}) custom-call(f32[256,128]{1,0:T(8,128)} %refs_0_.1, f32[256,128]{1,0:T(8,128)} %refs_1_.1, s32[2,128]{1,0:T(2,128)} %bitcast.3, s32[2,128]{1,0:T(2,128)} %bitcast.4, ...), custom_call_target="tpu_custom_call" | custom-call | bytes 15810560 | tf_op jit(solution)/shard_map/scale/pallas_call | solution.py:212
  5.2 3.0 %collective-permute-start.1 = (f32[1,256,128]{2,1,0:T(8,128)S(1)}, f32[1,256,128]{2,1,0:T(8,128)S(1)}, u32[]{:S(2)}, u32[]{:S(2)}) collective-permute-start(f32[1,256,128]{2,1,0:T(8,128)S(1)} %get-tuple-element.21.refs_0_), channel_id=1, source_target_pairs={{0,16},{1,9},{2,18},{3,11},{4,20},{5,13},{6,22},{7,15},{8,24},{9,1... | collective-permute-start | bytes 393224 | tf_op jit(solution)/shard_map/gather/ppermute | solution.py:260
  8.2 2.6 %collective-permute-start.2 = (f32[1,256,128]{2,1,0:T(8,128)S(1)}, f32[1,256,128]{2,1,0:T(8,128)S(1)}, u32[]{:S(2)}, u32[]{:S(2)}) collective-permute-start(f32[1,256,128]{2,1,0:T(8,128)S(1)} %get-tuple-element.22.refs_0_), channel_id=1, source_target_pairs={{0,4},{1,5},{2,6},{3,7},{4,0},{5,1},{6,2},{7,3},{8,12},{9,13},{10,... | collective-permute-start | bytes 393224 | tf_op jit(solution)/shard_map/ppermute | solution.py:198
  11.5 0.0 collective-permute-done.values_ref
  11.5 2.9 %split.1 = (bf16[1024,2048]{1,0:T(8,128)(2,1)S(1)}, bf16[1024,2048]{1,0:T(8,128)(2,1)S(1)}) custom-call(s32[2,128]{1,0:T(2,128)S(1)} %get-tuple-element.19.plan_ref._, s32[1,1]{1,0:T(1,128)S(6)} %copy.9.count_ref, f32[128,128,128]{2,1,0:T(8,128)S(1)} %collective-permute-done.values_ref), custom_call_target="tpu_custom_call" | custom-call | bytes 335564864 | tf_op jit(solution)/shard_map/split/pallas_call | solution.py:212
  14.4 0.0 collective-permute-done.1.refs_1_
  14.4 1.6 %collective-permute-start.3 = (f32[2,256,128]{2,1,0:T(8,128)S(1)}, f32[2,256,128]{2,1,0:T(8,128)S(1)}, u32[]{:S(2)}, u32[]{:S(2)}) collective-permute-start(f32[2,256,128]{2,1,0:T(8,128)S(1)} %gather.2._.refs_0_), channel_id=1, source_target_pairs={{0,8},{1,17},{2,10},{3,19},{4,12},{5,21},{6,14},{7,23},{8,0},{9,25... | collective-permute-start | bytes 786440 | tf_op jit(solution)/shard_map/gather/ppermute | solution.py:260
  16.0 0.8 %collective-permute-done.2.refs_1_ = f32[1,256,128]{2,1,0:T(8,128)S(1)} collective-permute-done((f32[1,256,128]{2,1,0:T(8,128)S(1)}, f32[1,256,128]{2,1,0:T(8,128)S(1)}, u32[]{:S(2)}, u32[]{:S(2)}) %collective-permute-start.2) | collective-permute-done | bytes 131104 | tf_op jit(solution)/shard_map/ppermute | solution.py:198
  16.9 0.8 %collective-permute-start.5 = (f32[2,256,128]{2,1,0:T(8,128)S(1)}, f32[2,256,128]{2,1,0:T(8,128)S(1)}, u32[]{:S(2)}, u32[]{:S(2)}) collective-permute-start(f32[2,256,128]{2,1,0:T(8,128)S(1)} %gather.3._.refs_0_), channel_id=1, source_target_pairs={{0,2},{1,3},{2,0},{3,1},{4,6},{5,7},{6,4},{7,5},{8,10},{9,11},{10,... | collective-permute-start | bytes 786440 | tf_op jit(solution)/shard_map/gather/ppermute | solution.py:198
  17.7 0.0 collective-permute-start.6
  17.7 3.2 %collective-permute-done.3.refs_1_ = f32[2,256,128]{2,1,0:T(8,128)S(1)} collective-permute-done((f32[2,256,128]{2,1,0:T(8,128)S(1)}, f32[2,256,128]{2,1,0:T(8,128)S(1)}, u32[]{:S(2)}, u32[]{:S(2)}) %collective-permute-start.3) | collective-permute-done | bytes 262176 | tf_op jit(solution)/shard_map/gather/ppermute | solution.py:260
  20.9 0.2 flip.1.refs_0_
  21.1 0.7 %backward.5._ = f32[2,256,128]{2,1,0:T(8,128)S(1)} custom-call(s32[2,128]{1,0:T(2,128)S(1)} %get-tuple-element.19.plan_ref._, bf16[256,1024]{1,0:T(8,128)(2,1)S(1)} %flip.1.refs_0_, bf16[1024,2048]{1,0:T(8,128)(2,1)S(1)} %get-tuple-element.20._.refs_1_.refs_2_, bf16[1024,2048]{1,0:T(8,128)(2,1)S(1)} %get-tuple-element.23.refs_2_.refs_3_), custom_call_target="tpu_custom_call" | custom-call | flops 8053063680 | bytes 183500800 | tf_op jit(solution)/shard_map/backward/pallas_call | solution.py:212
  21.8 0.1 collective-permute-start.4
  21.8 0.7 %backward.6.x_ref = f32[2,256,128]{2,1,0:T(8,128)S(1)} custom-call(f32[2,256,128]{2,1,0:T(8,128)S(1)} %backward.5._, bf16[256,1024]{1,0:T(8,128)(2,1)S(1)} %flip.1.refs_0_, bf16[1024,2048]{1,0:T(8,128)(2,1)S(1)} %get-tuple-element.20._.refs_1_.refs_2_, bf16[1024,2048]{1,0:T(8,128)(2,1)S(1)} %get-tuple-element.23.refs_2_.refs_3_), custom_call_target="tpu_custom_call" | custom-call | flops 8053063680 | bytes 183500800 | tf_op jit(solution)/shard_map/backward/pallas_call | solution.py:212
  22.5 0.8 %collective-permute-done.4.y_ref = f32[2,256,128]{2,1,0:T(8,128)S(1)} collective-permute-done((f32[2,256,128]{2,1,0:T(8,128)S(1)}, f32[2,256,128]{2,1,0:T(8,128)S(1)}, u32[]{:S(2)}, u32[]{:S(2)}) %collective-permute-start.4) | collective-permute-done | bytes 262176 | tf_op jit(solution)/shard_map/backward/ppermute | solution.py:198
  23.4 0.7 %backward.8._ = f32[2,256,128]{2,1,0:T(8,128)S(1)} custom-call(f32[1,256,128]{2,1,0:T(8,128)S(1)} %get-tuple-element.24._.refs_0_, bf16[256,1024]{1,0:T(8,128)(2,1)S(1)} %flip.1.refs_0_, bf16[1024,2048]{1,0:T(8,128)(2,1)S(1)} %get-tuple-element.20._.refs_1_.refs_2_, bf16[1024,2048]{1,0:T(8,128)(2,1)S(1)} %get-tuple-element.23.refs_2_.refs_3_), custom_call_target="tpu_custom_call" | custom-call | flops 8053063680 | bytes 183500800 | tf_op jit(solution)/shard_map/backward/pallas_call | solution.py:212
  24.1 0.7 %backward.9._.refs_0_ = f32[2,256,128]{2,1,0:T(8,128)S(1)} custom-call(f32[2,256,128]{2,1,0:T(8,128)S(1)} %backward.8._, bf16[256,1024]{1,0:T(8,128)(2,1)S(1)} %flip.1.refs_0_, bf16[1024,2048]{1,0:T(8,128)(2,1)S(1)} %get-tuple-element.20._.refs_1_.refs_2_, bf16[1024,2048]{1,0:T(8,128)(2,1)S(1)} %get-tuple-element.23.refs_2_.refs_3_), custom_call_target="tpu_custom_call" | custom-call | flops 8053063680 | bytes 183500800 | tf_op jit(solution)/shard_map/backward/pallas_call | solution.py:212
  24.8 0.2 collective-permute-start.9
  25.0 1.6 %collective-permute-start.7 = (f32[1,256,128]{2,1,0:T(8,128)S(1)}, f32[1,256,128]{2,1,0:T(8,128)S(1)}, u32[]{:S(2)}, u32[]{:S(2)}) collective-permute-start(f32[1,256,128]{2,1,0:T(8,128)S(1)} %get-tuple-element.26), channel_id=1, source_target_pairs={{0,2},{1,3},{2,0},{3,1},{4,6},{5,7},{6,4},{7,5},{8,10},{9,11},{10,... | collective-permute-start | bytes 393224 | tf_op jit(solution)/shard_map/reduce/ppermute | solution.py:198
  26.6 0.0 collective-permute-done.5.refs_0_
  26.7 0.1 collective-permute-start.8
  26.8 0.0 collective-permute-done.6.refs_1_
  26.8 1.3 %forward.4 = (f32[2,256,128]{2,1,0:T(8,128)S(1)}, f32[2,256,128]{2,1,0:T(8,128)S(1)}) custom-call(f32[2,256,128]{2,1,0:T(8,128)S(1)} %forward.3._.refs_0_, f32[2,256,128]{2,1,0:T(8,128)S(1)} %gather.3._.refs_0_, f32[2,256,128]{2,1,0:T(8,128)S(1)} %collective-permute-done.6.refs_1_, bf16[1024,2048]{1,0:T(8,128)(2,1)S(1)} %get-tuple-element.20._.refs_1_.refs_2_, ...), custom_call_target="tpu_custom_call" | custom-call | flops 16106127360 | bytes 188743680 | tf_op jit(solution)/shard_map/forward/pallas_call | solution.py:212
  28.1 2.7 %collective-permute-done.7.refs_1_ = f32[1,256,128]{2,1,0:T(8,128)S(1)} collective-permute-done((f32[1,256,128]{2,1,0:T(8,128)S(1)}, f32[1,256,128]{2,1,0:T(8,128)S(1)}, u32[]{:S(2)}, u32[]{:S(2)}) %collective-permute-start.7) | collective-permute-done | bytes 131104 | tf_op jit(solution)/shard_map/reduce/ppermute | solution.py:198
  30.8 0.0 collective-permute-done.8.refs_1_
  30.8 1.3 %forward.5 = (f32[2,256,128]{2,1,0:T(8,128)S(1)}, f32[2,256,128]{2,1,0:T(8,128)S(1)}) custom-call(f32[1,256,128]{2,1,0:T(8,128)S(1)} %reduce.3._, f32[2,256,128]{2,1,0:T(8,128)S(1)} %forward.3._.refs_0_, f32[2,256,128]{2,1,0:T(8,128)S(1)} %collective-permute-done.8.refs_1_, bf16[1024,2048]{1,0:T(8,128)(2,1)S(1)} %get-tuple-element.20._.refs_1_.refs_2_, ...), custom_call_target="tpu_custom_call" | custom-call | flops 16106127360 | bytes 199229440 | tf_op jit(solution)/shard_map/forward/pallas_call | solution.py:212
  32.1 1.6 %collective-permute-start.10 = (f32[2,256,128]{2,1,0:T(8,128)S(1)}, f32[2,256,128]{2,1,0:T(8,128)S(1)}, u32[]{:S(2)}, u32[]{:S(2)}) collective-permute-start(f32[2,256,128]{2,1,0:T(8,128)S(1)} %get-tuple-element.30), channel_id=1, source_target_pairs={{0,8},{1,17},{2,10},{3,19},{4,12},{5,21},{6,14},{7,23},{8,0},{9,25... | collective-permute-start | bytes 786440 | tf_op jit(solution)/shard_map/reduce/ppermute | solution.py:260
  33.7 0.3 collective-permute-start.13
  34.1 0.0 collective-permute-done.9.refs_1_
  34.1 1.6 %collective-permute-start.12 = (f32[1,256,128]{2,1,0:T(8,128)S(1)}, f32[1,256,128]{2,1,0:T(8,128)S(1)}, u32[]{:S(2)}, u32[]{:S(2)}) collective-permute-start(f32[1,256,128]{2,1,0:T(8,128)S(1)} %get-tuple-element.34), channel_id=1, source_target_pairs={{0,2},{1,3},{2,0},{3,1},{4,6},{5,7},{6,4},{7,5},{8,10},{9,11},{10,... | collective-permute-start | bytes 393224 | tf_op jit(solution)/shard_map/reduce/ppermute | solution.py:198
  35.7 2.9 %collective-permute-done.10.refs_1_ = f32[2,256,128]{2,1,0:T(8,128)S(1)} collective-permute-done((f32[2,256,128]{2,1,0:T(8,128)S(1)}, f32[2,256,128]{2,1,0:T(8,128)S(1)}, u32[]{:S(2)}, u32[]{:S(2)}) %collective-permute-start.10) | collective-permute-done | bytes 262176 | tf_op jit(solution)/shard_map/reduce/ppermute | solution.py:260
  38.6 0.6 %collective-permute-start.11 = (f32[1,256,128]{2,1,0:T(8,128)S(1)}, f32[1,256,128]{2,1,0:T(8,128)S(1)}, u32[]{:S(2)}, u32[]{:S(2)}) collective-permute-start(f32[1,256,128]{2,1,0:T(8,128)S(1)} %get-tuple-element.32), channel_id=1, source_target_pairs={{0,16},{1,9},{2,18},{3,11},{4,20},{5,13},{6,22},{7,15},{8,24},{9,1... | collective-permute-start | bytes 393224 | tf_op jit(solution)/shard_map/reduce/ppermute | solution.py:260
  39.2 2.0 %collective-permute-done.13.refs_2_ = f32[1,256,128]{2,1,0:T(8,128)S(1)} collective-permute-done((f32[1,256,128]{2,1,0:T(8,128)S(1)}, f32[1,256,128]{2,1,0:T(8,128)S(1)}, u32[]{:S(2)}, u32[]{:S(2)}) %collective-permute-start.13) | collective-permute-done | bytes 131104 | tf_op jit(solution)/shard_map/reduce/ppermute | solution.py:198
  41.2 0.0 collective-permute-done.12.refs_1_
  41.2 0.7 %finish.3 = f32[256,128]{1,0:T(8,128)} custom-call(f32[1,256,128]{2,1,0:T(8,128)S(1)} %get-tuple-element.29._.refs_0_, f32[1,256,128]{2,1,0:T(8,128)S(1)} %collective-permute-done.12.refs_1_, f32[1,256,128]{2,1,0:T(8,128)S(1)} %collective-permute-done.13.refs_2_, f32[256,128]{1,0:T(8,128)S(1)} %get-tuple-element.35.refs_3_), custom_call_target="tpu_custom_call" | custom-call | bytes 13107200 | tf_op jit(solution)/shard_map/finish/pallas_call | solution.py:212
  41.9 1.7 %collective-permute-done.11.refs_1_ = f32[1,256,128]{2,1,0:T(8,128)S(1)} collective-permute-done((f32[1,256,128]{2,1,0:T(8,128)S(1)}, f32[1,256,128]{2,1,0:T(8,128)S(1)}, u32[]{:S(2)}, u32[]{:S(2)}) %collective-permute-start.11) | collective-permute-done | bytes 131104 | tf_op jit(solution)/shard_map/reduce/ppermute | solution.py:260
  43.6 0.7 %finish.2 = f32[256,128]{1,0:T(8,128)} custom-call(f32[1,256,128]{2,1,0:T(8,128)S(1)} %get-tuple-element.31.refs_0_, f32[1,256,128]{2,1,0:T(8,128)S(1)} %collective-permute-done.11.refs_1_, f32[256,128]{1,0:T(8,128)S(1)} %get-tuple-element.33.refs_2_), custom_call_target="tpu_custom_call" | custom-call | bytes 10485760 | tf_op jit(solution)/shard_map/finish/pallas_call | solution.py:212
  (7 shorter events, 0.2 us)
Async XLA Ops:
  0.6 10.8 %collective-permute-start = (f32[128,128,128]{2,1,0:T(8,128)}, f32[128,128,128]{2,1,0:T(8,128)S(1)}, u32[]{:S(2)}, u32[]{:S(2)}) collective-permute-start(f32[128,128,128]{2,1,0:T(8,128)} %bitcast.5), channel_id=1, source_target_pairs={{0,0},{1,1},{2,2},{3,3},{4,4},{5,5},{6,6},{7,7},{8,8},{9,9},{10,10... | collective-permute-start | bytes 25165832 | tf_op jit(solution)/shard_map/fetch/ppermute | solution.py:198
  5.2 9.2 %collective-permute-start.1 = (f32[1,256,128]{2,1,0:T(8,128)S(1)}, f32[1,256,128]{2,1,0:T(8,128)S(1)}, u32[]{:S(2)}, u32[]{:S(2)}) collective-permute-start(f32[1,256,128]{2,1,0:T(8,128)S(1)} %get-tuple-element.21.refs_0_), channel_id=1, source_target_pairs={{0,16},{1,9},{2,18},{3,11},{4,20},{5,13},{6,22},{7,15},{8,24},{9,1... | collective-permute-start | bytes 393224 | tf_op jit(solution)/shard_map/gather/ppermute | solution.py:260
  8.2 8.6 %collective-permute-start.2 = (f32[1,256,128]{2,1,0:T(8,128)S(1)}, f32[1,256,128]{2,1,0:T(8,128)S(1)}, u32[]{:S(2)}, u32[]{:S(2)}) collective-permute-start(f32[1,256,128]{2,1,0:T(8,128)S(1)} %get-tuple-element.22.refs_0_), channel_id=1, source_target_pairs={{0,4},{1,5},{2,6},{3,7},{4,0},{5,1},{6,2},{7,3},{8,12},{9,13},{10,... | collective-permute-start | bytes 393224 | tf_op jit(solution)/shard_map/ppermute | solution.py:198
  14.4 6.4 %collective-permute-start.3 = (f32[2,256,128]{2,1,0:T(8,128)S(1)}, f32[2,256,128]{2,1,0:T(8,128)S(1)}, u32[]{:S(2)}, u32[]{:S(2)}) collective-permute-start(f32[2,256,128]{2,1,0:T(8,128)S(1)} %gather.2._.refs_0_), channel_id=1, source_target_pairs={{0,8},{1,17},{2,10},{3,19},{4,12},{5,21},{6,14},{7,23},{8,0},{9,25... | collective-permute-start | bytes 786440 | tf_op jit(solution)/shard_map/gather/ppermute | solution.py:260
  16.9 9.8 %collective-permute-start.5 = (f32[2,256,128]{2,1,0:T(8,128)S(1)}, f32[2,256,128]{2,1,0:T(8,128)S(1)}, u32[]{:S(2)}, u32[]{:S(2)}) collective-permute-start(f32[2,256,128]{2,1,0:T(8,128)S(1)} %gather.3._.refs_0_), channel_id=1, source_target_pairs={{0,2},{1,3},{2,0},{3,1},{4,6},{5,7},{6,4},{7,5},{8,10},{9,11},{10,... | collective-permute-start | bytes 786440 | tf_op jit(solution)/shard_map/gather/ppermute | solution.py:198
  17.7 9.1 %collective-permute-start.6 = (f32[2,256,128]{2,1,0:T(8,128)S(1)}, f32[2,256,128]{2,1,0:T(8,128)S(1)}, u32[]{:S(2)}, u32[]{:S(2)}) collective-permute-start(f32[2,256,128]{2,1,0:T(8,128)S(1)} %gather.3._.refs_0_), channel_id=1, source_target_pairs={{0,1},{1,0},{2,3},{3,2},{4,5},{5,4},{6,7},{7,6},{8,9},{9,8},{10,11... | collective-permute-start | bytes 786440 | tf_op jit(solution)/shard_map/gather/ppermute | solution.py:198
  21.8 1.6 %collective-permute-start.4 = (f32[2,256,128]{2,1,0:T(8,128)S(1)}, f32[2,256,128]{2,1,0:T(8,128)S(1)}, u32[]{:S(2)}, u32[]{:S(2)}) collective-permute-start(f32[2,256,128]{2,1,0:T(8,128)S(1)} %backward.5._), channel_id=1, source_target_pairs={{0,1},{1,0},{2,3},{3,2},{4,5},{5,4},{6,7},{7,6},{8,9},{9,8},{10,11... | collective-permute-start | bytes 786440 | tf_op jit(solution)/shard_map/backward/ppermute | solution.py:198
  24.8 9.3 %collective-permute-start.9 = (f32[2,256,128]{2,1,0:T(8,128)S(1)}, f32[2,256,128]{2,1,0:T(8,128)S(1)}, u32[]{:S(2)}, u32[]{:S(2)}) collective-permute-start(f32[2,256,128]{2,1,0:T(8,128)S(1)} %backward.8._), channel_id=1, source_target_pairs={{0,1},{1,0},{2,3},{3,2},{4,5},{5,4},{6,7},{7,6},{8,9},{9,8},{10,11... | collective-permute-start | bytes 786440 | tf_op jit(solution)/shard_map/reduce/ppermute | solution.py:198
  25.0 5.8 %collective-permute-start.7 = (f32[1,256,128]{2,1,0:T(8,128)S(1)}, f32[1,256,128]{2,1,0:T(8,128)S(1)}, u32[]{:S(2)}, u32[]{:S(2)}) collective-permute-start(f32[1,256,128]{2,1,0:T(8,128)S(1)} %get-tuple-element.26), channel_id=1, source_target_pairs={{0,2},{1,3},{2,0},{3,1},{4,6},{5,7},{6,4},{7,5},{8,10},{9,11},{10,... | collective-permute-start | bytes 393224 | tf_op jit(solution)/shard_map/reduce/ppermute | solution.py:198
  26.7 4.2 %collective-permute-start.8 = (f32[2,256,128]{2,1,0:T(8,128)S(1)}, f32[2,256,128]{2,1,0:T(8,128)S(1)}, u32[]{:S(2)}, u32[]{:S(2)}) collective-permute-start(f32[2,256,128]{2,1,0:T(8,128)S(1)} %forward.3._.refs_0_), channel_id=1, source_target_pairs={{0,1},{1,0},{2,3},{3,2},{4,5},{5,4},{6,7},{7,6},{8,9},{9,8},{10,11... | collective-permute-start | bytes 786440 | tf_op jit(solution)/shard_map/forward/ppermute | solution.py:198
  32.1 6.4 %collective-permute-start.10 = (f32[2,256,128]{2,1,0:T(8,128)S(1)}, f32[2,256,128]{2,1,0:T(8,128)S(1)}, u32[]{:S(2)}, u32[]{:S(2)}) collective-permute-start(f32[2,256,128]{2,1,0:T(8,128)S(1)} %get-tuple-element.30), channel_id=1, source_target_pairs={{0,8},{1,17},{2,10},{3,19},{4,12},{5,21},{6,14},{7,23},{8,0},{9,25... | collective-permute-start | bytes 786440 | tf_op jit(solution)/shard_map/reduce/ppermute | solution.py:260
  33.7 7.5 %collective-permute-start.13 = (f32[1,256,128]{2,1,0:T(8,128)S(1)}, f32[1,256,128]{2,1,0:T(8,128)S(1)}, u32[]{:S(2)}, u32[]{:S(2)}) collective-permute-start(f32[1,256,128]{2,1,0:T(8,128)S(1)} %reduce.3._), channel_id=1, source_target_pairs={{0,4},{1,5},{2,6},{3,7},{4,0},{5,1},{6,2},{7,3},{8,12},{9,13},{10,... | collective-permute-start | bytes 393224 | tf_op jit(solution)/shard_map/reduce/ppermute | solution.py:198
  34.1 7.1 %collective-permute-start.12 = (f32[1,256,128]{2,1,0:T(8,128)S(1)}, f32[1,256,128]{2,1,0:T(8,128)S(1)}, u32[]{:S(2)}, u32[]{:S(2)}) collective-permute-start(f32[1,256,128]{2,1,0:T(8,128)S(1)} %get-tuple-element.34), channel_id=1, source_target_pairs={{0,2},{1,3},{2,0},{3,1},{4,6},{5,7},{6,4},{7,5},{8,10},{9,11},{10,... | collective-permute-start | bytes 393224 | tf_op jit(solution)/shard_map/reduce/ppermute | solution.py:198
  38.6 5.0 %collective-permute-start.11 = (f32[1,256,128]{2,1,0:T(8,128)S(1)}, f32[1,256,128]{2,1,0:T(8,128)S(1)}, u32[]{:S(2)}, u32[]{:S(2)}) collective-permute-start(f32[1,256,128]{2,1,0:T(8,128)S(1)} %get-tuple-element.32), channel_id=1, source_target_pairs={{0,16},{1,9},{2,18},{3,11},{4,20},{5,13},{6,22},{7,15},{8,24},{9,1... | collective-permute-start | bytes 393224 | tf_op jit(solution)/shard_map/reduce/ppermute | solution.py:260

commit v5 on v3

v5 whole, which is shorter than its diff:
```python
import functools
import math

import jax
import jax.numpy as jnp
from jax import lax
from jax.experimental import pallas as pl
from jax.experimental.pallas import tpu as pltpu
from jax.sharding import PartitionSpec as P

F32 = jnp.float32
BF16 = jnp.bfloat16
WHOLE = pl.BlockSpec(memory_space=pltpu.VMEM)
ANYWHERE = pl.BlockSpec(memory_space=pl.ANY)
SCALARS = pl.BlockSpec(memory_space=pltpu.SMEM)


def params(mebibytes):
    return pltpu.CompilerParams(vmem_limit_bytes=mebibytes * 2**20)


def cost(flops, moved):
    return pl.CostEstimate(flops=flops, bytes_accessed=moved, transcendentals=0)


def halves(x):
    high = x.astype(BF16)
    return high, (x - high.astype(F32)).astype(BF16)


def product(left, right):
    return jnp.dot(left, right, preferred_element_type=F32)


def row_factors(degree_ref, at, width):
    factors = lax.rsqrt(degree_ref[at : at + 1, :].astype(F32))
    return jnp.broadcast_to(factors, (width, factors.shape[1])).T


def scale_kernel(tiles, pairs, *refs):
    in_refs, (grad_ref, scaled_ref, row_factor_ref, col_factor_ref, plan_ref) = refs[:5], refs[5:10]
    bufs, sems = refs[10:15], refs[15]
    copies = [pltpu.make_async_copy(*pair, sems.at[at]) for at, pair in enumerate(zip(in_refs, bufs))]
    for copy in copies:
        copy.start()
    for copy in copies:
        copy.wait()
    cotangent, embed, row_degree, col_degree, coords = bufs
    for x_buf, degree_buf, out_ref, factor_ref in (
        (embed, col_degree, scaled_ref, col_factor_ref),
        (cotangent, row_degree, grad_ref, row_factor_ref),
    ):
        tile = degree_buf.shape[1]
        for at in range(degree_buf.shape[0]):
            rows = pl.ds(at * tile, tile)
            factors = row_factors(degree_buf, at, x_buf.shape[1])
            factor_ref[rows, :] = factors
            out_ref[rows, :] = x_buf[rows, :] * factors
    plan_ref[0:1, :] = row_place(coords[0, 0], tiles) * tile
    plan_ref[1:2, :] = col_place(coords[1, 0], tiles, pairs) * tile


def finish_kernel(*refs):
    *part_refs, factor_ref, out_ref, token_ref = refs
    token_ref[...] = jnp.zeros_like(token_ref)
    total = part_refs[0][...]
    for part_ref in part_refs[1:]:
        total = total + part_ref[...]
    out_ref[...] = total * factor_ref[...]


def add_kernel(x_ref, y_ref, out_ref):
    out_ref[...] = x_ref[...] + y_ref[...]


def pair_kernel(kept_ref, got_ref, *out_refs):
    for at, out_ref in enumerate(out_refs):
        out_ref[...] = kept_ref[at] + got_ref[at]


def stack_kernel(*refs):
    *part_refs, out_ref, last_ref = refs
    for at, part_ref in enumerate(part_refs):
        out_ref[at] = part_ref[...]
    last_ref[...] = part_refs[-1][...]


def copy_kernel(*refs):
    *part_refs, out_ref = refs
    for at, part_ref in enumerate(part_refs):
        out_ref[at] = part_ref[...]


def row_place(tile_at, tiles):
    return tile_at ^ (lax.axis_index("row") * tiles)


def col_shard(distance, core, pairs):
    early = pairs // 2 + 1
    late = 2 * early + core * (pairs - early) + distance - early
    return jnp.where(distance < early, core * early + distance, late)


def col_place(tile_at, tiles, pairs):
    tile_at = tile_at ^ (lax.axis_index("col") * tiles)
    shard = lax.shift_right_logical(tile_at, tiles.bit_length() - 1)
    return col_shard(lax.shift_right_logical(shard, 1), shard & 1, pairs) * tiles + (tile_at & (tiles - 1))


def split_kernel(plan_ref, count_ref, values_ref, high_ref, low_ref, buf, sems):
    capacity, tile, _ = values_ref.shape
    groups = sems.shape[0]
    group = capacity // groups
    together = math.gcd(group, 2)
    copies = []
    for at in range(groups):
        slots = pl.ds(at * group, group)
        copies.append(pltpu.make_async_copy(values_ref.at[slots], buf.at[slots], sems.at[at]))
        copies[-1].start()
    for at, copy in enumerate(copies):
        copy.wait()

        @pl.loop(at * group, (at + 1) * group, step=together, unroll=2)
        def _(first):
            parts = []
            for slot in range(together):
                rows = pl.ds(pl.multiple_of(plan_ref[0, first + slot], tile), tile)
                cols = pl.ds(pl.multiple_of(plan_ref[1, first + slot], tile), tile)
                live = first + slot < count_ref[0, 0]
                parts.append((rows, cols, *halves(jnp.where(live, buf[first + slot], 0.0))))
            for rows, cols, high, low in parts:
                high_ref[rows, cols] = high
                low_ref[rows, cols] = low


def flip_kernel(tile, *refs):
    *grad_refs, out_ref = refs
    shard, width = grad_refs[0].shape
    for at, grad_ref in enumerate(grad_refs):
        for first in range(0, shard, tile):
            high, low = halves(grad_ref[pl.ds(first, tile), :].T)
            cols = pl.ds(at * shard + first, tile)
            out_ref[:width, cols] = high
            out_ref[width:, cols] = low


def backward_kernel(firsts, tile, grads_ref, high_ref, low_ref, out_ref):
    _, shard, width = out_ref.shape
    for at, first in enumerate(firsts):
        cols = pl.ds(first * shard, shard)
        both = product(grads_ref[...], high_ref[:, cols])
        total = both[:width] + both[width:] + product(grads_ref[:width, :], low_ref[:, cols])
        for row in range(0, shard, tile):
            out_ref[at, pl.ds(row, tile), :] = total[:, row : row + tile].T


def forward_kernel(first, count, bands, *refs):
    embed_refs, (high_ref, low_ref) = refs[:count], refs[count : count + 2]
    before_refs, out_refs, panel = refs[count + 2 : -1 - bands], refs[-1 - bands : -1], refs[-1]
    _, shard, width = embed_refs[0].shape
    done = 0
    for embeds_ref in embed_refs:
        for at in range(embeds_ref.shape[0]):
            high, low = halves(embeds_ref[at])
            panel[pl.ds(done, shard), :width] = high
            panel[pl.ds(done, shard), width:] = low
            done += shard
    cols = pl.ds(first * shard, done)
    for at, out_ref in enumerate(out_refs):
        rows = pl.ds(at * shard, shard)
        both = product(high_ref[rows, cols], panel[...])
        total = both[:, :width] + both[:, width:] + product(low_ref[rows, cols], panel[:, :width])
        if before_refs:
            total = total + before_refs[at][...]
        out_ref[...] = total


def slots_kernel(tiles, pairs, coords_ref, count_ref, values_ref, embed_ref, grad_ref, forward_ref, backward_ref):
    group, tile, _ = values_ref.shape
    first = pl.program_id(0) * group

    @pl.when(pl.program_id(0) == 0)
    def _():
        forward_ref[...] = jnp.zeros_like(forward_ref)
        backward_ref[...] = jnp.zeros_like(backward_ref)

    for slot in range(group):

        @pl.when(first + slot < count_ref[0, 0])
        def _():
            row_at = row_place(coords_ref[0, 0, 0, first + slot], tiles)
            col_at = col_place(coords_ref[1, 0, 0, first + slot], tiles, pairs)
            rows = pl.ds(pl.multiple_of(row_at * tile, tile), tile)
            cols = pl.ds(pl.multiple_of(col_at * tile, tile), tile)
            high, low = halves(values_ref[slot])
            embed_high, embed_low = halves(embed_ref[cols, :])
            forward_ref[rows, :] += product(high, embed_high) + product(high, embed_low) + product(low, embed_high)
            high, low = halves(values_ref[slot].T)
            grad_high, grad_low = halves(grad_ref[rows, :])
            backward_ref[cols, :] += product(high, grad_high) + product(high, grad_low) + product(low, grad_high)


def swap(x, axis, mask):
    return lax.ppermute(x, axis, [(at, at ^ mask) for at in range(lax.axis_size(axis))])


def call(kernel, out_shape, args, mebibytes=16, scratch=(), specs=None, after=None):
    outs = out_shape if isinstance(out_shape, tuple) else (out_shape,)
    specs = specs or [WHOLE] * len(args)
    body = kernel
    if after is not None:
        args, specs = (after, *args), [ANYWHERE, *specs]

        def body(_, *refs):
            kernel(*refs)

    return pl.pallas_call(
        body,
        out_shape=out_shape,
        in_specs=specs,
        out_specs=tuple(WHOLE for _ in outs) if isinstance(out_shape, tuple) else WHOLE,
        scratch_shapes=scratch,
        compiler_params=params(mebibytes),
        cost_estimate=cost(0, 1024),
    )(*args)


def per_device(embed, cotangent, tile_values, tile_coords, tile_count, row_degree, col_degree):
    shard, width = embed.shape
    capacity, tile = tile_values.shape[2:4]
    n_row, n_col = lax.axis_size("row"), lax.axis_size("col")
    pairs = n_col // 2
    half = pairs // 2
    tiles = shard // tile
    n_rows, n_cols = shard * n_row, shard * n_col
    dense = (n_rows // tile) * (n_cols // tile) <= capacity
    values = tile_values.reshape(tile_values.shape[2:])
    block = jax.ShapeDtypeStruct((shard, width), F32)

    def blocks(count):
        return jax.ShapeDtypeStruct((count, shard, width), F32)

    with jax.named_scope("scale"):
        args = (cotangent, embed, row_degree.reshape(-1, tile), col_degree.reshape(-1, tile), tile_coords)
        grad_scaled, scaled, row_factor, col_factor, plan = call(
            functools.partial(scale_kernel, tiles, pairs),
            (block,) * 4 + (jax.ShapeDtypeStruct((2, capacity), jnp.int32),),
            [pltpu.with_memory_space_constraint(x, pltpu.HBM) for x in args],
            mebibytes=4,
            specs=[pl.BlockSpec(memory_space=pltpu.HBM)] * len(args),
            scratch=[pltpu.VMEM(x.shape, x.dtype) for x in args] + [pltpu.SemaphoreType.DMA((len(args),))],
        )

    with jax.named_scope("gather"):
        crossed = swap(scaled, "col", 2 * half)
        grads = [grad_scaled] + [swap(grad_scaled, "row", k) for k in range(1, n_row)]
        near = {0: scaled}
        mask = half // 2
        while mask:
            near.update({at | mask: swap(x, "col", 2 * mask) for at, x in near.items()})
            mask //= 2

    def gathered(after):
        early, passed = call(
            stack_kernel,
            (blocks(half + 1), block),
            [near[at] for at in range(half)] + [crossed],
            after=after,
        )
        late, mask = {0: passed}, half // 2
        while mask:
            late.update({at | mask: swap(x, "col", 2 * mask) for at, x in late.items()})
            mask //= 2
        return early, [late[at] for at in range(1, half)]

    def chip_sums(kept, sent, after=None):
        return call(
            pair_kernel,
            (block,) * kept.shape[0],
            (kept, swap(sent, "col", 1)),
            after=after,
        )

    def halved(parts, after):
        parts, got, mask = dict(enumerate(parts)), [], 1
        while mask < half:
            for at in reversed(range(0, half, 2 * mask)):
                arrived = swap(parts.pop(at + mask), "col", 2 * mask)
                if at:
                    parts[at] = call(add_kernel, block, (parts[at], arrived), after=after)
                else:
                    got.append(arrived)
            mask *= 2
        return [parts[0], *got]

    def total(parts, after):
        out, *rest = parts
        for part in rest:
            out = call(add_kernel, block, (out, part), after=after)
        return out

    if dense:
        table = jax.ShapeDtypeStruct((n_rows, n_cols), BF16)
        groups = math.gcd(capacity, 8)
        with jax.named_scope("split"):
            high, low = call(
                split_kernel,
                (table, table),
                (plan, tile_count, pltpu.with_memory_space_constraint(values, pltpu.HBM)),
                mebibytes=32,
                specs=[SCALARS, SCALARS, pl.BlockSpec(memory_space=pltpu.HBM)],
                scratch=[pltpu.VMEM(values.shape, F32), pltpu.SemaphoreType.DMA((groups,))],
            )
        with jax.named_scope("gather"):
            early, late = gathered(high)
            other_early = swap(early, "col", 1)
        with jax.named_scope("flip"):
            flipped = call(
                functools.partial(flip_kernel, tile),
                jax.ShapeDtypeStruct((2 * width, n_rows), BF16),
                grads,
                after=early,
            )

        def backward_part(distances, core, after):
            shards = [shard_at(distance, core) for distance in distances]
            return call(
                functools.partial(backward_kernel, shards, tile),
                blocks(len(shards)),
                (flipped, high, low),
                mebibytes=24,
                after=after,
            )

        def shard_at(distance, core):
            count = half + 1
            if distance < count:
                return core * count + distance
            return 2 * count + core * (pairs - count) + distance - count

        def forward_part(embeds, first, before=(), after=None):
            count = sum(x.shape[0] for x in embeds)
            return call(
                functools.partial(forward_kernel, first, len(embeds), n_row),
                (block,) * n_row,
                (*embeds, high, low, *before),
                mebibytes=24,
                scratch=[pltpu.VMEM((count * shard, 2 * width), BF16)],
                after=after,
            )

        with jax.named_scope("backward"):
            far, close = range(half, pairs), range(half)
            far_sent = backward_part(far, 1, plan)
            sent = backward_part(close, 1, far_sent)
            far_sums = chip_sums(backward_part(far, 0, sent), far_sent)
            kept = backward_part(close, 0, far_sums[0])
        with jax.named_scope("gather"):
            late = call(copy_kernel, blocks(half - 1), late, after=kept)
            other_late = swap(late, "col", 1)
        with jax.named_scope("forward"):
            forwards = forward_part([early, other_early], 0, after=late)
        with jax.named_scope("reduce"):
            crossing = total(halved(far_sums, forwards[0]), forwards[0])
        with jax.named_scope("forward"):
            forwards = forward_part([late, other_late], 2 * (half + 1), forwards, crossing)
        with jax.named_scope("reduce"):
            close_sums = chip_sums(kept, sent)
            after = None
    else:
        group = 8
        with jax.named_scope("gather"):
            early, late = gathered(plan)
            late = call(copy_kernel, blocks(half - 1), late)
            panel = jnp.concatenate([early, swap(early, "col", 1), late, swap(late, "col", 1)])
        with jax.named_scope("slots"):
            forward, backward = pl.pallas_call(
                functools.partial(slots_kernel, tiles, pairs),
                out_shape=(
                    jax.ShapeDtypeStruct((n_rows, width), F32),
                    jax.ShapeDtypeStruct((n_cols, width), F32),
                ),
                grid=(capacity // group,),
                in_specs=[SCALARS, SCALARS, pl.BlockSpec((group, tile, tile), lambda at: (at, 0, 0)), WHOLE, WHOLE],
                out_specs=(WHOLE, WHOLE),
                compiler_params=params(40),
                cost_estimate=cost(12 * values.size * width, values.size * 4),
            )(tile_coords, tile_count, values, panel.reshape(-1, width), jnp.concatenate(grads))
            forwards = list(forward.reshape(n_row, shard, width))
            backward = backward.reshape(n_col, shard, width)
            count = half + 1
            kept, sent = (
                jnp.concatenate(
                    [
                        backward[core * count : (core + 1) * count],
                        backward[2 * count + core * (half - 1) : 2 * count + (core + 1) * (half - 1)],
                    ]
                )
                for core in range(2)
            )
        with jax.named_scope("reduce"):
            far_sums, close_sums = (chip_sums(kept[at : at + half], sent[at : at + half]) for at in (half, 0))
            crossing = total(halved(far_sums, forward), forward)
            after = forward

    with jax.named_scope("reduce"):
        mine, *grad_parts = halved(close_sums, after)
        mine = total([mine, swap(crossing, "col", 2 * half)], None)
        row_parts = [forwards[0]] + [swap(forwards[k], "row", k) for k in range(1, n_row)]

    with jax.named_scope("finish"):
        outs = (block, jax.ShapeDtypeStruct((8, tile), F32))
        propagated, token = call(finish_kernel, outs, (*row_parts, row_factor), mebibytes=4, after=mine)
        embed_grad, _ = call(finish_kernel, outs, (mine, *grad_parts, col_factor), mebibytes=4, after=token)
    return propagated, embed_grad


def solution(mesh):
    return jax.shard_map(
        per_device,
        mesh=mesh,
        in_specs=(
            P(("row", "col"), None),
            P(("col", "row"), None),
            P("col", "row", None, None, None),
            P(None, "col", "row", None),
            P("col", "row"),
            P(("col", "row")),
            P(("row", "col")),
        ),
        out_specs=(P(("col", "row"), None), P(("row", "col"), None)),
        check_vma=False,
    )
```

time: 41.7 us -> 38.1 us (0.914)
  waiting for transfers between devices: 8.81 us -> 6.74 us
  starting transfers between devices: 18.7 us -> 17.2 us
    ppermute x15 -> x16, waiting for transfers between devices: 8.81 us -> 6.74 us  [swap(): lax.ppermute(x, axis, [(at, at ^ mask) for at in range(lax.axis_size(axis...]
    ppermute x15 -> x16, starting transfers between devices: 18.7 us -> 17.2 us  [swap(): lax.ppermute(x, axis, [(at, at ^ mask) for at in range(lax.axis_size(axis...]
    pallas_call x15 -> x17, Pallas kernels: 12.6 us -> 12.5 us  [call(): pl.pallas_call(body, out_shape=out_shape, in_specs=specs, out_specs=tuple...]
  transfers between devices with their start and end apart: 15 -> 16, of which waited for: 7 -> 5; matrix products, arithmetic and copies ran while one was open for 0% -> 0% of each run, Pallas kernels for 26% -> 26%
where the time goes in v5:
time: 38.1 us; the launch traced here: 37.9 us
  starting transfers between devices  17.2 us (45%)
  Pallas kernels  12.5 us (33%)
  waiting for transfers between devices  6.74 us (18%)
  between operations  1.48 us (4%)
    ppermute x16, starting transfers between devices, swap(): lax.ppermute(x, axis, [(at, at ^ mask) for at in range(lax.axis_size(axis...  17.2 us
    pallas_call x17, Pallas kernels, call(): pl.pallas_call(body, out_shape=out_shape, in_specs=specs, out_specs=tuple...  12.5 us
    ppermute x16, waiting for transfers between devices, swap(): lax.ppermute(x, axis, [(at, at ^ mask) for at in range(lax.axis_size(axis...  6.74 us
  transfers between devices with their start and end apart: 16, of which 5 were waited for; matrix products, arithmetic and copies ran while one was open for 0% of the time, Pallas kernels for 26%

profile of v5, /device:TPU:0, one launch (start us, length us, event | category | flops | bytes accessed | tf_op | source)
XLA Modules:
  0.0 37.9 jit_solution(4396374355467103574)
XLA Ops:
  0.6 1.2 %scale.1 = (f32[256,128]{1,0:T(8,128)S(1)}, f32[256,128]{1,0:T(8,128)S(1)}, f32[256,128]{1,0:T(8,128)S(1)}, f32[256,128]{1,0:T(8,128)S(1)}, s32[2,128]{1,0:T(2,128)S(1)}) custom-call(f32[256,128]{1,0:T(8,128)} %refs_0_.1, f32[256,128]{1,0:T(8,128)} %refs_1_.1, s32[2,128]{1,0:T(2,128)} %bitcast.4, s32[2,128]{1,0:T(2,128)} %bitcast.5, s32[2,1,1,128]{3,2,1,0:T(1,128)} %refs_4_.1), custom_call_target="tpu_custom_call" | custom-call | bytes 1024 | tf_op jit(solution)/shard_map/scale/pallas_call | solution.py:217
  1.8 4.1 %collective-permute-start.1 = (f32[256,128]{1,0:T(8,128)S(1)}, f32[256,128]{1,0:T(8,128)S(1)}, u32[]{:S(2)}, u32[]{:S(2)}) collective-permute-start(f32[256,128]{1,0:T(8,128)S(1)} %get-tuple-element.28.refs_0_), channel_id=1, source_target_pairs={{0,4},{1,5},{2,6},{3,7},{4,0},{5,1},{6,2},{7,3},{8,12},{9,13},{10,... | collective-permute-start | bytes 393224 | tf_op jit(solution)/shard_map/gather/ppermute | solution.py:204
  5.9 1.6 %collective-permute-start = (f32[256,128]{1,0:T(8,128)S(1)}, f32[256,128]{1,0:T(8,128)S(1)}, u32[]{:S(2)}, u32[]{:S(2)}) collective-permute-start(f32[256,128]{1,0:T(8,128)S(1)} %get-tuple-element.28.refs_0_), channel_id=1, source_target_pairs={{0,2},{1,3},{2,0},{3,1},{4,6},{5,7},{6,4},{7,5},{8,10},{9,11},{10,... | collective-permute-start | bytes 393224 | tf_op jit(solution)/shard_map/gather/ppermute | solution.py:204
  7.5 2.4 %collective-permute-start.4 = (f32[256,128]{1,0:T(8,128)S(1)}, f32[256,128]{1,0:T(8,128)S(1)}, u32[]{:S(2)}, u32[]{:S(2)}) collective-permute-start(f32[256,128]{1,0:T(8,128)S(1)} %get-tuple-element.30.refs_0_), channel_id=1, source_target_pairs={{0,24},{8,16},{16,8},{24,0},{1,25},{9,17},{17,9},{25,1},{2,26},{10... | collective-permute-start | bytes 393224 | tf_op jit(solution)/shard_map/gather/ppermute | solution.py:204
  9.9 0.5 %collective-permute-start.3 = (f32[256,128]{1,0:T(8,128)S(1)}, f32[256,128]{1,0:T(8,128)S(1)}, u32[]{:S(2)}, u32[]{:S(2)}) collective-permute-start(f32[256,128]{1,0:T(8,128)S(1)} %get-tuple-element.30.refs_0_), channel_id=1, source_target_pairs={{0,16},{8,24},{16,0},{24,8},{1,17},{9,25},{17,1},{25,9},{2,18},{10... | collective-permute-start | bytes 393224 | tf_op jit(solution)/shard_map/gather/ppermute | solution.py:204
  10.4 0.5 %collective-permute-start.2 = (f32[256,128]{1,0:T(8,128)S(1)}, f32[256,128]{1,0:T(8,128)S(1)}, u32[]{:S(2)}, u32[]{:S(2)}) collective-permute-start(f32[256,128]{1,0:T(8,128)S(1)} %get-tuple-element.30.refs_0_), channel_id=1, source_target_pairs={{0,8},{8,0},{16,24},{24,16},{1,9},{9,1},{17,25},{25,17},{2,10},{10... | collective-permute-start | bytes 393224 | tf_op jit(solution)/shard_map/gather/ppermute | solution.py:204
  11.6 4.3 %split.1 = (bf16[1024,2048]{1,0:T(8,128)(2,1)S(1)}, bf16[1024,2048]{1,0:T(8,128)(2,1)S(1)}) custom-call(s32[2,128]{1,0:T(2,128)S(1)} %get-tuple-element.26.plan_ref._, s32[1,1]{1,0:T(1,128)S(6)} %copy.9.count_ref, f32[128,128,128]{2,1,0:T(8,128)} %bitcast.3), custom_call_target="tpu_custom_call" | custom-call | bytes 1024 | tf_op jit(solution)/shard_map/split/pallas_call | solution.py:217
  15.9 0.0 collective-permute-done.1.refs_2_
  16.0 0.0 collective-permute-done.refs_1_
  16.0 0.0 collective-permute-done.4.refs_3_
  16.0 0.0 collective-permute-done.3.refs_2_
  16.0 0.0 collective-permute-done.2.refs_1_
  16.0 0.2 flip.1.refs_0_
  16.3 0.7 %backward.5._ = f32[2,256,128]{2,1,0:T(8,128)S(1)} custom-call(s32[2,128]{1,0:T(2,128)S(1)} %get-tuple-element.26.plan_ref._, bf16[256,1024]{1,0:T(8,128)(2,1)S(1)} %flip.1.refs_0_, bf16[1024,2048]{1,0:T(8,128)(2,1)S(1)} %get-tuple-element.27._.refs_1_.refs_2_, bf16[1024,2048]{1,0:T(8,128)(2,1)S(1)} %get-tuple-element.31.refs_2_.refs_3_), custom_call_target="tpu_custom_call" | custom-call | bytes 1024 | tf_op jit(solution)/shard_map/backward/pallas_call | solution.py:217
  16.9 0.1 collective-permute-start.5
  17.0 0.5 %collective-permute-start.8 = (f32[3,256,128]{2,1,0:T(8,128)S(1)}, f32[3,256,128]{2,1,0:T(8,128)S(1)}, u32[]{:S(2)}, u32[]{:S(2)}) collective-permute-start(f32[3,256,128]{2,1,0:T(8,128)S(1)} %get-tuple-element.29._.refs_0_), channel_id=1, source_target_pairs={{0,1},{1,0},{2,3},{3,2},{4,5},{5,4},{6,7},{7,6},{8,9},{9,8},{10,11... | collective-permute-start | bytes 1179656 | tf_op jit(solution)/shard_map/gather/ppermute | solution.py:204
  17.5 0.4 %collective-permute-start.7 = (f32[256,128]{1,0:T(8,128)S(1)}, f32[256,128]{1,0:T(8,128)S(1)}, u32[]{:S(2)}, u32[]{:S(2)}) collective-permute-start(f32[256,128]{1,0:T(8,128)S(1)} %get-tuple-element.34), channel_id=1, source_target_pairs={{0,2},{1,3},{2,0},{3,1},{4,6},{5,7},{6,4},{7,5},{8,10},{9,11},{10,... | collective-permute-start | bytes 393224 | tf_op jit(solution)/shard_map/gather/ppermute | solution.py:204
  18.0 0.7 %backward.6._ = f32[2,256,128]{2,1,0:T(8,128)S(1)} custom-call(f32[2,256,128]{2,1,0:T(8,128)S(1)} %backward.5._, bf16[256,1024]{1,0:T(8,128)(2,1)S(1)} %flip.1.refs_0_, bf16[1024,2048]{1,0:T(8,128)(2,1)S(1)} %get-tuple-element.27._.refs_1_.refs_2_, bf16[1024,2048]{1,0:T(8,128)(2,1)S(1)} %get-tuple-element.31.refs_2_.refs_3_), custom_call_target="tpu_custom_call" | custom-call | bytes 1024 | tf_op jit(solution)/shard_map/backward/pallas_call | solution.py:217
  18.7 0.1 collective-permute-start.6
  18.7 0.7 %backward.7.kept_ref = f32[2,256,128]{2,1,0:T(8,128)S(1)} custom-call(f32[2,256,128]{2,1,0:T(8,128)S(1)} %backward.6._, bf16[256,1024]{1,0:T(8,128)(2,1)S(1)} %flip.1.refs_0_, bf16[1024,2048]{1,0:T(8,128)(2,1)S(1)} %get-tuple-element.27._.refs_1_.refs_2_, bf16[1024,2048]{1,0:T(8,128)(2,1)S(1)} %get-tuple-element.31.refs_2_.refs_3_), custom_call_target="tpu_custom_call" | custom-call | bytes 1024 | tf_op jit(solution)/shard_map/backward/pallas_call | solution.py:217
  19.4 0.0 collective-permute-done.5.got_ref
  19.5 1.7 %collective-permute-start.9 = (f32[256,128]{1,0:T(8,128)S(1)}, f32[256,128]{1,0:T(8,128)S(1)}, u32[]{:S(2)}, u32[]{:S(2)}) collective-permute-start(f32[256,128]{1,0:T(8,128)S(1)} %get-tuple-element.36), channel_id=1, source_target_pairs={{0,2},{1,3},{2,0},{3,1},{4,6},{5,7},{6,4},{7,5},{8,10},{9,11},{10,... | collective-permute-start | bytes 393224 | tf_op jit(solution)/shard_map/reduce/ppermute | solution.py:204
  21.1 0.7 %backward.9.kept_ref._ = f32[2,256,128]{2,1,0:T(8,128)S(1)} custom-call(f32[256,128]{1,0:T(8,128)S(1)} %get-tuple-element.32._.refs_0_, bf16[256,1024]{1,0:T(8,128)(2,1)S(1)} %flip.1.refs_0_, bf16[1024,2048]{1,0:T(8,128)(2,1)S(1)} %get-tuple-element.27._.refs_1_.refs_2_, bf16[1024,2048]{1,0:T(8,128)(2,1)S(1)} %get-tuple-element.31.refs_2_.refs_3_), custom_call_target="tpu_custom_call" | custom-call | bytes 1024 | tf_op jit(solution)/shard_map/backward/pallas_call | solution.py:217
  21.8 1.5 %collective-permute-done.7.refs_0_ = f32[256,128]{1,0:T(8,128)S(1)} collective-permute-done((f32[256,128]{1,0:T(8,128)S(1)}, f32[256,128]{1,0:T(8,128)S(1)}, u32[]{:S(2)}, u32[]{:S(2)}) %collective-permute-start.7) | collective-permute-done | bytes 131104 | tf_op jit(solution)/shard_map/gather/ppermute | solution.py:204
  23.3 0.1 collective-permute-start.11
  23.4 0.0 collective-permute-done.8.refs_1_
  23.4 1.9 %forward.2 = (f32[256,128]{1,0:T(8,128)S(1)}, f32[256,128]{1,0:T(8,128)S(1)}, f32[256,128]{1,0:T(8,128)S(1)}, f32[256,128]{1,0:T(8,128)S(1)}) custom-call(f32[1,256,128]{2,1,0:T(8,128)S(1)} %gather.3._.refs_0_, f32[3,256,128]{2,1,0:T(8,128)S(1)} %get-tuple-element.29._.refs_0_, f32[3,256,128]{2,1,0:T(8,128)S(1)} %collective-permute-done.8.refs_1_, ...), custom_call_target="tpu_custom_call" | custom-call | bytes 1024 | tf_op jit(solution)/shard_map/forward/pallas_call | solution.py:217
  25.3 0.5 %collective-permute-done.9.refs_1_ = f32[256,128]{1,0:T(8,128)S(1)} collective-permute-done((f32[256,128]{1,0:T(8,128)S(1)}, f32[256,128]{1,0:T(8,128)S(1)}, u32[]{:S(2)}, u32[]{:S(2)}) %collective-permute-start.9) | collective-permute-done | bytes 131104 | tf_op jit(solution)/shard_map/reduce/ppermute | solution.py:204
  25.8 0.4 %collective-permute-start.10 = (f32[256,128]{1,0:T(8,128)S(1)}, f32[256,128]{1,0:T(8,128)S(1)}, u32[]{:S(2)}, u32[]{:S(2)}) collective-permute-start(f32[256,128]{1,0:T(8,128)S(1)} %reduce.4._), channel_id=1, source_target_pairs={{0,4},{1,5},{2,6},{3,7},{4,0},{5,1},{6,2},{7,3},{8,12},{9,13},{10,... | collective-permute-start | bytes 393224 | tf_op jit(solution)/shard_map/reduce/ppermute | solution.py:204
  26.2 0.0 collective-permute-done.11.refs_1_
  26.2 0.7 %forward.3 = (f32[256,128]{1,0:T(8,128)S(1)}, f32[256,128]{1,0:T(8,128)S(1)}, f32[256,128]{1,0:T(8,128)S(1)}, f32[256,128]{1,0:T(8,128)S(1)}) custom-call(f32[256,128]{1,0:T(8,128)S(1)} %reduce.4._, f32[1,256,128]{2,1,0:T(8,128)S(1)} %gather.3._.refs_0_, f32[1,256,128]{2,1,0:T(8,128)S(1)} %collective-permute-done.11.refs_1_, ...), custom_call_target="tpu_custom_call" | custom-call | bytes 1024 | tf_op jit(solution)/shard_map/forward/pallas_call | solution.py:217
  27.0 1.6 %collective-permute-start.12 = (f32[256,128]{1,0:T(8,128)S(1)}, f32[256,128]{1,0:T(8,128)S(1)}, u32[]{:S(2)}, u32[]{:S(2)}) collective-permute-start(f32[256,128]{1,0:T(8,128)S(1)} %get-tuple-element.41), channel_id=1, source_target_pairs={{0,8},{8,0},{16,24},{24,16},{1,9},{9,1},{17,25},{25,17},{2,10},{10... | collective-permute-start | bytes 393224 | tf_op jit(solution)/shard_map/reduce/ppermute | solution.py:204
  28.5 1.5 %collective-permute-start.13 = (f32[256,128]{1,0:T(8,128)S(1)}, f32[256,128]{1,0:T(8,128)S(1)}, u32[]{:S(2)}, u32[]{:S(2)}) collective-permute-start(f32[256,128]{1,0:T(8,128)S(1)} %get-tuple-element.42), channel_id=1, source_target_pairs={{0,16},{8,24},{16,0},{24,8},{1,17},{9,25},{17,1},{25,9},{2,18},{10... | collective-permute-start | bytes 393224 | tf_op jit(solution)/shard_map/reduce/ppermute | solution.py:204
  30.1 0.5 %collective-permute-start.14 = (f32[256,128]{1,0:T(8,128)S(1)}, f32[256,128]{1,0:T(8,128)S(1)}, u32[]{:S(2)}, u32[]{:S(2)}) collective-permute-start(f32[256,128]{1,0:T(8,128)S(1)} %get-tuple-element.43), channel_id=1, source_target_pairs={{0,24},{8,16},{16,8},{24,0},{1,25},{9,17},{17,9},{25,1},{2,26},{10... | collective-permute-start | bytes 393224 | tf_op jit(solution)/shard_map/reduce/ppermute | solution.py:204
  30.5 0.0 collective-permute-done.6.got_ref
  30.6 1.3 %collective-permute-start.15 = (f32[256,128]{1,0:T(8,128)S(1)}, f32[256,128]{1,0:T(8,128)S(1)}, u32[]{:S(2)}, u32[]{:S(2)}) collective-permute-start(f32[256,128]{1,0:T(8,128)S(1)} %get-tuple-element.47), channel_id=1, source_target_pairs={{0,2},{1,3},{2,0},{3,1},{4,6},{5,7},{6,4},{7,5},{8,10},{9,11},{10,... | collective-permute-start | bytes 393224 | tf_op jit(solution)/shard_map/reduce/ppermute | solution.py:204
  31.8 3.2 %collective-permute-done.10.y_ref = f32[256,128]{1,0:T(8,128)S(1)} collective-permute-done((f32[256,128]{1,0:T(8,128)S(1)}, f32[256,128]{1,0:T(8,128)S(1)}, u32[]{:S(2)}, u32[]{:S(2)}) %collective-permute-start.10) | collective-permute-done | bytes 131104 | tf_op jit(solution)/shard_map/reduce/ppermute | solution.py:204
  35.1 0.0 collective-permute-done.12.refs_1_
  35.1 1.2 %collective-permute-done.13.refs_2_ = f32[256,128]{1,0:T(8,128)S(1)} collective-permute-done((f32[256,128]{1,0:T(8,128)S(1)}, f32[256,128]{1,0:T(8,128)S(1)}, u32[]{:S(2)}, u32[]{:S(2)}) %collective-permute-start.13) | collective-permute-done | bytes 131104 | tf_op jit(solution)/shard_map/reduce/ppermute | solution.py:204
  36.3 0.0 collective-permute-done.14.refs_3_
  36.3 0.7 %finish.2 = (f32[256,128]{1,0:T(8,128)}, f32[8,128]{1,0:T(8,128)S(1)}) custom-call(f32[256,128]{1,0:T(8,128)S(1)} %reduce.5._.refs_0_, f32[256,128]{1,0:T(8,128)S(1)} %get-tuple-element.40.refs_0_, f32[256,128]{1,0:T(8,128)S(1)} %collective-permute-done.12.refs_1_, f32[256,128]{1,0:T(8,128)S(1)} %collective-permute-done.13.refs_2_, ...), custom_call_target="tpu_custom_call" | custom-call | bytes 1024 | tf_op jit(solution)/shard_map/finish/pallas_call | solution.py:217
  37.0 0.2 collective-permute-done.15.refs_1_
  37.3 0.7 %finish.3 = (f32[256,128]{1,0:T(8,128)}, f32[8,128]{1,0:T(8,128)}) custom-call(f32[8,128]{1,0:T(8,128)S(1)} %get-tuple-element.46._, f32[256,128]{1,0:T(8,128)S(1)} %reduce.5._.refs_0_, f32[256,128]{1,0:T(8,128)S(1)} %collective-permute-done.15.refs_1_, f32[256,128]{1,0:T(8,128)S(1)} %get-tuple-element.48.refs_2_), custom_call_target="tpu_custom_call" | custom-call | bytes 1024 | tf_op jit(solution)/shard_map/finish/pallas_call | solution.py:217
  (6 shorter events, 0.1 us)
Async XLA Ops:
  1.8 14.1 %collective-permute-start.1 = (f32[256,128]{1,0:T(8,128)S(1)}, f32[256,128]{1,0:T(8,128)S(1)}, u32[]{:S(2)}, u32[]{:S(2)}) collective-permute-start(f32[256,128]{1,0:T(8,128)S(1)} %get-tuple-element.28.refs_0_), channel_id=1, source_target_pairs={{0,4},{1,5},{2,6},{3,7},{4,0},{5,1},{6,2},{7,3},{8,12},{9,13},{10,... | collective-permute-start | bytes 393224 | tf_op jit(solution)/shard_map/gather/ppermute | solution.py:204
  5.9 10.1 %collective-permute-start = (f32[256,128]{1,0:T(8,128)S(1)}, f32[256,128]{1,0:T(8,128)S(1)}, u32[]{:S(2)}, u32[]{:S(2)}) collective-permute-start(f32[256,128]{1,0:T(8,128)S(1)} %get-tuple-element.28.refs_0_), channel_id=1, source_target_pairs={{0,2},{1,3},{2,0},{3,1},{4,6},{5,7},{6,4},{7,5},{8,10},{9,11},{10,... | collective-permute-start | bytes 393224 | tf_op jit(solution)/shard_map/gather/ppermute | solution.py:204
  7.5 8.5 %collective-permute-start.4 = (f32[256,128]{1,0:T(8,128)S(1)}, f32[256,128]{1,0:T(8,128)S(1)}, u32[]{:S(2)}, u32[]{:S(2)}) collective-permute-start(f32[256,128]{1,0:T(8,128)S(1)} %get-tuple-element.30.refs_0_), channel_id=1, source_target_pairs={{0,24},{8,16},{16,8},{24,0},{1,25},{9,17},{17,9},{25,1},{2,26},{10... | collective-permute-start | bytes 393224 | tf_op jit(solution)/shard_map/gather/ppermute | solution.py:204
  9.9 6.1 %collective-permute-start.3 = (f32[256,128]{1,0:T(8,128)S(1)}, f32[256,128]{1,0:T(8,128)S(1)}, u32[]{:S(2)}, u32[]{:S(2)}) collective-permute-start(f32[256,128]{1,0:T(8,128)S(1)} %get-tuple-element.30.refs_0_), channel_id=1, source_target_pairs={{0,16},{8,24},{16,0},{24,8},{1,17},{9,25},{17,1},{25,9},{2,18},{10... | collective-permute-start | bytes 393224 | tf_op jit(solution)/shard_map/gather/ppermute | solution.py:204
  10.4 5.6 %collective-permute-start.2 = (f32[256,128]{1,0:T(8,128)S(1)}, f32[256,128]{1,0:T(8,128)S(1)}, u32[]{:S(2)}, u32[]{:S(2)}) collective-permute-start(f32[256,128]{1,0:T(8,128)S(1)} %get-tuple-element.30.refs_0_), channel_id=1, source_target_pairs={{0,8},{8,0},{16,24},{24,16},{1,9},{9,1},{17,25},{25,17},{2,10},{10... | collective-permute-start | bytes 393224 | tf_op jit(solution)/shard_map/gather/ppermute | solution.py:204
  16.9 2.5 %collective-permute-start.5 = (f32[2,256,128]{2,1,0:T(8,128)S(1)}, f32[2,256,128]{2,1,0:T(8,128)S(1)}, u32[]{:S(2)}, u32[]{:S(2)}) collective-permute-start(f32[2,256,128]{2,1,0:T(8,128)S(1)} %backward.5._), channel_id=1, source_target_pairs={{0,1},{1,0},{2,3},{3,2},{4,5},{5,4},{6,7},{7,6},{8,9},{9,8},{10,11... | collective-permute-start | bytes 786440 | tf_op jit(solution)/shard_map/backward/ppermute | solution.py:204
  17.0 6.4 %collective-permute-start.8 = (f32[3,256,128]{2,1,0:T(8,128)S(1)}, f32[3,256,128]{2,1,0:T(8,128)S(1)}, u32[]{:S(2)}, u32[]{:S(2)}) collective-permute-start(f32[3,256,128]{2,1,0:T(8,128)S(1)} %get-tuple-element.29._.refs_0_), channel_id=1, source_target_pairs={{0,1},{1,0},{2,3},{3,2},{4,5},{5,4},{6,7},{7,6},{8,9},{9,8},{10,11... | collective-permute-start | bytes 1179656 | tf_op jit(solution)/shard_map/gather/ppermute | solution.py:204
  17.5 5.8 %collective-permute-start.7 = (f32[256,128]{1,0:T(8,128)S(1)}, f32[256,128]{1,0:T(8,128)S(1)}, u32[]{:S(2)}, u32[]{:S(2)}) collective-permute-start(f32[256,128]{1,0:T(8,128)S(1)} %get-tuple-element.34), channel_id=1, source_target_pairs={{0,2},{1,3},{2,0},{3,1},{4,6},{5,7},{6,4},{7,5},{8,10},{9,11},{10,... | collective-permute-start | bytes 393224 | tf_op jit(solution)/shard_map/gather/ppermute | solution.py:204
  18.7 11.9 %collective-permute-start.6 = (f32[2,256,128]{2,1,0:T(8,128)S(1)}, f32[2,256,128]{2,1,0:T(8,128)S(1)}, u32[]{:S(2)}, u32[]{:S(2)}) collective-permute-start(f32[2,256,128]{2,1,0:T(8,128)S(1)} %backward.6._), channel_id=1, source_target_pairs={{0,1},{1,0},{2,3},{3,2},{4,5},{5,4},{6,7},{7,6},{8,9},{9,8},{10,11... | collective-permute-start | bytes 786440 | tf_op jit(solution)/shard_map/reduce/ppermute | solution.py:204
  19.5 6.3 %collective-permute-start.9 = (f32[256,128]{1,0:T(8,128)S(1)}, f32[256,128]{1,0:T(8,128)S(1)}, u32[]{:S(2)}, u32[]{:S(2)}) collective-permute-start(f32[256,128]{1,0:T(8,128)S(1)} %get-tuple-element.36), channel_id=1, source_target_pairs={{0,2},{1,3},{2,0},{3,1},{4,6},{5,7},{6,4},{7,5},{8,10},{9,11},{10,... | collective-permute-start | bytes 393224 | tf_op jit(solution)/shard_map/reduce/ppermute | solution.py:204
  23.3 2.9 %collective-permute-start.11 = (f32[1,256,128]{2,1,0:T(8,128)S(1)}, f32[1,256,128]{2,1,0:T(8,128)S(1)}, u32[]{:S(2)}, u32[]{:S(2)}) collective-permute-start(f32[1,256,128]{2,1,0:T(8,128)S(1)} %gather.3._.refs_0_), channel_id=1, source_target_pairs={{0,1},{1,0},{2,3},{3,2},{4,5},{5,4},{6,7},{7,6},{8,9},{9,8},{10,11... | collective-permute-start | bytes 393224 | tf_op jit(solution)/shard_map/gather/ppermute | solution.py:204
  25.8 9.2 %collective-permute-start.10 = (f32[256,128]{1,0:T(8,128)S(1)}, f32[256,128]{1,0:T(8,128)S(1)}, u32[]{:S(2)}, u32[]{:S(2)}) collective-permute-start(f32[256,128]{1,0:T(8,128)S(1)} %reduce.4._), channel_id=1, source_target_pairs={{0,4},{1,5},{2,6},{3,7},{4,0},{5,1},{6,2},{7,3},{8,12},{9,13},{10,... | collective-permute-start | bytes 393224 | tf_op jit(solution)/shard_map/reduce/ppermute | solution.py:204
  27.0 8.1 %collective-permute-start.12 = (f32[256,128]{1,0:T(8,128)S(1)}, f32[256,128]{1,0:T(8,128)S(1)}, u32[]{:S(2)}, u32[]{:S(2)}) collective-permute-start(f32[256,128]{1,0:T(8,128)S(1)} %get-tuple-element.41), channel_id=1, source_target_pairs={{0,8},{8,0},{16,24},{24,16},{1,9},{9,1},{17,25},{25,17},{2,10},{10... | collective-permute-start | bytes 393224 | tf_op jit(solution)/shard_map/reduce/ppermute | solution.py:204
  28.5 7.8 %collective-permute-start.13 = (f32[256,128]{1,0:T(8,128)S(1)}, f32[256,128]{1,0:T(8,128)S(1)}, u32[]{:S(2)}, u32[]{:S(2)}) collective-permute-start(f32[256,128]{1,0:T(8,128)S(1)} %get-tuple-element.42), channel_id=1, source_target_pairs={{0,16},{8,24},{16,0},{24,8},{1,17},{9,25},{17,1},{25,9},{2,18},{10... | collective-permute-start | bytes 393224 | tf_op jit(solution)/shard_map/reduce/ppermute | solution.py:204
  30.1 6.3 %collective-permute-start.14 = (f32[256,128]{1,0:T(8,128)S(1)}, f32[256,128]{1,0:T(8,128)S(1)}, u32[]{:S(2)}, u32[]{:S(2)}) collective-permute-start(f32[256,128]{1,0:T(8,128)S(1)} %get-tuple-element.43), channel_id=1, source_target_pairs={{0,24},{8,16},{16,8},{24,0},{1,25},{9,17},{17,9},{25,1},{2,26},{10... | collective-permute-start | bytes 393224 | tf_op jit(solution)/shard_map/reduce/ppermute | solution.py:204
  30.6 6.7 %collective-permute-start.15 = (f32[256,128]{1,0:T(8,128)S(1)}, f32[256,128]{1,0:T(8,128)S(1)}, u32[]{:S(2)}, u32[]{:S(2)}) collective-permute-start(f32[256,128]{1,0:T(8,128)S(1)} %get-tuple-element.47), channel_id=1, source_target_pairs={{0,2},{1,3},{2,0},{3,1},{4,6},{5,7},{6,4},{7,5},{8,10},{9,11},{10,... | collective-permute-start | bytes 393224 | tf_op jit(solution)/shard_map/reduce/ppermute | solution.py:204

commit v6 on v5

--- a/solution.py
+++ b/solution.py
@@ -60,13 +60,19 @@
     plan_ref[1:2, :] = col_place(coords[1, 0], tiles, pairs) * tile
 
 
-def finish_kernel(*refs):
-    *part_refs, factor_ref, out_ref, token_ref = refs
-    token_ref[...] = jnp.zeros_like(token_ref)
+def sum_kernel(*refs):
+    *part_refs, out_ref = refs
     total = part_refs[0][...]
     for part_ref in part_refs[1:]:
         total = total + part_ref[...]
-    out_ref[...] = total * factor_ref[...]
+    out_ref[...] = total
+
+
+def finish_kernel(row_ref, row_factor_ref, col_factor_ref, *refs):
+    *part_refs, row_out_ref, col_out_ref = refs
+    row_out_ref[...] = row_ref[...] * row_factor_ref[...]
+    sum_kernel(*part_refs, col_out_ref)
+    col_out_ref[...] = col_out_ref[...] * col_factor_ref[...]
 
 
 def add_kernel(x_ref, y_ref, out_ref):
@@ -111,26 +117,46 @@
     capacity, tile, _ = values_ref.shape
     groups = sems.shape[0]
     group = capacity // groups
-    together = math.gcd(group, 2)
-    copies = []
+    count = count_ref[0, 0]
+
+    def copy(at):
+        slots = pl.ds(at * group, group)
+        return pltpu.make_async_copy(values_ref.at[slots], buf.at[slots], sems.at[at])
+
+    def store(slot, high, low):
+        rows = pl.ds(pl.multiple_of(plan_ref[0, slot], tile), tile)
+        cols = pl.ds(pl.multiple_of(plan_ref[1, slot], tile), tile)
+        high_ref[rows, cols] = high
+        low_ref[rows, cols] = low
+
     for at in range(groups):
-        slots = pl.ds(at * group, group)
-        copies.append(pltpu.make_async_copy(values_ref.at[slots], buf.at[slots], sems.at[at]))
-        copies[-1].start()
-    for at, copy in enumerate(copies):
-        copy.wait()
-
-        @pl.loop(at * group, (at + 1) * group, step=together, unroll=2)
-        def _(first):
-            parts = []
-            for slot in range(together):
-                rows = pl.ds(pl.multiple_of(plan_ref[0, first + slot], tile), tile)
-                cols = pl.ds(pl.multiple_of(plan_ref[1, first + slot], tile), tile)
-                live = first + slot < count_ref[0, 0]
-                parts.append((rows, cols, *halves(jnp.where(live, buf[first + slot], 0.0))))
-            for rows, cols, high, low in parts:
-                high_ref[rows, cols] = high
-                low_ref[rows, cols] = low
+
+        @pl.when(at * group < count)
+        def _():
+            copy(at).start()
+
+    @pl.loop(count, capacity)
+    def _(slot):
+        zeros = jnp.zeros((tile, tile), BF16)
+        store(slot, zeros, zeros)
+
+    for at in range(groups):
+
+        @pl.when(at * group < count)
+        def _():
+            copy(at).wait()
+
+        @pl.when((at + 1) * group <= count)
+        def _():
+            @pl.loop(at * group, (at + 1) * group, unroll=4)
+            def _(slot):
+                store(slot, *halves(buf[slot]))
+
+        @pl.when((at * group < count) & ((at + 1) * group > count))
+        def _():
+            @pl.loop(at * group, count)
+            def _(slot):
+                store(slot, *halves(buf[slot]))
 
 
 def flip_kernel(tile, *refs):
@@ -301,7 +327,7 @@
 
     if dense:
         table = jax.ShapeDtypeStruct((n_rows, n_cols), BF16)
-        groups = math.gcd(capacity, 8)
+        groups = math.gcd(capacity, 16)
         with jax.named_scope("split"):
             high, low = call(
                 split_kernel,
@@ -409,10 +435,10 @@
         row_parts = [forwards[0]] + [swap(forwards[k], "row", k) for k in range(1, n_row)]
 
     with jax.named_scope("finish"):
-        outs = (block, jax.ShapeDtypeStruct((8, tile), F32))
-        propagated, token = call(finish_kernel, outs, (*row_parts, row_factor), mebibytes=4, after=mine)
-        embed_grad, _ = call(finish_kernel, outs, (mine, *grad_parts, col_factor), mebibytes=4, after=token)
-    return propagated, embed_grad
+        row_sum = call(sum_kernel, block, row_parts, after=mine)
+        return call(
+            finish_kernel, (block, block), (row_sum, row_factor, col_factor, mine, *grad_parts), mebibytes=4
+        )
 
 
 def solution(mesh):

time: 38.1 us -> 38 us (level)
  Pallas kernels: 12.5 us -> 10.5 us
  waiting for transfers between devices: 6.74 us -> 8.67 us
    pallas_call x17, Pallas kernels: 12.5 us -> 10.5 us  [call(): pl.pallas_call(body, out_shape=out_shape, in_specs=specs, out_specs=tuple...]
    ppermute x16, waiting for transfers between devices: 6.74 us -> 8.67 us  [swap(): lax.ppermute(x, axis, [(at, at ^ mask) for at in range(lax.axis_size(axis...]
  transfers between devices with their start and end apart: 16 -> 16, of which waited for: 5 -> 7; matrix products, arithmetic and copies ran while one was open for 0% -> 0% of each run, Pallas kernels for 26% -> 20%
where the time goes in v6:
time: 38 us; the launch traced here: 37.9 us
  starting transfers between devices  17.2 us (45%)
  Pallas kernels  10.5 us (28%)
  waiting for transfers between devices  8.67 us (23%)
  between operations  1.47 us (4%)
    ppermute x16, starting transfers between devices, swap(): lax.ppermute(x, axis, [(at, at ^ mask) for at in range(lax.axis_size(axis...  17.2 us
    pallas_call x17, Pallas kernels, call(): pl.pallas_call(body, out_shape=out_shape, in_specs=specs, out_specs=tuple...  10.5 us
    ppermute x16, waiting for transfers between devices, swap(): lax.ppermute(x, axis, [(at, at ^ mask) for at in range(lax.axis_size(axis...  8.67 us
  transfers between devices with their start and end apart: 16, of which 7 were waited for; matrix products, arithmetic and copies ran while one was open for 0% of the time, Pallas kernels for 20%

profile of v6, /device:TPU:0, one launch (start us, length us, event | category | flops | bytes accessed | tf_op | source)
XLA Modules:
  0.0 37.9 jit_solution(7397475563993788356)
XLA Ops:
  0.6 1.2 %scale.1 = (f32[256,128]{1,0:T(8,128)S(1)}, f32[256,128]{1,0:T(8,128)S(1)}, f32[256,128]{1,0:T(8,128)S(1)}, f32[256,128]{1,0:T(8,128)S(1)}, s32[2,128]{1,0:T(2,128)S(1)}) custom-call(f32[256,128]{1,0:T(8,128)} %refs_0_.1, f32[256,128]{1,0:T(8,128)} %refs_1_.1, s32[2,128]{1,0:T(2,128)} %bitcast.4, s32[2,128]{1,0:T(2,128)} %bitcast.5, s32[2,1,1,128]{3,2,1,0:T(1,128)} %refs_4_.1), custom_call_target="tpu_custom_call" | custom-call | bytes 1024 | tf_op jit(solution)/shard_map/scale/pallas_call | solution.py:243
  1.8 4.1 %collective-permute-start.1 = (f32[256,128]{1,0:T(8,128)S(1)}, f32[256,128]{1,0:T(8,128)S(1)}, u32[]{:S(2)}, u32[]{:S(2)}) collective-permute-start(f32[256,128]{1,0:T(8,128)S(1)} %get-tuple-element.25.refs_0_), channel_id=1, source_target_pairs={{0,4},{1,5},{2,6},{3,7},{4,0},{5,1},{6,2},{7,3},{8,12},{9,13},{10,... | collective-permute-start | bytes 393224 | tf_op jit(solution)/shard_map/gather/ppermute | solution.py:230
  5.9 1.6 %collective-permute-start = (f32[256,128]{1,0:T(8,128)S(1)}, f32[256,128]{1,0:T(8,128)S(1)}, u32[]{:S(2)}, u32[]{:S(2)}) collective-permute-start(f32[256,128]{1,0:T(8,128)S(1)} %get-tuple-element.25.refs_0_), channel_id=1, source_target_pairs={{0,2},{1,3},{2,0},{3,1},{4,6},{5,7},{6,4},{7,5},{8,10},{9,11},{10,... | collective-permute-start | bytes 393224 | tf_op jit(solution)/shard_map/gather/ppermute | solution.py:230
  7.5 2.4 %collective-permute-start.4 = (f32[256,128]{1,0:T(8,128)S(1)}, f32[256,128]{1,0:T(8,128)S(1)}, u32[]{:S(2)}, u32[]{:S(2)}) collective-permute-start(f32[256,128]{1,0:T(8,128)S(1)} %get-tuple-element.27.refs_0_), channel_id=1, source_target_pairs={{0,24},{8,16},{16,8},{24,0},{1,25},{9,17},{17,9},{25,1},{2,26},{10... | collective-permute-start | bytes 393224 | tf_op jit(solution)/shard_map/gather/ppermute | solution.py:230
  9.9 0.5 %collective-permute-start.3 = (f32[256,128]{1,0:T(8,128)S(1)}, f32[256,128]{1,0:T(8,128)S(1)}, u32[]{:S(2)}, u32[]{:S(2)}) collective-permute-start(f32[256,128]{1,0:T(8,128)S(1)} %get-tuple-element.27.refs_0_), channel_id=1, source_target_pairs={{0,16},{8,24},{16,0},{24,8},{1,17},{9,25},{17,1},{25,9},{2,18},{10... | collective-permute-start | bytes 393224 | tf_op jit(solution)/shard_map/gather/ppermute | solution.py:230
  10.4 0.5 %collective-permute-start.2 = (f32[256,128]{1,0:T(8,128)S(1)}, f32[256,128]{1,0:T(8,128)S(1)}, u32[]{:S(2)}, u32[]{:S(2)}) collective-permute-start(f32[256,128]{1,0:T(8,128)S(1)} %get-tuple-element.27.refs_0_), channel_id=1, source_target_pairs={{0,8},{8,0},{16,24},{24,16},{1,9},{9,1},{17,25},{25,17},{2,10},{10... | collective-permute-start | bytes 393224 | tf_op jit(solution)/shard_map/gather/ppermute | solution.py:230
  11.6 2.9 %split.1 = (bf16[1024,2048]{1,0:T(8,128)(2,1)S(1)}, bf16[1024,2048]{1,0:T(8,128)(2,1)S(1)}) custom-call(s32[2,128]{1,0:T(2,128)S(1)} %get-tuple-element.23.plan_ref._, s32[1,1]{1,0:T(1,128)S(6)} %copy.9.count_ref, f32[128,128,128]{2,1,0:T(8,128)} %bitcast.3), custom_call_target="tpu_custom_call" | custom-call | bytes 1024 | tf_op jit(solution)/shard_map/split/pallas_call | solution.py:243
  14.5 0.0 collective-permute-done.1.refs_2_
  14.5 0.0 collective-permute-done.refs_1_
  14.6 0.0 collective-permute-done.4.refs_3_
  14.6 1.2 %collective-permute-done.3.refs_2_ = f32[256,128]{1,0:T(8,128)S(1)} collective-permute-done((f32[256,128]{1,0:T(8,128)S(1)}, f32[256,128]{1,0:T(8,128)S(1)}, u32[]{:S(2)}, u32[]{:S(2)}) %collective-permute-start.3) | collective-permute-done | bytes 131104 | tf_op jit(solution)/shard_map/gather/ppermute | solution.py:230
  15.9 0.1 collective-permute-done.2.refs_1_
  16.0 0.2 flip.1.refs_0_
  16.2 0.7 %backward.5._ = f32[2,256,128]{2,1,0:T(8,128)S(1)} custom-call(s32[2,128]{1,0:T(2,128)S(1)} %get-tuple-element.23.plan_ref._, bf16[256,1024]{1,0:T(8,128)(2,1)S(1)} %flip.1.refs_0_, bf16[1024,2048]{1,0:T(8,128)(2,1)S(1)} %get-tuple-element.24._.refs_1_.refs_2_, bf16[1024,2048]{1,0:T(8,128)(2,1)S(1)} %get-tuple-element.28.refs_2_.refs_3_), custom_call_target="tpu_custom_call" | custom-call | bytes 1024 | tf_op jit(solution)/shard_map/backward/pallas_call | solution.py:243
  16.9 0.1 collective-permute-start.5
  16.9 0.5 %collective-permute-start.8 = (f32[3,256,128]{2,1,0:T(8,128)S(1)}, f32[3,256,128]{2,1,0:T(8,128)S(1)}, u32[]{:S(2)}, u32[]{:S(2)}) collective-permute-start(f32[3,256,128]{2,1,0:T(8,128)S(1)} %get-tuple-element.26._.refs_0_), channel_id=1, source_target_pairs={{0,1},{1,0},{2,3},{3,2},{4,5},{5,4},{6,7},{7,6},{8,9},{9,8},{10,11... | collective-permute-start | bytes 1179656 | tf_op jit(solution)/shard_map/gather/ppermute | solution.py:230
  17.4 0.4 %collective-permute-start.7 = (f32[256,128]{1,0:T(8,128)S(1)}, f32[256,128]{1,0:T(8,128)S(1)}, u32[]{:S(2)}, u32[]{:S(2)}) collective-permute-start(f32[256,128]{1,0:T(8,128)S(1)} %get-tuple-element.31), channel_id=1, source_target_pairs={{0,2},{1,3},{2,0},{3,1},{4,6},{5,7},{6,4},{7,5},{8,10},{9,11},{10,... | collective-permute-start | bytes 393224 | tf_op jit(solution)/shard_map/gather/ppermute | solution.py:230
  17.9 0.7 %backward.6._ = f32[2,256,128]{2,1,0:T(8,128)S(1)} custom-call(f32[2,256,128]{2,1,0:T(8,128)S(1)} %backward.5._, bf16[256,1024]{1,0:T(8,128)(2,1)S(1)} %flip.1.refs_0_, bf16[1024,2048]{1,0:T(8,128)(2,1)S(1)} %get-tuple-element.24._.refs_1_.refs_2_, bf16[1024,2048]{1,0:T(8,128)(2,1)S(1)} %get-tuple-element.28.refs_2_.refs_3_), custom_call_target="tpu_custom_call" | custom-call | bytes 1024 | tf_op jit(solution)/shard_map/backward/pallas_call | solution.py:243
  18.6 0.1 collective-permute-start.6
  18.7 0.7 %backward.7.kept_ref = f32[2,256,128]{2,1,0:T(8,128)S(1)} custom-call(f32[2,256,128]{2,1,0:T(8,128)S(1)} %backward.6._, bf16[256,1024]{1,0:T(8,128)(2,1)S(1)} %flip.1.refs_0_, bf16[1024,2048]{1,0:T(8,128)(2,1)S(1)} %get-tuple-element.24._.refs_1_.refs_2_, bf16[1024,2048]{1,0:T(8,128)(2,1)S(1)} %get-tuple-element.28.refs_2_.refs_3_), custom_call_target="tpu_custom_call" | custom-call | bytes 1024 | tf_op jit(solution)/shard_map/backward/pallas_call | solution.py:243
  19.3 0.0 collective-permute-done.5.got_ref
  19.4 1.7 %collective-permute-start.9 = (f32[256,128]{1,0:T(8,128)S(1)}, f32[256,128]{1,0:T(8,128)S(1)}, u32[]{:S(2)}, u32[]{:S(2)}) collective-permute-start(f32[256,128]{1,0:T(8,128)S(1)} %get-tuple-element.33), channel_id=1, source_target_pairs={{0,2},{1,3},{2,0},{3,1},{4,6},{5,7},{6,4},{7,5},{8,10},{9,11},{10,... | collective-permute-start | bytes 393224 | tf_op jit(solution)/shard_map/reduce/ppermute | solution.py:230
  21.0 0.7 %backward.9.kept_ref._ = f32[2,256,128]{2,1,0:T(8,128)S(1)} custom-call(f32[256,128]{1,0:T(8,128)S(1)} %get-tuple-element.29._.refs_0_, bf16[256,1024]{1,0:T(8,128)(2,1)S(1)} %flip.1.refs_0_, bf16[1024,2048]{1,0:T(8,128)(2,1)S(1)} %get-tuple-element.24._.refs_1_.refs_2_, bf16[1024,2048]{1,0:T(8,128)(2,1)S(1)} %get-tuple-element.28.refs_2_.refs_3_), custom_call_target="tpu_custom_call" | custom-call | bytes 1024 | tf_op jit(solution)/shard_map/backward/pallas_call | solution.py:243
  21.7 1.5 %collective-permute-done.7.refs_0_ = f32[256,128]{1,0:T(8,128)S(1)} collective-permute-done((f32[256,128]{1,0:T(8,128)S(1)}, f32[256,128]{1,0:T(8,128)S(1)}, u32[]{:S(2)}, u32[]{:S(2)}) %collective-permute-start.7) | collective-permute-done | bytes 131104 | tf_op jit(solution)/shard_map/gather/ppermute | solution.py:230
  23.2 0.1 collective-permute-start.11
  23.3 0.0 collective-permute-done.8.refs_1_
  23.3 1.9 %forward.2 = (f32[256,128]{1,0:T(8,128)S(1)}, f32[256,128]{1,0:T(8,128)S(1)}, f32[256,128]{1,0:T(8,128)S(1)}, f32[256,128]{1,0:T(8,128)S(1)}) custom-call(f32[1,256,128]{2,1,0:T(8,128)S(1)} %gather.3._.refs_0_, f32[3,256,128]{2,1,0:T(8,128)S(1)} %get-tuple-element.26._.refs_0_, f32[3,256,128]{2,1,0:T(8,128)S(1)} %collective-permute-done.8.refs_1_, ...), custom_call_target="tpu_custom_call" | custom-call | bytes 1024 | tf_op jit(solution)/shard_map/forward/pallas_call | solution.py:243
  25.2 0.5 %collective-permute-done.9.refs_1_ = f32[256,128]{1,0:T(8,128)S(1)} collective-permute-done((f32[256,128]{1,0:T(8,128)S(1)}, f32[256,128]{1,0:T(8,128)S(1)}, u32[]{:S(2)}, u32[]{:S(2)}) %collective-permute-start.9) | collective-permute-done | bytes 131104 | tf_op jit(solution)/shard_map/reduce/ppermute | solution.py:230
  25.7 0.4 %collective-permute-start.10 = (f32[256,128]{1,0:T(8,128)S(1)}, f32[256,128]{1,0:T(8,128)S(1)}, u32[]{:S(2)}, u32[]{:S(2)}) collective-permute-start(f32[256,128]{1,0:T(8,128)S(1)} %reduce.4._), channel_id=1, source_target_pairs={{0,4},{1,5},{2,6},{3,7},{4,0},{5,1},{6,2},{7,3},{8,12},{9,13},{10,... | collective-permute-start | bytes 393224 | tf_op jit(solution)/shard_map/reduce/ppermute | solution.py:230
  26.2 0.0 collective-permute-done.11.refs_1_
  26.2 0.7 %forward.3 = (f32[256,128]{1,0:T(8,128)S(1)}, f32[256,128]{1,0:T(8,128)S(1)}, f32[256,128]{1,0:T(8,128)S(1)}, f32[256,128]{1,0:T(8,128)S(1)}) custom-call(f32[256,128]{1,0:T(8,128)S(1)} %reduce.4._, f32[1,256,128]{2,1,0:T(8,128)S(1)} %gather.3._.refs_0_, f32[1,256,128]{2,1,0:T(8,128)S(1)} %collective-permute-done.11.refs_1_, ...), custom_call_target="tpu_custom_call" | custom-call | bytes 1024 | tf_op jit(solution)/shard_map/forward/pallas_call | solution.py:243
  26.9 1.6 %collective-permute-start.12 = (f32[256,128]{1,0:T(8,128)S(1)}, f32[256,128]{1,0:T(8,128)S(1)}, u32[]{:S(2)}, u32[]{:S(2)}) collective-permute-start(f32[256,128]{1,0:T(8,128)S(1)} %get-tuple-element.38), channel_id=1, source_target_pairs={{0,8},{8,0},{16,24},{24,16},{1,9},{9,1},{17,25},{25,17},{2,10},{10... | collective-permute-start | bytes 393224 | tf_op jit(solution)/shard_map/reduce/ppermute | solution.py:230
  28.5 0.8 %collective-permute-start.13 = (f32[256,128]{1,0:T(8,128)S(1)}, f32[256,128]{1,0:T(8,128)S(1)}, u32[]{:S(2)}, u32[]{:S(2)}) collective-permute-start(f32[256,128]{1,0:T(8,128)S(1)} %get-tuple-element.39), channel_id=1, source_target_pairs={{0,16},{8,24},{16,0},{24,8},{1,17},{9,25},{17,1},{25,9},{2,18},{10... | collective-permute-start | bytes 393224 | tf_op jit(solution)/shard_map/reduce/ppermute | solution.py:230
  29.2 1.2 %collective-permute-start.14 = (f32[256,128]{1,0:T(8,128)S(1)}, f32[256,128]{1,0:T(8,128)S(1)}, u32[]{:S(2)}, u32[]{:S(2)}) collective-permute-start(f32[256,128]{1,0:T(8,128)S(1)} %get-tuple-element.40), channel_id=1, source_target_pairs={{0,24},{8,16},{16,8},{24,0},{1,25},{9,17},{17,9},{25,1},{2,26},{10... | collective-permute-start | bytes 393224 | tf_op jit(solution)/shard_map/reduce/ppermute | solution.py:230
  30.5 0.0 collective-permute-done.6.got_ref
  30.5 1.3 %collective-permute-start.15 = (f32[256,128]{1,0:T(8,128)S(1)}, f32[256,128]{1,0:T(8,128)S(1)}, u32[]{:S(2)}, u32[]{:S(2)}) collective-permute-start(f32[256,128]{1,0:T(8,128)S(1)} %get-tuple-element.43), channel_id=1, source_target_pairs={{0,2},{1,3},{2,0},{3,1},{4,6},{5,7},{6,4},{7,5},{8,10},{9,11},{10,... | collective-permute-start | bytes 393224 | tf_op jit(solution)/shard_map/reduce/ppermute | solution.py:230
  31.8 3.2 %collective-permute-done.10.y_ref = f32[256,128]{1,0:T(8,128)S(1)} collective-permute-done((f32[256,128]{1,0:T(8,128)S(1)}, f32[256,128]{1,0:T(8,128)S(1)}, u32[]{:S(2)}, u32[]{:S(2)}) %collective-permute-start.10) | collective-permute-done | bytes 131104 | tf_op jit(solution)/shard_map/reduce/ppermute | solution.py:230
  35.0 0.0 collective-permute-done.12.refs_1_
  35.0 1.1 %collective-permute-done.13.refs_2_ = f32[256,128]{1,0:T(8,128)S(1)} collective-permute-done((f32[256,128]{1,0:T(8,128)S(1)}, f32[256,128]{1,0:T(8,128)S(1)}, u32[]{:S(2)}, u32[]{:S(2)}) %collective-permute-start.13) | collective-permute-done | bytes 131104 | tf_op jit(solution)/shard_map/reduce/ppermute | solution.py:230
  36.1 0.0 collective-permute-done.14.refs_3_
  36.1 1.0 %collective-permute-done.15.refs_1_ = f32[256,128]{1,0:T(8,128)S(1)} collective-permute-done((f32[256,128]{1,0:T(8,128)S(1)}, f32[256,128]{1,0:T(8,128)S(1)}, u32[]{:S(2)}, u32[]{:S(2)}) %collective-permute-start.15) | collective-permute-done | bytes 131104 | tf_op jit(solution)/shard_map/reduce/ppermute | solution.py:230
  37.1 0.7 %finish.3 = (f32[256,128]{1,0:T(8,128)}, f32[256,128]{1,0:T(8,128)}) custom-call(f32[256,128]{1,0:T(8,128)S(1)} %finish.2.row_ref, f32[256,128]{1,0:T(8,128)S(1)} %get-tuple-element.41.row_factor_ref, f32[256,128]{1,0:T(8,128)S(1)} %get-tuple-element.42.col_factor_ref, f32[256,128]{1,0:T(8,128)S(1)} %reduce.5._.refs_0_, ...), custom_call_target="tpu_custom_call" | custom-call | bytes 1024 | tf_op jit(solution)/shard_map/finish/pallas_call | solution.py:243
  (7 shorter events, 0.2 us)
Async XLA Ops:
  1.8 12.7 %collective-permute-start.1 = (f32[256,128]{1,0:T(8,128)S(1)}, f32[256,128]{1,0:T(8,128)S(1)}, u32[]{:S(2)}, u32[]{:S(2)}) collective-permute-start(f32[256,128]{1,0:T(8,128)S(1)} %get-tuple-element.25.refs_0_), channel_id=1, source_target_pairs={{0,4},{1,5},{2,6},{3,7},{4,0},{5,1},{6,2},{7,3},{8,12},{9,13},{10,... | collective-permute-start | bytes 393224 | tf_op jit(solution)/shard_map/gather/ppermute | solution.py:230
  5.9 8.6 %collective-permute-start = (f32[256,128]{1,0:T(8,128)S(1)}, f32[256,128]{1,0:T(8,128)S(1)}, u32[]{:S(2)}, u32[]{:S(2)}) collective-permute-start(f32[256,128]{1,0:T(8,128)S(1)} %get-tuple-element.25.refs_0_), channel_id=1, source_target_pairs={{0,2},{1,3},{2,0},{3,1},{4,6},{5,7},{6,4},{7,5},{8,10},{9,11},{10,... | collective-permute-start | bytes 393224 | tf_op jit(solution)/shard_map/gather/ppermute | solution.py:230
  7.5 7.1 %collective-permute-start.4 = (f32[256,128]{1,0:T(8,128)S(1)}, f32[256,128]{1,0:T(8,128)S(1)}, u32[]{:S(2)}, u32[]{:S(2)}) collective-permute-start(f32[256,128]{1,0:T(8,128)S(1)} %get-tuple-element.27.refs_0_), channel_id=1, source_target_pairs={{0,24},{8,16},{16,8},{24,0},{1,25},{9,17},{17,9},{25,1},{2,26},{10... | collective-permute-start | bytes 393224 | tf_op jit(solution)/shard_map/gather/ppermute | solution.py:230
  9.9 5.9 %collective-permute-start.3 = (f32[256,128]{1,0:T(8,128)S(1)}, f32[256,128]{1,0:T(8,128)S(1)}, u32[]{:S(2)}, u32[]{:S(2)}) collective-permute-start(f32[256,128]{1,0:T(8,128)S(1)} %get-tuple-element.27.refs_0_), channel_id=1, source_target_pairs={{0,16},{8,24},{16,0},{24,8},{1,17},{9,25},{17,1},{25,9},{2,18},{10... | collective-permute-start | bytes 393224 | tf_op jit(solution)/shard_map/gather/ppermute | solution.py:230
  10.4 5.5 %collective-permute-start.2 = (f32[256,128]{1,0:T(8,128)S(1)}, f32[256,128]{1,0:T(8,128)S(1)}, u32[]{:S(2)}, u32[]{:S(2)}) collective-permute-start(f32[256,128]{1,0:T(8,128)S(1)} %get-tuple-element.27.refs_0_), channel_id=1, source_target_pairs={{0,8},{8,0},{16,24},{24,16},{1,9},{9,1},{17,25},{25,17},{2,10},{10... | collective-permute-start | bytes 393224 | tf_op jit(solution)/shard_map/gather/ppermute | solution.py:230
  16.9 2.5 %collective-permute-start.5 = (f32[2,256,128]{2,1,0:T(8,128)S(1)}, f32[2,256,128]{2,1,0:T(8,128)S(1)}, u32[]{:S(2)}, u32[]{:S(2)}) collective-permute-start(f32[2,256,128]{2,1,0:T(8,128)S(1)} %backward.5._), channel_id=1, source_target_pairs={{0,1},{1,0},{2,3},{3,2},{4,5},{5,4},{6,7},{7,6},{8,9},{9,8},{10,11... | collective-permute-start | bytes 786440 | tf_op jit(solution)/shard_map/backward/ppermute | solution.py:230
  16.9 6.4 %collective-permute-start.8 = (f32[3,256,128]{2,1,0:T(8,128)S(1)}, f32[3,256,128]{2,1,0:T(8,128)S(1)}, u32[]{:S(2)}, u32[]{:S(2)}) collective-permute-start(f32[3,256,128]{2,1,0:T(8,128)S(1)} %get-tuple-element.26._.refs_0_), channel_id=1, source_target_pairs={{0,1},{1,0},{2,3},{3,2},{4,5},{5,4},{6,7},{7,6},{8,9},{9,8},{10,11... | collective-permute-start | bytes 1179656 | tf_op jit(solution)/shard_map/gather/ppermute | solution.py:230
  17.4 5.8 %collective-permute-start.7 = (f32[256,128]{1,0:T(8,128)S(1)}, f32[256,128]{1,0:T(8,128)S(1)}, u32[]{:S(2)}, u32[]{:S(2)}) collective-permute-start(f32[256,128]{1,0:T(8,128)S(1)} %get-tuple-element.31), channel_id=1, source_target_pairs={{0,2},{1,3},{2,0},{3,1},{4,6},{5,7},{6,4},{7,5},{8,10},{9,11},{10,... | collective-permute-start | bytes 393224 | tf_op jit(solution)/shard_map/gather/ppermute | solution.py:230
  18.6 11.9 %collective-permute-start.6 = (f32[2,256,128]{2,1,0:T(8,128)S(1)}, f32[2,256,128]{2,1,0:T(8,128)S(1)}, u32[]{:S(2)}, u32[]{:S(2)}) collective-permute-start(f32[2,256,128]{2,1,0:T(8,128)S(1)} %backward.6._), channel_id=1, source_target_pairs={{0,1},{1,0},{2,3},{3,2},{4,5},{5,4},{6,7},{7,6},{8,9},{9,8},{10,11... | collective-permute-start | bytes 786440 | tf_op jit(solution)/shard_map/reduce/ppermute | solution.py:230
  19.4 6.3 %collective-permute-start.9 = (f32[256,128]{1,0:T(8,128)S(1)}, f32[256,128]{1,0:T(8,128)S(1)}, u32[]{:S(2)}, u32[]{:S(2)}) collective-permute-start(f32[256,128]{1,0:T(8,128)S(1)} %get-tuple-element.33), channel_id=1, source_target_pairs={{0,2},{1,3},{2,0},{3,1},{4,6},{5,7},{6,4},{7,5},{8,10},{9,11},{10,... | collective-permute-start | bytes 393224 | tf_op jit(solution)/shard_map/reduce/ppermute | solution.py:230
  23.2 2.9 %collective-permute-start.11 = (f32[1,256,128]{2,1,0:T(8,128)S(1)}, f32[1,256,128]{2,1,0:T(8,128)S(1)}, u32[]{:S(2)}, u32[]{:S(2)}) collective-permute-start(f32[1,256,128]{2,1,0:T(8,128)S(1)} %gather.3._.refs_0_), channel_id=1, source_target_pairs={{0,1},{1,0},{2,3},{3,2},{4,5},{5,4},{6,7},{7,6},{8,9},{9,8},{10,11... | collective-permute-start | bytes 393224 | tf_op jit(solution)/shard_map/gather/ppermute | solution.py:230
  25.7 9.2 %collective-permute-start.10 = (f32[256,128]{1,0:T(8,128)S(1)}, f32[256,128]{1,0:T(8,128)S(1)}, u32[]{:S(2)}, u32[]{:S(2)}) collective-permute-start(f32[256,128]{1,0:T(8,128)S(1)} %reduce.4._), channel_id=1, source_target_pairs={{0,4},{1,5},{2,6},{3,7},{4,0},{5,1},{6,2},{7,3},{8,12},{9,13},{10,... | collective-permute-start | bytes 393224 | tf_op jit(solution)/shard_map/reduce/ppermute | solution.py:230
  26.9 8.1 %collective-permute-start.12 = (f32[256,128]{1,0:T(8,128)S(1)}, f32[256,128]{1,0:T(8,128)S(1)}, u32[]{:S(2)}, u32[]{:S(2)}) collective-permute-start(f32[256,128]{1,0:T(8,128)S(1)} %get-tuple-element.38), channel_id=1, source_target_pairs={{0,8},{8,0},{16,24},{24,16},{1,9},{9,1},{17,25},{25,17},{2,10},{10... | collective-permute-start | bytes 393224 | tf_op jit(solution)/shard_map/reduce/ppermute | solution.py:230
  28.5 7.6 %collective-permute-start.13 = (f32[256,128]{1,0:T(8,128)S(1)}, f32[256,128]{1,0:T(8,128)S(1)}, u32[]{:S(2)}, u32[]{:S(2)}) collective-permute-start(f32[256,128]{1,0:T(8,128)S(1)} %get-tuple-element.39), channel_id=1, source_target_pairs={{0,16},{8,24},{16,0},{24,8},{1,17},{9,25},{17,1},{25,9},{2,18},{10... | collective-permute-start | bytes 393224 | tf_op jit(solution)/shard_map/reduce/ppermute | solution.py:230
  29.2 6.9 %collective-permute-start.14 = (f32[256,128]{1,0:T(8,128)S(1)}, f32[256,128]{1,0:T(8,128)S(1)}, u32[]{:S(2)}, u32[]{:S(2)}) collective-permute-start(f32[256,128]{1,0:T(8,128)S(1)} %get-tuple-element.40), channel_id=1, source_target_pairs={{0,24},{8,16},{16,8},{24,0},{1,25},{9,17},{17,9},{25,1},{2,26},{10... | collective-permute-start | bytes 393224 | tf_op jit(solution)/shard_map/reduce/ppermute | solution.py:230
  30.5 6.6 %collective-permute-start.15 = (f32[256,128]{1,0:T(8,128)S(1)}, f32[256,128]{1,0:T(8,128)S(1)}, u32[]{:S(2)}, u32[]{:S(2)}) collective-permute-start(f32[256,128]{1,0:T(8,128)S(1)} %get-tuple-element.43), channel_id=1, source_target_pairs={{0,2},{1,3},{2,0},{3,1},{4,6},{5,7},{6,4},{7,5},{8,10},{9,11},{10,... | collective-permute-start | bytes 393224 | tf_op jit(solution)/shard_map/reduce/ppermute | solution.py:230

commit v7 on v6

--- a/solution.py
+++ b/solution.py
@@ -91,6 +91,10 @@
     last_ref[...] = part_refs[-1][...]
 
 
+def pass_kernel(x_ref, out_ref):
+    out_ref[...] = x_ref[...]
+
+
 def copy_kernel(*refs):
     *part_refs, out_ref = refs
     for at, part_ref in enumerate(part_refs):
@@ -182,7 +186,7 @@
 
 def forward_kernel(first, count, bands, *refs):
     embed_refs, (high_ref, low_ref) = refs[:count], refs[count : count + 2]
-    before_refs, out_refs, panel = refs[count + 2 : -1 - bands], refs[-1 - bands : -1], refs[-1]
+    before_refs, out_refs, panel = refs[count + 2 : -1 - len(bands)], refs[-1 - len(bands) : -1], refs[-1]
     _, shard, width = embed_refs[0].shape
     done = 0
     for embeds_ref in embed_refs:
@@ -192,8 +196,8 @@
             panel[pl.ds(done, shard), width:] = low
             done += shard
     cols = pl.ds(first * shard, done)
-    for at, out_ref in enumerate(out_refs):
-        rows = pl.ds(at * shard, shard)
+    for at, (band, out_ref) in enumerate(zip(bands, out_refs)):
+        rows = pl.ds(band * shard, shard)
         both = product(high_ref[rows, cols], panel[...])
         total = both[:, :width] + both[:, width:] + product(low_ref[rows, cols], panel[:, :width])
         if before_refs:
@@ -337,15 +341,12 @@
                 specs=[SCALARS, SCALARS, pl.BlockSpec(memory_space=pltpu.HBM)],
                 scratch=[pltpu.VMEM(values.shape, F32), pltpu.SemaphoreType.DMA((groups,))],
             )
-        with jax.named_scope("gather"):
-            early, late = gathered(high)
-            other_early = swap(early, "col", 1)
         with jax.named_scope("flip"):
             flipped = call(
                 functools.partial(flip_kernel, tile),
                 jax.ShapeDtypeStruct((2 * width, n_rows), BF16),
                 grads,
-                after=early,
+                after=high,
             )
 
         def backward_part(distances, core, after):
@@ -364,11 +365,11 @@
                 return core * count + distance
             return 2 * count + core * (pairs - count) + distance - count
 
-        def forward_part(embeds, first, before=(), after=None):
+        def forward_part(embeds, first, bands, before=(), after=None):
             count = sum(x.shape[0] for x in embeds)
             return call(
-                functools.partial(forward_kernel, first, len(embeds), n_row),
-                (block,) * n_row,
+                functools.partial(forward_kernel, first, len(embeds), bands),
+                (block,) * len(bands),
                 (*embeds, high, low, *before),
                 mebibytes=24,
                 scratch=[pltpu.VMEM((count * shard, 2 * width), BF16)],
@@ -379,17 +380,27 @@
             far, close = range(half, pairs), range(half)
             far_sent = backward_part(far, 1, plan)
             sent = backward_part(close, 1, far_sent)
-            far_sums = chip_sums(backward_part(far, 0, sent), far_sent)
+        with jax.named_scope("gather"):
+            early, late = gathered(sent)
+            other_early = swap(early, "col", 1)
+        with jax.named_scope("backward"):
+            far_sums = chip_sums(backward_part(far, 0, early), far_sent)
             kept = backward_part(close, 0, far_sums[0])
         with jax.named_scope("gather"):
             late = call(copy_kernel, blocks(half - 1), late, after=kept)
             other_late = swap(late, "col", 1)
         with jax.named_scope("forward"):
-            forwards = forward_part([early, other_early], 0, after=late)
+            bands = range(n_row)
+            before = forward_part([early, other_early], 0, bands, after=late)
         with jax.named_scope("reduce"):
-            crossing = total(halved(far_sums, forwards[0]), forwards[0])
+            *far_parts, arrived = halved(far_sums, before[0])
+            arrived = call(pass_kernel, block, [arrived], after=before[0])
         with jax.named_scope("forward"):
-            forwards = forward_part([late, other_late], 2 * (half + 1), forwards, crossing)
+            last = forward_part([late, other_late], 2 * (half + 1), bands[-1:], before[-1:], arrived)
+        with jax.named_scope("reduce"):
+            crossing = total([*far_parts, arrived], last[0])
+        with jax.named_scope("forward"):
+            forwards = forward_part([late, other_late], 2 * (half + 1), bands[:-1], before[:-1], crossing) + last
         with jax.named_scope("reduce"):
             close_sums = chip_sums(kept, sent)
             after = None
@@ -431,8 +442,9 @@
 
     with jax.named_scope("reduce"):
         mine, *grad_parts = halved(close_sums, after)
-        mine = total([mine, swap(crossing, "col", 2 * half)], None)
-        row_parts = [forwards[0]] + [swap(forwards[k], "row", k) for k in range(1, n_row)]
+        row_sum = call(add_kernel, block, (forwards[0], swap(forwards[-1], "row", n_row - 1)))
+        mine = total([mine, swap(crossing, "col", 2 * half)], row_sum)
+        row_parts = [row_sum] + [swap(forwards[k], "row", k) for k in range(1, n_row - 1)]
 
     with jax.named_scope("finish"):
         row_sum = call(sum_kernel, block, row_parts, after=mine)

time: 38 us -> 39.6 us (1.042)
  starting transfers between devices: 17.2 us -> 18 us
  waiting for transfers between devices: 8.67 us -> 9.32 us
    ppermute x16, starting transfers between devices: 17.2 us -> 18 us  [swap(): lax.ppermute(x, axis, [(at, at ^ mask) for at in range(lax.axis_size(axis...]
    ppermute x16, waiting for transfers between devices: 8.67 us -> 9.32 us  [swap(): lax.ppermute(x, axis, [(at, at ^ mask) for at in range(lax.axis_size(axis...]
    pallas_call x17 -> x20, Pallas kernels: 10.5 us -> 10.7 us  [call(): pl.pallas_call(body, out_shape=out_shape, in_specs=specs, out_specs=tuple...]
  transfers between devices with their start and end apart: 16 -> 16, of which waited for: 7 -> 5; matrix products, arithmetic and copies ran while one was open for 0% -> 0% of each run, Pallas kernels for 20% -> 21%
where the time goes in v7:
time: 39.6 us; the launch traced here: 39.5 us
  starting transfers between devices  18 us (45%)
  Pallas kernels  10.7 us (27%)
  waiting for transfers between devices  9.32 us (24%)
  between operations  1.51 us (4%)
    ppermute x16, starting transfers between devices, swap(): lax.ppermute(x, axis, [(at, at ^ mask) for at in range(lax.axis_size(axis...  18 us
    pallas_call x20, Pallas kernels, call(): pl.pallas_call(body, out_shape=out_shape, in_specs=specs, out_specs=tuple...  10.7 us
    ppermute x16, waiting for transfers between devices, swap(): lax.ppermute(x, axis, [(at, at ^ mask) for at in range(lax.axis_size(axis...  9.32 us
  transfers between devices with their start and end apart: 16, of which 5 were waited for; matrix products, arithmetic and copies ran while one was open for 0% of the time, Pallas kernels for 21%

profile of v7, /device:TPU:0, one launch (start us, length us, event | category | flops | bytes accessed | tf_op | source)
XLA Modules:
  0.0 39.5 jit_solution(8048825205633763440)
XLA Ops:
  0.6 1.2 %scale.1 = (f32[256,128]{1,0:T(8,128)S(1)}, f32[256,128]{1,0:T(8,128)S(1)}, f32[256,128]{1,0:T(8,128)S(1)}, f32[256,128]{1,0:T(8,128)S(1)}, s32[2,128]{1,0:T(2,128)S(1)}) custom-call(f32[256,128]{1,0:T(8,128)} %refs_0_.1, f32[256,128]{1,0:T(8,128)} %refs_1_.1, s32[2,128]{1,0:T(2,128)} %bitcast.4, s32[2,128]{1,0:T(2,128)} %bitcast.5, s32[2,1,1,128]{3,2,1,0:T(1,128)} %refs_4_.1), custom_call_target="tpu_custom_call" | custom-call | bytes 1024 | tf_op jit(solution)/shard_map/scale/pallas_call | solution.py:247
  1.8 4.0 %collective-permute-start.2 = (f32[256,128]{1,0:T(8,128)S(1)}, f32[256,128]{1,0:T(8,128)S(1)}, u32[]{:S(2)}, u32[]{:S(2)}) collective-permute-start(f32[256,128]{1,0:T(8,128)S(1)} %get-tuple-element.24.refs_0_), channel_id=1, source_target_pairs={{0,24},{8,16},{16,8},{24,0},{1,25},{9,17},{17,9},{25,1},{2,26},{10... | collective-permute-start | bytes 393224 | tf_op jit(solution)/shard_map/gather/ppermute | solution.py:234
  5.8 0.5 %collective-permute-start.1 = (f32[256,128]{1,0:T(8,128)S(1)}, f32[256,128]{1,0:T(8,128)S(1)}, u32[]{:S(2)}, u32[]{:S(2)}) collective-permute-start(f32[256,128]{1,0:T(8,128)S(1)} %get-tuple-element.24.refs_0_), channel_id=1, source_target_pairs={{0,16},{8,24},{16,0},{24,8},{1,17},{9,25},{17,1},{25,9},{2,18},{10... | collective-permute-start | bytes 393224 | tf_op jit(solution)/shard_map/gather/ppermute | solution.py:234
  6.3 0.1 collective-permute-start
  6.4 3.0 %collective-permute-start.4 = (f32[256,128]{1,0:T(8,128)S(1)}, f32[256,128]{1,0:T(8,128)S(1)}, u32[]{:S(2)}, u32[]{:S(2)}) collective-permute-start(f32[256,128]{1,0:T(8,128)S(1)} %get-tuple-element.26.refs_0_), channel_id=1, source_target_pairs={{0,4},{1,5},{2,6},{3,7},{4,0},{5,1},{6,2},{7,3},{8,12},{9,13},{10,... | collective-permute-start | bytes 393224 | tf_op jit(solution)/shard_map/gather/ppermute | solution.py:234
  9.4 1.6 %collective-permute-start.3 = (f32[256,128]{1,0:T(8,128)S(1)}, f32[256,128]{1,0:T(8,128)S(1)}, u32[]{:S(2)}, u32[]{:S(2)}) collective-permute-start(f32[256,128]{1,0:T(8,128)S(1)} %get-tuple-element.26.refs_0_), channel_id=1, source_target_pairs={{0,2},{1,3},{2,0},{3,1},{4,6},{5,7},{6,4},{7,5},{8,10},{9,11},{10,... | collective-permute-start | bytes 393224 | tf_op jit(solution)/shard_map/gather/ppermute | solution.py:234
  11.6 2.9 %split.1 = (bf16[1024,2048]{1,0:T(8,128)(2,1)S(1)}, bf16[1024,2048]{1,0:T(8,128)(2,1)S(1)}) custom-call(s32[2,128]{1,0:T(2,128)S(1)} %get-tuple-element.22.plan_ref._, s32[1,1]{1,0:T(1,128)S(6)} %copy.9.count_ref, f32[128,128,128]{2,1,0:T(8,128)} %bitcast.3), custom_call_target="tpu_custom_call" | custom-call | bytes 1024 | tf_op jit(solution)/shard_map/split/pallas_call | solution.py:247
  14.6 0.0 collective-permute-done.2.refs_3_
  14.6 0.0 collective-permute-done.1.refs_2_
  14.6 0.0 collective-permute-done.refs_1_
  14.6 0.2 flip.1.refs_0_
  14.8 0.7 %backward.5._ = f32[2,256,128]{2,1,0:T(8,128)S(1)} custom-call(s32[2,128]{1,0:T(2,128)S(1)} %get-tuple-element.22.plan_ref._, bf16[256,1024]{1,0:T(8,128)(2,1)S(1)} %flip.1.refs_0_, bf16[1024,2048]{1,0:T(8,128)(2,1)S(1)} %get-tuple-element.23._.refs_1_.refs_2_, bf16[1024,2048]{1,0:T(8,128)(2,1)S(1)} %get-tuple-element.25.refs_2_.refs_3_), custom_call_target="tpu_custom_call" | custom-call | bytes 1024 | tf_op jit(solution)/shard_map/backward/pallas_call | solution.py:247
  15.5 0.7 %backward.6._ = f32[2,256,128]{2,1,0:T(8,128)S(1)} custom-call(f32[2,256,128]{2,1,0:T(8,128)S(1)} %backward.5._, bf16[256,1024]{1,0:T(8,128)(2,1)S(1)} %flip.1.refs_0_, bf16[1024,2048]{1,0:T(8,128)(2,1)S(1)} %get-tuple-element.23._.refs_1_.refs_2_, bf16[1024,2048]{1,0:T(8,128)(2,1)S(1)} %get-tuple-element.25.refs_2_.refs_3_), custom_call_target="tpu_custom_call" | custom-call | bytes 1024 | tf_op jit(solution)/shard_map/backward/pallas_call | solution.py:247
  16.2 0.1 collective-permute-start.5
  16.3 0.0 collective-permute-done.4.refs_2_
  16.3 0.0 collective-permute-done.3.refs_1_
  16.3 0.5 %collective-permute-start.7 = (f32[3,256,128]{2,1,0:T(8,128)S(1)}, f32[3,256,128]{2,1,0:T(8,128)S(1)}, u32[]{:S(2)}, u32[]{:S(2)}) collective-permute-start(f32[3,256,128]{2,1,0:T(8,128)S(1)} %get-tuple-element.27._.refs_0_), channel_id=1, source_target_pairs={{0,1},{1,0},{2,3},{3,2},{4,5},{5,4},{6,7},{7,6},{8,9},{9,8},{10,11... | collective-permute-start | bytes 1179656 | tf_op jit(solution)/shard_map/gather/ppermute | solution.py:234
  16.9 0.1 collective-permute-start.11
  17.0 0.6 %collective-permute-start.6 = (f32[256,128]{1,0:T(8,128)S(1)}, f32[256,128]{1,0:T(8,128)S(1)}, u32[]{:S(2)}, u32[]{:S(2)}) collective-permute-start(f32[256,128]{1,0:T(8,128)S(1)} %get-tuple-element.29), channel_id=1, source_target_pairs={{0,2},{1,3},{2,0},{3,1},{4,6},{5,7},{6,4},{7,5},{8,10},{9,11},{10,... | collective-permute-start | bytes 393224 | tf_op jit(solution)/shard_map/gather/ppermute | solution.py:234
  17.5 0.7 %backward.7.kept_ref = f32[2,256,128]{2,1,0:T(8,128)S(1)} custom-call(f32[3,256,128]{2,1,0:T(8,128)S(1)} %get-tuple-element.27._.refs_0_, bf16[256,1024]{1,0:T(8,128)(2,1)S(1)} %flip.1.refs_0_, bf16[1024,2048]{1,0:T(8,128)(2,1)S(1)} %get-tuple-element.23._.refs_1_.refs_2_, bf16[1024,2048]{1,0:T(8,128)(2,1)S(1)} %get-tuple-element.25.refs_2_.refs_3_), custom_call_target="tpu_custom_call" | custom-call | bytes 1024 | tf_op jit(solution)/shard_map/backward/pallas_call | solution.py:247
  18.2 0.0 collective-permute-done.5.got_ref
  18.3 0.7 %backward.9._.kept_ref = f32[2,256,128]{2,1,0:T(8,128)S(1)} custom-call(f32[256,128]{1,0:T(8,128)S(1)} %get-tuple-element.28._.refs_0_, bf16[256,1024]{1,0:T(8,128)(2,1)S(1)} %flip.1.refs_0_, bf16[1024,2048]{1,0:T(8,128)(2,1)S(1)} %get-tuple-element.23._.refs_1_.refs_2_, bf16[1024,2048]{1,0:T(8,128)(2,1)S(1)} %get-tuple-element.25.refs_2_.refs_3_), custom_call_target="tpu_custom_call" | custom-call | bytes 1024 | tf_op jit(solution)/shard_map/backward/pallas_call | solution.py:247
  18.9 1.5 %collective-permute-start.8 = (f32[256,128]{1,0:T(8,128)S(1)}, f32[256,128]{1,0:T(8,128)S(1)}, u32[]{:S(2)}, u32[]{:S(2)}) collective-permute-start(f32[256,128]{1,0:T(8,128)S(1)} %get-tuple-element.31), channel_id=1, source_target_pairs={{0,2},{1,3},{2,0},{3,1},{4,6},{5,7},{6,4},{7,5},{8,10},{9,11},{10,... | collective-permute-start | bytes 393224 | tf_op jit(solution)/shard_map/reduce/ppermute | solution.py:234
  20.5 2.8 %collective-permute-done.6.refs_0_ = f32[256,128]{1,0:T(8,128)S(1)} collective-permute-done((f32[256,128]{1,0:T(8,128)S(1)}, f32[256,128]{1,0:T(8,128)S(1)}, u32[]{:S(2)}, u32[]{:S(2)}) %collective-permute-start.6) | collective-permute-done | bytes 131104 | tf_op jit(solution)/shard_map/gather/ppermute | solution.py:234
  23.3 0.1 collective-permute-start.9
  23.4 0.0 collective-permute-done.11.got_ref
  23.4 0.0 collective-permute-done.7.refs_1_
  23.4 1.9 %forward.3 = (f32[256,128]{1,0:T(8,128)S(1)}, f32[256,128]{1,0:T(8,128)S(1)}, f32[256,128]{1,0:T(8,128)S(1)}, f32[256,128]{1,0:T(8,128)S(1)}) custom-call(f32[1,256,128]{2,1,0:T(8,128)S(1)} %gather.3._.refs_0_, f32[3,256,128]{2,1,0:T(8,128)S(1)} %get-tuple-element.27._.refs_0_, f32[3,256,128]{2,1,0:T(8,128)S(1)} %collective-permute-done.7.refs_1_, ...), custom_call_target="tpu_custom_call" | custom-call | bytes 1024 | tf_op jit(solution)/shard_map/forward/pallas_call | solution.py:247
  25.3 0.3 collective-permute-done.8.refs_0_
  25.6 0.0 collective-permute-done.9.refs_1_
  25.6 0.3 forward.4._
  26.0 3.6 %collective-permute-start.10 = (f32[256,128]{1,0:T(8,128)S(1)}, f32[256,128]{1,0:T(8,128)S(1)}, u32[]{:S(2)}, u32[]{:S(2)}) collective-permute-start(f32[256,128]{1,0:T(8,128)S(1)} %forward.4._), channel_id=1, source_target_pairs={{0,24},{8,16},{16,8},{24,0},{1,25},{9,17},{17,9},{25,1},{2,26},{10... | collective-permute-start | bytes 393224 | tf_op jit(solution)/shard_map/reduce/ppermute | solution.py:234
  29.6 0.0 collective-permute-start.12
  29.6 0.6 %forward.5 = (f32[256,128]{1,0:T(8,128)S(1)}, f32[256,128]{1,0:T(8,128)S(1)}, f32[256,128]{1,0:T(8,128)S(1)}) custom-call(f32[256,128]{1,0:T(8,128)S(1)} %reduce.6._, f32[1,256,128]{2,1,0:T(8,128)S(1)} %gather.3._.refs_0_, f32[1,256,128]{2,1,0:T(8,128)S(1)} %collective-permute-done.9.refs_1_, bf16[1024,2048]{1,0:T(8,128)(2,1)S(1)} %get-tuple-element.23._.refs_1_.refs_2_, ...), custom_call_target="tpu_custom_call" | custom-call | bytes 1024 | tf_op jit(solution)/shard_map/forward/pallas_call | solution.py:247
  30.2 1.1 %collective-permute-start.13 = (f32[256,128]{1,0:T(8,128)S(1)}, f32[256,128]{1,0:T(8,128)S(1)}, u32[]{:S(2)}, u32[]{:S(2)}) collective-permute-start(f32[256,128]{1,0:T(8,128)S(1)} %get-tuple-element.37), channel_id=1, source_target_pairs={{0,8},{8,0},{16,24},{24,16},{1,9},{9,1},{17,25},{25,17},{2,10},{10... | collective-permute-start | bytes 393224 | tf_op jit(solution)/shard_map/reduce/ppermute | solution.py:234
  31.3 0.0 collective-permute-start.14
  31.3 1.2 %collective-permute-start.15 = (f32[256,128]{1,0:T(8,128)S(1)}, f32[256,128]{1,0:T(8,128)S(1)}, u32[]{:S(2)}, u32[]{:S(2)}) collective-permute-start(f32[256,128]{1,0:T(8,128)S(1)} %get-tuple-element.41), channel_id=1, source_target_pairs={{0,2},{1,3},{2,0},{3,1},{4,6},{5,7},{6,4},{7,5},{8,10},{9,11},{10,... | collective-permute-start | bytes 393224 | tf_op jit(solution)/shard_map/reduce/ppermute | solution.py:234
  32.5 1.3 %collective-permute-done.10.y_ref = f32[256,128]{1,0:T(8,128)S(1)} collective-permute-done((f32[256,128]{1,0:T(8,128)S(1)}, f32[256,128]{1,0:T(8,128)S(1)}, u32[]{:S(2)}, u32[]{:S(2)}) %collective-permute-start.10) | collective-permute-done | bytes 131104 | tf_op jit(solution)/shard_map/reduce/ppermute | solution.py:234
  33.9 4.0 %collective-permute-done.12.refs_1_ = f32[256,128]{1,0:T(8,128)S(1)} collective-permute-done((f32[256,128]{1,0:T(8,128)S(1)}, f32[256,128]{1,0:T(8,128)S(1)}, u32[]{:S(2)}, u32[]{:S(2)}) %collective-permute-start.12) | collective-permute-done | bytes 131104 | tf_op jit(solution)/shard_map/reduce/ppermute | solution.py:234
  37.9 0.0 collective-permute-done.13.refs_1_
  37.9 0.0 collective-permute-done.14.refs_2_
  38.0 0.8 %collective-permute-done.15.refs_1_ = f32[256,128]{1,0:T(8,128)S(1)} collective-permute-done((f32[256,128]{1,0:T(8,128)S(1)}, f32[256,128]{1,0:T(8,128)S(1)}, u32[]{:S(2)}, u32[]{:S(2)}) %collective-permute-start.15) | collective-permute-done | bytes 131104 | tf_op jit(solution)/shard_map/reduce/ppermute | solution.py:234
  38.8 0.7 %finish.3 = (f32[256,128]{1,0:T(8,128)}, f32[256,128]{1,0:T(8,128)}) custom-call(f32[256,128]{1,0:T(8,128)S(1)} %finish.2.row_ref, f32[256,128]{1,0:T(8,128)S(1)} %get-tuple-element.39.row_factor_ref, f32[256,128]{1,0:T(8,128)S(1)} %get-tuple-element.40.col_factor_ref, f32[256,128]{1,0:T(8,128)S(1)} %reduce.9._.refs_0_, ...), custom_call_target="tpu_custom_call" | custom-call | bytes 1024 | tf_op jit(solution)/shard_map/finish/pallas_call | solution.py:247
  (9 shorter events, 0.2 us)
Async XLA Ops:
  1.8 12.8 %collective-permute-start.2 = (f32[256,128]{1,0:T(8,128)S(1)}, f32[256,128]{1,0:T(8,128)S(1)}, u32[]{:S(2)}, u32[]{:S(2)}) collective-permute-start(f32[256,128]{1,0:T(8,128)S(1)} %get-tuple-element.24.refs_0_), channel_id=1, source_target_pairs={{0,24},{8,16},{16,8},{24,0},{1,25},{9,17},{17,9},{25,1},{2,26},{10... | collective-permute-start | bytes 393224 | tf_op jit(solution)/shard_map/gather/ppermute | solution.py:234
  5.8 8.8 %collective-permute-start.1 = (f32[256,128]{1,0:T(8,128)S(1)}, f32[256,128]{1,0:T(8,128)S(1)}, u32[]{:S(2)}, u32[]{:S(2)}) collective-permute-start(f32[256,128]{1,0:T(8,128)S(1)} %get-tuple-element.24.refs_0_), channel_id=1, source_target_pairs={{0,16},{8,24},{16,0},{24,8},{1,17},{9,25},{17,1},{25,9},{2,18},{10... | collective-permute-start | bytes 393224 | tf_op jit(solution)/shard_map/gather/ppermute | solution.py:234
  6.3 8.3 %collective-permute-start = (f32[256,128]{1,0:T(8,128)S(1)}, f32[256,128]{1,0:T(8,128)S(1)}, u32[]{:S(2)}, u32[]{:S(2)}) collective-permute-start(f32[256,128]{1,0:T(8,128)S(1)} %get-tuple-element.24.refs_0_), channel_id=1, source_target_pairs={{0,8},{8,0},{16,24},{24,16},{1,9},{9,1},{17,25},{25,17},{2,10},{10... | collective-permute-start | bytes 393224 | tf_op jit(solution)/shard_map/gather/ppermute | solution.py:234
  6.4 9.9 %collective-permute-start.4 = (f32[256,128]{1,0:T(8,128)S(1)}, f32[256,128]{1,0:T(8,128)S(1)}, u32[]{:S(2)}, u32[]{:S(2)}) collective-permute-start(f32[256,128]{1,0:T(8,128)S(1)} %get-tuple-element.26.refs_0_), channel_id=1, source_target_pairs={{0,4},{1,5},{2,6},{3,7},{4,0},{5,1},{6,2},{7,3},{8,12},{9,13},{10,... | collective-permute-start | bytes 393224 | tf_op jit(solution)/shard_map/gather/ppermute | solution.py:234
  9.4 6.9 %collective-permute-start.3 = (f32[256,128]{1,0:T(8,128)S(1)}, f32[256,128]{1,0:T(8,128)S(1)}, u32[]{:S(2)}, u32[]{:S(2)}) collective-permute-start(f32[256,128]{1,0:T(8,128)S(1)} %get-tuple-element.26.refs_0_), channel_id=1, source_target_pairs={{0,2},{1,3},{2,0},{3,1},{4,6},{5,7},{6,4},{7,5},{8,10},{9,11},{10,... | collective-permute-start | bytes 393224 | tf_op jit(solution)/shard_map/gather/ppermute | solution.py:234
  16.2 2.0 %collective-permute-start.5 = (f32[2,256,128]{2,1,0:T(8,128)S(1)}, f32[2,256,128]{2,1,0:T(8,128)S(1)}, u32[]{:S(2)}, u32[]{:S(2)}) collective-permute-start(f32[2,256,128]{2,1,0:T(8,128)S(1)} %backward.5._), channel_id=1, source_target_pairs={{0,1},{1,0},{2,3},{3,2},{4,5},{5,4},{6,7},{7,6},{8,9},{9,8},{10,11... | collective-permute-start | bytes 786440 | tf_op jit(solution)/shard_map/backward/ppermute | solution.py:234
  16.3 7.1 %collective-permute-start.7 = (f32[3,256,128]{2,1,0:T(8,128)S(1)}, f32[3,256,128]{2,1,0:T(8,128)S(1)}, u32[]{:S(2)}, u32[]{:S(2)}) collective-permute-start(f32[3,256,128]{2,1,0:T(8,128)S(1)} %get-tuple-element.27._.refs_0_), channel_id=1, source_target_pairs={{0,1},{1,0},{2,3},{3,2},{4,5},{5,4},{6,7},{7,6},{8,9},{9,8},{10,11... | collective-permute-start | bytes 1179656 | tf_op jit(solution)/shard_map/gather/ppermute | solution.py:234
  16.9 6.5 %collective-permute-start.11 = (f32[2,256,128]{2,1,0:T(8,128)S(1)}, f32[2,256,128]{2,1,0:T(8,128)S(1)}, u32[]{:S(2)}, u32[]{:S(2)}) collective-permute-start(f32[2,256,128]{2,1,0:T(8,128)S(1)} %backward.6._), channel_id=1, source_target_pairs={{0,1},{1,0},{2,3},{3,2},{4,5},{5,4},{6,7},{7,6},{8,9},{9,8},{10,11... | collective-permute-start | bytes 786440 | tf_op jit(solution)/shard_map/reduce/ppermute | solution.py:234
  17.0 6.3 %collective-permute-start.6 = (f32[256,128]{1,0:T(8,128)S(1)}, f32[256,128]{1,0:T(8,128)S(1)}, u32[]{:S(2)}, u32[]{:S(2)}) collective-permute-start(f32[256,128]{1,0:T(8,128)S(1)} %get-tuple-element.29), channel_id=1, source_target_pairs={{0,2},{1,3},{2,0},{3,1},{4,6},{5,7},{6,4},{7,5},{8,10},{9,11},{10,... | collective-permute-start | bytes 393224 | tf_op jit(solution)/shard_map/gather/ppermute | solution.py:234
  18.9 6.7 %collective-permute-start.8 = (f32[256,128]{1,0:T(8,128)S(1)}, f32[256,128]{1,0:T(8,128)S(1)}, u32[]{:S(2)}, u32[]{:S(2)}) collective-permute-start(f32[256,128]{1,0:T(8,128)S(1)} %get-tuple-element.31), channel_id=1, source_target_pairs={{0,2},{1,3},{2,0},{3,1},{4,6},{5,7},{6,4},{7,5},{8,10},{9,11},{10,... | collective-permute-start | bytes 393224 | tf_op jit(solution)/shard_map/reduce/ppermute | solution.py:234
  23.3 2.4 %collective-permute-start.9 = (f32[1,256,128]{2,1,0:T(8,128)S(1)}, f32[1,256,128]{2,1,0:T(8,128)S(1)}, u32[]{:S(2)}, u32[]{:S(2)}) collective-permute-start(f32[1,256,128]{2,1,0:T(8,128)S(1)} %gather.3._.refs_0_), channel_id=1, source_target_pairs={{0,1},{1,0},{2,3},{3,2},{4,5},{5,4},{6,7},{7,6},{8,9},{9,8},{10,11... | collective-permute-start | bytes 393224 | tf_op jit(solution)/shard_map/gather/ppermute | solution.py:234
  26.0 7.9 %collective-permute-start.10 = (f32[256,128]{1,0:T(8,128)S(1)}, f32[256,128]{1,0:T(8,128)S(1)}, u32[]{:S(2)}, u32[]{:S(2)}) collective-permute-start(f32[256,128]{1,0:T(8,128)S(1)} %forward.4._), channel_id=1, source_target_pairs={{0,24},{8,16},{16,8},{24,0},{1,25},{9,17},{17,9},{25,1},{2,26},{10... | collective-permute-start | bytes 393224 | tf_op jit(solution)/shard_map/reduce/ppermute | solution.py:234
  29.6 8.3 %collective-permute-start.12 = (f32[256,128]{1,0:T(8,128)S(1)}, f32[256,128]{1,0:T(8,128)S(1)}, u32[]{:S(2)}, u32[]{:S(2)}) collective-permute-start(f32[256,128]{1,0:T(8,128)S(1)} %reduce.6._), channel_id=1, source_target_pairs={{0,4},{1,5},{2,6},{3,7},{4,0},{5,1},{6,2},{7,3},{8,12},{9,13},{10,... | collective-permute-start | bytes 393224 | tf_op jit(solution)/shard_map/reduce/ppermute | solution.py:234
  30.2 7.8 %collective-permute-start.13 = (f32[256,128]{1,0:T(8,128)S(1)}, f32[256,128]{1,0:T(8,128)S(1)}, u32[]{:S(2)}, u32[]{:S(2)}) collective-permute-start(f32[256,128]{1,0:T(8,128)S(1)} %get-tuple-element.37), channel_id=1, source_target_pairs={{0,8},{8,0},{16,24},{24,16},{1,9},{9,1},{17,25},{25,17},{2,10},{10... | collective-permute-start | bytes 393224 | tf_op jit(solution)/shard_map/reduce/ppermute | solution.py:234
  31.3 6.6 %collective-permute-start.14 = (f32[256,128]{1,0:T(8,128)S(1)}, f32[256,128]{1,0:T(8,128)S(1)}, u32[]{:S(2)}, u32[]{:S(2)}) collective-permute-start(f32[256,128]{1,0:T(8,128)S(1)} %get-tuple-element.38), channel_id=1, source_target_pairs={{0,16},{8,24},{16,0},{24,8},{1,17},{9,25},{17,1},{25,9},{2,18},{10... | collective-permute-start | bytes 393224 | tf_op jit(solution)/shard_map/reduce/ppermute | solution.py:234
  31.3 7.5 %collective-permute-start.15 = (f32[256,128]{1,0:T(8,128)S(1)}, f32[256,128]{1,0:T(8,128)S(1)}, u32[]{:S(2)}, u32[]{:S(2)}) collective-permute-start(f32[256,128]{1,0:T(8,128)S(1)} %get-tuple-element.41), channel_id=1, source_target_pairs={{0,2},{1,3},{2,0},{3,1},{4,6},{5,7},{6,4},{7,5},{8,10},{9,11},{10,... | collective-permute-start | bytes 393224 | tf_op jit(solution)/shard_map/reduce/ppermute | solution.py:234

commit v8 on v6

--- a/solution.py
+++ b/solution.py
@@ -84,11 +84,8 @@
         out_ref[...] = kept_ref[at] + got_ref[at]
 
 
-def stack_kernel(*refs):
-    *part_refs, out_ref, last_ref = refs
-    for at, part_ref in enumerate(part_refs):
-        out_ref[at] = part_ref[...]
-    last_ref[...] = part_refs[-1][...]
+def pass_kernel(x_ref, out_ref):
+    out_ref[...] = x_ref[...]
 
 
 def copy_kernel(*refs):
@@ -230,7 +227,7 @@
     return lax.ppermute(x, axis, [(at, at ^ mask) for at in range(lax.axis_size(axis))])
 
 
-def call(kernel, out_shape, args, mebibytes=16, scratch=(), specs=None, after=None):
+def call(kernel, out_shape, args, mebibytes=16, flops=0, scratch=(), specs=None, after=None):
     outs = out_shape if isinstance(out_shape, tuple) else (out_shape,)
     specs = specs or [WHOLE] * len(args)
     body = kernel
@@ -247,7 +244,7 @@
         out_specs=tuple(WHOLE for _ in outs) if isinstance(out_shape, tuple) else WHOLE,
         scratch_shapes=scratch,
         compiler_params=params(mebibytes),
-        cost_estimate=cost(0, 1024),
+        cost_estimate=cost(flops, 1024),
     )(*args)
 
 
@@ -287,12 +284,8 @@
             mask //= 2
 
     def gathered(after):
-        early, passed = call(
-            stack_kernel,
-            (blocks(half + 1), block),
-            [near[at] for at in range(half)] + [crossed],
-            after=after,
-        )
+        passed = call(pass_kernel, block, [crossed], after=after)
+        early = call(copy_kernel, blocks(half + 1), [near[at] for at in range(half)] + [passed], after=passed)
         late, mask = {0: passed}, half // 2
         while mask:
             late.update({at | mask: swap(x, "col", 2 * mask) for at, x in late.items()})
@@ -364,7 +357,7 @@
                 return core * count + distance
             return 2 * count + core * (pairs - count) + distance - count
 
-        def forward_part(embeds, first, before=(), after=None):
+        def forward_part(embeds, first, before=(), after=None, flops=0):
             count = sum(x.shape[0] for x in embeds)
             return call(
                 functools.partial(forward_kernel, first, len(embeds), n_row),
@@ -373,25 +366,28 @@
                 mebibytes=24,
                 scratch=[pltpu.VMEM((count * shard, 2 * width), BF16)],
                 after=after,
+                flops=flops,
             )
 
         with jax.named_scope("backward"):
             far, close = range(half, pairs), range(half)
             far_sent = backward_part(far, 1, plan)
-            sent = backward_part(close, 1, far_sent)
-            far_sums = chip_sums(backward_part(far, 0, sent), far_sent)
-            kept = backward_part(close, 0, far_sums[0])
+            far_kept = backward_part(far, 0, far_sent)
         with jax.named_scope("gather"):
-            late = call(copy_kernel, blocks(half - 1), late, after=kept)
+            late = call(copy_kernel, blocks(half - 1), late, after=far_kept, flops=2 * 10**9)
             other_late = swap(late, "col", 1)
+        with jax.named_scope("backward"):
+            far_sums = chip_sums(far_kept, far_sent, late)
+            sent = backward_part(close, 1, far_sums[0])
+            kept = backward_part(close, 0, sent)
         with jax.named_scope("forward"):
-            forwards = forward_part([early, other_early], 0, after=late)
+            forwards = forward_part([early, other_early], 0, after=kept)
         with jax.named_scope("reduce"):
             crossing = total(halved(far_sums, forwards[0]), forwards[0])
         with jax.named_scope("forward"):
-            forwards = forward_part([late, other_late], 2 * (half + 1), forwards, crossing)
+            forwards = forward_part([late, other_late], 2 * (half + 1), forwards, crossing, 2 * 10**9)
         with jax.named_scope("reduce"):
-            close_sums = chip_sums(kept, sent)
+            close_sums = chip_sums(kept, sent, forwards[0])
             after = None
     else:
         group = 8
@@ -435,7 +431,8 @@
         row_parts = [forwards[0]] + [swap(forwards[k], "row", k) for k in range(1, n_row)]
 
     with jax.named_scope("finish"):
-        row_sum = call(sum_kernel, block, row_parts, after=mine)
+        row_sum = call(sum_kernel, block, [row_parts[0], row_parts[-1]], after=mine)
+        row_sum = call(sum_kernel, block, [row_sum, *row_parts[1:-1]])
         return call(
             finish_kernel, (block, block), (row_sum, row_factor, col_factor, mine, *grad_parts), mebibytes=4
         )

time: 38 us -> 37.5 us (0.987); the launches traced: 37.9 us -> 37.8 us
  waiting for transfers between devices: 8.67 us -> 6.95 us
  starting transfers between devices: 17.2 us -> 18.8 us
    ppermute x16, waiting for transfers between devices: 8.67 us -> 6.95 us  [swap(): lax.ppermute(x, axis, [(at, at ^ mask) for at in range(lax.axis_size(axis...]
    ppermute x16, starting transfers between devices: 17.2 us -> 18.8 us  [swap(): lax.ppermute(x, axis, [(at, at ^ mask) for at in range(lax.axis_size(axis...]
    pallas_call x17 -> x19, Pallas kernels: 10.5 us -> 10.5 us  [call(): pl.pallas_call(body, out_shape=out_shape, in_specs=specs, out_specs=tuple...]
  transfers between devices with their start and end apart: 16 -> 16, of which waited for: 7 -> 5; matrix products, arithmetic and copies ran while one was open for 0% -> 0% of each run, Pallas kernels for 20% -> 23%
where the time goes in v8:
time: 37.5 us; the launch traced here: 37.8 us
  starting transfers between devices  18.8 us (50%)
  Pallas kernels  10.5 us (28%)
  waiting for transfers between devices  6.95 us (19%)
  between operations  1.47 us (4%)
    ppermute x16, starting transfers between devices, swap(): lax.ppermute(x, axis, [(at, at ^ mask) for at in range(lax.axis_size(axis...  18.8 us
    pallas_call x19, Pallas kernels, call(): pl.pallas_call(body, out_shape=out_shape, in_specs=specs, out_specs=tuple...  10.5 us
    ppermute x16, waiting for transfers between devices, swap(): lax.ppermute(x, axis, [(at, at ^ mask) for at in range(lax.axis_size(axis...  6.95 us
  transfers between devices with their start and end apart: 16, of which 5 were waited for; matrix products, arithmetic and copies ran while one was open for 0% of the time, Pallas kernels for 23%

profile of v8, /device:TPU:0, one launch (start us, length us, event | category | flops | bytes accessed | tf_op | source)
XLA Modules:
  0.0 37.8 jit_solution(14823242000639195668)
XLA Ops:
  0.6 1.2 %scale.1 = (f32[256,128]{1,0:T(8,128)S(1)}, f32[256,128]{1,0:T(8,128)S(1)}, f32[256,128]{1,0:T(8,128)S(1)}, f32[256,128]{1,0:T(8,128)S(1)}, s32[2,128]{1,0:T(2,128)S(1)}) custom-call(f32[256,128]{1,0:T(8,128)} %refs_0_.1, f32[256,128]{1,0:T(8,128)} %refs_1_.1, s32[2,128]{1,0:T(2,128)} %bitcast.4, s32[2,128]{1,0:T(2,128)} %bitcast.5, s32[2,1,1,128]{3,2,1,0:T(1,128)} %refs_4_.1), custom_call_target="tpu_custom_call" | custom-call | bytes 1024 | tf_op jit(solution)/shard_map/scale/pallas_call | solution.py:240
  1.8 4.1 %collective-permute-start = (f32[256,128]{1,0:T(8,128)S(1)}, f32[256,128]{1,0:T(8,128)S(1)}, u32[]{:S(2)}, u32[]{:S(2)}) collective-permute-start(f32[256,128]{1,0:T(8,128)S(1)} %get-tuple-element.23.refs_0_), channel_id=1, source_target_pairs={{0,4},{1,5},{2,6},{3,7},{4,0},{5,1},{6,2},{7,3},{8,12},{9,13},{10,... | collective-permute-start | bytes 393224 | tf_op jit(solution)/shard_map/gather/ppermute | solution.py:227
  5.9 1.6 %collective-permute-start.1 = (f32[256,128]{1,0:T(8,128)S(1)}, f32[256,128]{1,0:T(8,128)S(1)}, u32[]{:S(2)}, u32[]{:S(2)}) collective-permute-start(f32[256,128]{1,0:T(8,128)S(1)} %get-tuple-element.23.refs_0_), channel_id=1, source_target_pairs={{0,2},{1,3},{2,0},{3,1},{4,6},{5,7},{6,4},{7,5},{8,10},{9,11},{10,... | collective-permute-start | bytes 393224 | tf_op jit(solution)/shard_map/gather/ppermute | solution.py:227
  7.5 1.5 %collective-permute-start.2 = (f32[256,128]{1,0:T(8,128)S(1)}, f32[256,128]{1,0:T(8,128)S(1)}, u32[]{:S(2)}, u32[]{:S(2)}) collective-permute-start(f32[256,128]{1,0:T(8,128)S(1)} %get-tuple-element.24.refs_0_), channel_id=1, source_target_pairs={{0,8},{8,0},{16,24},{24,16},{1,9},{9,1},{17,25},{25,17},{2,10},{10... | collective-permute-start | bytes 393224 | tf_op jit(solution)/shard_map/gather/ppermute | solution.py:227
  9.0 1.5 %collective-permute-start.3 = (f32[256,128]{1,0:T(8,128)S(1)}, f32[256,128]{1,0:T(8,128)S(1)}, u32[]{:S(2)}, u32[]{:S(2)}) collective-permute-start(f32[256,128]{1,0:T(8,128)S(1)} %get-tuple-element.24.refs_0_), channel_id=1, source_target_pairs={{0,16},{8,24},{16,0},{24,8},{1,17},{9,25},{17,1},{25,9},{2,18},{10... | collective-permute-start | bytes 393224 | tf_op jit(solution)/shard_map/gather/ppermute | solution.py:227
  10.5 0.5 %collective-permute-start.4 = (f32[256,128]{1,0:T(8,128)S(1)}, f32[256,128]{1,0:T(8,128)S(1)}, u32[]{:S(2)}, u32[]{:S(2)}) collective-permute-start(f32[256,128]{1,0:T(8,128)S(1)} %get-tuple-element.24.refs_0_), channel_id=1, source_target_pairs={{0,24},{8,16},{16,8},{24,0},{1,25},{9,17},{17,9},{25,1},{2,26},{10... | collective-permute-start | bytes 393224 | tf_op jit(solution)/shard_map/gather/ppermute | solution.py:227
  11.6 2.9 %split.1 = (bf16[1024,2048]{1,0:T(8,128)(2,1)S(1)}, bf16[1024,2048]{1,0:T(8,128)(2,1)S(1)}) custom-call(s32[2,128]{1,0:T(2,128)S(1)} %get-tuple-element.21.plan_ref._, s32[1,1]{1,0:T(1,128)S(6)} %copy.9.count_ref, f32[128,128,128]{2,1,0:T(8,128)} %bitcast.3), custom_call_target="tpu_custom_call" | custom-call | bytes 1024 | tf_op jit(solution)/shard_map/split/pallas_call | solution.py:240
  14.6 0.0 collective-permute-done.refs_0_
  14.6 1.5 %collective-permute-start.5 = (f32[256,128]{1,0:T(8,128)S(1)}, f32[256,128]{1,0:T(8,128)S(1)}, u32[]{:S(2)}, u32[]{:S(2)}) collective-permute-start(f32[256,128]{1,0:T(8,128)S(1)} %gather.3._.refs_2_), channel_id=1, source_target_pairs={{0,2},{1,3},{2,0},{3,1},{4,6},{5,7},{6,4},{7,5},{8,10},{9,11},{10,... | collective-permute-start | bytes 393224 | tf_op jit(solution)/shard_map/gather/ppermute | solution.py:227
  16.1 0.0 collective-permute-done.1.refs_1_
  16.1 0.0 collective-permute-done.2.refs_1_
  16.1 0.6 %collective-permute-done.3.refs_2_ = f32[256,128]{1,0:T(8,128)S(1)} collective-permute-done((f32[256,128]{1,0:T(8,128)S(1)}, f32[256,128]{1,0:T(8,128)S(1)}, u32[]{:S(2)}, u32[]{:S(2)}) %collective-permute-start.3) | collective-permute-done | bytes 131104 | tf_op jit(solution)/shard_map/gather/ppermute | solution.py:227
  16.7 0.0 collective-permute-done.4.refs_3_
  16.8 0.2 flip.1.refs_0_
  17.0 0.7 %backward.5._ = f32[2,256,128]{2,1,0:T(8,128)S(1)} custom-call(s32[2,128]{1,0:T(2,128)S(1)} %get-tuple-element.21.plan_ref._, bf16[256,1024]{1,0:T(8,128)(2,1)S(1)} %flip.1.refs_0_, bf16[1024,2048]{1,0:T(8,128)(2,1)S(1)} %get-tuple-element.22._.refs_1_.refs_2_, bf16[1024,2048]{1,0:T(8,128)(2,1)S(1)} %get-tuple-element.25.refs_2_.refs_3_), custom_call_target="tpu_custom_call" | custom-call | bytes 1024 | tf_op jit(solution)/shard_map/backward/pallas_call | solution.py:240
  17.7 0.1 collective-permute-start.6
  17.7 0.5 %collective-permute-start.7 = (f32[3,256,128]{2,1,0:T(8,128)S(1)}, f32[3,256,128]{2,1,0:T(8,128)S(1)}, u32[]{:S(2)}, u32[]{:S(2)}) collective-permute-start(f32[3,256,128]{2,1,0:T(8,128)S(1)} %gather.4._.refs_0_), channel_id=1, source_target_pairs={{0,1},{1,0},{2,3},{3,2},{4,5},{5,4},{6,7},{7,6},{8,9},{9,8},{10,11... | collective-permute-start | bytes 1179656 | tf_op jit(solution)/shard_map/gather/ppermute | solution.py:227
  18.2 0.7 %backward.6._.refs_0_ = f32[2,256,128]{2,1,0:T(8,128)S(1)} custom-call(f32[2,256,128]{2,1,0:T(8,128)S(1)} %backward.5._, bf16[256,1024]{1,0:T(8,128)(2,1)S(1)} %flip.1.refs_0_, bf16[1024,2048]{1,0:T(8,128)(2,1)S(1)} %get-tuple-element.22._.refs_1_.refs_2_, bf16[1024,2048]{1,0:T(8,128)(2,1)S(1)} %get-tuple-element.25.refs_2_.refs_3_), custom_call_target="tpu_custom_call" | custom-call | bytes 1024 | tf_op jit(solution)/shard_map/backward/pallas_call | solution.py:240
  18.9 0.7 %collective-permute-done.5.refs_0_ = f32[256,128]{1,0:T(8,128)S(1)} collective-permute-done((f32[256,128]{1,0:T(8,128)S(1)}, f32[256,128]{1,0:T(8,128)S(1)}, u32[]{:S(2)}, u32[]{:S(2)}) %collective-permute-start.5) | collective-permute-done | bytes 131104 | tf_op jit(solution)/shard_map/gather/ppermute | solution.py:227
  19.6 0.0 collective-permute-done.6.refs_1_
  19.7 1.5 %collective-permute-start.8 = (f32[256,128]{1,0:T(8,128)S(1)}, f32[256,128]{1,0:T(8,128)S(1)}, u32[]{:S(2)}, u32[]{:S(2)}) collective-permute-start(f32[256,128]{1,0:T(8,128)S(1)} %get-tuple-element.28), channel_id=1, source_target_pairs={{0,2},{1,3},{2,0},{3,1},{4,6},{5,7},{6,4},{7,5},{8,10},{9,11},{10,... | collective-permute-start | bytes 393224 | tf_op jit(solution)/shard_map/reduce/ppermute | solution.py:227
  21.2 0.0 collective-permute-start.9
  21.2 0.7 %backward.8._ = f32[2,256,128]{2,1,0:T(8,128)S(1)} custom-call(f32[256,128]{1,0:T(8,128)S(1)} %get-tuple-element.26._.refs_0_, bf16[256,1024]{1,0:T(8,128)(2,1)S(1)} %flip.1.refs_0_, bf16[1024,2048]{1,0:T(8,128)(2,1)S(1)} %get-tuple-element.22._.refs_1_.refs_2_, bf16[1024,2048]{1,0:T(8,128)(2,1)S(1)} %get-tuple-element.25.refs_2_.refs_3_), custom_call_target="tpu_custom_call" | custom-call | bytes 1024 | tf_op jit(solution)/shard_map/backward/pallas_call | solution.py:240
  21.9 0.6 %collective-permute-start.10 = (f32[2,256,128]{2,1,0:T(8,128)S(1)}, f32[2,256,128]{2,1,0:T(8,128)S(1)}, u32[]{:S(2)}, u32[]{:S(2)}) collective-permute-start(f32[2,256,128]{2,1,0:T(8,128)S(1)} %backward.8._), channel_id=1, source_target_pairs={{0,1},{1,0},{2,3},{3,2},{4,5},{5,4},{6,7},{7,6},{8,9},{9,8},{10,11... | collective-permute-start | bytes 786440 | tf_op jit(solution)/shard_map/reduce/ppermute | solution.py:227
  22.5 0.7 %backward.9._.refs_0_ = f32[2,256,128]{2,1,0:T(8,128)S(1)} custom-call(f32[2,256,128]{2,1,0:T(8,128)S(1)} %backward.8._, bf16[256,1024]{1,0:T(8,128)(2,1)S(1)} %flip.1.refs_0_, bf16[1024,2048]{1,0:T(8,128)(2,1)S(1)} %get-tuple-element.22._.refs_1_.refs_2_, bf16[1024,2048]{1,0:T(8,128)(2,1)S(1)} %get-tuple-element.25.refs_2_.refs_3_), custom_call_target="tpu_custom_call" | custom-call | bytes 1024 | tf_op jit(solution)/shard_map/backward/pallas_call | solution.py:240
  23.1 0.0 collective-permute-done.7.refs_1_
  23.2 1.9 %forward.2 = (f32[256,128]{1,0:T(8,128)S(1)}, f32[256,128]{1,0:T(8,128)S(1)}, f32[256,128]{1,0:T(8,128)S(1)}, f32[256,128]{1,0:T(8,128)S(1)}) custom-call(f32[2,256,128]{2,1,0:T(8,128)S(1)} %backward.9._.refs_0_, f32[3,256,128]{2,1,0:T(8,128)S(1)} %gather.4._.refs_0_, f32[3,256,128]{2,1,0:T(8,128)S(1)} %collective-permute-done.7.refs_1_, ...), custom_call_target="tpu_custom_call" | custom-call | bytes 1024 | tf_op jit(solution)/shard_map/forward/pallas_call | solution.py:240
  25.0 0.0 collective-permute-done.8.refs_1_
  25.1 0.8 %collective-permute-start.11 = (f32[256,128]{1,0:T(8,128)S(1)}, f32[256,128]{1,0:T(8,128)S(1)}, u32[]{:S(2)}, u32[]{:S(2)}) collective-permute-start(f32[256,128]{1,0:T(8,128)S(1)} %reduce.3._), channel_id=1, source_target_pairs={{0,4},{1,5},{2,6},{3,7},{4,0},{5,1},{6,2},{7,3},{8,12},{9,13},{10,... | collective-permute-start | bytes 393224 | tf_op jit(solution)/shard_map/reduce/ppermute | solution.py:227
  25.9 0.0 collective-permute-done.9.refs_1_
  25.9 0.7 %forward.3 = (f32[256,128]{1,0:T(8,128)S(1)}, f32[256,128]{1,0:T(8,128)S(1)}, f32[256,128]{1,0:T(8,128)S(1)}, f32[256,128]{1,0:T(8,128)S(1)}) custom-call(f32[256,128]{1,0:T(8,128)S(1)} %reduce.3._, f32[1,256,128]{2,1,0:T(8,128)S(1)} %gather.5._.refs_0_, f32[1,256,128]{2,1,0:T(8,128)S(1)} %collective-permute-done.9.refs_1_, ...), custom_call_target="tpu_custom_call" | custom-call | flops 2000000000 | bytes 1024 | tf_op jit(solution)/shard_map/forward/pallas_call | solution.py:240
  26.6 2.5 %collective-permute-start.12 = (f32[256,128]{1,0:T(8,128)S(1)}, f32[256,128]{1,0:T(8,128)S(1)}, u32[]{:S(2)}, u32[]{:S(2)}) collective-permute-start(f32[256,128]{1,0:T(8,128)S(1)} %get-tuple-element.34), channel_id=1, source_target_pairs={{0,24},{8,16},{16,8},{24,0},{1,25},{9,17},{17,9},{25,1},{2,26},{10... | collective-permute-start | bytes 393224 | tf_op jit(solution)/shard_map/reduce/ppermute | solution.py:227
  29.1 0.5 %collective-permute-start.13 = (f32[256,128]{1,0:T(8,128)S(1)}, f32[256,128]{1,0:T(8,128)S(1)}, u32[]{:S(2)}, u32[]{:S(2)}) collective-permute-start(f32[256,128]{1,0:T(8,128)S(1)} %get-tuple-element.35), channel_id=1, source_target_pairs={{0,8},{8,0},{16,24},{24,16},{1,9},{9,1},{17,25},{25,17},{2,10},{10... | collective-permute-start | bytes 393224 | tf_op jit(solution)/shard_map/reduce/ppermute | solution.py:227
  29.7 0.5 %collective-permute-start.14 = (f32[256,128]{1,0:T(8,128)S(1)}, f32[256,128]{1,0:T(8,128)S(1)}, u32[]{:S(2)}, u32[]{:S(2)}) collective-permute-start(f32[256,128]{1,0:T(8,128)S(1)} %get-tuple-element.36), channel_id=1, source_target_pairs={{0,16},{8,24},{16,0},{24,8},{1,17},{9,25},{17,1},{25,9},{2,18},{10... | collective-permute-start | bytes 393224 | tf_op jit(solution)/shard_map/reduce/ppermute | solution.py:227
  30.2 0.0 collective-permute-done.10.refs_1_
  30.2 1.2 %collective-permute-start.15 = (f32[256,128]{1,0:T(8,128)S(1)}, f32[256,128]{1,0:T(8,128)S(1)}, u32[]{:S(2)}, u32[]{:S(2)}) collective-permute-start(f32[256,128]{1,0:T(8,128)S(1)} %get-tuple-element.39), channel_id=1, source_target_pairs={{0,2},{1,3},{2,0},{3,1},{4,6},{5,7},{6,4},{7,5},{8,10},{9,11},{10,... | collective-permute-start | bytes 393224 | tf_op jit(solution)/shard_map/reduce/ppermute | solution.py:227
  31.4 3.0 %collective-permute-done.11.y_ref = f32[256,128]{1,0:T(8,128)S(1)} collective-permute-done((f32[256,128]{1,0:T(8,128)S(1)}, f32[256,128]{1,0:T(8,128)S(1)}, u32[]{:S(2)}, u32[]{:S(2)}) %collective-permute-start.11) | collective-permute-done | bytes 131104 | tf_op jit(solution)/shard_map/reduce/ppermute | solution.py:227
  34.4 0.0 collective-permute-done.12.refs_1_
  34.4 1.2 %collective-permute-done.13.refs_1_ = f32[256,128]{1,0:T(8,128)S(1)} collective-permute-done((f32[256,128]{1,0:T(8,128)S(1)}, f32[256,128]{1,0:T(8,128)S(1)}, u32[]{:S(2)}, u32[]{:S(2)}) %collective-permute-start.13) | collective-permute-done | bytes 131104 | tf_op jit(solution)/shard_map/reduce/ppermute | solution.py:227
  35.6 0.0 collective-permute-done.14.refs_2_
  35.6 1.4 %collective-permute-done.15.refs_1_ = f32[256,128]{1,0:T(8,128)S(1)} collective-permute-done((f32[256,128]{1,0:T(8,128)S(1)}, f32[256,128]{1,0:T(8,128)S(1)}, u32[]{:S(2)}, u32[]{:S(2)}) %collective-permute-start.15) | collective-permute-done | bytes 131104 | tf_op jit(solution)/shard_map/reduce/ppermute | solution.py:227
  37.1 0.7 %finish.5 = (f32[256,128]{1,0:T(8,128)}, f32[256,128]{1,0:T(8,128)}) custom-call(f32[256,128]{1,0:T(8,128)S(1)} %finish.4.row_ref, f32[256,128]{1,0:T(8,128)S(1)} %get-tuple-element.37.row_factor_ref, f32[256,128]{1,0:T(8,128)S(1)} %get-tuple-element.38.col_factor_ref, f32[256,128]{1,0:T(8,128)S(1)} %reduce.5._.refs_0_, ...), custom_call_target="tpu_custom_call" | custom-call | bytes 1024 | tf_op jit(solution)/shard_map/finish/pallas_call | solution.py:240
  (9 shorter events, 0.2 us)
Async XLA Ops:
  1.8 12.8 %collective-permute-start = (f32[256,128]{1,0:T(8,128)S(1)}, f32[256,128]{1,0:T(8,128)S(1)}, u32[]{:S(2)}, u32[]{:S(2)}) collective-permute-start(f32[256,128]{1,0:T(8,128)S(1)} %get-tuple-element.23.refs_0_), channel_id=1, source_target_pairs={{0,4},{1,5},{2,6},{3,7},{4,0},{5,1},{6,2},{7,3},{8,12},{9,13},{10,... | collective-permute-start | bytes 393224 | tf_op jit(solution)/shard_map/gather/ppermute | solution.py:227
  5.9 10.2 %collective-permute-start.1 = (f32[256,128]{1,0:T(8,128)S(1)}, f32[256,128]{1,0:T(8,128)S(1)}, u32[]{:S(2)}, u32[]{:S(2)}) collective-permute-start(f32[256,128]{1,0:T(8,128)S(1)} %get-tuple-element.23.refs_0_), channel_id=1, source_target_pairs={{0,2},{1,3},{2,0},{3,1},{4,6},{5,7},{6,4},{7,5},{8,10},{9,11},{10,... | collective-permute-start | bytes 393224 | tf_op jit(solution)/shard_map/gather/ppermute | solution.py:227
  7.5 8.6 %collective-permute-start.2 = (f32[256,128]{1,0:T(8,128)S(1)}, f32[256,128]{1,0:T(8,128)S(1)}, u32[]{:S(2)}, u32[]{:S(2)}) collective-permute-start(f32[256,128]{1,0:T(8,128)S(1)} %get-tuple-element.24.refs_0_), channel_id=1, source_target_pairs={{0,8},{8,0},{16,24},{24,16},{1,9},{9,1},{17,25},{25,17},{2,10},{10... | collective-permute-start | bytes 393224 | tf_op jit(solution)/shard_map/gather/ppermute | solution.py:227
  9.0 7.8 %collective-permute-start.3 = (f32[256,128]{1,0:T(8,128)S(1)}, f32[256,128]{1,0:T(8,128)S(1)}, u32[]{:S(2)}, u32[]{:S(2)}) collective-permute-start(f32[256,128]{1,0:T(8,128)S(1)} %get-tuple-element.24.refs_0_), channel_id=1, source_target_pairs={{0,16},{8,24},{16,0},{24,8},{1,17},{9,25},{17,1},{25,9},{2,18},{10... | collective-permute-start | bytes 393224 | tf_op jit(solution)/shard_map/gather/ppermute | solution.py:227
  10.5 6.3 %collective-permute-start.4 = (f32[256,128]{1,0:T(8,128)S(1)}, f32[256,128]{1,0:T(8,128)S(1)}, u32[]{:S(2)}, u32[]{:S(2)}) collective-permute-start(f32[256,128]{1,0:T(8,128)S(1)} %get-tuple-element.24.refs_0_), channel_id=1, source_target_pairs={{0,24},{8,16},{16,8},{24,0},{1,25},{9,17},{17,9},{25,1},{2,26},{10... | collective-permute-start | bytes 393224 | tf_op jit(solution)/shard_map/gather/ppermute | solution.py:227
  14.6 5.0 %collective-permute-start.5 = (f32[256,128]{1,0:T(8,128)S(1)}, f32[256,128]{1,0:T(8,128)S(1)}, u32[]{:S(2)}, u32[]{:S(2)}) collective-permute-start(f32[256,128]{1,0:T(8,128)S(1)} %gather.3._.refs_2_), channel_id=1, source_target_pairs={{0,2},{1,3},{2,0},{3,1},{4,6},{5,7},{6,4},{7,5},{8,10},{9,11},{10,... | collective-permute-start | bytes 393224 | tf_op jit(solution)/shard_map/gather/ppermute | solution.py:227
  17.7 2.0 %collective-permute-start.6 = (f32[2,256,128]{2,1,0:T(8,128)S(1)}, f32[2,256,128]{2,1,0:T(8,128)S(1)}, u32[]{:S(2)}, u32[]{:S(2)}) collective-permute-start(f32[2,256,128]{2,1,0:T(8,128)S(1)} %backward.5._), channel_id=1, source_target_pairs={{0,1},{1,0},{2,3},{3,2},{4,5},{5,4},{6,7},{7,6},{8,9},{9,8},{10,11... | collective-permute-start | bytes 786440 | tf_op jit(solution)/shard_map/backward/ppermute | solution.py:227
  17.7 5.4 %collective-permute-start.7 = (f32[3,256,128]{2,1,0:T(8,128)S(1)}, f32[3,256,128]{2,1,0:T(8,128)S(1)}, u32[]{:S(2)}, u32[]{:S(2)}) collective-permute-start(f32[3,256,128]{2,1,0:T(8,128)S(1)} %gather.4._.refs_0_), channel_id=1, source_target_pairs={{0,1},{1,0},{2,3},{3,2},{4,5},{5,4},{6,7},{7,6},{8,9},{9,8},{10,11... | collective-permute-start | bytes 1179656 | tf_op jit(solution)/shard_map/gather/ppermute | solution.py:227
  19.7 5.3 %collective-permute-start.8 = (f32[256,128]{1,0:T(8,128)S(1)}, f32[256,128]{1,0:T(8,128)S(1)}, u32[]{:S(2)}, u32[]{:S(2)}) collective-permute-start(f32[256,128]{1,0:T(8,128)S(1)} %get-tuple-element.28), channel_id=1, source_target_pairs={{0,2},{1,3},{2,0},{3,1},{4,6},{5,7},{6,4},{7,5},{8,10},{9,11},{10,... | collective-permute-start | bytes 393224 | tf_op jit(solution)/shard_map/reduce/ppermute | solution.py:227
  21.2 4.7 %collective-permute-start.9 = (f32[1,256,128]{2,1,0:T(8,128)S(1)}, f32[1,256,128]{2,1,0:T(8,128)S(1)}, u32[]{:S(2)}, u32[]{:S(2)}) collective-permute-start(f32[1,256,128]{2,1,0:T(8,128)S(1)} %gather.5._.refs_0_), channel_id=1, source_target_pairs={{0,1},{1,0},{2,3},{3,2},{4,5},{5,4},{6,7},{7,6},{8,9},{9,8},{10,11... | collective-permute-start | bytes 393224 | tf_op jit(solution)/shard_map/gather/ppermute | solution.py:227
  21.9 8.3 %collective-permute-start.10 = (f32[2,256,128]{2,1,0:T(8,128)S(1)}, f32[2,256,128]{2,1,0:T(8,128)S(1)}, u32[]{:S(2)}, u32[]{:S(2)}) collective-permute-start(f32[2,256,128]{2,1,0:T(8,128)S(1)} %backward.8._), channel_id=1, source_target_pairs={{0,1},{1,0},{2,3},{3,2},{4,5},{5,4},{6,7},{7,6},{8,9},{9,8},{10,11... | collective-permute-start | bytes 786440 | tf_op jit(solution)/shard_map/reduce/ppermute | solution.py:227
  25.1 9.3 %collective-permute-start.11 = (f32[256,128]{1,0:T(8,128)S(1)}, f32[256,128]{1,0:T(8,128)S(1)}, u32[]{:S(2)}, u32[]{:S(2)}) collective-permute-start(f32[256,128]{1,0:T(8,128)S(1)} %reduce.3._), channel_id=1, source_target_pairs={{0,4},{1,5},{2,6},{3,7},{4,0},{5,1},{6,2},{7,3},{8,12},{9,13},{10,... | collective-permute-start | bytes 393224 | tf_op jit(solution)/shard_map/reduce/ppermute | solution.py:227
  26.6 7.8 %collective-permute-start.12 = (f32[256,128]{1,0:T(8,128)S(1)}, f32[256,128]{1,0:T(8,128)S(1)}, u32[]{:S(2)}, u32[]{:S(2)}) collective-permute-start(f32[256,128]{1,0:T(8,128)S(1)} %get-tuple-element.34), channel_id=1, source_target_pairs={{0,24},{8,16},{16,8},{24,0},{1,25},{9,17},{17,9},{25,1},{2,26},{10... | collective-permute-start | bytes 393224 | tf_op jit(solution)/shard_map/reduce/ppermute | solution.py:227
  29.1 6.5 %collective-permute-start.13 = (f32[256,128]{1,0:T(8,128)S(1)}, f32[256,128]{1,0:T(8,128)S(1)}, u32[]{:S(2)}, u32[]{:S(2)}) collective-permute-start(f32[256,128]{1,0:T(8,128)S(1)} %get-tuple-element.35), channel_id=1, source_target_pairs={{0,8},{8,0},{16,24},{24,16},{1,9},{9,1},{17,25},{25,17},{2,10},{10... | collective-permute-start | bytes 393224 | tf_op jit(solution)/shard_map/reduce/ppermute | solution.py:227
  29.7 5.9 %collective-permute-start.14 = (f32[256,128]{1,0:T(8,128)S(1)}, f32[256,128]{1,0:T(8,128)S(1)}, u32[]{:S(2)}, u32[]{:S(2)}) collective-permute-start(f32[256,128]{1,0:T(8,128)S(1)} %get-tuple-element.36), channel_id=1, source_target_pairs={{0,16},{8,24},{16,0},{24,8},{1,17},{9,25},{17,1},{25,9},{2,18},{10... | collective-permute-start | bytes 393224 | tf_op jit(solution)/shard_map/reduce/ppermute | solution.py:227
  30.2 6.9 %collective-permute-start.15 = (f32[256,128]{1,0:T(8,128)S(1)}, f32[256,128]{1,0:T(8,128)S(1)}, u32[]{:S(2)}, u32[]{:S(2)}) collective-permute-start(f32[256,128]{1,0:T(8,128)S(1)} %get-tuple-element.39), channel_id=1, source_target_pairs={{0,2},{1,3},{2,0},{3,1},{4,6},{5,7},{6,4},{7,5},{8,10},{9,11},{10,... | collective-permute-start | bytes 393224 | tf_op jit(solution)/shard_map/reduce/ppermute | solution.py:227

commit v9 on v8

--- a/solution.py
+++ b/solution.py
@@ -285,12 +285,14 @@
 
     def gathered(after):
         passed = call(pass_kernel, block, [crossed], after=after)
-        early = call(copy_kernel, blocks(half + 1), [near[at] for at in range(half)] + [passed], after=passed)
         late, mask = {0: passed}, half // 2
         while mask:
             late.update({at | mask: swap(x, "col", 2 * mask) for at, x in late.items()})
             mask //= 2
-        return early, [late[at] for at in range(1, half)]
+        return passed, [late[at] for at in range(1, half)]
+
+    def stacked(passed, after):
+        return call(copy_kernel, blocks(half + 1), [near[at] for at in range(half)] + [passed], after=after)
 
     def chip_sums(kept, sent, after=None):
         return call(
@@ -331,15 +333,17 @@
                 scratch=[pltpu.VMEM(values.shape, F32), pltpu.SemaphoreType.DMA((groups,))],
             )
         with jax.named_scope("gather"):
-            early, late = gathered(high)
-            other_early = swap(early, "col", 1)
+            passed, late = gathered(high)
         with jax.named_scope("flip"):
             flipped = call(
                 functools.partial(flip_kernel, tile),
                 jax.ShapeDtypeStruct((2 * width, n_rows), BF16),
                 grads,
-                after=early,
+                after=passed,
             )
+        with jax.named_scope("gather"):
+            early = stacked(passed, flipped)
+            other_early = swap(early, "col", 1)
 
         def backward_part(distances, core, after):
             shards = [shard_at(distance, core) for distance in distances]
@@ -371,15 +375,15 @@
 
         with jax.named_scope("backward"):
             far, close = range(half, pairs), range(half)
-            far_sent = backward_part(far, 1, plan)
+            far_sent = backward_part(far, 1, early)
             far_kept = backward_part(far, 0, far_sent)
+            sent = backward_part(close, 1, far_kept)
         with jax.named_scope("gather"):
-            late = call(copy_kernel, blocks(half - 1), late, after=far_kept, flops=2 * 10**9)
+            late = call(copy_kernel, blocks(half - 1), late, after=sent, flops=2 * 10**9)
             other_late = swap(late, "col", 1)
         with jax.named_scope("backward"):
             far_sums = chip_sums(far_kept, far_sent, late)
-            sent = backward_part(close, 1, far_sums[0])
-            kept = backward_part(close, 0, sent)
+            kept = backward_part(close, 0, far_sums[0])
         with jax.named_scope("forward"):
             forwards = forward_part([early, other_early], 0, after=kept)
         with jax.named_scope("reduce"):
@@ -392,7 +396,8 @@
     else:
         group = 8
         with jax.named_scope("gather"):
-            early, late = gathered(plan)
+            passed, late = gathered(plan)
+            early = stacked(passed, plan)
             late = call(copy_kernel, blocks(half - 1), late)
             panel = jnp.concatenate([early, swap(early, "col", 1), late, swap(late, "col", 1)])
         with jax.named_scope("slots"):
@@ -431,8 +436,7 @@
         row_parts = [forwards[0]] + [swap(forwards[k], "row", k) for k in range(1, n_row)]
 
     with jax.named_scope("finish"):
-        row_sum = call(sum_kernel, block, [row_parts[0], row_parts[-1]], after=mine)
-        row_sum = call(sum_kernel, block, [row_sum, *row_parts[1:-1]])
+        row_sum = call(sum_kernel, block, row_parts, after=mine)
         return call(
             finish_kernel, (block, block), (row_sum, row_factor, col_factor, mine, *grad_parts), mebibytes=4
         )

time: 37.5 us -> 36.9 us (0.984); the launches traced: 37.8 us -> 36.8 us
  starting transfers between devices: 18.8 us -> 17.2 us
  waiting for transfers between devices: 6.95 us -> 7.62 us
    ppermute x16, starting transfers between devices: 18.8 us -> 17.2 us  [swap(): lax.ppermute(x, axis, [(at, at ^ mask) for at in range(lax.axis_size(axis...]
    ppermute x16, waiting for transfers between devices: 6.95 us -> 7.62 us  [swap(): lax.ppermute(x, axis, [(at, at ^ mask) for at in range(lax.axis_size(axis...]
    pallas_call x19 -> x18, Pallas kernels: 10.5 us -> 10.5 us  [call(): pl.pallas_call(body, out_shape=out_shape, in_specs=specs, out_specs=tuple...]
  transfers between devices with their start and end apart: 16 -> 16, of which waited for: 5 -> 6; matrix products, arithmetic and copies ran while one was open for 0% -> 0% of each run, Pallas kernels for 23% -> 23%
where the time goes in v9:
time: 36.9 us; the launch traced here: 36.8 us
  starting transfers between devices  17.2 us (47%)
  Pallas kernels  10.5 us (28%)
  waiting for transfers between devices  7.62 us (21%)
  between operations  1.45 us (4%)
    ppermute x16, starting transfers between devices, swap(): lax.ppermute(x, axis, [(at, at ^ mask) for at in range(lax.axis_size(axis...  17.2 us
    pallas_call x18, Pallas kernels, call(): pl.pallas_call(body, out_shape=out_shape, in_specs=specs, out_specs=tuple...  10.5 us
    ppermute x16, waiting for transfers between devices, swap(): lax.ppermute(x, axis, [(at, at ^ mask) for at in range(lax.axis_size(axis...  7.62 us
  transfers between devices with their start and end apart: 16, of which 6 were waited for; matrix products, arithmetic and copies ran while one was open for 0% of the time, Pallas kernels for 23%

profile of v9, /device:TPU:0, one launch (start us, length us, event | category | flops | bytes accessed | tf_op | source)
XLA Modules:
  0.0 36.8 jit_solution(13976456299861484643)
XLA Ops:
  0.6 1.2 %scale.1 = (f32[256,128]{1,0:T(8,128)S(1)}, f32[256,128]{1,0:T(8,128)S(1)}, f32[256,128]{1,0:T(8,128)S(1)}, f32[256,128]{1,0:T(8,128)S(1)}, s32[2,128]{1,0:T(2,128)S(1)}) custom-call(f32[256,128]{1,0:T(8,128)} %refs_0_.1, f32[256,128]{1,0:T(8,128)} %refs_1_.1, s32[2,128]{1,0:T(2,128)} %bitcast.4, s32[2,128]{1,0:T(2,128)} %bitcast.5, s32[2,1,1,128]{3,2,1,0:T(1,128)} %refs_4_.1), custom_call_target="tpu_custom_call" | custom-call | bytes 1024 | tf_op jit(solution)/shard_map/scale/pallas_call | solution.py:240
  1.8 4.1 %collective-permute-start = (f32[256,128]{1,0:T(8,128)S(1)}, f32[256,128]{1,0:T(8,128)S(1)}, u32[]{:S(2)}, u32[]{:S(2)}) collective-permute-start(f32[256,128]{1,0:T(8,128)S(1)} %get-tuple-element.23.refs_0_), channel_id=1, source_target_pairs={{0,4},{1,5},{2,6},{3,7},{4,0},{5,1},{6,2},{7,3},{8,12},{9,13},{10,... | collective-permute-start | bytes 393224 | tf_op jit(solution)/shard_map/gather/ppermute | solution.py:227
  5.9 1.5 %collective-permute-start.1 = (f32[256,128]{1,0:T(8,128)S(1)}, f32[256,128]{1,0:T(8,128)S(1)}, u32[]{:S(2)}, u32[]{:S(2)}) collective-permute-start(f32[256,128]{1,0:T(8,128)S(1)} %get-tuple-element.24.refs_0_), channel_id=1, source_target_pairs={{0,8},{8,0},{16,24},{24,16},{1,9},{9,1},{17,25},{25,17},{2,10},{10... | collective-permute-start | bytes 393224 | tf_op jit(solution)/shard_map/gather/ppermute | solution.py:227
  7.4 1.5 %collective-permute-start.2 = (f32[256,128]{1,0:T(8,128)S(1)}, f32[256,128]{1,0:T(8,128)S(1)}, u32[]{:S(2)}, u32[]{:S(2)}) collective-permute-start(f32[256,128]{1,0:T(8,128)S(1)} %get-tuple-element.24.refs_0_), channel_id=1, source_target_pairs={{0,16},{8,24},{16,0},{24,8},{1,17},{9,25},{17,1},{25,9},{2,18},{10... | collective-permute-start | bytes 393224 | tf_op jit(solution)/shard_map/gather/ppermute | solution.py:227
  8.9 0.5 %collective-permute-start.3 = (f32[256,128]{1,0:T(8,128)S(1)}, f32[256,128]{1,0:T(8,128)S(1)}, u32[]{:S(2)}, u32[]{:S(2)}) collective-permute-start(f32[256,128]{1,0:T(8,128)S(1)} %get-tuple-element.24.refs_0_), channel_id=1, source_target_pairs={{0,24},{8,16},{16,8},{24,0},{1,25},{9,17},{17,9},{25,1},{2,26},{10... | collective-permute-start | bytes 393224 | tf_op jit(solution)/shard_map/gather/ppermute | solution.py:227
  9.4 1.6 %collective-permute-start.4 = (f32[256,128]{1,0:T(8,128)S(1)}, f32[256,128]{1,0:T(8,128)S(1)}, u32[]{:S(2)}, u32[]{:S(2)}) collective-permute-start(f32[256,128]{1,0:T(8,128)S(1)} %get-tuple-element.23.refs_0_), channel_id=1, source_target_pairs={{0,2},{1,3},{2,0},{3,1},{4,6},{5,7},{6,4},{7,5},{8,10},{9,11},{10,... | collective-permute-start | bytes 393224 | tf_op jit(solution)/shard_map/gather/ppermute | solution.py:227
  11.6 2.9 %split.1 = (bf16[1024,2048]{1,0:T(8,128)(2,1)S(1)}, bf16[1024,2048]{1,0:T(8,128)(2,1)S(1)}) custom-call(s32[2,128]{1,0:T(2,128)S(1)} %get-tuple-element.21.plan_ref, s32[1,1]{1,0:T(1,128)S(6)} %copy.9.count_ref, f32[128,128,128]{2,1,0:T(8,128)} %bitcast.3), custom_call_target="tpu_custom_call" | custom-call | bytes 1024 | tf_op jit(solution)/shard_map/split/pallas_call | solution.py:240
  14.6 0.0 collective-permute-done.refs_0_
  14.6 0.5 %collective-permute-start.5 = (f32[256,128]{1,0:T(8,128)S(1)}, f32[256,128]{1,0:T(8,128)S(1)}, u32[]{:S(2)}, u32[]{:S(2)}) collective-permute-start(f32[256,128]{1,0:T(8,128)S(1)} %gather.3._.refs_2_), channel_id=1, source_target_pairs={{0,2},{1,3},{2,0},{3,1},{4,6},{5,7},{6,4},{7,5},{8,10},{9,11},{10,... | collective-permute-start | bytes 393224 | tf_op jit(solution)/shard_map/gather/ppermute | solution.py:227
  15.1 0.0 collective-permute-done.1.refs_1_
  15.1 0.1 collective-permute-done.2.refs_2_
  15.2 0.0 collective-permute-done.3.refs_3_
  15.2 0.2 flip.1._.refs_0_
  15.4 0.0 collective-permute-done.4.refs_1_
  15.4 0.7 %backward.5._ = f32[2,256,128]{2,1,0:T(8,128)S(1)} custom-call(f32[3,256,128]{2,1,0:T(8,128)S(1)} %gather.4._.refs_0_, bf16[256,1024]{1,0:T(8,128)(2,1)S(1)} %flip.1._.refs_0_, bf16[1024,2048]{1,0:T(8,128)(2,1)S(1)} %get-tuple-element.22._.refs_1_.refs_2_, bf16[1024,2048]{1,0:T(8,128)(2,1)S(1)} %get-tuple-element.25.refs_2_.refs_3_), custom_call_target="tpu_custom_call" | custom-call | bytes 1024 | tf_op jit(solution)/shard_map/backward/pallas_call | solution.py:240
  16.1 0.1 collective-permute-start.6
  16.2 0.5 %collective-permute-start.7 = (f32[3,256,128]{2,1,0:T(8,128)S(1)}, f32[3,256,128]{2,1,0:T(8,128)S(1)}, u32[]{:S(2)}, u32[]{:S(2)}) collective-permute-start(f32[3,256,128]{2,1,0:T(8,128)S(1)} %gather.4._.refs_0_), channel_id=1, source_target_pairs={{0,1},{1,0},{2,3},{3,2},{4,5},{5,4},{6,7},{7,6},{8,9},{9,8},{10,11... | collective-permute-start | bytes 1179656 | tf_op jit(solution)/shard_map/gather/ppermute | solution.py:227
  16.7 0.7 %backward.6._.refs_0_ = f32[2,256,128]{2,1,0:T(8,128)S(1)} custom-call(f32[2,256,128]{2,1,0:T(8,128)S(1)} %backward.5._, bf16[256,1024]{1,0:T(8,128)(2,1)S(1)} %flip.1._.refs_0_, bf16[1024,2048]{1,0:T(8,128)(2,1)S(1)} %get-tuple-element.22._.refs_1_.refs_2_, bf16[1024,2048]{1,0:T(8,128)(2,1)S(1)} %get-tuple-element.25.refs_2_.refs_3_), custom_call_target="tpu_custom_call" | custom-call | bytes 1024 | tf_op jit(solution)/shard_map/backward/pallas_call | solution.py:240
  17.4 0.7 %backward.7._ = f32[2,256,128]{2,1,0:T(8,128)S(1)} custom-call(f32[2,256,128]{2,1,0:T(8,128)S(1)} %backward.6._.refs_0_, bf16[256,1024]{1,0:T(8,128)(2,1)S(1)} %flip.1._.refs_0_, bf16[1024,2048]{1,0:T(8,128)(2,1)S(1)} %get-tuple-element.22._.refs_1_.refs_2_, bf16[1024,2048]{1,0:T(8,128)(2,1)S(1)} %get-tuple-element.25.refs_2_.refs_3_), custom_call_target="tpu_custom_call" | custom-call | bytes 1024 | tf_op jit(solution)/shard_map/backward/pallas_call | solution.py:240
  18.1 1.5 %collective-permute-done.5.refs_0_ = f32[256,128]{1,0:T(8,128)S(1)} collective-permute-done((f32[256,128]{1,0:T(8,128)S(1)}, f32[256,128]{1,0:T(8,128)S(1)}, u32[]{:S(2)}, u32[]{:S(2)}) %collective-permute-start.5) | collective-permute-done | bytes 131104 | tf_op jit(solution)/shard_map/gather/ppermute | solution.py:227
  19.6 0.0 collective-permute-done.6.refs_1_
  19.7 0.5 %collective-permute-start.8 = (f32[256,128]{1,0:T(8,128)S(1)}, f32[256,128]{1,0:T(8,128)S(1)}, u32[]{:S(2)}, u32[]{:S(2)}) collective-permute-start(f32[256,128]{1,0:T(8,128)S(1)} %get-tuple-element.28), channel_id=1, source_target_pairs={{0,2},{1,3},{2,0},{3,1},{4,6},{5,7},{6,4},{7,5},{8,10},{9,11},{10,... | collective-permute-start | bytes 393224 | tf_op jit(solution)/shard_map/reduce/ppermute | solution.py:227
  20.2 0.0 collective-permute-start.9
  20.2 0.5 %collective-permute-start.10 = (f32[2,256,128]{2,1,0:T(8,128)S(1)}, f32[2,256,128]{2,1,0:T(8,128)S(1)}, u32[]{:S(2)}, u32[]{:S(2)}) collective-permute-start(f32[2,256,128]{2,1,0:T(8,128)S(1)} %backward.7._), channel_id=1, source_target_pairs={{0,1},{1,0},{2,3},{3,2},{4,5},{5,4},{6,7},{7,6},{8,9},{9,8},{10,11... | collective-permute-start | bytes 786440 | tf_op jit(solution)/shard_map/reduce/ppermute | solution.py:227
  20.7 0.7 %backward.9._.refs_0_ = f32[2,256,128]{2,1,0:T(8,128)S(1)} custom-call(f32[256,128]{1,0:T(8,128)S(1)} %get-tuple-element.26._.refs_0_, bf16[256,1024]{1,0:T(8,128)(2,1)S(1)} %flip.1._.refs_0_, bf16[1024,2048]{1,0:T(8,128)(2,1)S(1)} %get-tuple-element.22._.refs_1_.refs_2_, bf16[1024,2048]{1,0:T(8,128)(2,1)S(1)} %get-tuple-element.25.refs_2_.refs_3_), custom_call_target="tpu_custom_call" | custom-call | bytes 1024 | tf_op jit(solution)/shard_map/backward/pallas_call | solution.py:240
  21.4 0.0 collective-permute-done.7.refs_1_
  21.4 1.9 %forward.2 = (f32[256,128]{1,0:T(8,128)S(1)}, f32[256,128]{1,0:T(8,128)S(1)}, f32[256,128]{1,0:T(8,128)S(1)}, f32[256,128]{1,0:T(8,128)S(1)}) custom-call(f32[2,256,128]{2,1,0:T(8,128)S(1)} %backward.9._.refs_0_, f32[3,256,128]{2,1,0:T(8,128)S(1)} %gather.4._.refs_0_, f32[3,256,128]{2,1,0:T(8,128)S(1)} %collective-permute-done.7.refs_1_, ...), custom_call_target="tpu_custom_call" | custom-call | bytes 1024 | tf_op jit(solution)/shard_map/forward/pallas_call | solution.py:240
  23.3 1.5 %collective-permute-done.8.refs_1_ = f32[256,128]{1,0:T(8,128)S(1)} collective-permute-done((f32[256,128]{1,0:T(8,128)S(1)}, f32[256,128]{1,0:T(8,128)S(1)}, u32[]{:S(2)}, u32[]{:S(2)}) %collective-permute-start.8) | collective-permute-done | bytes 131104 | tf_op jit(solution)/shard_map/reduce/ppermute | solution.py:227
  24.7 0.5 %collective-permute-start.11 = (f32[256,128]{1,0:T(8,128)S(1)}, f32[256,128]{1,0:T(8,128)S(1)}, u32[]{:S(2)}, u32[]{:S(2)}) collective-permute-start(f32[256,128]{1,0:T(8,128)S(1)} %reduce.3._), channel_id=1, source_target_pairs={{0,4},{1,5},{2,6},{3,7},{4,0},{5,1},{6,2},{7,3},{8,12},{9,13},{10,... | collective-permute-start | bytes 393224 | tf_op jit(solution)/shard_map/reduce/ppermute | solution.py:227
  25.3 0.0 collective-permute-done.9.refs_1_
  25.3 0.7 %forward.3 = (f32[256,128]{1,0:T(8,128)S(1)}, f32[256,128]{1,0:T(8,128)S(1)}, f32[256,128]{1,0:T(8,128)S(1)}, f32[256,128]{1,0:T(8,128)S(1)}) custom-call(f32[256,128]{1,0:T(8,128)S(1)} %reduce.3._, f32[1,256,128]{2,1,0:T(8,128)S(1)} %gather.5._.refs_0_, f32[1,256,128]{2,1,0:T(8,128)S(1)} %collective-permute-done.9.refs_1_, ...), custom_call_target="tpu_custom_call" | custom-call | flops 2000000000 | bytes 1024 | tf_op jit(solution)/shard_map/forward/pallas_call | solution.py:240
  26.0 1.6 %collective-permute-start.12 = (f32[256,128]{1,0:T(8,128)S(1)}, f32[256,128]{1,0:T(8,128)S(1)}, u32[]{:S(2)}, u32[]{:S(2)}) collective-permute-start(f32[256,128]{1,0:T(8,128)S(1)} %get-tuple-element.34), channel_id=1, source_target_pairs={{0,8},{8,0},{16,24},{24,16},{1,9},{9,1},{17,25},{25,17},{2,10},{10... | collective-permute-start | bytes 393224 | tf_op jit(solution)/shard_map/reduce/ppermute | solution.py:227
  27.6 2.5 %collective-permute-start.13 = (f32[256,128]{1,0:T(8,128)S(1)}, f32[256,128]{1,0:T(8,128)S(1)}, u32[]{:S(2)}, u32[]{:S(2)}) collective-permute-start(f32[256,128]{1,0:T(8,128)S(1)} %get-tuple-element.35), channel_id=1, source_target_pairs={{0,16},{8,24},{16,0},{24,8},{1,17},{9,25},{17,1},{25,9},{2,18},{10... | collective-permute-start | bytes 393224 | tf_op jit(solution)/shard_map/reduce/ppermute | solution.py:227
  30.1 0.0 collective-permute-start.14
  30.1 0.0 collective-permute-done.10.refs_1_
  30.2 1.3 %collective-permute-start.15 = (f32[256,128]{1,0:T(8,128)S(1)}, f32[256,128]{1,0:T(8,128)S(1)}, u32[]{:S(2)}, u32[]{:S(2)}) collective-permute-start(f32[256,128]{1,0:T(8,128)S(1)} %get-tuple-element.39), channel_id=1, source_target_pairs={{0,2},{1,3},{2,0},{3,1},{4,6},{5,7},{6,4},{7,5},{8,10},{9,11},{10,... | collective-permute-start | bytes 393224 | tf_op jit(solution)/shard_map/reduce/ppermute | solution.py:227
  31.4 1.2 %collective-permute-done.11.y_ref = f32[256,128]{1,0:T(8,128)S(1)} collective-permute-done((f32[256,128]{1,0:T(8,128)S(1)}, f32[256,128]{1,0:T(8,128)S(1)}, u32[]{:S(2)}, u32[]{:S(2)}) %collective-permute-start.11) | collective-permute-done | bytes 131104 | tf_op jit(solution)/shard_map/reduce/ppermute | solution.py:227
  32.6 0.0 collective-permute-done.12.refs_1_
  32.6 1.8 %collective-permute-done.13.refs_2_ = f32[256,128]{1,0:T(8,128)S(1)} collective-permute-done((f32[256,128]{1,0:T(8,128)S(1)}, f32[256,128]{1,0:T(8,128)S(1)}, u32[]{:S(2)}, u32[]{:S(2)}) %collective-permute-start.13) | collective-permute-done | bytes 131104 | tf_op jit(solution)/shard_map/reduce/ppermute | solution.py:227
  34.4 1.5 %collective-permute-done.14.refs_3_ = f32[256,128]{1,0:T(8,128)S(1)} collective-permute-done((f32[256,128]{1,0:T(8,128)S(1)}, f32[256,128]{1,0:T(8,128)S(1)}, u32[]{:S(2)}, u32[]{:S(2)}) %collective-permute-start.14) | collective-permute-done | bytes 131104 | tf_op jit(solution)/shard_map/reduce/ppermute | solution.py:227
  36.0 0.0 collective-permute-done.15.refs_1_
  36.0 0.7 %finish.3 = (f32[256,128]{1,0:T(8,128)}, f32[256,128]{1,0:T(8,128)}) custom-call(f32[256,128]{1,0:T(8,128)S(1)} %finish.2.row_ref, f32[256,128]{1,0:T(8,128)S(1)} %get-tuple-element.37.row_factor_ref, f32[256,128]{1,0:T(8,128)S(1)} %get-tuple-element.38.col_factor_ref, f32[256,128]{1,0:T(8,128)S(1)} %reduce.5._.refs_0_, ...), custom_call_target="tpu_custom_call" | custom-call | bytes 1024 | tf_op jit(solution)/shard_map/finish/pallas_call | solution.py:240
  (8 shorter events, 0.2 us)
Async XLA Ops:
  1.8 12.8 %collective-permute-start = (f32[256,128]{1,0:T(8,128)S(1)}, f32[256,128]{1,0:T(8,128)S(1)}, u32[]{:S(2)}, u32[]{:S(2)}) collective-permute-start(f32[256,128]{1,0:T(8,128)S(1)} %get-tuple-element.23.refs_0_), channel_id=1, source_target_pairs={{0,4},{1,5},{2,6},{3,7},{4,0},{5,1},{6,2},{7,3},{8,12},{9,13},{10,... | collective-permute-start | bytes 393224 | tf_op jit(solution)/shard_map/gather/ppermute | solution.py:227
  5.9 9.2 %collective-permute-start.1 = (f32[256,128]{1,0:T(8,128)S(1)}, f32[256,128]{1,0:T(8,128)S(1)}, u32[]{:S(2)}, u32[]{:S(2)}) collective-permute-start(f32[256,128]{1,0:T(8,128)S(1)} %get-tuple-element.24.refs_0_), channel_id=1, source_target_pairs={{0,8},{8,0},{16,24},{24,16},{1,9},{9,1},{17,25},{25,17},{2,10},{10... | collective-permute-start | bytes 393224 | tf_op jit(solution)/shard_map/gather/ppermute | solution.py:227
  7.4 7.8 %collective-permute-start.2 = (f32[256,128]{1,0:T(8,128)S(1)}, f32[256,128]{1,0:T(8,128)S(1)}, u32[]{:S(2)}, u32[]{:S(2)}) collective-permute-start(f32[256,128]{1,0:T(8,128)S(1)} %get-tuple-element.24.refs_0_), channel_id=1, source_target_pairs={{0,16},{8,24},{16,0},{24,8},{1,17},{9,25},{17,1},{25,9},{2,18},{10... | collective-permute-start | bytes 393224 | tf_op jit(solution)/shard_map/gather/ppermute | solution.py:227
  8.9 6.3 %collective-permute-start.3 = (f32[256,128]{1,0:T(8,128)S(1)}, f32[256,128]{1,0:T(8,128)S(1)}, u32[]{:S(2)}, u32[]{:S(2)}) collective-permute-start(f32[256,128]{1,0:T(8,128)S(1)} %get-tuple-element.24.refs_0_), channel_id=1, source_target_pairs={{0,24},{8,16},{16,8},{24,0},{1,25},{9,17},{17,9},{25,1},{2,26},{10... | collective-permute-start | bytes 393224 | tf_op jit(solution)/shard_map/gather/ppermute | solution.py:227
  9.4 6.0 %collective-permute-start.4 = (f32[256,128]{1,0:T(8,128)S(1)}, f32[256,128]{1,0:T(8,128)S(1)}, u32[]{:S(2)}, u32[]{:S(2)}) collective-permute-start(f32[256,128]{1,0:T(8,128)S(1)} %get-tuple-element.23.refs_0_), channel_id=1, source_target_pairs={{0,2},{1,3},{2,0},{3,1},{4,6},{5,7},{6,4},{7,5},{8,10},{9,11},{10,... | collective-permute-start | bytes 393224 | tf_op jit(solution)/shard_map/gather/ppermute | solution.py:227
  14.6 5.0 %collective-permute-start.5 = (f32[256,128]{1,0:T(8,128)S(1)}, f32[256,128]{1,0:T(8,128)S(1)}, u32[]{:S(2)}, u32[]{:S(2)}) collective-permute-start(f32[256,128]{1,0:T(8,128)S(1)} %gather.3._.refs_2_), channel_id=1, source_target_pairs={{0,2},{1,3},{2,0},{3,1},{4,6},{5,7},{6,4},{7,5},{8,10},{9,11},{10,... | collective-permute-start | bytes 393224 | tf_op jit(solution)/shard_map/gather/ppermute | solution.py:227
  16.1 3.5 %collective-permute-start.6 = (f32[2,256,128]{2,1,0:T(8,128)S(1)}, f32[2,256,128]{2,1,0:T(8,128)S(1)}, u32[]{:S(2)}, u32[]{:S(2)}) collective-permute-start(f32[2,256,128]{2,1,0:T(8,128)S(1)} %backward.5._), channel_id=1, source_target_pairs={{0,1},{1,0},{2,3},{3,2},{4,5},{5,4},{6,7},{7,6},{8,9},{9,8},{10,11... | collective-permute-start | bytes 786440 | tf_op jit(solution)/shard_map/backward/ppermute | solution.py:227
  16.2 5.2 %collective-permute-start.7 = (f32[3,256,128]{2,1,0:T(8,128)S(1)}, f32[3,256,128]{2,1,0:T(8,128)S(1)}, u32[]{:S(2)}, u32[]{:S(2)}) collective-permute-start(f32[3,256,128]{2,1,0:T(8,128)S(1)} %gather.4._.refs_0_), channel_id=1, source_target_pairs={{0,1},{1,0},{2,3},{3,2},{4,5},{5,4},{6,7},{7,6},{8,9},{9,8},{10,11... | collective-permute-start | bytes 1179656 | tf_op jit(solution)/shard_map/gather/ppermute | solution.py:227
  19.7 5.0 %collective-permute-start.8 = (f32[256,128]{1,0:T(8,128)S(1)}, f32[256,128]{1,0:T(8,128)S(1)}, u32[]{:S(2)}, u32[]{:S(2)}) collective-permute-start(f32[256,128]{1,0:T(8,128)S(1)} %get-tuple-element.28), channel_id=1, source_target_pairs={{0,2},{1,3},{2,0},{3,1},{4,6},{5,7},{6,4},{7,5},{8,10},{9,11},{10,... | collective-permute-start | bytes 393224 | tf_op jit(solution)/shard_map/reduce/ppermute | solution.py:227
  20.2 5.1 %collective-permute-start.9 = (f32[1,256,128]{2,1,0:T(8,128)S(1)}, f32[1,256,128]{2,1,0:T(8,128)S(1)}, u32[]{:S(2)}, u32[]{:S(2)}) collective-permute-start(f32[1,256,128]{2,1,0:T(8,128)S(1)} %gather.5._.refs_0_), channel_id=1, source_target_pairs={{0,1},{1,0},{2,3},{3,2},{4,5},{5,4},{6,7},{7,6},{8,9},{9,8},{10,11... | collective-permute-start | bytes 393224 | tf_op jit(solution)/shard_map/gather/ppermute | solution.py:227
  20.2 9.9 %collective-permute-start.10 = (f32[2,256,128]{2,1,0:T(8,128)S(1)}, f32[2,256,128]{2,1,0:T(8,128)S(1)}, u32[]{:S(2)}, u32[]{:S(2)}) collective-permute-start(f32[2,256,128]{2,1,0:T(8,128)S(1)} %backward.7._), channel_id=1, source_target_pairs={{0,1},{1,0},{2,3},{3,2},{4,5},{5,4},{6,7},{7,6},{8,9},{9,8},{10,11... | collective-permute-start | bytes 786440 | tf_op jit(solution)/shard_map/reduce/ppermute | solution.py:227
  24.7 7.8 %collective-permute-start.11 = (f32[256,128]{1,0:T(8,128)S(1)}, f32[256,128]{1,0:T(8,128)S(1)}, u32[]{:S(2)}, u32[]{:S(2)}) collective-permute-start(f32[256,128]{1,0:T(8,128)S(1)} %reduce.3._), channel_id=1, source_target_pairs={{0,4},{1,5},{2,6},{3,7},{4,0},{5,1},{6,2},{7,3},{8,12},{9,13},{10,... | collective-permute-start | bytes 393224 | tf_op jit(solution)/shard_map/reduce/ppermute | solution.py:227
  26.0 6.6 %collective-permute-start.12 = (f32[256,128]{1,0:T(8,128)S(1)}, f32[256,128]{1,0:T(8,128)S(1)}, u32[]{:S(2)}, u32[]{:S(2)}) collective-permute-start(f32[256,128]{1,0:T(8,128)S(1)} %get-tuple-element.34), channel_id=1, source_target_pairs={{0,8},{8,0},{16,24},{24,16},{1,9},{9,1},{17,25},{25,17},{2,10},{10... | collective-permute-start | bytes 393224 | tf_op jit(solution)/shard_map/reduce/ppermute | solution.py:227
  27.6 6.8 %collective-permute-start.13 = (f32[256,128]{1,0:T(8,128)S(1)}, f32[256,128]{1,0:T(8,128)S(1)}, u32[]{:S(2)}, u32[]{:S(2)}) collective-permute-start(f32[256,128]{1,0:T(8,128)S(1)} %get-tuple-element.35), channel_id=1, source_target_pairs={{0,16},{8,24},{16,0},{24,8},{1,17},{9,25},{17,1},{25,9},{2,18},{10... | collective-permute-start | bytes 393224 | tf_op jit(solution)/shard_map/reduce/ppermute | solution.py:227
  30.1 5.9 %collective-permute-start.14 = (f32[256,128]{1,0:T(8,128)S(1)}, f32[256,128]{1,0:T(8,128)S(1)}, u32[]{:S(2)}, u32[]{:S(2)}) collective-permute-start(f32[256,128]{1,0:T(8,128)S(1)} %get-tuple-element.36), channel_id=1, source_target_pairs={{0,24},{8,16},{16,8},{24,0},{1,25},{9,17},{17,9},{25,1},{2,26},{10... | collective-permute-start | bytes 393224 | tf_op jit(solution)/shard_map/reduce/ppermute | solution.py:227
  30.2 5.9 %collective-permute-start.15 = (f32[256,128]{1,0:T(8,128)S(1)}, f32[256,128]{1,0:T(8,128)S(1)}, u32[]{:S(2)}, u32[]{:S(2)}) collective-permute-start(f32[256,128]{1,0:T(8,128)S(1)} %get-tuple-element.39), channel_id=1, source_target_pairs={{0,2},{1,3},{2,0},{3,1},{4,6},{5,7},{6,4},{7,5},{8,10},{9,11},{10,... | collective-permute-start | bytes 393224 | tf_op jit(solution)/shard_map/reduce/ppermute | solution.py:227

commit v10 on v9

--- a/solution.py
+++ b/solution.py
@@ -177,9 +177,8 @@
             out_ref[at, pl.ds(row, tile), :] = total[:, row : row + tile].T
 
 
-def forward_kernel(first, count, bands, *refs):
-    embed_refs, (high_ref, low_ref) = refs[:count], refs[count : count + 2]
-    before_refs, out_refs, panel = refs[count + 2 : -1 - bands], refs[-1 - bands : -1], refs[-1]
+def forward_kernel(count, *refs):
+    embed_refs, (high_ref, low_ref), out_refs, panel = refs[:count], refs[count : count + 2], refs[count + 2 : -1], refs[-1]
     _, shard, width = embed_refs[0].shape
     done = 0
     for embeds_ref in embed_refs:
@@ -188,14 +187,10 @@
             panel[pl.ds(done, shard), :width] = high
             panel[pl.ds(done, shard), width:] = low
             done += shard
-    cols = pl.ds(first * shard, done)
     for at, out_ref in enumerate(out_refs):
         rows = pl.ds(at * shard, shard)
-        both = product(high_ref[rows, cols], panel[...])
-        total = both[:, :width] + both[:, width:] + product(low_ref[rows, cols], panel[:, :width])
-        if before_refs:
-            total = total + before_refs[at][...]
-        out_ref[...] = total
+        both = product(high_ref[rows, :], panel[...])
+        out_ref[...] = both[:, :width] + both[:, width:] + product(low_ref[rows, :], panel[:, :width])
 
 
 def slots_kernel(tiles, pairs, coords_ref, count_ref, values_ref, embed_ref, grad_ref, forward_ref, backward_ref):
@@ -314,10 +309,10 @@
             mask *= 2
         return [parts[0], *got]
 
-    def total(parts, after):
+    def total(parts, after, flops=0):
         out, *rest = parts
         for part in rest:
-            out = call(add_kernel, block, (out, part), after=after)
+            out = call(add_kernel, block, (out, part), after=after, flops=flops)
         return out
 
     if dense:
@@ -361,16 +356,14 @@
                 return core * count + distance
             return 2 * count + core * (pairs - count) + distance - count
 
-        def forward_part(embeds, first, before=(), after=None, flops=0):
-            count = sum(x.shape[0] for x in embeds)
+        def forward(embeds, after):
             return call(
-                functools.partial(forward_kernel, first, len(embeds), n_row),
+                functools.partial(forward_kernel, len(embeds)),
                 (block,) * n_row,
-                (*embeds, high, low, *before),
+                (*embeds, high, low),
                 mebibytes=24,
-                scratch=[pltpu.VMEM((count * shard, 2 * width), BF16)],
+                scratch=[pltpu.VMEM((n_cols, 2 * width), BF16)],
                 after=after,
-                flops=flops,
             )
 
         with jax.named_scope("backward"):
@@ -385,11 +378,9 @@
             far_sums = chip_sums(far_kept, far_sent, late)
             kept = backward_part(close, 0, far_sums[0])
         with jax.named_scope("forward"):
-            forwards = forward_part([early, other_early], 0, after=kept)
+            forwards = forward([early, other_early, late, other_late], kept)
         with jax.named_scope("reduce"):
-            crossing = total(halved(far_sums, forwards[0]), forwards[0])
-        with jax.named_scope("forward"):
-            forwards = forward_part([late, other_late], 2 * (half + 1), forwards, crossing, 2 * 10**9)
+            crossing = total(halved(far_sums, forwards[0]), forwards[0], 1 * 10**9)
         with jax.named_scope("reduce"):
             close_sums = chip_sums(kept, sent, forwards[0])
             after = None

time: 36.9 us -> 37.6 us (1.019)
  starting transfers between devices: 17.2 us -> 19.8 us
  waiting for transfers between devices: 7.62 us -> 5.88 us
    ppermute x16, starting transfers between devices: 17.2 us -> 19.8 us  [swap(): lax.ppermute(x, axis, [(at, at ^ mask) for at in range(lax.axis_size(axis...]
    ppermute x16, waiting for transfers between devices: 7.62 us -> 5.88 us  [swap(): lax.ppermute(x, axis, [(at, at ^ mask) for at in range(lax.axis_size(axis...]
    pallas_call x18 -> x17, Pallas kernels: 10.5 us -> 10.3 us  [call(): pl.pallas_call(body, out_shape=out_shape, in_specs=specs, out_specs=tuple...]
  transfers between devices with their start and end apart: 16 -> 16, of which waited for: 6 -> 3; matrix products, arithmetic and copies ran while one was open for 0% -> 0% of each run, Pallas kernels for 23% -> 22%
where the time goes in v10:
time: 37.6 us; the launch traced here: 37.5 us
  starting transfers between devices  19.8 us (53%)
  Pallas kernels  10.3 us (27%)
  waiting for transfers between devices  5.88 us (16%)
  between operations  1.46 us (4%)
    ppermute x16, starting transfers between devices, swap(): lax.ppermute(x, axis, [(at, at ^ mask) for at in range(lax.axis_size(axis...  19.8 us
    pallas_call x17, Pallas kernels, call(): pl.pallas_call(body, out_shape=out_shape, in_specs=specs, out_specs=tuple...  10.3 us
    ppermute x16, waiting for transfers between devices, swap(): lax.ppermute(x, axis, [(at, at ^ mask) for at in range(lax.axis_size(axis...  5.88 us
  transfers between devices with their start and end apart: 16, of which 3 were waited for; matrix products, arithmetic and copies ran while one was open for 0% of the time, Pallas kernels for 22%

profile of v10, /device:TPU:0, one launch (start us, length us, event | category | flops | bytes accessed | tf_op | source)
XLA Modules:
  0.0 37.5 jit_solution(13861811053087925552)
XLA Ops:
  0.6 1.2 %scale.1 = (f32[256,128]{1,0:T(8,128)S(1)}, f32[256,128]{1,0:T(8,128)S(1)}, f32[256,128]{1,0:T(8,128)S(1)}, f32[256,128]{1,0:T(8,128)S(1)}, s32[2,128]{1,0:T(2,128)S(1)}) custom-call(f32[256,128]{1,0:T(8,128)} %refs_0_.1, f32[256,128]{1,0:T(8,128)} %refs_1_.1, s32[2,128]{1,0:T(2,128)} %bitcast.4, s32[2,128]{1,0:T(2,128)} %bitcast.5, s32[2,1,1,128]{3,2,1,0:T(1,128)} %refs_4_.1), custom_call_target="tpu_custom_call" | custom-call | bytes 1024 | tf_op jit(solution)/shard_map/scale/pallas_call | solution.py:235
  1.8 4.1 %collective-permute-start = (f32[256,128]{1,0:T(8,128)S(1)}, f32[256,128]{1,0:T(8,128)S(1)}, u32[]{:S(2)}, u32[]{:S(2)}) collective-permute-start(f32[256,128]{1,0:T(8,128)S(1)} %get-tuple-element.19.refs_0_), channel_id=1, source_target_pairs={{0,4},{1,5},{2,6},{3,7},{4,0},{5,1},{6,2},{7,3},{8,12},{9,13},{10,... | collective-permute-start | bytes 393224 | tf_op jit(solution)/shard_map/gather/ppermute | solution.py:222
  5.9 2.4 %collective-permute-start.3 = (f32[256,128]{1,0:T(8,128)S(1)}, f32[256,128]{1,0:T(8,128)S(1)}, u32[]{:S(2)}, u32[]{:S(2)}) collective-permute-start(f32[256,128]{1,0:T(8,128)S(1)} %get-tuple-element.20.refs_0_), channel_id=1, source_target_pairs={{0,24},{8,16},{16,8},{24,0},{1,25},{9,17},{17,9},{25,1},{2,26},{10... | collective-permute-start | bytes 393224 | tf_op jit(solution)/shard_map/gather/ppermute | solution.py:222
  8.3 0.5 %collective-permute-start.2 = (f32[256,128]{1,0:T(8,128)S(1)}, f32[256,128]{1,0:T(8,128)S(1)}, u32[]{:S(2)}, u32[]{:S(2)}) collective-permute-start(f32[256,128]{1,0:T(8,128)S(1)} %get-tuple-element.20.refs_0_), channel_id=1, source_target_pairs={{0,16},{8,24},{16,0},{24,8},{1,17},{9,25},{17,1},{25,9},{2,18},{10... | collective-permute-start | bytes 393224 | tf_op jit(solution)/shard_map/gather/ppermute | solution.py:222
  8.9 0.5 %collective-permute-start.1 = (f32[256,128]{1,0:T(8,128)S(1)}, f32[256,128]{1,0:T(8,128)S(1)}, u32[]{:S(2)}, u32[]{:S(2)}) collective-permute-start(f32[256,128]{1,0:T(8,128)S(1)} %get-tuple-element.20.refs_0_), channel_id=1, source_target_pairs={{0,8},{8,0},{16,24},{24,16},{1,9},{9,1},{17,25},{25,17},{2,10},{10... | collective-permute-start | bytes 393224 | tf_op jit(solution)/shard_map/gather/ppermute | solution.py:222
  9.4 1.6 %collective-permute-start.4 = (f32[256,128]{1,0:T(8,128)S(1)}, f32[256,128]{1,0:T(8,128)S(1)}, u32[]{:S(2)}, u32[]{:S(2)}) collective-permute-start(f32[256,128]{1,0:T(8,128)S(1)} %get-tuple-element.19.refs_0_), channel_id=1, source_target_pairs={{0,2},{1,3},{2,0},{3,1},{4,6},{5,7},{6,4},{7,5},{8,10},{9,11},{10,... | collective-permute-start | bytes 393224 | tf_op jit(solution)/shard_map/gather/ppermute | solution.py:222
  11.6 2.9 %split.1 = (bf16[1024,2048]{1,0:T(8,128)(2,1)S(1)}, bf16[1024,2048]{1,0:T(8,128)(2,1)S(1)}) custom-call(s32[2,128]{1,0:T(2,128)S(1)} %get-tuple-element.17.plan_ref, s32[1,1]{1,0:T(1,128)S(6)} %copy.9.count_ref, f32[128,128,128]{2,1,0:T(8,128)} %bitcast.3), custom_call_target="tpu_custom_call" | custom-call | bytes 1024 | tf_op jit(solution)/shard_map/split/pallas_call | solution.py:235
  14.6 0.0 collective-permute-done.refs_0_
  14.6 1.7 %collective-permute-start.5 = (f32[256,128]{1,0:T(8,128)S(1)}, f32[256,128]{1,0:T(8,128)S(1)}, u32[]{:S(2)}, u32[]{:S(2)}) collective-permute-start(f32[256,128]{1,0:T(8,128)S(1)} %gather.3._.refs_2_), channel_id=1, source_target_pairs={{0,2},{1,3},{2,0},{3,1},{4,6},{5,7},{6,4},{7,5},{8,10},{9,11},{10,... | collective-permute-start | bytes 393224 | tf_op jit(solution)/shard_map/gather/ppermute | solution.py:222
  16.3 0.0 collective-permute-done.3.refs_3_
  16.3 0.0 collective-permute-done.2.refs_2_
  16.3 0.0 collective-permute-done.1.refs_1_
  16.3 0.2 flip.1._.refs_0_
  16.5 0.0 collective-permute-done.4.refs_1_
  16.6 0.1 collective-permute-start.7
  16.6 0.7 %backward.5._ = f32[2,256,128]{2,1,0:T(8,128)S(1)} custom-call(f32[3,256,128]{2,1,0:T(8,128)S(1)} %gather.4._.refs_0_, bf16[256,1024]{1,0:T(8,128)(2,1)S(1)} %flip.1._.refs_0_, bf16[1024,2048]{1,0:T(8,128)(2,1)S(1)} %get-tuple-element.18._.refs_1_.refs_4_, bf16[1024,2048]{1,0:T(8,128)(2,1)S(1)} %get-tuple-element.21.refs_2_.refs_5_), custom_call_target="tpu_custom_call" | custom-call | bytes 1024 | tf_op jit(solution)/shard_map/backward/pallas_call | solution.py:235
  17.3 0.6 %collective-permute-start.6 = (f32[2,256,128]{2,1,0:T(8,128)S(1)}, f32[2,256,128]{2,1,0:T(8,128)S(1)}, u32[]{:S(2)}, u32[]{:S(2)}) collective-permute-start(f32[2,256,128]{2,1,0:T(8,128)S(1)} %backward.5._), channel_id=1, source_target_pairs={{0,1},{1,0},{2,3},{3,2},{4,5},{5,4},{6,7},{7,6},{8,9},{9,8},{10,11... | collective-permute-start | bytes 786440 | tf_op jit(solution)/shard_map/backward/ppermute | solution.py:222
  17.9 0.7 %backward.6._.refs_0_ = f32[2,256,128]{2,1,0:T(8,128)S(1)} custom-call(f32[2,256,128]{2,1,0:T(8,128)S(1)} %backward.5._, bf16[256,1024]{1,0:T(8,128)(2,1)S(1)} %flip.1._.refs_0_, bf16[1024,2048]{1,0:T(8,128)(2,1)S(1)} %get-tuple-element.18._.refs_1_.refs_4_, bf16[1024,2048]{1,0:T(8,128)(2,1)S(1)} %get-tuple-element.21.refs_2_.refs_5_), custom_call_target="tpu_custom_call" | custom-call | bytes 1024 | tf_op jit(solution)/shard_map/backward/pallas_call | solution.py:235
  18.6 0.7 %backward.7._ = f32[2,256,128]{2,1,0:T(8,128)S(1)} custom-call(f32[2,256,128]{2,1,0:T(8,128)S(1)} %backward.6._.refs_0_, bf16[256,1024]{1,0:T(8,128)(2,1)S(1)} %flip.1._.refs_0_, bf16[1024,2048]{1,0:T(8,128)(2,1)S(1)} %get-tuple-element.18._.refs_1_.refs_4_, bf16[1024,2048]{1,0:T(8,128)(2,1)S(1)} %get-tuple-element.21.refs_2_.refs_5_), custom_call_target="tpu_custom_call" | custom-call | bytes 1024 | tf_op jit(solution)/shard_map/backward/pallas_call | solution.py:235
  19.3 0.1 collective-permute-start.9
  19.4 0.3 collective-permute-done.5.refs_0_
  19.6 0.3 collective-permute-start.8
  19.9 0.0 collective-permute-done.6.refs_1_
  20.0 1.5 %collective-permute-start.10 = (f32[256,128]{1,0:T(8,128)S(1)}, f32[256,128]{1,0:T(8,128)S(1)}, u32[]{:S(2)}, u32[]{:S(2)}) collective-permute-start(f32[256,128]{1,0:T(8,128)S(1)} %get-tuple-element.25), channel_id=1, source_target_pairs={{0,2},{1,3},{2,0},{3,1},{4,6},{5,7},{6,4},{7,5},{8,10},{9,11},{10,... | collective-permute-start | bytes 393224 | tf_op jit(solution)/shard_map/reduce/ppermute | solution.py:222
  21.5 0.7 %backward.9._.refs_0_ = f32[2,256,128]{2,1,0:T(8,128)S(1)} custom-call(f32[256,128]{1,0:T(8,128)S(1)} %get-tuple-element.22._.refs_0_, bf16[256,1024]{1,0:T(8,128)(2,1)S(1)} %flip.1._.refs_0_, bf16[1024,2048]{1,0:T(8,128)(2,1)S(1)} %get-tuple-element.18._.refs_1_.refs_4_, bf16[1024,2048]{1,0:T(8,128)(2,1)S(1)} %get-tuple-element.21.refs_2_.refs_5_), custom_call_target="tpu_custom_call" | custom-call | bytes 1024 | tf_op jit(solution)/shard_map/backward/pallas_call | solution.py:235
  22.2 0.0 collective-permute-done.8.refs_3_
  22.2 0.0 collective-permute-done.7.refs_1_
  22.2 2.4 %forward.1 = (f32[256,128]{1,0:T(8,128)S(1)}, f32[256,128]{1,0:T(8,128)S(1)}, f32[256,128]{1,0:T(8,128)S(1)}, f32[256,128]{1,0:T(8,128)S(1)}) custom-call(f32[2,256,128]{2,1,0:T(8,128)S(1)} %backward.9._.refs_0_, f32[3,256,128]{2,1,0:T(8,128)S(1)} %gather.4._.refs_0_, f32[3,256,128]{2,1,0:T(8,128)S(1)} %collective-permute-done.7.refs_1_, ...), custom_call_target="tpu_custom_call" | custom-call | bytes 1024 | tf_op jit(solution)/shard_map/forward/pallas_call | solution.py:235
  24.6 1.8 %collective-permute-start.12 = (f32[256,128]{1,0:T(8,128)S(1)}, f32[256,128]{1,0:T(8,128)S(1)}, u32[]{:S(2)}, u32[]{:S(2)}) collective-permute-start(f32[256,128]{1,0:T(8,128)S(1)} %get-tuple-element.26), channel_id=1, source_target_pairs={{0,8},{8,0},{16,24},{24,16},{1,9},{9,1},{17,25},{25,17},{2,10},{10... | collective-permute-start | bytes 393224 | tf_op jit(solution)/shard_map/reduce/ppermute | solution.py:222
  26.4 0.0 collective-permute-done.10.refs_1_
  26.4 0.4 %collective-permute-start.11 = (f32[256,128]{1,0:T(8,128)S(1)}, f32[256,128]{1,0:T(8,128)S(1)}, u32[]{:S(2)}, u32[]{:S(2)}) collective-permute-start(f32[256,128]{1,0:T(8,128)S(1)} %reduce.4), channel_id=1, source_target_pairs={{0,4},{1,5},{2,6},{3,7},{4,0},{5,1},{6,2},{7,3},{8,12},{9,13},{10,... | collective-permute-start | bytes 393224 | tf_op jit(solution)/shard_map/reduce/ppermute | solution.py:222
  26.8 1.5 %collective-permute-start.13 = (f32[256,128]{1,0:T(8,128)S(1)}, f32[256,128]{1,0:T(8,128)S(1)}, u32[]{:S(2)}, u32[]{:S(2)}) collective-permute-start(f32[256,128]{1,0:T(8,128)S(1)} %get-tuple-element.27), channel_id=1, source_target_pairs={{0,16},{8,24},{16,0},{24,8},{1,17},{9,25},{17,1},{25,9},{2,18},{10... | collective-permute-start | bytes 393224 | tf_op jit(solution)/shard_map/reduce/ppermute | solution.py:222
  28.3 1.8 %collective-permute-start.14 = (f32[256,128]{1,0:T(8,128)S(1)}, f32[256,128]{1,0:T(8,128)S(1)}, u32[]{:S(2)}, u32[]{:S(2)}) collective-permute-start(f32[256,128]{1,0:T(8,128)S(1)} %get-tuple-element.28), channel_id=1, source_target_pairs={{0,24},{8,16},{16,8},{24,0},{1,25},{9,17},{17,9},{25,1},{2,26},{10... | collective-permute-start | bytes 393224 | tf_op jit(solution)/shard_map/reduce/ppermute | solution.py:222
  30.1 0.0 collective-permute-done.9.refs_1_
  30.1 1.0 %collective-permute-start.15 = (f32[256,128]{1,0:T(8,128)S(1)}, f32[256,128]{1,0:T(8,128)S(1)}, u32[]{:S(2)}, u32[]{:S(2)}) collective-permute-start(f32[256,128]{1,0:T(8,128)S(1)} %get-tuple-element.31), channel_id=1, source_target_pairs={{0,2},{1,3},{2,0},{3,1},{4,6},{5,7},{6,4},{7,5},{8,10},{9,11},{10,... | collective-permute-start | bytes 393224 | tf_op jit(solution)/shard_map/reduce/ppermute | solution.py:222
  31.1 4.4 %collective-permute-done.11.y_ref = f32[256,128]{1,0:T(8,128)S(1)} collective-permute-done((f32[256,128]{1,0:T(8,128)S(1)}, f32[256,128]{1,0:T(8,128)S(1)}, u32[]{:S(2)}, u32[]{:S(2)}) %collective-permute-start.11) | collective-permute-done | bytes 131104 | tf_op jit(solution)/shard_map/reduce/ppermute | solution.py:222
  35.5 0.0 collective-permute-done.12.refs_1_
  35.5 0.0 collective-permute-done.13.refs_2_
  35.5 0.0 collective-permute-done.14.refs_3_
  35.5 1.2 %collective-permute-done.15.refs_1_ = f32[256,128]{1,0:T(8,128)S(1)} collective-permute-done((f32[256,128]{1,0:T(8,128)S(1)}, f32[256,128]{1,0:T(8,128)S(1)}, u32[]{:S(2)}, u32[]{:S(2)}) %collective-permute-start.15) | collective-permute-done | bytes 131104 | tf_op jit(solution)/shard_map/reduce/ppermute | solution.py:222
  36.8 0.7 %finish.3 = (f32[256,128]{1,0:T(8,128)}, f32[256,128]{1,0:T(8,128)}) custom-call(f32[256,128]{1,0:T(8,128)S(1)} %finish.2.row_ref, f32[256,128]{1,0:T(8,128)S(1)} %get-tuple-element.29.row_factor_ref, f32[256,128]{1,0:T(8,128)S(1)} %get-tuple-element.30.col_factor_ref, f32[256,128]{1,0:T(8,128)S(1)} %reduce.5._.refs_0_, ...), custom_call_target="tpu_custom_call" | custom-call | bytes 1024 | tf_op jit(solution)/shard_map/finish/pallas_call | solution.py:235
  (8 shorter events, 0.2 us)
Async XLA Ops:
  1.8 12.8 %collective-permute-start = (f32[256,128]{1,0:T(8,128)S(1)}, f32[256,128]{1,0:T(8,128)S(1)}, u32[]{:S(2)}, u32[]{:S(2)}) collective-permute-start(f32[256,128]{1,0:T(8,128)S(1)} %get-tuple-element.19.refs_0_), channel_id=1, source_target_pairs={{0,4},{1,5},{2,6},{3,7},{4,0},{5,1},{6,2},{7,3},{8,12},{9,13},{10,... | collective-permute-start | bytes 393224 | tf_op jit(solution)/shard_map/gather/ppermute | solution.py:222
  5.9 10.4 %collective-permute-start.3 = (f32[256,128]{1,0:T(8,128)S(1)}, f32[256,128]{1,0:T(8,128)S(1)}, u32[]{:S(2)}, u32[]{:S(2)}) collective-permute-start(f32[256,128]{1,0:T(8,128)S(1)} %get-tuple-element.20.refs_0_), channel_id=1, source_target_pairs={{0,24},{8,16},{16,8},{24,0},{1,25},{9,17},{17,9},{25,1},{2,26},{10... | collective-permute-start | bytes 393224 | tf_op jit(solution)/shard_map/gather/ppermute | solution.py:222
  8.3 8.0 %collective-permute-start.2 = (f32[256,128]{1,0:T(8,128)S(1)}, f32[256,128]{1,0:T(8,128)S(1)}, u32[]{:S(2)}, u32[]{:S(2)}) collective-permute-start(f32[256,128]{1,0:T(8,128)S(1)} %get-tuple-element.20.refs_0_), channel_id=1, source_target_pairs={{0,16},{8,24},{16,0},{24,8},{1,17},{9,25},{17,1},{25,9},{2,18},{10... | collective-permute-start | bytes 393224 | tf_op jit(solution)/shard_map/gather/ppermute | solution.py:222
  8.9 7.5 %collective-permute-start.1 = (f32[256,128]{1,0:T(8,128)S(1)}, f32[256,128]{1,0:T(8,128)S(1)}, u32[]{:S(2)}, u32[]{:S(2)}) collective-permute-start(f32[256,128]{1,0:T(8,128)S(1)} %get-tuple-element.20.refs_0_), channel_id=1, source_target_pairs={{0,8},{8,0},{16,24},{24,16},{1,9},{9,1},{17,25},{25,17},{2,10},{10... | collective-permute-start | bytes 393224 | tf_op jit(solution)/shard_map/gather/ppermute | solution.py:222
  9.4 7.1 %collective-permute-start.4 = (f32[256,128]{1,0:T(8,128)S(1)}, f32[256,128]{1,0:T(8,128)S(1)}, u32[]{:S(2)}, u32[]{:S(2)}) collective-permute-start(f32[256,128]{1,0:T(8,128)S(1)} %get-tuple-element.19.refs_0_), channel_id=1, source_target_pairs={{0,2},{1,3},{2,0},{3,1},{4,6},{5,7},{6,4},{7,5},{8,10},{9,11},{10,... | collective-permute-start | bytes 393224 | tf_op jit(solution)/shard_map/gather/ppermute | solution.py:222
  14.6 5.0 %collective-permute-start.5 = (f32[256,128]{1,0:T(8,128)S(1)}, f32[256,128]{1,0:T(8,128)S(1)}, u32[]{:S(2)}, u32[]{:S(2)}) collective-permute-start(f32[256,128]{1,0:T(8,128)S(1)} %gather.3._.refs_2_), channel_id=1, source_target_pairs={{0,2},{1,3},{2,0},{3,1},{4,6},{5,7},{6,4},{7,5},{8,10},{9,11},{10,... | collective-permute-start | bytes 393224 | tf_op jit(solution)/shard_map/gather/ppermute | solution.py:222
  16.6 5.6 %collective-permute-start.7 = (f32[3,256,128]{2,1,0:T(8,128)S(1)}, f32[3,256,128]{2,1,0:T(8,128)S(1)}, u32[]{:S(2)}, u32[]{:S(2)}) collective-permute-start(f32[3,256,128]{2,1,0:T(8,128)S(1)} %gather.4._.refs_0_), channel_id=1, source_target_pairs={{0,1},{1,0},{2,3},{3,2},{4,5},{5,4},{6,7},{7,6},{8,9},{9,8},{10,11... | collective-permute-start | bytes 1179656 | tf_op jit(solution)/shard_map/gather/ppermute | solution.py:222
  17.3 2.6 %collective-permute-start.6 = (f32[2,256,128]{2,1,0:T(8,128)S(1)}, f32[2,256,128]{2,1,0:T(8,128)S(1)}, u32[]{:S(2)}, u32[]{:S(2)}) collective-permute-start(f32[2,256,128]{2,1,0:T(8,128)S(1)} %backward.5._), channel_id=1, source_target_pairs={{0,1},{1,0},{2,3},{3,2},{4,5},{5,4},{6,7},{7,6},{8,9},{9,8},{10,11... | collective-permute-start | bytes 786440 | tf_op jit(solution)/shard_map/backward/ppermute | solution.py:222
  19.3 10.8 %collective-permute-start.9 = (f32[2,256,128]{2,1,0:T(8,128)S(1)}, f32[2,256,128]{2,1,0:T(8,128)S(1)}, u32[]{:S(2)}, u32[]{:S(2)}) collective-permute-start(f32[2,256,128]{2,1,0:T(8,128)S(1)} %backward.7._), channel_id=1, source_target_pairs={{0,1},{1,0},{2,3},{3,2},{4,5},{5,4},{6,7},{7,6},{8,9},{9,8},{10,11... | collective-permute-start | bytes 786440 | tf_op jit(solution)/shard_map/reduce/ppermute | solution.py:222
  19.6 2.5 %collective-permute-start.8 = (f32[1,256,128]{2,1,0:T(8,128)S(1)}, f32[1,256,128]{2,1,0:T(8,128)S(1)}, u32[]{:S(2)}, u32[]{:S(2)}) collective-permute-start(f32[1,256,128]{2,1,0:T(8,128)S(1)} %gather.5._.refs_2_), channel_id=1, source_target_pairs={{0,1},{1,0},{2,3},{3,2},{4,5},{5,4},{6,7},{7,6},{8,9},{9,8},{10,11... | collective-permute-start | bytes 393224 | tf_op jit(solution)/shard_map/gather/ppermute | solution.py:222
  20.0 6.4 %collective-permute-start.10 = (f32[256,128]{1,0:T(8,128)S(1)}, f32[256,128]{1,0:T(8,128)S(1)}, u32[]{:S(2)}, u32[]{:S(2)}) collective-permute-start(f32[256,128]{1,0:T(8,128)S(1)} %get-tuple-element.25), channel_id=1, source_target_pairs={{0,2},{1,3},{2,0},{3,1},{4,6},{5,7},{6,4},{7,5},{8,10},{9,11},{10,... | collective-permute-start | bytes 393224 | tf_op jit(solution)/shard_map/reduce/ppermute | solution.py:222
  24.6 10.9 %collective-permute-start.12 = (f32[256,128]{1,0:T(8,128)S(1)}, f32[256,128]{1,0:T(8,128)S(1)}, u32[]{:S(2)}, u32[]{:S(2)}) collective-permute-start(f32[256,128]{1,0:T(8,128)S(1)} %get-tuple-element.26), channel_id=1, source_target_pairs={{0,8},{8,0},{16,24},{24,16},{1,9},{9,1},{17,25},{25,17},{2,10},{10... | collective-permute-start | bytes 393224 | tf_op jit(solution)/shard_map/reduce/ppermute | solution.py:222
  26.4 9.1 %collective-permute-start.11 = (f32[256,128]{1,0:T(8,128)S(1)}, f32[256,128]{1,0:T(8,128)S(1)}, u32[]{:S(2)}, u32[]{:S(2)}) collective-permute-start(f32[256,128]{1,0:T(8,128)S(1)} %reduce.4), channel_id=1, source_target_pairs={{0,4},{1,5},{2,6},{3,7},{4,0},{5,1},{6,2},{7,3},{8,12},{9,13},{10,... | collective-permute-start | bytes 393224 | tf_op jit(solution)/shard_map/reduce/ppermute | solution.py:222
  26.8 8.7 %collective-permute-start.13 = (f32[256,128]{1,0:T(8,128)S(1)}, f32[256,128]{1,0:T(8,128)S(1)}, u32[]{:S(2)}, u32[]{:S(2)}) collective-permute-start(f32[256,128]{1,0:T(8,128)S(1)} %get-tuple-element.27), channel_id=1, source_target_pairs={{0,16},{8,24},{16,0},{24,8},{1,17},{9,25},{17,1},{25,9},{2,18},{10... | collective-permute-start | bytes 393224 | tf_op jit(solution)/shard_map/reduce/ppermute | solution.py:222
  28.3 7.1 %collective-permute-start.14 = (f32[256,128]{1,0:T(8,128)S(1)}, f32[256,128]{1,0:T(8,128)S(1)}, u32[]{:S(2)}, u32[]{:S(2)}) collective-permute-start(f32[256,128]{1,0:T(8,128)S(1)} %get-tuple-element.28), channel_id=1, source_target_pairs={{0,24},{8,16},{16,8},{24,0},{1,25},{9,17},{17,9},{25,1},{2,26},{10... | collective-permute-start | bytes 393224 | tf_op jit(solution)/shard_map/reduce/ppermute | solution.py:222
  30.1 6.6 %collective-permute-start.15 = (f32[256,128]{1,0:T(8,128)S(1)}, f32[256,128]{1,0:T(8,128)S(1)}, u32[]{:S(2)}, u32[]{:S(2)}) collective-permute-start(f32[256,128]{1,0:T(8,128)S(1)} %get-tuple-element.31), channel_id=1, source_target_pairs={{0,2},{1,3},{2,0},{3,1},{4,6},{5,7},{6,4},{7,5},{8,10},{9,11},{10,... | collective-permute-start | bytes 393224 | tf_op jit(solution)/shard_map/reduce/ppermute | solution.py:222

commit v11 on v9

--- a/solution.py
+++ b/solution.py
@@ -110,50 +110,44 @@
     return col_shard(lax.shift_right_logical(shard, 1), shard & 1, pairs) * tiles + (tile_at & (tiles - 1))
 
 
-def split_kernel(plan_ref, count_ref, values_ref, high_ref, low_ref, buf, sems):
+def split_kernel(count_ref, plan_ref, values_ref, high_ref, low_ref, buf, places, sems, place_sem):
     capacity, tile, _ = values_ref.shape
     groups = sems.shape[0]
     group = capacity // groups
     count = count_ref[0, 0]
+    live_groups = lax.div(count + (group - 1), group)
 
     def copy(at):
         slots = pl.ds(at * group, group)
         return pltpu.make_async_copy(values_ref.at[slots], buf.at[slots], sems.at[at])
 
     def store(slot, high, low):
-        rows = pl.ds(pl.multiple_of(plan_ref[0, slot], tile), tile)
-        cols = pl.ds(pl.multiple_of(plan_ref[1, slot], tile), tile)
+        rows = pl.ds(pl.multiple_of(places[0, slot], tile), tile)
+        cols = pl.ds(pl.multiple_of(places[1, slot], tile), tile)
         high_ref[rows, cols] = high
         low_ref[rows, cols] = low
 
-    for at in range(groups):
-
-        @pl.when(at * group < count)
-        def _():
-            copy(at).start()
-
-    @pl.loop(count, capacity)
+    @pl.loop(0, live_groups)
+    def _(at):
+        copy(at).start()
+
+    place_copy = pltpu.make_async_copy(plan_ref, places, place_sem)
+    place_copy.start()
+    place_copy.wait()
+
+    @pl.loop(live_groups * group, capacity, unroll=1)
     def _(slot):
         zeros = jnp.zeros((tile, tile), BF16)
         store(slot, zeros, zeros)
 
-    for at in range(groups):
-
-        @pl.when(at * group < count)
-        def _():
-            copy(at).wait()
-
-        @pl.when((at + 1) * group <= count)
-        def _():
-            @pl.loop(at * group, (at + 1) * group, unroll=4)
-            def _(slot):
-                store(slot, *halves(buf[slot]))
-
-        @pl.when((at * group < count) & ((at + 1) * group > count))
-        def _():
-            @pl.loop(at * group, count)
-            def _(slot):
-                store(slot, *halves(buf[slot]))
+    @pl.loop(0, live_groups)
+    def _(at):
+        copy(at).wait()
+
+        @pl.loop(0, group, unroll=math.gcd(group, 8))
+        def _(step):
+            slot = at * group + step
+            store(slot, *halves(jnp.where(slot < count, buf[slot], 0.0)))
 
 
 def flip_kernel(tile, *refs):
@@ -322,15 +316,20 @@
 
     if dense:
         table = jax.ShapeDtypeStruct((n_rows, n_cols), BF16)
-        groups = math.gcd(capacity, 16)
+        groups = math.gcd(capacity, 8)
         with jax.named_scope("split"):
             high, low = call(
                 split_kernel,
                 (table, table),
-                (plan, tile_count, pltpu.with_memory_space_constraint(values, pltpu.HBM)),
+                (tile_count, plan, pltpu.with_memory_space_constraint(values, pltpu.HBM)),
                 mebibytes=32,
-                specs=[SCALARS, SCALARS, pl.BlockSpec(memory_space=pltpu.HBM)],
-                scratch=[pltpu.VMEM(values.shape, F32), pltpu.SemaphoreType.DMA((groups,))],
+                specs=[SCALARS, WHOLE, pl.BlockSpec(memory_space=pltpu.HBM)],
+                scratch=[
+                    pltpu.VMEM(values.shape, F32),
+                    pltpu.SMEM(plan.shape, jnp.int32),
+                    pltpu.SemaphoreType.DMA((groups,)),
+                    pltpu.SemaphoreType.DMA,
+                ],
             )
         with jax.named_scope("gather"):
             passed, late = gathered(high)

time: 36.9 us -> 36.5 us (0.989)
  starting transfers between devices: 17.2 us -> 15.4 us
  Pallas kernels: 10.5 us -> 11.5 us
    ppermute x16, starting transfers between devices: 17.2 us -> 15.4 us  [swap(): lax.ppermute(x, axis, [(at, at ^ mask) for at in range(lax.axis_size(axis...]
    pallas_call x18, Pallas kernels: 10.5 us -> 11.5 us  [call(): pl.pallas_call(body, out_shape=out_shape, in_specs=specs, out_specs=tuple...]
  transfers between devices with their start and end apart: 16 -> 16, of which waited for: 6 -> 5; matrix products, arithmetic and copies ran while one was open for 0% -> 0% of each run, Pallas kernels for 23% -> 26%
where the time goes in v11:
time: 36.5 us; the launch traced here: 36.2 us
  starting transfers between devices  15.4 us (42%)
  Pallas kernels  11.5 us (32%)
  waiting for transfers between devices  7.81 us (21%)
  between operations  1.51 us (4%)
    ppermute x16, starting transfers between devices, swap(): lax.ppermute(x, axis, [(at, at ^ mask) for at in range(lax.axis_size(axis...  15.4 us
    pallas_call x18, Pallas kernels, call(): pl.pallas_call(body, out_shape=out_shape, in_specs=specs, out_specs=tuple...  11.5 us
    ppermute x16, waiting for transfers between devices, swap(): lax.ppermute(x, axis, [(at, at ^ mask) for at in range(lax.axis_size(axis...  7.81 us
  transfers between devices with their start and end apart: 16, of which 5 were waited for; matrix products, arithmetic and copies ran while one was open for 0% of the time, Pallas kernels for 26%

profile of v11, /device:TPU:0, one launch (start us, length us, event | category | flops | bytes accessed | tf_op | source)
XLA Modules:
  0.0 36.2 jit_solution(17189907673506301852)
XLA Ops:
  0.6 1.2 %scale.1 = (f32[256,128]{1,0:T(8,128)S(1)}, f32[256,128]{1,0:T(8,128)S(1)}, f32[256,128]{1,0:T(8,128)S(1)}, f32[256,128]{1,0:T(8,128)S(1)}, s32[2,128]{1,0:T(2,128)S(1)}) custom-call(f32[256,128]{1,0:T(8,128)} %refs_0_.1, f32[256,128]{1,0:T(8,128)} %refs_1_.1, s32[2,128]{1,0:T(2,128)} %bitcast.4, s32[2,128]{1,0:T(2,128)} %bitcast.5, s32[2,1,1,128]{3,2,1,0:T(1,128)} %refs_4_.1), custom_call_target="tpu_custom_call" | custom-call | bytes 1024 | tf_op jit(solution)/shard_map/scale/pallas_call | solution.py:234
  1.8 4.1 %collective-permute-start = (f32[256,128]{1,0:T(8,128)S(1)}, f32[256,128]{1,0:T(8,128)S(1)}, u32[]{:S(2)}, u32[]{:S(2)}) collective-permute-start(f32[256,128]{1,0:T(8,128)S(1)} %get-tuple-element.23.refs_0_), channel_id=1, source_target_pairs={{0,4},{1,5},{2,6},{3,7},{4,0},{5,1},{6,2},{7,3},{8,12},{9,13},{10,... | collective-permute-start | bytes 393224 | tf_op jit(solution)/shard_map/gather/ppermute | solution.py:221
  5.9 1.5 %collective-permute-start.1 = (f32[256,128]{1,0:T(8,128)S(1)}, f32[256,128]{1,0:T(8,128)S(1)}, u32[]{:S(2)}, u32[]{:S(2)}) collective-permute-start(f32[256,128]{1,0:T(8,128)S(1)} %get-tuple-element.24.refs_0_), channel_id=1, source_target_pairs={{0,8},{8,0},{16,24},{24,16},{1,9},{9,1},{17,25},{25,17},{2,10},{10... | collective-permute-start | bytes 393224 | tf_op jit(solution)/shard_map/gather/ppermute | solution.py:221
  7.4 1.5 %collective-permute-start.2 = (f32[256,128]{1,0:T(8,128)S(1)}, f32[256,128]{1,0:T(8,128)S(1)}, u32[]{:S(2)}, u32[]{:S(2)}) collective-permute-start(f32[256,128]{1,0:T(8,128)S(1)} %get-tuple-element.24.refs_0_), channel_id=1, source_target_pairs={{0,16},{8,24},{16,0},{24,8},{1,17},{9,25},{17,1},{25,9},{2,18},{10... | collective-permute-start | bytes 393224 | tf_op jit(solution)/shard_map/gather/ppermute | solution.py:221
  8.9 0.5 %collective-permute-start.3 = (f32[256,128]{1,0:T(8,128)S(1)}, f32[256,128]{1,0:T(8,128)S(1)}, u32[]{:S(2)}, u32[]{:S(2)}) collective-permute-start(f32[256,128]{1,0:T(8,128)S(1)} %get-tuple-element.24.refs_0_), channel_id=1, source_target_pairs={{0,24},{8,16},{16,8},{24,0},{1,25},{9,17},{17,9},{25,1},{2,26},{10... | collective-permute-start | bytes 393224 | tf_op jit(solution)/shard_map/gather/ppermute | solution.py:221
  9.4 1.6 %collective-permute-start.4 = (f32[256,128]{1,0:T(8,128)S(1)}, f32[256,128]{1,0:T(8,128)S(1)}, u32[]{:S(2)}, u32[]{:S(2)}) collective-permute-start(f32[256,128]{1,0:T(8,128)S(1)} %get-tuple-element.23.refs_0_), channel_id=1, source_target_pairs={{0,2},{1,3},{2,0},{3,1},{4,6},{5,7},{6,4},{7,5},{8,10},{9,11},{10,... | collective-permute-start | bytes 393224 | tf_op jit(solution)/shard_map/gather/ppermute | solution.py:221
  11.6 3.8 %split.1 = (bf16[1024,2048]{1,0:T(8,128)(2,1)S(1)}, bf16[1024,2048]{1,0:T(8,128)(2,1)S(1)}) custom-call(s32[1,1]{1,0:T(1,128)S(6)} %copy.9.count_ref, s32[2,128]{1,0:T(2,128)S(1)} %get-tuple-element.21.plan_ref, f32[128,128,128]{2,1,0:T(8,128)} %bitcast.3), custom_call_target="tpu_custom_call" | custom-call | bytes 1024 | tf_op jit(solution)/shard_map/split/pallas_call | solution.py:234
  15.5 0.0 collective-permute-done.refs_0_
  15.5 0.1 collective-permute-start.5
  15.6 0.0 collective-permute-done.1.refs_1_
  15.6 0.0 collective-permute-done.2.refs_2_
  15.6 0.0 collective-permute-done.3.refs_3_
  15.6 0.2 flip.1._.refs_0_
  15.8 0.0 collective-permute-done.4.refs_1_
  15.9 0.7 %backward.5._ = f32[2,256,128]{2,1,0:T(8,128)S(1)} custom-call(f32[3,256,128]{2,1,0:T(8,128)S(1)} %gather.4._.refs_0_, bf16[256,1024]{1,0:T(8,128)(2,1)S(1)} %flip.1._.refs_0_, bf16[1024,2048]{1,0:T(8,128)(2,1)S(1)} %get-tuple-element.22._.refs_1_.refs_2_, bf16[1024,2048]{1,0:T(8,128)(2,1)S(1)} %get-tuple-element.25.refs_2_.refs_3_), custom_call_target="tpu_custom_call" | custom-call | bytes 1024 | tf_op jit(solution)/shard_map/backward/pallas_call | solution.py:234
  16.6 0.1 collective-permute-start.6
  16.6 0.5 %collective-permute-start.7 = (f32[3,256,128]{2,1,0:T(8,128)S(1)}, f32[3,256,128]{2,1,0:T(8,128)S(1)}, u32[]{:S(2)}, u32[]{:S(2)}) collective-permute-start(f32[3,256,128]{2,1,0:T(8,128)S(1)} %gather.4._.refs_0_), channel_id=1, source_target_pairs={{0,1},{1,0},{2,3},{3,2},{4,5},{5,4},{6,7},{7,6},{8,9},{9,8},{10,11... | collective-permute-start | bytes 1179656 | tf_op jit(solution)/shard_map/gather/ppermute | solution.py:221
  17.1 0.7 %backward.6._.refs_0_ = f32[2,256,128]{2,1,0:T(8,128)S(1)} custom-call(f32[2,256,128]{2,1,0:T(8,128)S(1)} %backward.5._, bf16[256,1024]{1,0:T(8,128)(2,1)S(1)} %flip.1._.refs_0_, bf16[1024,2048]{1,0:T(8,128)(2,1)S(1)} %get-tuple-element.22._.refs_1_.refs_2_, bf16[1024,2048]{1,0:T(8,128)(2,1)S(1)} %get-tuple-element.25.refs_2_.refs_3_), custom_call_target="tpu_custom_call" | custom-call | bytes 1024 | tf_op jit(solution)/shard_map/backward/pallas_call | solution.py:234
  17.8 0.7 %backward.7._ = f32[2,256,128]{2,1,0:T(8,128)S(1)} custom-call(f32[2,256,128]{2,1,0:T(8,128)S(1)} %backward.6._.refs_0_, bf16[256,1024]{1,0:T(8,128)(2,1)S(1)} %flip.1._.refs_0_, bf16[1024,2048]{1,0:T(8,128)(2,1)S(1)} %get-tuple-element.22._.refs_1_.refs_2_, bf16[1024,2048]{1,0:T(8,128)(2,1)S(1)} %get-tuple-element.25.refs_2_.refs_3_), custom_call_target="tpu_custom_call" | custom-call | bytes 1024 | tf_op jit(solution)/shard_map/backward/pallas_call | solution.py:234
  18.5 2.0 %collective-permute-done.5.refs_0_ = f32[256,128]{1,0:T(8,128)S(1)} collective-permute-done((f32[256,128]{1,0:T(8,128)S(1)}, f32[256,128]{1,0:T(8,128)S(1)}, u32[]{:S(2)}, u32[]{:S(2)}) %collective-permute-start.5) | collective-permute-done | bytes 131104 | tf_op jit(solution)/shard_map/gather/ppermute | solution.py:221
  20.6 0.0 collective-permute-done.6.refs_1_
  20.6 0.1 collective-permute-start.8
  20.7 0.1 collective-permute-start.9
  20.8 0.5 %collective-permute-start.10 = (f32[2,256,128]{2,1,0:T(8,128)S(1)}, f32[2,256,128]{2,1,0:T(8,128)S(1)}, u32[]{:S(2)}, u32[]{:S(2)}) collective-permute-start(f32[2,256,128]{2,1,0:T(8,128)S(1)} %backward.7._), channel_id=1, source_target_pairs={{0,1},{1,0},{2,3},{3,2},{4,5},{5,4},{6,7},{7,6},{8,9},{9,8},{10,11... | collective-permute-start | bytes 786440 | tf_op jit(solution)/shard_map/reduce/ppermute | solution.py:221
  21.3 0.7 %backward.9._.refs_0_ = f32[2,256,128]{2,1,0:T(8,128)S(1)} custom-call(f32[256,128]{1,0:T(8,128)S(1)} %get-tuple-element.26._.refs_0_, bf16[256,1024]{1,0:T(8,128)(2,1)S(1)} %flip.1._.refs_0_, bf16[1024,2048]{1,0:T(8,128)(2,1)S(1)} %get-tuple-element.22._.refs_1_.refs_2_, bf16[1024,2048]{1,0:T(8,128)(2,1)S(1)} %get-tuple-element.25.refs_2_.refs_3_), custom_call_target="tpu_custom_call" | custom-call | bytes 1024 | tf_op jit(solution)/shard_map/backward/pallas_call | solution.py:234
  21.9 0.0 collective-permute-done.7.refs_1_
  22.0 1.9 %forward.2 = (f32[256,128]{1,0:T(8,128)S(1)}, f32[256,128]{1,0:T(8,128)S(1)}, f32[256,128]{1,0:T(8,128)S(1)}, f32[256,128]{1,0:T(8,128)S(1)}) custom-call(f32[2,256,128]{2,1,0:T(8,128)S(1)} %backward.9._.refs_0_, f32[3,256,128]{2,1,0:T(8,128)S(1)} %gather.4._.refs_0_, f32[3,256,128]{2,1,0:T(8,128)S(1)} %collective-permute-done.7.refs_1_, ...), custom_call_target="tpu_custom_call" | custom-call | bytes 1024 | tf_op jit(solution)/shard_map/forward/pallas_call | solution.py:234
  23.8 1.8 %collective-permute-done.8.refs_1_ = f32[256,128]{1,0:T(8,128)S(1)} collective-permute-done((f32[256,128]{1,0:T(8,128)S(1)}, f32[256,128]{1,0:T(8,128)S(1)}, u32[]{:S(2)}, u32[]{:S(2)}) %collective-permute-start.8) | collective-permute-done | bytes 131104 | tf_op jit(solution)/shard_map/reduce/ppermute | solution.py:221
  25.7 0.1 collective-permute-start.11
  25.7 0.0 collective-permute-done.9.refs_1_
  25.7 0.7 %forward.3 = (f32[256,128]{1,0:T(8,128)S(1)}, f32[256,128]{1,0:T(8,128)S(1)}, f32[256,128]{1,0:T(8,128)S(1)}, f32[256,128]{1,0:T(8,128)S(1)}) custom-call(f32[256,128]{1,0:T(8,128)S(1)} %reduce.3._, f32[1,256,128]{2,1,0:T(8,128)S(1)} %gather.5._.refs_0_, f32[1,256,128]{2,1,0:T(8,128)S(1)} %collective-permute-done.9.refs_1_, ...), custom_call_target="tpu_custom_call" | custom-call | flops 2000000000 | bytes 1024 | tf_op jit(solution)/shard_map/forward/pallas_call | solution.py:234
  26.5 1.1 %collective-permute-start.12 = (f32[256,128]{1,0:T(8,128)S(1)}, f32[256,128]{1,0:T(8,128)S(1)}, u32[]{:S(2)}, u32[]{:S(2)}) collective-permute-start(f32[256,128]{1,0:T(8,128)S(1)} %get-tuple-element.34), channel_id=1, source_target_pairs={{0,8},{8,0},{16,24},{24,16},{1,9},{9,1},{17,25},{25,17},{2,10},{10... | collective-permute-start | bytes 393224 | tf_op jit(solution)/shard_map/reduce/ppermute | solution.py:221
  27.6 2.0 %collective-permute-start.13 = (f32[256,128]{1,0:T(8,128)S(1)}, f32[256,128]{1,0:T(8,128)S(1)}, u32[]{:S(2)}, u32[]{:S(2)}) collective-permute-start(f32[256,128]{1,0:T(8,128)S(1)} %get-tuple-element.35), channel_id=1, source_target_pairs={{0,16},{8,24},{16,0},{24,8},{1,17},{9,25},{17,1},{25,9},{2,18},{10... | collective-permute-start | bytes 393224 | tf_op jit(solution)/shard_map/reduce/ppermute | solution.py:221
  29.6 0.5 %collective-permute-start.14 = (f32[256,128]{1,0:T(8,128)S(1)}, f32[256,128]{1,0:T(8,128)S(1)}, u32[]{:S(2)}, u32[]{:S(2)}) collective-permute-start(f32[256,128]{1,0:T(8,128)S(1)} %get-tuple-element.36), channel_id=1, source_target_pairs={{0,24},{8,16},{16,8},{24,0},{1,25},{9,17},{17,9},{25,1},{2,26},{10... | collective-permute-start | bytes 393224 | tf_op jit(solution)/shard_map/reduce/ppermute | solution.py:221
  30.0 0.0 collective-permute-done.10.refs_1_
  30.1 1.4 %collective-permute-start.15 = (f32[256,128]{1,0:T(8,128)S(1)}, f32[256,128]{1,0:T(8,128)S(1)}, u32[]{:S(2)}, u32[]{:S(2)}) collective-permute-start(f32[256,128]{1,0:T(8,128)S(1)} %get-tuple-element.39), channel_id=1, source_target_pairs={{0,2},{1,3},{2,0},{3,1},{4,6},{5,7},{6,4},{7,5},{8,10},{9,11},{10,... | collective-permute-start | bytes 393224 | tf_op jit(solution)/shard_map/reduce/ppermute | solution.py:221
  31.4 1.8 %collective-permute-done.11.y_ref = f32[256,128]{1,0:T(8,128)S(1)} collective-permute-done((f32[256,128]{1,0:T(8,128)S(1)}, f32[256,128]{1,0:T(8,128)S(1)}, u32[]{:S(2)}, u32[]{:S(2)}) %collective-permute-start.11) | collective-permute-done | bytes 131104 | tf_op jit(solution)/shard_map/reduce/ppermute | solution.py:221
  33.2 0.0 collective-permute-done.12.refs_1_
  33.2 1.1 %collective-permute-done.13.refs_2_ = f32[256,128]{1,0:T(8,128)S(1)} collective-permute-done((f32[256,128]{1,0:T(8,128)S(1)}, f32[256,128]{1,0:T(8,128)S(1)}, u32[]{:S(2)}, u32[]{:S(2)}) %collective-permute-start.13) | collective-permute-done | bytes 131104 | tf_op jit(solution)/shard_map/reduce/ppermute | solution.py:221
  34.3 1.1 %collective-permute-done.14.refs_3_ = f32[256,128]{1,0:T(8,128)S(1)} collective-permute-done((f32[256,128]{1,0:T(8,128)S(1)}, f32[256,128]{1,0:T(8,128)S(1)}, u32[]{:S(2)}, u32[]{:S(2)}) %collective-permute-start.14) | collective-permute-done | bytes 131104 | tf_op jit(solution)/shard_map/reduce/ppermute | solution.py:221
  35.5 0.0 collective-permute-done.15.refs_1_
  35.5 0.7 %finish.3 = (f32[256,128]{1,0:T(8,128)}, f32[256,128]{1,0:T(8,128)}) custom-call(f32[256,128]{1,0:T(8,128)S(1)} %finish.2.row_ref, f32[256,128]{1,0:T(8,128)S(1)} %get-tuple-element.37.row_factor_ref, f32[256,128]{1,0:T(8,128)S(1)} %get-tuple-element.38.col_factor_ref, f32[256,128]{1,0:T(8,128)S(1)} %reduce.5._.refs_0_, ...), custom_call_target="tpu_custom_call" | custom-call | bytes 1024 | tf_op jit(solution)/shard_map/finish/pallas_call | solution.py:234
  (8 shorter events, 0.2 us)
Async XLA Ops:
  1.8 13.7 %collective-permute-start = (f32[256,128]{1,0:T(8,128)S(1)}, f32[256,128]{1,0:T(8,128)S(1)}, u32[]{:S(2)}, u32[]{:S(2)}) collective-permute-start(f32[256,128]{1,0:T(8,128)S(1)} %get-tuple-element.23.refs_0_), channel_id=1, source_target_pairs={{0,4},{1,5},{2,6},{3,7},{4,0},{5,1},{6,2},{7,3},{8,12},{9,13},{10,... | collective-permute-start | bytes 393224 | tf_op jit(solution)/shard_map/gather/ppermute | solution.py:221
  5.9 9.7 %collective-permute-start.1 = (f32[256,128]{1,0:T(8,128)S(1)}, f32[256,128]{1,0:T(8,128)S(1)}, u32[]{:S(2)}, u32[]{:S(2)}) collective-permute-start(f32[256,128]{1,0:T(8,128)S(1)} %get-tuple-element.24.refs_0_), channel_id=1, source_target_pairs={{0,8},{8,0},{16,24},{24,16},{1,9},{9,1},{17,25},{25,17},{2,10},{10... | collective-permute-start | bytes 393224 | tf_op jit(solution)/shard_map/gather/ppermute | solution.py:221
  7.4 8.2 %collective-permute-start.2 = (f32[256,128]{1,0:T(8,128)S(1)}, f32[256,128]{1,0:T(8,128)S(1)}, u32[]{:S(2)}, u32[]{:S(2)}) collective-permute-start(f32[256,128]{1,0:T(8,128)S(1)} %get-tuple-element.24.refs_0_), channel_id=1, source_target_pairs={{0,16},{8,24},{16,0},{24,8},{1,17},{9,25},{17,1},{25,9},{2,18},{10... | collective-permute-start | bytes 393224 | tf_op jit(solution)/shard_map/gather/ppermute | solution.py:221
  8.9 6.7 %collective-permute-start.3 = (f32[256,128]{1,0:T(8,128)S(1)}, f32[256,128]{1,0:T(8,128)S(1)}, u32[]{:S(2)}, u32[]{:S(2)}) collective-permute-start(f32[256,128]{1,0:T(8,128)S(1)} %get-tuple-element.24.refs_0_), channel_id=1, source_target_pairs={{0,24},{8,16},{16,8},{24,0},{1,25},{9,17},{17,9},{25,1},{2,26},{10... | collective-permute-start | bytes 393224 | tf_op jit(solution)/shard_map/gather/ppermute | solution.py:221
  9.4 6.4 %collective-permute-start.4 = (f32[256,128]{1,0:T(8,128)S(1)}, f32[256,128]{1,0:T(8,128)S(1)}, u32[]{:S(2)}, u32[]{:S(2)}) collective-permute-start(f32[256,128]{1,0:T(8,128)S(1)} %get-tuple-element.23.refs_0_), channel_id=1, source_target_pairs={{0,2},{1,3},{2,0},{3,1},{4,6},{5,7},{6,4},{7,5},{8,10},{9,11},{10,... | collective-permute-start | bytes 393224 | tf_op jit(solution)/shard_map/gather/ppermute | solution.py:221
  15.5 5.0 %collective-permute-start.5 = (f32[256,128]{1,0:T(8,128)S(1)}, f32[256,128]{1,0:T(8,128)S(1)}, u32[]{:S(2)}, u32[]{:S(2)}) collective-permute-start(f32[256,128]{1,0:T(8,128)S(1)} %gather.3._.refs_2_), channel_id=1, source_target_pairs={{0,2},{1,3},{2,0},{3,1},{4,6},{5,7},{6,4},{7,5},{8,10},{9,11},{10,... | collective-permute-start | bytes 393224 | tf_op jit(solution)/shard_map/gather/ppermute | solution.py:221
  16.6 4.0 %collective-permute-start.6 = (f32[2,256,128]{2,1,0:T(8,128)S(1)}, f32[2,256,128]{2,1,0:T(8,128)S(1)}, u32[]{:S(2)}, u32[]{:S(2)}) collective-permute-start(f32[2,256,128]{2,1,0:T(8,128)S(1)} %backward.5._), channel_id=1, source_target_pairs={{0,1},{1,0},{2,3},{3,2},{4,5},{5,4},{6,7},{7,6},{8,9},{9,8},{10,11... | collective-permute-start | bytes 786440 | tf_op jit(solution)/shard_map/backward/ppermute | solution.py:221
  16.6 5.3 %collective-permute-start.7 = (f32[3,256,128]{2,1,0:T(8,128)S(1)}, f32[3,256,128]{2,1,0:T(8,128)S(1)}, u32[]{:S(2)}, u32[]{:S(2)}) collective-permute-start(f32[3,256,128]{2,1,0:T(8,128)S(1)} %gather.4._.refs_0_), channel_id=1, source_target_pairs={{0,1},{1,0},{2,3},{3,2},{4,5},{5,4},{6,7},{7,6},{8,9},{9,8},{10,11... | collective-permute-start | bytes 1179656 | tf_op jit(solution)/shard_map/gather/ppermute | solution.py:221
  20.6 5.0 %collective-permute-start.8 = (f32[256,128]{1,0:T(8,128)S(1)}, f32[256,128]{1,0:T(8,128)S(1)}, u32[]{:S(2)}, u32[]{:S(2)}) collective-permute-start(f32[256,128]{1,0:T(8,128)S(1)} %get-tuple-element.28), channel_id=1, source_target_pairs={{0,2},{1,3},{2,0},{3,1},{4,6},{5,7},{6,4},{7,5},{8,10},{9,11},{10,... | collective-permute-start | bytes 393224 | tf_op jit(solution)/shard_map/reduce/ppermute | solution.py:221
  20.7 5.1 %collective-permute-start.9 = (f32[1,256,128]{2,1,0:T(8,128)S(1)}, f32[1,256,128]{2,1,0:T(8,128)S(1)}, u32[]{:S(2)}, u32[]{:S(2)}) collective-permute-start(f32[1,256,128]{2,1,0:T(8,128)S(1)} %gather.5._.refs_0_), channel_id=1, source_target_pairs={{0,1},{1,0},{2,3},{3,2},{4,5},{5,4},{6,7},{7,6},{8,9},{9,8},{10,11... | collective-permute-start | bytes 393224 | tf_op jit(solution)/shard_map/gather/ppermute | solution.py:221
  20.8 9.3 %collective-permute-start.10 = (f32[2,256,128]{2,1,0:T(8,128)S(1)}, f32[2,256,128]{2,1,0:T(8,128)S(1)}, u32[]{:S(2)}, u32[]{:S(2)}) collective-permute-start(f32[2,256,128]{2,1,0:T(8,128)S(1)} %backward.7._), channel_id=1, source_target_pairs={{0,1},{1,0},{2,3},{3,2},{4,5},{5,4},{6,7},{7,6},{8,9},{9,8},{10,11... | collective-permute-start | bytes 786440 | tf_op jit(solution)/shard_map/reduce/ppermute | solution.py:221
  25.7 7.6 %collective-permute-start.11 = (f32[256,128]{1,0:T(8,128)S(1)}, f32[256,128]{1,0:T(8,128)S(1)}, u32[]{:S(2)}, u32[]{:S(2)}) collective-permute-start(f32[256,128]{1,0:T(8,128)S(1)} %reduce.3._), channel_id=1, source_target_pairs={{0,4},{1,5},{2,6},{3,7},{4,0},{5,1},{6,2},{7,3},{8,12},{9,13},{10,... | collective-permute-start | bytes 393224 | tf_op jit(solution)/shard_map/reduce/ppermute | solution.py:221
  26.5 6.8 %collective-permute-start.12 = (f32[256,128]{1,0:T(8,128)S(1)}, f32[256,128]{1,0:T(8,128)S(1)}, u32[]{:S(2)}, u32[]{:S(2)}) collective-permute-start(f32[256,128]{1,0:T(8,128)S(1)} %get-tuple-element.34), channel_id=1, source_target_pairs={{0,8},{8,0},{16,24},{24,16},{1,9},{9,1},{17,25},{25,17},{2,10},{10... | collective-permute-start | bytes 393224 | tf_op jit(solution)/shard_map/reduce/ppermute | solution.py:221
  27.6 6.7 %collective-permute-start.13 = (f32[256,128]{1,0:T(8,128)S(1)}, f32[256,128]{1,0:T(8,128)S(1)}, u32[]{:S(2)}, u32[]{:S(2)}) collective-permute-start(f32[256,128]{1,0:T(8,128)S(1)} %get-tuple-element.35), channel_id=1, source_target_pairs={{0,16},{8,24},{16,0},{24,8},{1,17},{9,25},{17,1},{25,9},{2,18},{10... | collective-permute-start | bytes 393224 | tf_op jit(solution)/shard_map/reduce/ppermute | solution.py:221
  29.6 5.9 %collective-permute-start.14 = (f32[256,128]{1,0:T(8,128)S(1)}, f32[256,128]{1,0:T(8,128)S(1)}, u32[]{:S(2)}, u32[]{:S(2)}) collective-permute-start(f32[256,128]{1,0:T(8,128)S(1)} %get-tuple-element.36), channel_id=1, source_target_pairs={{0,24},{8,16},{16,8},{24,0},{1,25},{9,17},{17,9},{25,1},{2,26},{10... | collective-permute-start | bytes 393224 | tf_op jit(solution)/shard_map/reduce/ppermute | solution.py:221
  30.1 5.4 %collective-permute-start.15 = (f32[256,128]{1,0:T(8,128)S(1)}, f32[256,128]{1,0:T(8,128)S(1)}, u32[]{:S(2)}, u32[]{:S(2)}) collective-permute-start(f32[256,128]{1,0:T(8,128)S(1)} %get-tuple-element.39), channel_id=1, source_target_pairs={{0,2},{1,3},{2,0},{3,1},{4,6},{5,7},{6,4},{7,5},{8,10},{9,11},{10,... | collective-permute-start | bytes 393224 | tf_op jit(solution)/shard_map/reduce/ppermute | solution.py:221

commit v12 on v11

--- a/solution.py
+++ b/solution.py
@@ -88,6 +88,34 @@
     out_ref[...] = x_ref[...]
 
 
+def stack_kernel(*refs):
+    *part_refs, last_ref, out_ref = refs
+    for at, part_ref in enumerate(part_refs):
+        out_ref[pl.ds(2 * at, 2)] = part_ref[...]
+    out_ref[2 * len(part_refs)] = last_ref[...]
+
+
+def panel_kernel(own_ref, beside_ref, crossed_ref, mine_ref, theirs_ref, own_out_ref, other_out_ref):
+    half = own_out_ref.shape[0] - 1
+    own_out_ref[0] = own_ref[...]
+    other_out_ref[0] = beside_ref[...]
+    own_out_ref[half] = crossed_ref[...]
+    other_out_ref[half] = theirs_ref[2 * half - 2]
+    core = lax.axis_index("col") % 2
+    for at in range(1, half):
+        first = 2 * at - 2
+
+        @pl.when(core == 1)
+        def _():
+            own_out_ref[at] = mine_ref[first]
+            other_out_ref[at] = mine_ref[first + 1]
+
+        @pl.when(core == 0)
+        def _():
+            own_out_ref[at] = theirs_ref[first + 1]
+            other_out_ref[at] = theirs_ref[first]
+
+
 def copy_kernel(*refs):
     *part_refs, out_ref = refs
     for at, part_ref in enumerate(part_refs):
@@ -271,10 +299,12 @@
     with jax.named_scope("gather"):
         crossed = swap(scaled, "col", 2 * half)
         grads = [grad_scaled] + [swap(grad_scaled, "row", k) for k in range(1, n_row)]
-        near = {0: scaled}
+        beside = swap(scaled, "col", 1)
+        near = {0: call(copy_kernel, blocks(2), [scaled, beside])}
         mask = half // 2
         while mask:
-            near.update({at | mask: swap(x, "col", 2 * mask) for at, x in near.items()})
+            pairs_of_core = [(at, at ^ (2 * mask)) for at in range(1, n_col, 2)]
+            near.update({at | mask: lax.ppermute(x, "col", pairs_of_core) for at, x in near.items()})
             mask //= 2
 
     def gathered(after):
@@ -285,8 +315,12 @@
             mask //= 2
         return passed, [late[at] for at in range(1, half)]
 
-    def stacked(passed, after):
-        return call(copy_kernel, blocks(half + 1), [near[at] for at in range(half)] + [passed], after=after)
+    def panels(passed, after):
+        parts = [near[at] for at in range(1, half)]
+        mine = call(stack_kernel, blocks(2 * half - 1), [*parts, passed], after=after)
+        return call(
+            panel_kernel, (blocks(half + 1), blocks(half + 1)), (scaled, beside, passed, mine, swap(mine, "col", 1))
+        )
 
     def chip_sums(kept, sent, after=None):
         return call(
@@ -339,10 +373,10 @@
                 jax.ShapeDtypeStruct((2 * width, n_rows), BF16),
                 grads,
                 after=passed,
+                flops=2 * 10**9,
             )
         with jax.named_scope("gather"):
-            early = stacked(passed, flipped)
-            other_early = swap(early, "col", 1)
+            early, other_early = panels(passed, flipped)
 
         def backward_part(distances, core, after):
             shards = [shard_at(distance, core) for distance in distances]
@@ -374,7 +408,7 @@
 
         with jax.named_scope("backward"):
             far, close = range(half, pairs), range(half)
-            far_sent = backward_part(far, 1, early)
+            far_sent = backward_part(far, 1, flipped)
             far_kept = backward_part(far, 0, far_sent)
             sent = backward_part(close, 1, far_kept)
         with jax.named_scope("gather"):
@@ -396,9 +430,9 @@
         group = 8
         with jax.named_scope("gather"):
             passed, late = gathered(plan)
-            early = stacked(passed, plan)
+            early, other_early = panels(passed, plan)
             late = call(copy_kernel, blocks(half - 1), late)
-            panel = jnp.concatenate([early, swap(early, "col", 1), late, swap(late, "col", 1)])
+            panel = jnp.concatenate([early, other_early, late, swap(late, "col", 1)])
         with jax.named_scope("slots"):
             forward, backward = pl.pallas_call(
                 functools.partial(slots_kernel, tiles, pairs),

time: 36.5 us -> 38.7 us (1.060)
  starting transfers between devices: 15.4 us -> 18.3 us
  waiting for transfers between devices: 7.81 us -> 6.87 us
    ppermute x16, starting transfers between devices: 15.4 us -> 17.7 us  [swap(): lax.ppermute(x, axis, [(at, at ^ mask) for at in range(lax.axis_size(axis...]
    ppermute x16, waiting for transfers between devices: 7.81 us -> 6.86 us  [swap(): lax.ppermute(x, axis, [(at, at ^ mask) for at in range(lax.axis_size(axis...]
    ppermute x0 -> x1, starting transfers between devices: none -> 0.68 us  [per_device(): lax.ppermute(x, 'col', pairs_of_core)]
    pallas_call x18 -> x20, Pallas kernels: 11.5 us -> 11.5 us  [call(): pl.pallas_call(body, out_shape=out_shape, in_specs=specs, out_specs=tuple...]
  transfers between devices with their start and end apart: 16 -> 17, of which waited for: 5 -> 5; matrix products, arithmetic and copies ran while one was open for 0% -> 0% of each run, Pallas kernels for 26% -> 25%
where the time goes in v12:
time: 38.7 us; the launch traced here: 38.2 us
  starting transfers between devices  18.3 us (47%)
  Pallas kernels  11.5 us (30%)
  waiting for transfers between devices  6.87 us (18%)
  between operations  1.46 us (4%)
    ppermute x16, starting transfers between devices, swap(): lax.ppermute(x, axis, [(at, at ^ mask) for at in range(lax.axis_size(axis...  17.7 us
    pallas_call x20, Pallas kernels, call(): pl.pallas_call(body, out_shape=out_shape, in_specs=specs, out_specs=tuple...  11.5 us
    ppermute x16, waiting for transfers between devices, swap(): lax.ppermute(x, axis, [(at, at ^ mask) for at in range(lax.axis_size(axis...  6.86 us
  transfers between devices with their start and end apart: 17, of which 5 were waited for; matrix products, arithmetic and copies ran while one was open for 0% of the time, Pallas kernels for 25%

profile of v12, /device:TPU:0, one launch (start us, length us, event | category | flops | bytes accessed | tf_op | source)
XLA Modules:
  0.0 38.2 jit_solution(3014577357025094072)
XLA Ops:
  0.6 1.2 %scale.1 = (f32[256,128]{1,0:T(8,128)S(1)}, f32[256,128]{1,0:T(8,128)S(1)}, f32[256,128]{1,0:T(8,128)S(1)}, f32[256,128]{1,0:T(8,128)S(1)}, s32[2,128]{1,0:T(2,128)S(1)}) custom-call(f32[256,128]{1,0:T(8,128)} %refs_0_.1, f32[256,128]{1,0:T(8,128)} %refs_1_.1, s32[2,128]{1,0:T(2,128)} %bitcast.4, s32[2,128]{1,0:T(2,128)} %bitcast.5, s32[2,1,1,128]{3,2,1,0:T(1,128)} %refs_4_.1), custom_call_target="tpu_custom_call" | custom-call | bytes 1024 | tf_op jit(solution)/shard_map/scale/pallas_call | solution.py:262
  1.8 0.5 %collective-permute-start.6 = (f32[256,128]{1,0:T(8,128)S(1)}, f32[256,128]{1,0:T(8,128)S(1)}, u32[]{:S(2)}, u32[]{:S(2)}) collective-permute-start(f32[256,128]{1,0:T(8,128)S(1)} %get-tuple-element.25.refs_0_.own_ref), channel_id=1, source_target_pairs={{0,1},{1,0},{2,3},{3,2},{4,5},{5,4},{6,7},{7,6},{8,9},{9,8},{10,11... | collective-permute-start | bytes 393224 | tf_op jit(solution)/shard_map/gather/ppermute | solution.py:249
  2.3 3.7 %collective-permute-start = (f32[256,128]{1,0:T(8,128)S(1)}, f32[256,128]{1,0:T(8,128)S(1)}, u32[]{:S(2)}, u32[]{:S(2)}) collective-permute-start(f32[256,128]{1,0:T(8,128)S(1)} %get-tuple-element.25.refs_0_.own_ref), channel_id=1, source_target_pairs={{0,4},{1,5},{2,6},{3,7},{4,0},{5,1},{6,2},{7,3},{8,12},{9,13},{10,... | collective-permute-start | bytes 393224 | tf_op jit(solution)/shard_map/gather/ppermute | solution.py:249
  6.0 1.5 %collective-permute-start.1 = (f32[256,128]{1,0:T(8,128)S(1)}, f32[256,128]{1,0:T(8,128)S(1)}, u32[]{:S(2)}, u32[]{:S(2)}) collective-permute-start(f32[256,128]{1,0:T(8,128)S(1)} %get-tuple-element.26.refs_0_), channel_id=1, source_target_pairs={{0,8},{8,0},{16,24},{24,16},{1,9},{9,1},{17,25},{25,17},{2,10},{10... | collective-permute-start | bytes 393224 | tf_op jit(solution)/shard_map/gather/ppermute | solution.py:249
  7.5 1.5 %collective-permute-start.2 = (f32[256,128]{1,0:T(8,128)S(1)}, f32[256,128]{1,0:T(8,128)S(1)}, u32[]{:S(2)}, u32[]{:S(2)}) collective-permute-start(f32[256,128]{1,0:T(8,128)S(1)} %get-tuple-element.26.refs_0_), channel_id=1, source_target_pairs={{0,16},{8,24},{16,0},{24,8},{1,17},{9,25},{17,1},{25,9},{2,18},{10... | collective-permute-start | bytes 393224 | tf_op jit(solution)/shard_map/gather/ppermute | solution.py:249
  9.0 0.5 %collective-permute-start.3 = (f32[256,128]{1,0:T(8,128)S(1)}, f32[256,128]{1,0:T(8,128)S(1)}, u32[]{:S(2)}, u32[]{:S(2)}) collective-permute-start(f32[256,128]{1,0:T(8,128)S(1)} %get-tuple-element.26.refs_0_), channel_id=1, source_target_pairs={{0,24},{8,16},{16,8},{24,0},{1,25},{9,17},{17,9},{25,1},{2,26},{10... | collective-permute-start | bytes 393224 | tf_op jit(solution)/shard_map/gather/ppermute | solution.py:249
  9.5 0.0 collective-permute-done.6.refs_1_.beside_ref
  9.5 0.7 %collective-permute-start.7 = (f32[2,256,128]{2,1,0:T(8,128)S(1)}, f32[2,256,128]{2,1,0:T(8,128)S(1)}, u32[]{:S(2)}, u32[]{:S(2)}) collective-permute-start(f32[2,256,128]{2,1,0:T(8,128)S(1)} %gather.7), channel_id=1, source_target_pairs={{1,3},{3,1},{5,7},{7,5},{9,11},{11,9},{13,15},{15,13},{17,19},{19,... | collective-permute-start | bytes 786440 | tf_op jit(solution)/shard_map/gather/ppermute | solution.py:307
  10.8 3.8 %split.1 = (bf16[1024,2048]{1,0:T(8,128)(2,1)S(1)}, bf16[1024,2048]{1,0:T(8,128)(2,1)S(1)}) custom-call(s32[1,1]{1,0:T(1,128)S(6)} %copy.9.count_ref, s32[2,128]{1,0:T(2,128)S(1)} %get-tuple-element.23.plan_ref, f32[128,128,128]{2,1,0:T(8,128)} %bitcast.3), custom_call_target="tpu_custom_call" | custom-call | bytes 1024 | tf_op jit(solution)/shard_map/split/pallas_call | solution.py:262
  14.7 0.0 collective-permute-done.refs_0_
  14.7 1.6 %collective-permute-start.4 = (f32[256,128]{1,0:T(8,128)S(1)}, f32[256,128]{1,0:T(8,128)S(1)}, u32[]{:S(2)}, u32[]{:S(2)}) collective-permute-start(f32[256,128]{1,0:T(8,128)S(1)} %gather.5._.refs_1_.crossed_ref), channel_id=1, source_target_pairs={{0,2},{1,3},{2,0},{3,1},{4,6},{5,7},{6,4},{7,5},{8,10},{9,11},{10,... | collective-permute-start | bytes 393224 | tf_op jit(solution)/shard_map/gather/ppermute | solution.py:249
  16.3 0.0 collective-permute-done.1.refs_1_
  16.3 0.0 collective-permute-done.2.refs_2_
  16.3 0.0 collective-permute-done.3.refs_3_
  16.4 0.2 flip.1._.refs_0_
  16.6 0.0 collective-permute-done.7.refs_0_
  16.6 0.4 %collective-permute-start.8 = (f32[3,256,128]{2,1,0:T(8,128)S(1)}, f32[3,256,128]{2,1,0:T(8,128)S(1)}, u32[]{:S(2)}, u32[]{:S(2)}) collective-permute-start(f32[3,256,128]{2,1,0:T(8,128)S(1)} %gather.8.mine_ref), channel_id=1, source_target_pairs={{0,1},{1,0},{2,3},{3,2},{4,5},{5,4},{6,7},{7,6},{8,9},{9,8},{10,11... | collective-permute-start | bytes 1179656 | tf_op jit(solution)/shard_map/gather/ppermute | solution.py:249
  17.0 0.7 %backward.5._ = f32[2,256,128]{2,1,0:T(8,128)S(1)} custom-call(bf16[256,1024]{1,0:T(8,128)(2,1)S(1)} %flip.1._.refs_0_, bf16[256,1024]{1,0:T(8,128)(2,1)S(1)} %flip.1._.refs_0_, bf16[1024,2048]{1,0:T(8,128)(2,1)S(1)} %get-tuple-element.24._.refs_1_.refs_2_, bf16[1024,2048]{1,0:T(8,128)(2,1)S(1)} %get-tuple-element.27.refs_2_.refs_3_), custom_call_target="tpu_custom_call" | custom-call | bytes 1024 | tf_op jit(solution)/shard_map/backward/pallas_call | solution.py:262
  17.7 0.3 collective-permute-start.5
  17.9 0.7 %backward.6._.refs_0_ = f32[2,256,128]{2,1,0:T(8,128)S(1)} custom-call(f32[2,256,128]{2,1,0:T(8,128)S(1)} %backward.5._, bf16[256,1024]{1,0:T(8,128)(2,1)S(1)} %flip.1._.refs_0_, bf16[1024,2048]{1,0:T(8,128)(2,1)S(1)} %get-tuple-element.24._.refs_1_.refs_2_, bf16[1024,2048]{1,0:T(8,128)(2,1)S(1)} %get-tuple-element.27.refs_2_.refs_3_), custom_call_target="tpu_custom_call" | custom-call | bytes 1024 | tf_op jit(solution)/shard_map/backward/pallas_call | solution.py:262
  18.6 0.7 %backward.7._ = f32[2,256,128]{2,1,0:T(8,128)S(1)} custom-call(f32[2,256,128]{2,1,0:T(8,128)S(1)} %backward.6._.refs_0_, bf16[256,1024]{1,0:T(8,128)(2,1)S(1)} %flip.1._.refs_0_, bf16[1024,2048]{1,0:T(8,128)(2,1)S(1)} %get-tuple-element.24._.refs_1_.refs_2_, bf16[1024,2048]{1,0:T(8,128)(2,1)S(1)} %get-tuple-element.27.refs_2_.refs_3_), custom_call_target="tpu_custom_call" | custom-call | bytes 1024 | tf_op jit(solution)/shard_map/backward/pallas_call | solution.py:262
  19.3 0.9 %collective-permute-done.4.refs_0_ = f32[256,128]{1,0:T(8,128)S(1)} collective-permute-done((f32[256,128]{1,0:T(8,128)S(1)}, f32[256,128]{1,0:T(8,128)S(1)}, u32[]{:S(2)}, u32[]{:S(2)}) %collective-permute-start.4) | collective-permute-done | bytes 131104 | tf_op jit(solution)/shard_map/gather/ppermute | solution.py:249
  20.3 0.0 collective-permute-done.5.refs_1_
  20.3 2.1 %collective-permute-start.9 = (f32[256,128]{1,0:T(8,128)S(1)}, f32[256,128]{1,0:T(8,128)S(1)}, u32[]{:S(2)}, u32[]{:S(2)}) collective-permute-start(f32[256,128]{1,0:T(8,128)S(1)} %get-tuple-element.32), channel_id=1, source_target_pairs={{0,2},{1,3},{2,0},{3,1},{4,6},{5,7},{6,4},{7,5},{8,10},{9,11},{10,... | collective-permute-start | bytes 393224 | tf_op jit(solution)/shard_map/reduce/ppermute | solution.py:249
  22.4 0.0 collective-permute-start.10
  22.5 0.5 %collective-permute-start.11 = (f32[2,256,128]{2,1,0:T(8,128)S(1)}, f32[2,256,128]{2,1,0:T(8,128)S(1)}, u32[]{:S(2)}, u32[]{:S(2)}) collective-permute-start(f32[2,256,128]{2,1,0:T(8,128)S(1)} %backward.7._), channel_id=1, source_target_pairs={{0,1},{1,0},{2,3},{3,2},{4,5},{5,4},{6,7},{7,6},{8,9},{9,8},{10,11... | collective-permute-start | bytes 786440 | tf_op jit(solution)/shard_map/reduce/ppermute | solution.py:249
  23.0 0.7 %backward.9._.refs_0_ = f32[2,256,128]{2,1,0:T(8,128)S(1)} custom-call(f32[256,128]{1,0:T(8,128)S(1)} %get-tuple-element.28._.refs_0_, bf16[256,1024]{1,0:T(8,128)(2,1)S(1)} %flip.1._.refs_0_, bf16[1024,2048]{1,0:T(8,128)(2,1)S(1)} %get-tuple-element.24._.refs_1_.refs_2_, bf16[1024,2048]{1,0:T(8,128)(2,1)S(1)} %get-tuple-element.27.refs_2_.refs_3_), custom_call_target="tpu_custom_call" | custom-call | bytes 1024 | tf_op jit(solution)/shard_map/backward/pallas_call | solution.py:262
  23.7 0.0 collective-permute-done.8.theirs_ref
  23.7 0.1 gather.9
  23.7 1.9 %forward.2 = (f32[256,128]{1,0:T(8,128)S(1)}, f32[256,128]{1,0:T(8,128)S(1)}, f32[256,128]{1,0:T(8,128)S(1)}, f32[256,128]{1,0:T(8,128)S(1)}) custom-call(f32[2,256,128]{2,1,0:T(8,128)S(1)} %backward.9._.refs_0_, f32[3,256,128]{2,1,0:T(8,128)S(1)} %get-tuple-element.29.refs_0_, f32[3,256,128]{2,1,0:T(8,128)S(1)} %get-tuple-element.30.refs_1_, ...), custom_call_target="tpu_custom_call" | custom-call | bytes 1024 | tf_op jit(solution)/shard_map/forward/pallas_call | solution.py:262
  25.6 0.9 %collective-permute-done.9.refs_1_ = f32[256,128]{1,0:T(8,128)S(1)} collective-permute-done((f32[256,128]{1,0:T(8,128)S(1)}, f32[256,128]{1,0:T(8,128)S(1)}, u32[]{:S(2)}, u32[]{:S(2)}) %collective-permute-start.9) | collective-permute-done | bytes 131104 | tf_op jit(solution)/shard_map/reduce/ppermute | solution.py:249
  26.5 0.6 %collective-permute-start.12 = (f32[256,128]{1,0:T(8,128)S(1)}, f32[256,128]{1,0:T(8,128)S(1)}, u32[]{:S(2)}, u32[]{:S(2)}) collective-permute-start(f32[256,128]{1,0:T(8,128)S(1)} %reduce.3._), channel_id=1, source_target_pairs={{0,4},{1,5},{2,6},{3,7},{4,0},{5,1},{6,2},{7,3},{8,12},{9,13},{10,... | collective-permute-start | bytes 393224 | tf_op jit(solution)/shard_map/reduce/ppermute | solution.py:249
  27.1 0.0 collective-permute-done.10.refs_1_
  27.1 0.7 %forward.3 = (f32[256,128]{1,0:T(8,128)S(1)}, f32[256,128]{1,0:T(8,128)S(1)}, f32[256,128]{1,0:T(8,128)S(1)}, f32[256,128]{1,0:T(8,128)S(1)}) custom-call(f32[256,128]{1,0:T(8,128)S(1)} %reduce.3._, f32[1,256,128]{2,1,0:T(8,128)S(1)} %gather.6._.refs_0_, f32[1,256,128]{2,1,0:T(8,128)S(1)} %collective-permute-done.10.refs_1_, ...), custom_call_target="tpu_custom_call" | custom-call | flops 2000000000 | bytes 1024 | tf_op jit(solution)/shard_map/forward/pallas_call | solution.py:262
  27.8 1.6 %collective-permute-start.13 = (f32[256,128]{1,0:T(8,128)S(1)}, f32[256,128]{1,0:T(8,128)S(1)}, u32[]{:S(2)}, u32[]{:S(2)}) collective-permute-start(f32[256,128]{1,0:T(8,128)S(1)} %get-tuple-element.38), channel_id=1, source_target_pairs={{0,8},{8,0},{16,24},{24,16},{1,9},{9,1},{17,25},{25,17},{2,10},{10... | collective-permute-start | bytes 393224 | tf_op jit(solution)/shard_map/reduce/ppermute | solution.py:249
  29.4 1.6 %collective-permute-start.14 = (f32[256,128]{1,0:T(8,128)S(1)}, f32[256,128]{1,0:T(8,128)S(1)}, u32[]{:S(2)}, u32[]{:S(2)}) collective-permute-start(f32[256,128]{1,0:T(8,128)S(1)} %get-tuple-element.39), channel_id=1, source_target_pairs={{0,16},{8,24},{16,0},{24,8},{1,17},{9,25},{17,1},{25,9},{2,18},{10... | collective-permute-start | bytes 393224 | tf_op jit(solution)/shard_map/reduce/ppermute | solution.py:249
  31.0 0.4 collective-permute-start.15
  31.4 0.0 collective-permute-done.11.refs_1_
  31.4 1.0 %collective-permute-start.16 = (f32[256,128]{1,0:T(8,128)S(1)}, f32[256,128]{1,0:T(8,128)S(1)}, u32[]{:S(2)}, u32[]{:S(2)}) collective-permute-start(f32[256,128]{1,0:T(8,128)S(1)} %get-tuple-element.43), channel_id=1, source_target_pairs={{0,2},{1,3},{2,0},{3,1},{4,6},{5,7},{6,4},{7,5},{8,10},{9,11},{10,... | collective-permute-start | bytes 393224 | tf_op jit(solution)/shard_map/reduce/ppermute | solution.py:249
  32.4 2.9 %collective-permute-done.12.y_ref = f32[256,128]{1,0:T(8,128)S(1)} collective-permute-done((f32[256,128]{1,0:T(8,128)S(1)}, f32[256,128]{1,0:T(8,128)S(1)}, u32[]{:S(2)}, u32[]{:S(2)}) %collective-permute-start.12) | collective-permute-done | bytes 131104 | tf_op jit(solution)/shard_map/reduce/ppermute | solution.py:249
  35.3 0.0 collective-permute-done.13.refs_1_
  35.4 1.8 %collective-permute-done.14.refs_2_ = f32[256,128]{1,0:T(8,128)S(1)} collective-permute-done((f32[256,128]{1,0:T(8,128)S(1)}, f32[256,128]{1,0:T(8,128)S(1)}, u32[]{:S(2)}, u32[]{:S(2)}) %collective-permute-start.14) | collective-permute-done | bytes 131104 | tf_op jit(solution)/shard_map/reduce/ppermute | solution.py:249
  37.2 0.0 collective-permute-done.15.refs_3_
  37.2 0.2 collective-permute-done.16.refs_1_
  37.4 0.7 %finish.3 = (f32[256,128]{1,0:T(8,128)}, f32[256,128]{1,0:T(8,128)}) custom-call(f32[256,128]{1,0:T(8,128)S(1)} %finish.2.row_ref, f32[256,128]{1,0:T(8,128)S(1)} %get-tuple-element.41.row_factor_ref, f32[256,128]{1,0:T(8,128)S(1)} %get-tuple-element.42.col_factor_ref, f32[256,128]{1,0:T(8,128)S(1)} %reduce.5._.refs_0_, ...), custom_call_target="tpu_custom_call" | custom-call | bytes 1024 | tf_op jit(solution)/shard_map/finish/pallas_call | solution.py:262
  (9 shorter events, 0.2 us)
Async XLA Ops:
  1.8 7.7 %collective-permute-start.6 = (f32[256,128]{1,0:T(8,128)S(1)}, f32[256,128]{1,0:T(8,128)S(1)}, u32[]{:S(2)}, u32[]{:S(2)}) collective-permute-start(f32[256,128]{1,0:T(8,128)S(1)} %get-tuple-element.25.refs_0_.own_ref), channel_id=1, source_target_pairs={{0,1},{1,0},{2,3},{3,2},{4,5},{5,4},{6,7},{7,6},{8,9},{9,8},{10,11... | collective-permute-start | bytes 393224 | tf_op jit(solution)/shard_map/gather/ppermute | solution.py:249
  2.3 12.4 %collective-permute-start = (f32[256,128]{1,0:T(8,128)S(1)}, f32[256,128]{1,0:T(8,128)S(1)}, u32[]{:S(2)}, u32[]{:S(2)}) collective-permute-start(f32[256,128]{1,0:T(8,128)S(1)} %get-tuple-element.25.refs_0_.own_ref), channel_id=1, source_target_pairs={{0,4},{1,5},{2,6},{3,7},{4,0},{5,1},{6,2},{7,3},{8,12},{9,13},{10,... | collective-permute-start | bytes 393224 | tf_op jit(solution)/shard_map/gather/ppermute | solution.py:249
  6.0 10.4 %collective-permute-start.1 = (f32[256,128]{1,0:T(8,128)S(1)}, f32[256,128]{1,0:T(8,128)S(1)}, u32[]{:S(2)}, u32[]{:S(2)}) collective-permute-start(f32[256,128]{1,0:T(8,128)S(1)} %get-tuple-element.26.refs_0_), channel_id=1, source_target_pairs={{0,8},{8,0},{16,24},{24,16},{1,9},{9,1},{17,25},{25,17},{2,10},{10... | collective-permute-start | bytes 393224 | tf_op jit(solution)/shard_map/gather/ppermute | solution.py:249
  7.5 8.9 %collective-permute-start.2 = (f32[256,128]{1,0:T(8,128)S(1)}, f32[256,128]{1,0:T(8,128)S(1)}, u32[]{:S(2)}, u32[]{:S(2)}) collective-permute-start(f32[256,128]{1,0:T(8,128)S(1)} %get-tuple-element.26.refs_0_), channel_id=1, source_target_pairs={{0,16},{8,24},{16,0},{24,8},{1,17},{9,25},{17,1},{25,9},{2,18},{10... | collective-permute-start | bytes 393224 | tf_op jit(solution)/shard_map/gather/ppermute | solution.py:249
  9.0 7.4 %collective-permute-start.3 = (f32[256,128]{1,0:T(8,128)S(1)}, f32[256,128]{1,0:T(8,128)S(1)}, u32[]{:S(2)}, u32[]{:S(2)}) collective-permute-start(f32[256,128]{1,0:T(8,128)S(1)} %get-tuple-element.26.refs_0_), channel_id=1, source_target_pairs={{0,24},{8,16},{16,8},{24,0},{1,25},{9,17},{17,9},{25,1},{2,26},{10... | collective-permute-start | bytes 393224 | tf_op jit(solution)/shard_map/gather/ppermute | solution.py:249
  9.5 7.1 %collective-permute-start.7 = (f32[2,256,128]{2,1,0:T(8,128)S(1)}, f32[2,256,128]{2,1,0:T(8,128)S(1)}, u32[]{:S(2)}, u32[]{:S(2)}) collective-permute-start(f32[2,256,128]{2,1,0:T(8,128)S(1)} %gather.7), channel_id=1, source_target_pairs={{1,3},{3,1},{5,7},{7,5},{9,11},{11,9},{13,15},{15,13},{17,19},{19,... | collective-permute-start | bytes 786440 | tf_op jit(solution)/shard_map/gather/ppermute | solution.py:307
  14.7 5.6 %collective-permute-start.4 = (f32[256,128]{1,0:T(8,128)S(1)}, f32[256,128]{1,0:T(8,128)S(1)}, u32[]{:S(2)}, u32[]{:S(2)}) collective-permute-start(f32[256,128]{1,0:T(8,128)S(1)} %gather.5._.refs_1_.crossed_ref), channel_id=1, source_target_pairs={{0,2},{1,3},{2,0},{3,1},{4,6},{5,7},{6,4},{7,5},{8,10},{9,11},{10,... | collective-permute-start | bytes 393224 | tf_op jit(solution)/shard_map/gather/ppermute | solution.py:249
  16.6 7.0 %collective-permute-start.8 = (f32[3,256,128]{2,1,0:T(8,128)S(1)}, f32[3,256,128]{2,1,0:T(8,128)S(1)}, u32[]{:S(2)}, u32[]{:S(2)}) collective-permute-start(f32[3,256,128]{2,1,0:T(8,128)S(1)} %gather.8.mine_ref), channel_id=1, source_target_pairs={{0,1},{1,0},{2,3},{3,2},{4,5},{5,4},{6,7},{7,6},{8,9},{9,8},{10,11... | collective-permute-start | bytes 1179656 | tf_op jit(solution)/shard_map/gather/ppermute | solution.py:249
  17.7 2.6 %collective-permute-start.5 = (f32[2,256,128]{2,1,0:T(8,128)S(1)}, f32[2,256,128]{2,1,0:T(8,128)S(1)}, u32[]{:S(2)}, u32[]{:S(2)}) collective-permute-start(f32[2,256,128]{2,1,0:T(8,128)S(1)} %backward.5._), channel_id=1, source_target_pairs={{0,1},{1,0},{2,3},{3,2},{4,5},{5,4},{6,7},{7,6},{8,9},{9,8},{10,11... | collective-permute-start | bytes 786440 | tf_op jit(solution)/shard_map/backward/ppermute | solution.py:249
  20.3 6.2 %collective-permute-start.9 = (f32[256,128]{1,0:T(8,128)S(1)}, f32[256,128]{1,0:T(8,128)S(1)}, u32[]{:S(2)}, u32[]{:S(2)}) collective-permute-start(f32[256,128]{1,0:T(8,128)S(1)} %get-tuple-element.32), channel_id=1, source_target_pairs={{0,2},{1,3},{2,0},{3,1},{4,6},{5,7},{6,4},{7,5},{8,10},{9,11},{10,... | collective-permute-start | bytes 393224 | tf_op jit(solution)/shard_map/reduce/ppermute | solution.py:249
  22.4 4.6 %collective-permute-start.10 = (f32[1,256,128]{2,1,0:T(8,128)S(1)}, f32[1,256,128]{2,1,0:T(8,128)S(1)}, u32[]{:S(2)}, u32[]{:S(2)}) collective-permute-start(f32[1,256,128]{2,1,0:T(8,128)S(1)} %gather.6._.refs_0_), channel_id=1, source_target_pairs={{0,1},{1,0},{2,3},{3,2},{4,5},{5,4},{6,7},{7,6},{8,9},{9,8},{10,11... | collective-permute-start | bytes 393224 | tf_op jit(solution)/shard_map/gather/ppermute | solution.py:249
  22.5 8.9 %collective-permute-start.11 = (f32[2,256,128]{2,1,0:T(8,128)S(1)}, f32[2,256,128]{2,1,0:T(8,128)S(1)}, u32[]{:S(2)}, u32[]{:S(2)}) collective-permute-start(f32[2,256,128]{2,1,0:T(8,128)S(1)} %backward.7._), channel_id=1, source_target_pairs={{0,1},{1,0},{2,3},{3,2},{4,5},{5,4},{6,7},{7,6},{8,9},{9,8},{10,11... | collective-permute-start | bytes 786440 | tf_op jit(solution)/shard_map/reduce/ppermute | solution.py:249
  26.5 8.8 %collective-permute-start.12 = (f32[256,128]{1,0:T(8,128)S(1)}, f32[256,128]{1,0:T(8,128)S(1)}, u32[]{:S(2)}, u32[]{:S(2)}) collective-permute-start(f32[256,128]{1,0:T(8,128)S(1)} %reduce.3._), channel_id=1, source_target_pairs={{0,4},{1,5},{2,6},{3,7},{4,0},{5,1},{6,2},{7,3},{8,12},{9,13},{10,... | collective-permute-start | bytes 393224 | tf_op jit(solution)/shard_map/reduce/ppermute | solution.py:249
  27.8 7.5 %collective-permute-start.13 = (f32[256,128]{1,0:T(8,128)S(1)}, f32[256,128]{1,0:T(8,128)S(1)}, u32[]{:S(2)}, u32[]{:S(2)}) collective-permute-start(f32[256,128]{1,0:T(8,128)S(1)} %get-tuple-element.38), channel_id=1, source_target_pairs={{0,8},{8,0},{16,24},{24,16},{1,9},{9,1},{17,25},{25,17},{2,10},{10... | collective-permute-start | bytes 393224 | tf_op jit(solution)/shard_map/reduce/ppermute | solution.py:249
  29.4 7.8 %collective-permute-start.14 = (f32[256,128]{1,0:T(8,128)S(1)}, f32[256,128]{1,0:T(8,128)S(1)}, u32[]{:S(2)}, u32[]{:S(2)}) collective-permute-start(f32[256,128]{1,0:T(8,128)S(1)} %get-tuple-element.39), channel_id=1, source_target_pairs={{0,16},{8,24},{16,0},{24,8},{1,17},{9,25},{17,1},{25,9},{2,18},{10... | collective-permute-start | bytes 393224 | tf_op jit(solution)/shard_map/reduce/ppermute | solution.py:249
  31.0 6.2 %collective-permute-start.15 = (f32[256,128]{1,0:T(8,128)S(1)}, f32[256,128]{1,0:T(8,128)S(1)}, u32[]{:S(2)}, u32[]{:S(2)}) collective-permute-start(f32[256,128]{1,0:T(8,128)S(1)} %get-tuple-element.40), channel_id=1, source_target_pairs={{0,24},{8,16},{16,8},{24,0},{1,25},{9,17},{17,9},{25,1},{2,26},{10... | collective-permute-start | bytes 393224 | tf_op jit(solution)/shard_map/reduce/ppermute | solution.py:249
  31.4 6.0 %collective-permute-start.16 = (f32[256,128]{1,0:T(8,128)S(1)}, f32[256,128]{1,0:T(8,128)S(1)}, u32[]{:S(2)}, u32[]{:S(2)}) collective-permute-start(f32[256,128]{1,0:T(8,128)S(1)} %get-tuple-element.43), channel_id=1, source_target_pairs={{0,2},{1,3},{2,0},{3,1},{4,6},{5,7},{6,4},{7,5},{8,10},{9,11},{10,... | collective-permute-start | bytes 393224 | tf_op jit(solution)/shard_map/reduce/ppermute | solution.py:249

commit v13 on v11

--- a/solution.py
+++ b/solution.py
@@ -171,9 +171,8 @@
             out_ref[at, pl.ds(row, tile), :] = total[:, row : row + tile].T
 
 
-def forward_kernel(first, count, bands, *refs):
-    embed_refs, (high_ref, low_ref) = refs[:count], refs[count : count + 2]
-    before_refs, out_refs, panel = refs[count + 2 : -1 - bands], refs[-1 - bands : -1], refs[-1]
+def forward_kernel(count, *refs):
+    embed_refs, (high_ref, low_ref), out_refs, panel = refs[:count], refs[count : count + 2], refs[count + 2 : -1], refs[-1]
     _, shard, width = embed_refs[0].shape
     done = 0
     for embeds_ref in embed_refs:
@@ -182,14 +181,10 @@
             panel[pl.ds(done, shard), :width] = high
             panel[pl.ds(done, shard), width:] = low
             done += shard
-    cols = pl.ds(first * shard, done)
     for at, out_ref in enumerate(out_refs):
         rows = pl.ds(at * shard, shard)
-        both = product(high_ref[rows, cols], panel[...])
-        total = both[:, :width] + both[:, width:] + product(low_ref[rows, cols], panel[:, :width])
-        if before_refs:
-            total = total + before_refs[at][...]
-        out_ref[...] = total
+        both = product(high_ref[rows, :], panel[...])
+        out_ref[...] = both[:, :width] + both[:, width:] + product(low_ref[rows, :], panel[:, :width])
 
 
 def slots_kernel(tiles, pairs, coords_ref, count_ref, values_ref, embed_ref, grad_ref, forward_ref, backward_ref):
@@ -308,10 +303,10 @@
             mask *= 2
         return [parts[0], *got]
 
-    def total(parts, after):
+    def total(parts, after, flops=0):
         out, *rest = parts
         for part in rest:
-            out = call(add_kernel, block, (out, part), after=after)
+            out = call(add_kernel, block, (out, part), after=after, flops=flops)
         return out
 
     if dense:
@@ -360,16 +355,14 @@
                 return core * count + distance
             return 2 * count + core * (pairs - count) + distance - count
 
-        def forward_part(embeds, first, before=(), after=None, flops=0):
-            count = sum(x.shape[0] for x in embeds)
+        def forward(embeds, after):
             return call(
-                functools.partial(forward_kernel, first, len(embeds), n_row),
+                functools.partial(forward_kernel, len(embeds)),
                 (block,) * n_row,
-                (*embeds, high, low, *before),
+                (*embeds, high, low),
                 mebibytes=24,
-                scratch=[pltpu.VMEM((count * shard, 2 * width), BF16)],
+                scratch=[pltpu.VMEM((n_cols, 2 * width), BF16)],
                 after=after,
-                flops=flops,
             )
 
         with jax.named_scope("backward"):
@@ -377,18 +370,16 @@
             far_sent = backward_part(far, 1, early)
             far_kept = backward_part(far, 0, far_sent)
             sent = backward_part(close, 1, far_kept)
+            kept = backward_part(close, 0, sent)
         with jax.named_scope("gather"):
-            late = call(copy_kernel, blocks(half - 1), late, after=sent, flops=2 * 10**9)
+            late = call(copy_kernel, blocks(half - 1), late, after=kept, flops=2 * 10**9)
             other_late = swap(late, "col", 1)
         with jax.named_scope("backward"):
             far_sums = chip_sums(far_kept, far_sent, late)
-            kept = backward_part(close, 0, far_sums[0])
         with jax.named_scope("forward"):
-            forwards = forward_part([early, other_early], 0, after=kept)
+            forwards = forward([early, other_early, late, other_late], far_sums[0])
         with jax.named_scope("reduce"):
-            crossing = total(halved(far_sums, forwards[0]), forwards[0])
-        with jax.named_scope("forward"):
-            forwards = forward_part([late, other_late], 2 * (half + 1), forwards, crossing, 2 * 10**9)
+            crossing = total(halved(far_sums, forwards[0]), forwards[0], 10**9)
         with jax.named_scope("reduce"):
             close_sums = chip_sums(kept, sent, forwards[0])
             after = None
@@ -431,11 +422,10 @@
 
     with jax.named_scope("reduce"):
         mine, *grad_parts = halved(close_sums, after)
-        mine = total([mine, swap(crossing, "col", 2 * half)], None)
-        row_parts = [forwards[0]] + [swap(forwards[k], "row", k) for k in range(1, n_row)]
-
-    with jax.named_scope("finish"):
-        row_sum = call(sum_kernel, block, row_parts, after=mine)
+        first = [swap(forwards[k], "row", k) for k in range(1, n_row - 1)]
+        row_sum = call(sum_kernel, block, [forwards[0], *first])
+        mine = total([mine, swap(crossing, "col", 2 * half)], row_sum)
+        row_sum = call(sum_kernel, block, [row_sum, swap(forwards[-1], "row", n_row - 1)], after=mine)
         return call(
             finish_kernel, (block, block), (row_sum, row_factor, col_factor, mine, *grad_parts), mebibytes=4
         )

time: 36.5 us -> 37.3 us (1.022)
  starting transfers between devices: 15.4 us -> 17.5 us
  waiting for transfers between devices: 7.81 us -> 6.96 us
    ppermute x16, starting transfers between devices: 15.4 us -> 17.5 us  [swap(): lax.ppermute(x, axis, [(at, at ^ mask) for at in range(lax.axis_size(axis...]
    ppermute x16, waiting for transfers between devices: 7.81 us -> 6.96 us  [swap(): lax.ppermute(x, axis, [(at, at ^ mask) for at in range(lax.axis_size(axis...]
  transfers between devices with their start and end apart: 16 -> 16, of which waited for: 5 -> 3; matrix products, arithmetic and copies ran while one was open for 0% -> 0% of each run, Pallas kernels for 26% -> 25%
where the time goes in v13:
time: 37.3 us; the launch traced here: 37.1 us
  starting transfers between devices  17.5 us (47%)
  Pallas kernels  11.3 us (30%)
  waiting for transfers between devices  6.96 us (19%)
  between operations  1.48 us (4%)
    ppermute x16, starting transfers between devices, swap(): lax.ppermute(x, axis, [(at, at ^ mask) for at in range(lax.axis_size(axis...  17.5 us
    pallas_call x18, Pallas kernels, call(): pl.pallas_call(body, out_shape=out_shape, in_specs=specs, out_specs=tuple...  11.3 us
    ppermute x16, waiting for transfers between devices, swap(): lax.ppermute(x, axis, [(at, at ^ mask) for at in range(lax.axis_size(axis...  6.96 us
  transfers between devices with their start and end apart: 16, of which 3 were waited for; matrix products, arithmetic and copies ran while one was open for 0% of the time, Pallas kernels for 25%

profile of v13, /device:TPU:0, one launch (start us, length us, event | category | flops | bytes accessed | tf_op | source)
XLA Modules:
  0.0 37.1 jit_solution(4275399198900424118)
XLA Ops:
  0.6 1.2 %scale.1 = (f32[256,128]{1,0:T(8,128)S(1)}, f32[256,128]{1,0:T(8,128)S(1)}, f32[256,128]{1,0:T(8,128)S(1)}, f32[256,128]{1,0:T(8,128)S(1)}, s32[2,128]{1,0:T(2,128)S(1)}) custom-call(f32[256,128]{1,0:T(8,128)} %refs_0_.1, f32[256,128]{1,0:T(8,128)} %refs_1_.1, s32[2,128]{1,0:T(2,128)} %bitcast.4, s32[2,128]{1,0:T(2,128)} %bitcast.5, s32[2,1,1,128]{3,2,1,0:T(1,128)} %refs_4_.1), custom_call_target="tpu_custom_call" | custom-call | bytes 1024 | tf_op jit(solution)/shard_map/scale/pallas_call | solution.py:229
  1.8 4.1 %collective-permute-start = (f32[256,128]{1,0:T(8,128)S(1)}, f32[256,128]{1,0:T(8,128)S(1)}, u32[]{:S(2)}, u32[]{:S(2)}) collective-permute-start(f32[256,128]{1,0:T(8,128)S(1)} %get-tuple-element.19.refs_0_), channel_id=1, source_target_pairs={{0,4},{1,5},{2,6},{3,7},{4,0},{5,1},{6,2},{7,3},{8,12},{9,13},{10,... | collective-permute-start | bytes 393224 | tf_op jit(solution)/shard_map/gather/ppermute | solution.py:216
  5.9 2.4 %collective-permute-start.3 = (f32[256,128]{1,0:T(8,128)S(1)}, f32[256,128]{1,0:T(8,128)S(1)}, u32[]{:S(2)}, u32[]{:S(2)}) collective-permute-start(f32[256,128]{1,0:T(8,128)S(1)} %get-tuple-element.20.refs_0_), channel_id=1, source_target_pairs={{0,24},{8,16},{16,8},{24,0},{1,25},{9,17},{17,9},{25,1},{2,26},{10... | collective-permute-start | bytes 393224 | tf_op jit(solution)/shard_map/gather/ppermute | solution.py:216
  8.3 0.5 %collective-permute-start.2 = (f32[256,128]{1,0:T(8,128)S(1)}, f32[256,128]{1,0:T(8,128)S(1)}, u32[]{:S(2)}, u32[]{:S(2)}) collective-permute-start(f32[256,128]{1,0:T(8,128)S(1)} %get-tuple-element.20.refs_0_), channel_id=1, source_target_pairs={{0,16},{8,24},{16,0},{24,8},{1,17},{9,25},{17,1},{25,9},{2,18},{10... | collective-permute-start | bytes 393224 | tf_op jit(solution)/shard_map/gather/ppermute | solution.py:216
  8.9 0.5 %collective-permute-start.1 = (f32[256,128]{1,0:T(8,128)S(1)}, f32[256,128]{1,0:T(8,128)S(1)}, u32[]{:S(2)}, u32[]{:S(2)}) collective-permute-start(f32[256,128]{1,0:T(8,128)S(1)} %get-tuple-element.20.refs_0_), channel_id=1, source_target_pairs={{0,8},{8,0},{16,24},{24,16},{1,9},{9,1},{17,25},{25,17},{2,10},{10... | collective-permute-start | bytes 393224 | tf_op jit(solution)/shard_map/gather/ppermute | solution.py:216
  9.4 1.6 %collective-permute-start.4 = (f32[256,128]{1,0:T(8,128)S(1)}, f32[256,128]{1,0:T(8,128)S(1)}, u32[]{:S(2)}, u32[]{:S(2)}) collective-permute-start(f32[256,128]{1,0:T(8,128)S(1)} %get-tuple-element.19.refs_0_), channel_id=1, source_target_pairs={{0,2},{1,3},{2,0},{3,1},{4,6},{5,7},{6,4},{7,5},{8,10},{9,11},{10,... | collective-permute-start | bytes 393224 | tf_op jit(solution)/shard_map/gather/ppermute | solution.py:216
  11.6 3.8 %split.1 = (bf16[1024,2048]{1,0:T(8,128)(2,1)S(1)}, bf16[1024,2048]{1,0:T(8,128)(2,1)S(1)}) custom-call(s32[1,1]{1,0:T(1,128)S(6)} %copy.9.count_ref, s32[2,128]{1,0:T(2,128)S(1)} %get-tuple-element.17.plan_ref, f32[128,128,128]{2,1,0:T(8,128)} %bitcast.3), custom_call_target="tpu_custom_call" | custom-call | bytes 1024 | tf_op jit(solution)/shard_map/split/pallas_call | solution.py:229
  15.5 0.0 collective-permute-done.refs_0_
  15.5 0.1 collective-permute-start.5
  15.6 0.0 collective-permute-done.3.refs_3_
  15.6 0.0 collective-permute-done.2.refs_2_
  15.6 0.0 collective-permute-done.1.refs_1_
  15.6 0.2 flip.1._.refs_0_
  15.8 0.0 collective-permute-done.4.refs_1_
  15.9 0.1 collective-permute-start.7
  15.9 0.7 %backward.5._ = f32[2,256,128]{2,1,0:T(8,128)S(1)} custom-call(f32[3,256,128]{2,1,0:T(8,128)S(1)} %gather.4._.refs_0_, bf16[256,1024]{1,0:T(8,128)(2,1)S(1)} %flip.1._.refs_0_, bf16[1024,2048]{1,0:T(8,128)(2,1)S(1)} %get-tuple-element.18._.refs_1_.refs_4_, bf16[1024,2048]{1,0:T(8,128)(2,1)S(1)} %get-tuple-element.21.refs_2_.refs_5_), custom_call_target="tpu_custom_call" | custom-call | bytes 1024 | tf_op jit(solution)/shard_map/backward/pallas_call | solution.py:229
  16.6 0.6 %collective-permute-start.6 = (f32[2,256,128]{2,1,0:T(8,128)S(1)}, f32[2,256,128]{2,1,0:T(8,128)S(1)}, u32[]{:S(2)}, u32[]{:S(2)}) collective-permute-start(f32[2,256,128]{2,1,0:T(8,128)S(1)} %backward.5._), channel_id=1, source_target_pairs={{0,1},{1,0},{2,3},{3,2},{4,5},{5,4},{6,7},{7,6},{8,9},{9,8},{10,11... | collective-permute-start | bytes 786440 | tf_op jit(solution)/shard_map/backward/ppermute | solution.py:216
  17.2 0.7 %backward.6._.refs_0_ = f32[2,256,128]{2,1,0:T(8,128)S(1)} custom-call(f32[2,256,128]{2,1,0:T(8,128)S(1)} %backward.5._, bf16[256,1024]{1,0:T(8,128)(2,1)S(1)} %flip.1._.refs_0_, bf16[1024,2048]{1,0:T(8,128)(2,1)S(1)} %get-tuple-element.18._.refs_1_.refs_4_, bf16[1024,2048]{1,0:T(8,128)(2,1)S(1)} %get-tuple-element.21.refs_2_.refs_5_), custom_call_target="tpu_custom_call" | custom-call | bytes 1024 | tf_op jit(solution)/shard_map/backward/pallas_call | solution.py:229
  17.9 0.7 %backward.7._ = f32[2,256,128]{2,1,0:T(8,128)S(1)} custom-call(f32[2,256,128]{2,1,0:T(8,128)S(1)} %backward.6._.refs_0_, bf16[256,1024]{1,0:T(8,128)(2,1)S(1)} %flip.1._.refs_0_, bf16[1024,2048]{1,0:T(8,128)(2,1)S(1)} %get-tuple-element.18._.refs_1_.refs_4_, bf16[1024,2048]{1,0:T(8,128)(2,1)S(1)} %get-tuple-element.21.refs_2_.refs_5_), custom_call_target="tpu_custom_call" | custom-call | bytes 1024 | tf_op jit(solution)/shard_map/backward/pallas_call | solution.py:229
  18.6 0.7 %backward.8._.refs_0_ = f32[2,256,128]{2,1,0:T(8,128)S(1)} custom-call(f32[2,256,128]{2,1,0:T(8,128)S(1)} %backward.7._, bf16[256,1024]{1,0:T(8,128)(2,1)S(1)} %flip.1._.refs_0_, bf16[1024,2048]{1,0:T(8,128)(2,1)S(1)} %get-tuple-element.18._.refs_1_.refs_4_, bf16[1024,2048]{1,0:T(8,128)(2,1)S(1)} %get-tuple-element.21.refs_2_.refs_5_), custom_call_target="tpu_custom_call" | custom-call | bytes 1024 | tf_op jit(solution)/shard_map/backward/pallas_call | solution.py:229
  19.3 0.1 collective-permute-start.11
  19.4 1.2 %collective-permute-done.5.refs_0_ = f32[256,128]{1,0:T(8,128)S(1)} collective-permute-done((f32[256,128]{1,0:T(8,128)S(1)}, f32[256,128]{1,0:T(8,128)S(1)}, u32[]{:S(2)}, u32[]{:S(2)}) %collective-permute-start.5) | collective-permute-done | bytes 131104 | tf_op jit(solution)/shard_map/gather/ppermute | solution.py:216
  20.5 0.1 collective-permute-start.8
  20.6 0.0 collective-permute-done.6.refs_1_
  20.7 1.4 %collective-permute-start.12 = (f32[256,128]{1,0:T(8,128)S(1)}, f32[256,128]{1,0:T(8,128)S(1)}, u32[]{:S(2)}, u32[]{:S(2)}) collective-permute-start(f32[256,128]{1,0:T(8,128)S(1)} %get-tuple-element.27), channel_id=1, source_target_pairs={{0,2},{1,3},{2,0},{3,1},{4,6},{5,7},{6,4},{7,5},{8,10},{9,11},{10,... | collective-permute-start | bytes 393224 | tf_op jit(solution)/shard_map/reduce/ppermute | solution.py:216
  22.0 0.0 collective-permute-done.8.refs_3_
  22.0 0.0 collective-permute-done.7.refs_1_
  22.0 2.4 %forward.1 = (f32[256,128]{1,0:T(8,128)S(1)}, f32[256,128]{1,0:T(8,128)S(1)}, f32[256,128]{1,0:T(8,128)S(1)}, f32[256,128]{1,0:T(8,128)S(1)}) custom-call(f32[256,128]{1,0:T(8,128)S(1)} %get-tuple-element.22._.refs_0_, f32[3,256,128]{2,1,0:T(8,128)S(1)} %gather.4._.refs_0_, f32[3,256,128]{2,1,0:T(8,128)S(1)} %collective-permute-done.7.refs_1_, ...), custom_call_target="tpu_custom_call" | custom-call | bytes 1024 | tf_op jit(solution)/shard_map/forward/pallas_call | solution.py:229
  24.4 0.6 %collective-permute-start.9 = (f32[256,128]{1,0:T(8,128)S(1)}, f32[256,128]{1,0:T(8,128)S(1)}, u32[]{:S(2)}, u32[]{:S(2)}) collective-permute-start(f32[256,128]{1,0:T(8,128)S(1)} %get-tuple-element.24), channel_id=1, source_target_pairs={{0,8},{8,0},{16,24},{24,16},{1,9},{9,1},{17,25},{25,17},{2,10},{10... | collective-permute-start | bytes 393224 | tf_op jit(solution)/shard_map/reduce/ppermute | solution.py:216
  25.1 2.4 %collective-permute-start.10 = (f32[256,128]{1,0:T(8,128)S(1)}, f32[256,128]{1,0:T(8,128)S(1)}, u32[]{:S(2)}, u32[]{:S(2)}) collective-permute-start(f32[256,128]{1,0:T(8,128)S(1)} %get-tuple-element.25), channel_id=1, source_target_pairs={{0,16},{8,24},{16,0},{24,8},{1,17},{9,25},{17,1},{25,9},{2,18},{10... | collective-permute-start | bytes 393224 | tf_op jit(solution)/shard_map/reduce/ppermute | solution.py:216
  27.5 0.0 collective-permute-done.12.refs_1_
  27.5 0.4 %collective-permute-start.13 = (f32[256,128]{1,0:T(8,128)S(1)}, f32[256,128]{1,0:T(8,128)S(1)}, u32[]{:S(2)}, u32[]{:S(2)}) collective-permute-start(f32[256,128]{1,0:T(8,128)S(1)} %reduce.8), channel_id=1, source_target_pairs={{0,4},{1,5},{2,6},{3,7},{4,0},{5,1},{6,2},{7,3},{8,12},{9,13},{10,... | collective-permute-start | bytes 393224 | tf_op jit(solution)/shard_map/reduce/ppermute | solution.py:216
  27.9 1.3 %collective-permute-start.14 = (f32[256,128]{1,0:T(8,128)S(1)}, f32[256,128]{1,0:T(8,128)S(1)}, u32[]{:S(2)}, u32[]{:S(2)}) collective-permute-start(f32[256,128]{1,0:T(8,128)S(1)} %get-tuple-element.28), channel_id=1, source_target_pairs={{0,24},{8,16},{16,8},{24,0},{1,25},{9,17},{17,9},{25,1},{2,26},{10... | collective-permute-start | bytes 393224 | tf_op jit(solution)/shard_map/reduce/ppermute | solution.py:216
  29.2 0.0 collective-permute-done.11.refs_1_
  29.3 1.3 %collective-permute-start.15 = (f32[256,128]{1,0:T(8,128)S(1)}, f32[256,128]{1,0:T(8,128)S(1)}, u32[]{:S(2)}, u32[]{:S(2)}) collective-permute-start(f32[256,128]{1,0:T(8,128)S(1)} %get-tuple-element.31), channel_id=1, source_target_pairs={{0,2},{1,3},{2,0},{3,1},{4,6},{5,7},{6,4},{7,5},{8,10},{9,11},{10,... | collective-permute-start | bytes 393224 | tf_op jit(solution)/shard_map/reduce/ppermute | solution.py:216
  30.6 0.0 collective-permute-done.9.refs_1_
  30.6 2.5 %collective-permute-done.10.refs_2_ = f32[256,128]{1,0:T(8,128)S(1)} collective-permute-done((f32[256,128]{1,0:T(8,128)S(1)}, f32[256,128]{1,0:T(8,128)S(1)}, u32[]{:S(2)}, u32[]{:S(2)}) %collective-permute-start.10) | collective-permute-done | bytes 131104 | tf_op jit(solution)/shard_map/reduce/ppermute | solution.py:216
  33.1 3.3 %collective-permute-done.13.refs_1_ = f32[256,128]{1,0:T(8,128)S(1)} collective-permute-done((f32[256,128]{1,0:T(8,128)S(1)}, f32[256,128]{1,0:T(8,128)S(1)}, u32[]{:S(2)}, u32[]{:S(2)}) %collective-permute-start.13) | collective-permute-done | bytes 131104 | tf_op jit(solution)/shard_map/reduce/ppermute | solution.py:216
  36.4 0.0 collective-permute-done.14.refs_1_
  36.4 0.0 collective-permute-done.15.refs_1_
  36.4 0.7 %reduce.11 = (f32[256,128]{1,0:T(8,128)}, f32[256,128]{1,0:T(8,128)}) custom-call(f32[256,128]{1,0:T(8,128)S(1)} %reduce.10.row_ref, f32[256,128]{1,0:T(8,128)S(1)} %get-tuple-element.29.row_factor_ref, f32[256,128]{1,0:T(8,128)S(1)} %get-tuple-element.30.col_factor_ref, f32[256,128]{1,0:T(8,128)S(1)} %reduce.9._.refs_0_, ...), custom_call_target="tpu_custom_call" | custom-call | bytes 1024 | tf_op jit(solution)/shard_map/reduce/pallas_call | solution.py:229
  (9 shorter events, 0.2 us)
Async XLA Ops:
  1.8 13.7 %collective-permute-start = (f32[256,128]{1,0:T(8,128)S(1)}, f32[256,128]{1,0:T(8,128)S(1)}, u32[]{:S(2)}, u32[]{:S(2)}) collective-permute-start(f32[256,128]{1,0:T(8,128)S(1)} %get-tuple-element.19.refs_0_), channel_id=1, source_target_pairs={{0,4},{1,5},{2,6},{3,7},{4,0},{5,1},{6,2},{7,3},{8,12},{9,13},{10,... | collective-permute-start | bytes 393224 | tf_op jit(solution)/shard_map/gather/ppermute | solution.py:216
  5.9 9.7 %collective-permute-start.3 = (f32[256,128]{1,0:T(8,128)S(1)}, f32[256,128]{1,0:T(8,128)S(1)}, u32[]{:S(2)}, u32[]{:S(2)}) collective-permute-start(f32[256,128]{1,0:T(8,128)S(1)} %get-tuple-element.20.refs_0_), channel_id=1, source_target_pairs={{0,24},{8,16},{16,8},{24,0},{1,25},{9,17},{17,9},{25,1},{2,26},{10... | collective-permute-start | bytes 393224 | tf_op jit(solution)/shard_map/gather/ppermute | solution.py:216
  8.3 7.2 %collective-permute-start.2 = (f32[256,128]{1,0:T(8,128)S(1)}, f32[256,128]{1,0:T(8,128)S(1)}, u32[]{:S(2)}, u32[]{:S(2)}) collective-permute-start(f32[256,128]{1,0:T(8,128)S(1)} %get-tuple-element.20.refs_0_), channel_id=1, source_target_pairs={{0,16},{8,24},{16,0},{24,8},{1,17},{9,25},{17,1},{25,9},{2,18},{10... | collective-permute-start | bytes 393224 | tf_op jit(solution)/shard_map/gather/ppermute | solution.py:216
  8.9 6.7 %collective-permute-start.1 = (f32[256,128]{1,0:T(8,128)S(1)}, f32[256,128]{1,0:T(8,128)S(1)}, u32[]{:S(2)}, u32[]{:S(2)}) collective-permute-start(f32[256,128]{1,0:T(8,128)S(1)} %get-tuple-element.20.refs_0_), channel_id=1, source_target_pairs={{0,8},{8,0},{16,24},{24,16},{1,9},{9,1},{17,25},{25,17},{2,10},{10... | collective-permute-start | bytes 393224 | tf_op jit(solution)/shard_map/gather/ppermute | solution.py:216
  9.4 6.4 %collective-permute-start.4 = (f32[256,128]{1,0:T(8,128)S(1)}, f32[256,128]{1,0:T(8,128)S(1)}, u32[]{:S(2)}, u32[]{:S(2)}) collective-permute-start(f32[256,128]{1,0:T(8,128)S(1)} %get-tuple-element.19.refs_0_), channel_id=1, source_target_pairs={{0,2},{1,3},{2,0},{3,1},{4,6},{5,7},{6,4},{7,5},{8,10},{9,11},{10,... | collective-permute-start | bytes 393224 | tf_op jit(solution)/shard_map/gather/ppermute | solution.py:216
  15.5 5.0 %collective-permute-start.5 = (f32[256,128]{1,0:T(8,128)S(1)}, f32[256,128]{1,0:T(8,128)S(1)}, u32[]{:S(2)}, u32[]{:S(2)}) collective-permute-start(f32[256,128]{1,0:T(8,128)S(1)} %gather.3._.refs_2_), channel_id=1, source_target_pairs={{0,2},{1,3},{2,0},{3,1},{4,6},{5,7},{6,4},{7,5},{8,10},{9,11},{10,... | collective-permute-start | bytes 393224 | tf_op jit(solution)/shard_map/gather/ppermute | solution.py:216
  15.9 6.2 %collective-permute-start.7 = (f32[3,256,128]{2,1,0:T(8,128)S(1)}, f32[3,256,128]{2,1,0:T(8,128)S(1)}, u32[]{:S(2)}, u32[]{:S(2)}) collective-permute-start(f32[3,256,128]{2,1,0:T(8,128)S(1)} %gather.4._.refs_0_), channel_id=1, source_target_pairs={{0,1},{1,0},{2,3},{3,2},{4,5},{5,4},{6,7},{7,6},{8,9},{9,8},{10,11... | collective-permute-start | bytes 1179656 | tf_op jit(solution)/shard_map/gather/ppermute | solution.py:216
  16.6 4.0 %collective-permute-start.6 = (f32[2,256,128]{2,1,0:T(8,128)S(1)}, f32[2,256,128]{2,1,0:T(8,128)S(1)}, u32[]{:S(2)}, u32[]{:S(2)}) collective-permute-start(f32[2,256,128]{2,1,0:T(8,128)S(1)} %backward.5._), channel_id=1, source_target_pairs={{0,1},{1,0},{2,3},{3,2},{4,5},{5,4},{6,7},{7,6},{8,9},{9,8},{10,11... | collective-permute-start | bytes 786440 | tf_op jit(solution)/shard_map/backward/ppermute | solution.py:216
  19.3 10.0 %collective-permute-start.11 = (f32[2,256,128]{2,1,0:T(8,128)S(1)}, f32[2,256,128]{2,1,0:T(8,128)S(1)}, u32[]{:S(2)}, u32[]{:S(2)}) collective-permute-start(f32[2,256,128]{2,1,0:T(8,128)S(1)} %backward.7._), channel_id=1, source_target_pairs={{0,1},{1,0},{2,3},{3,2},{4,5},{5,4},{6,7},{7,6},{8,9},{9,8},{10,11... | collective-permute-start | bytes 786440 | tf_op jit(solution)/shard_map/reduce/ppermute | solution.py:216
  20.5 1.5 %collective-permute-start.8 = (f32[1,256,128]{2,1,0:T(8,128)S(1)}, f32[1,256,128]{2,1,0:T(8,128)S(1)}, u32[]{:S(2)}, u32[]{:S(2)}) collective-permute-start(f32[1,256,128]{2,1,0:T(8,128)S(1)} %gather.5._.refs_2_), channel_id=1, source_target_pairs={{0,1},{1,0},{2,3},{3,2},{4,5},{5,4},{6,7},{7,6},{8,9},{9,8},{10,11... | collective-permute-start | bytes 393224 | tf_op jit(solution)/shard_map/gather/ppermute | solution.py:216
  20.7 6.9 %collective-permute-start.12 = (f32[256,128]{1,0:T(8,128)S(1)}, f32[256,128]{1,0:T(8,128)S(1)}, u32[]{:S(2)}, u32[]{:S(2)}) collective-permute-start(f32[256,128]{1,0:T(8,128)S(1)} %get-tuple-element.27), channel_id=1, source_target_pairs={{0,2},{1,3},{2,0},{3,1},{4,6},{5,7},{6,4},{7,5},{8,10},{9,11},{10,... | collective-permute-start | bytes 393224 | tf_op jit(solution)/shard_map/reduce/ppermute | solution.py:216
  24.4 6.1 %collective-permute-start.9 = (f32[256,128]{1,0:T(8,128)S(1)}, f32[256,128]{1,0:T(8,128)S(1)}, u32[]{:S(2)}, u32[]{:S(2)}) collective-permute-start(f32[256,128]{1,0:T(8,128)S(1)} %get-tuple-element.24), channel_id=1, source_target_pairs={{0,8},{8,0},{16,24},{24,16},{1,9},{9,1},{17,25},{25,17},{2,10},{10... | collective-permute-start | bytes 393224 | tf_op jit(solution)/shard_map/reduce/ppermute | solution.py:216
  25.1 8.0 %collective-permute-start.10 = (f32[256,128]{1,0:T(8,128)S(1)}, f32[256,128]{1,0:T(8,128)S(1)}, u32[]{:S(2)}, u32[]{:S(2)}) collective-permute-start(f32[256,128]{1,0:T(8,128)S(1)} %get-tuple-element.25), channel_id=1, source_target_pairs={{0,16},{8,24},{16,0},{24,8},{1,17},{9,25},{17,1},{25,9},{2,18},{10... | collective-permute-start | bytes 393224 | tf_op jit(solution)/shard_map/reduce/ppermute | solution.py:216
  27.5 8.8 %collective-permute-start.13 = (f32[256,128]{1,0:T(8,128)S(1)}, f32[256,128]{1,0:T(8,128)S(1)}, u32[]{:S(2)}, u32[]{:S(2)}) collective-permute-start(f32[256,128]{1,0:T(8,128)S(1)} %reduce.8), channel_id=1, source_target_pairs={{0,4},{1,5},{2,6},{3,7},{4,0},{5,1},{6,2},{7,3},{8,12},{9,13},{10,... | collective-permute-start | bytes 393224 | tf_op jit(solution)/shard_map/reduce/ppermute | solution.py:216
  27.9 8.4 %collective-permute-start.14 = (f32[256,128]{1,0:T(8,128)S(1)}, f32[256,128]{1,0:T(8,128)S(1)}, u32[]{:S(2)}, u32[]{:S(2)}) collective-permute-start(f32[256,128]{1,0:T(8,128)S(1)} %get-tuple-element.28), channel_id=1, source_target_pairs={{0,24},{8,16},{16,8},{24,0},{1,25},{9,17},{17,9},{25,1},{2,26},{10... | collective-permute-start | bytes 393224 | tf_op jit(solution)/shard_map/reduce/ppermute | solution.py:216
  29.3 7.1 %collective-permute-start.15 = (f32[256,128]{1,0:T(8,128)S(1)}, f32[256,128]{1,0:T(8,128)S(1)}, u32[]{:S(2)}, u32[]{:S(2)}) collective-permute-start(f32[256,128]{1,0:T(8,128)S(1)} %get-tuple-element.31), channel_id=1, source_target_pairs={{0,2},{1,3},{2,0},{3,1},{4,6},{5,7},{6,4},{7,5},{8,10},{9,11},{10,... | collective-permute-start | bytes 393224 | tf_op jit(solution)/shard_map/reduce/ppermute | solution.py:216

commit v14 on v13

--- a/solution.py
+++ b/solution.py
@@ -422,10 +422,9 @@
 
     with jax.named_scope("reduce"):
         mine, *grad_parts = halved(close_sums, after)
-        first = [swap(forwards[k], "row", k) for k in range(1, n_row - 1)]
-        row_sum = call(sum_kernel, block, [forwards[0], *first])
-        mine = total([mine, swap(crossing, "col", 2 * half)], row_sum)
-        row_sum = call(sum_kernel, block, [row_sum, swap(forwards[-1], "row", n_row - 1)], after=mine)
+        row_sum = call(sum_kernel, block, [forwards[0], swap(forwards[1], "row", 1)])
+        mine = total([mine, swap(crossing, "col", 2 * half)], row_sum, 10**9)
+        row_sum = call(sum_kernel, block, [row_sum] + [swap(forwards[k], "row", k) for k in range(2, n_row)], after=mine)
         return call(
             finish_kernel, (block, block), (row_sum, row_factor, col_factor, mine, *grad_parts), mebibytes=4
         )

time: 37.3 us -> 37.6 us (level)
  waiting for transfers between devices: 6.96 us -> 8.4 us
  starting transfers between devices: 17.5 us -> 16.4 us
    ppermute x16, waiting for transfers between devices: 6.96 us -> 8.4 us  [swap(): lax.ppermute(x, axis, [(at, at ^ mask) for at in range(lax.axis_size(axis...]
    ppermute x16, starting transfers between devices: 17.5 us -> 16.4 us  [swap(): lax.ppermute(x, axis, [(at, at ^ mask) for at in range(lax.axis_size(axis...]
  transfers between devices with their start and end apart: 16 -> 16, of which waited for: 3 -> 5; matrix products, arithmetic and copies ran while one was open for 0% -> 0% of each run, Pallas kernels for 25% -> 25%
where the time goes in v14:
time: 37.6 us; the launch traced here: 37.5 us
  starting transfers between devices  16.4 us (44%)
  Pallas kernels  11.3 us (30%)
  waiting for transfers between devices  8.4 us (22%)
  between operations  1.47 us (4%)
    ppermute x16, starting transfers between devices, swap(): lax.ppermute(x, axis, [(at, at ^ mask) for at in range(lax.axis_size(axis...  16.4 us
    pallas_call x18, Pallas kernels, call(): pl.pallas_call(body, out_shape=out_shape, in_specs=specs, out_specs=tuple...  11.3 us
    ppermute x16, waiting for transfers between devices, swap(): lax.ppermute(x, axis, [(at, at ^ mask) for at in range(lax.axis_size(axis...  8.4 us
  transfers between devices with their start and end apart: 16, of which 5 were waited for; matrix products, arithmetic and copies ran while one was open for 0% of the time, Pallas kernels for 25%

profile of v14, /device:TPU:0, one launch (start us, length us, event | category | flops | bytes accessed | tf_op | source)
XLA Modules:
  0.0 37.5 jit_solution(1634517258558713366)
XLA Ops:
  0.6 1.2 %scale.1 = (f32[256,128]{1,0:T(8,128)S(1)}, f32[256,128]{1,0:T(8,128)S(1)}, f32[256,128]{1,0:T(8,128)S(1)}, f32[256,128]{1,0:T(8,128)S(1)}, s32[2,128]{1,0:T(2,128)S(1)}) custom-call(f32[256,128]{1,0:T(8,128)} %refs_0_.1, f32[256,128]{1,0:T(8,128)} %refs_1_.1, s32[2,128]{1,0:T(2,128)} %bitcast.4, s32[2,128]{1,0:T(2,128)} %bitcast.5, s32[2,1,1,128]{3,2,1,0:T(1,128)} %refs_4_.1), custom_call_target="tpu_custom_call" | custom-call | bytes 1024 | tf_op jit(solution)/shard_map/scale/pallas_call | solution.py:229
  1.8 4.1 %collective-permute-start = (f32[256,128]{1,0:T(8,128)S(1)}, f32[256,128]{1,0:T(8,128)S(1)}, u32[]{:S(2)}, u32[]{:S(2)}) collective-permute-start(f32[256,128]{1,0:T(8,128)S(1)} %get-tuple-element.19.refs_0_), channel_id=1, source_target_pairs={{0,4},{1,5},{2,6},{3,7},{4,0},{5,1},{6,2},{7,3},{8,12},{9,13},{10,... | collective-permute-start | bytes 393224 | tf_op jit(solution)/shard_map/gather/ppermute | solution.py:216
  5.9 2.4 %collective-permute-start.3 = (f32[256,128]{1,0:T(8,128)S(1)}, f32[256,128]{1,0:T(8,128)S(1)}, u32[]{:S(2)}, u32[]{:S(2)}) collective-permute-start(f32[256,128]{1,0:T(8,128)S(1)} %get-tuple-element.20.refs_0_), channel_id=1, source_target_pairs={{0,24},{8,16},{16,8},{24,0},{1,25},{9,17},{17,9},{25,1},{2,26},{10... | collective-permute-start | bytes 393224 | tf_op jit(solution)/shard_map/gather/ppermute | solution.py:216
  8.3 0.5 %collective-permute-start.2 = (f32[256,128]{1,0:T(8,128)S(1)}, f32[256,128]{1,0:T(8,128)S(1)}, u32[]{:S(2)}, u32[]{:S(2)}) collective-permute-start(f32[256,128]{1,0:T(8,128)S(1)} %get-tuple-element.20.refs_0_), channel_id=1, source_target_pairs={{0,16},{8,24},{16,0},{24,8},{1,17},{9,25},{17,1},{25,9},{2,18},{10... | collective-permute-start | bytes 393224 | tf_op jit(solution)/shard_map/gather/ppermute | solution.py:216
  8.9 0.5 %collective-permute-start.1 = (f32[256,128]{1,0:T(8,128)S(1)}, f32[256,128]{1,0:T(8,128)S(1)}, u32[]{:S(2)}, u32[]{:S(2)}) collective-permute-start(f32[256,128]{1,0:T(8,128)S(1)} %get-tuple-element.20.refs_0_), channel_id=1, source_target_pairs={{0,8},{8,0},{16,24},{24,16},{1,9},{9,1},{17,25},{25,17},{2,10},{10... | collective-permute-start | bytes 393224 | tf_op jit(solution)/shard_map/gather/ppermute | solution.py:216
  9.4 1.6 %collective-permute-start.4 = (f32[256,128]{1,0:T(8,128)S(1)}, f32[256,128]{1,0:T(8,128)S(1)}, u32[]{:S(2)}, u32[]{:S(2)}) collective-permute-start(f32[256,128]{1,0:T(8,128)S(1)} %get-tuple-element.19.refs_0_), channel_id=1, source_target_pairs={{0,2},{1,3},{2,0},{3,1},{4,6},{5,7},{6,4},{7,5},{8,10},{9,11},{10,... | collective-permute-start | bytes 393224 | tf_op jit(solution)/shard_map/gather/ppermute | solution.py:216
  11.6 3.8 %split.1 = (bf16[1024,2048]{1,0:T(8,128)(2,1)S(1)}, bf16[1024,2048]{1,0:T(8,128)(2,1)S(1)}) custom-call(s32[1,1]{1,0:T(1,128)S(6)} %copy.9.count_ref, s32[2,128]{1,0:T(2,128)S(1)} %get-tuple-element.17.plan_ref, f32[128,128,128]{2,1,0:T(8,128)} %bitcast.3), custom_call_target="tpu_custom_call" | custom-call | bytes 1024 | tf_op jit(solution)/shard_map/split/pallas_call | solution.py:229
  15.5 0.0 collective-permute-done.refs_0_
  15.5 0.5 %collective-permute-start.5 = (f32[256,128]{1,0:T(8,128)S(1)}, f32[256,128]{1,0:T(8,128)S(1)}, u32[]{:S(2)}, u32[]{:S(2)}) collective-permute-start(f32[256,128]{1,0:T(8,128)S(1)} %gather.3._.refs_2_), channel_id=1, source_target_pairs={{0,2},{1,3},{2,0},{3,1},{4,6},{5,7},{6,4},{7,5},{8,10},{9,11},{10,... | collective-permute-start | bytes 393224 | tf_op jit(solution)/shard_map/gather/ppermute | solution.py:216
  16.0 0.0 collective-permute-done.3.refs_3_
  16.0 0.0 collective-permute-done.2.refs_2_
  16.0 0.0 collective-permute-done.1.refs_1_
  16.0 0.2 flip.1._.refs_0_
  16.2 0.0 collective-permute-done.4.refs_1_
  16.3 0.1 collective-permute-start.7
  16.4 0.7 %backward.5._ = f32[2,256,128]{2,1,0:T(8,128)S(1)} custom-call(f32[3,256,128]{2,1,0:T(8,128)S(1)} %gather.4._.refs_0_, bf16[256,1024]{1,0:T(8,128)(2,1)S(1)} %flip.1._.refs_0_, bf16[1024,2048]{1,0:T(8,128)(2,1)S(1)} %get-tuple-element.18._.refs_1_.refs_4_, bf16[1024,2048]{1,0:T(8,128)(2,1)S(1)} %get-tuple-element.21.refs_2_.refs_5_), custom_call_target="tpu_custom_call" | custom-call | bytes 1024 | tf_op jit(solution)/shard_map/backward/pallas_call | solution.py:229
  17.1 0.6 %collective-permute-start.6 = (f32[2,256,128]{2,1,0:T(8,128)S(1)}, f32[2,256,128]{2,1,0:T(8,128)S(1)}, u32[]{:S(2)}, u32[]{:S(2)}) collective-permute-start(f32[2,256,128]{2,1,0:T(8,128)S(1)} %backward.5._), channel_id=1, source_target_pairs={{0,1},{1,0},{2,3},{3,2},{4,5},{5,4},{6,7},{7,6},{8,9},{9,8},{10,11... | collective-permute-start | bytes 786440 | tf_op jit(solution)/shard_map/backward/ppermute | solution.py:216
  17.6 0.7 %backward.6._.refs_0_ = f32[2,256,128]{2,1,0:T(8,128)S(1)} custom-call(f32[2,256,128]{2,1,0:T(8,128)S(1)} %backward.5._, bf16[256,1024]{1,0:T(8,128)(2,1)S(1)} %flip.1._.refs_0_, bf16[1024,2048]{1,0:T(8,128)(2,1)S(1)} %get-tuple-element.18._.refs_1_.refs_4_, bf16[1024,2048]{1,0:T(8,128)(2,1)S(1)} %get-tuple-element.21.refs_2_.refs_5_), custom_call_target="tpu_custom_call" | custom-call | bytes 1024 | tf_op jit(solution)/shard_map/backward/pallas_call | solution.py:229
  18.3 0.7 %backward.7._ = f32[2,256,128]{2,1,0:T(8,128)S(1)} custom-call(f32[2,256,128]{2,1,0:T(8,128)S(1)} %backward.6._.refs_0_, bf16[256,1024]{1,0:T(8,128)(2,1)S(1)} %flip.1._.refs_0_, bf16[1024,2048]{1,0:T(8,128)(2,1)S(1)} %get-tuple-element.18._.refs_1_.refs_4_, bf16[1024,2048]{1,0:T(8,128)(2,1)S(1)} %get-tuple-element.21.refs_2_.refs_5_), custom_call_target="tpu_custom_call" | custom-call | bytes 1024 | tf_op jit(solution)/shard_map/backward/pallas_call | solution.py:229
  19.0 0.7 %backward.8._.refs_0_ = f32[2,256,128]{2,1,0:T(8,128)S(1)} custom-call(f32[2,256,128]{2,1,0:T(8,128)S(1)} %backward.7._, bf16[256,1024]{1,0:T(8,128)(2,1)S(1)} %flip.1._.refs_0_, bf16[1024,2048]{1,0:T(8,128)(2,1)S(1)} %get-tuple-element.18._.refs_1_.refs_4_, bf16[1024,2048]{1,0:T(8,128)(2,1)S(1)} %get-tuple-element.21.refs_2_.refs_5_), custom_call_target="tpu_custom_call" | custom-call | bytes 1024 | tf_op jit(solution)/shard_map/backward/pallas_call | solution.py:229
  19.7 0.8 %collective-permute-done.5.refs_0_ = f32[256,128]{1,0:T(8,128)S(1)} collective-permute-done((f32[256,128]{1,0:T(8,128)S(1)}, f32[256,128]{1,0:T(8,128)S(1)}, u32[]{:S(2)}, u32[]{:S(2)}) %collective-permute-start.5) | collective-permute-done | bytes 131104 | tf_op jit(solution)/shard_map/gather/ppermute | solution.py:216
  20.5 0.1 collective-permute-start.8
  20.6 0.0 collective-permute-done.6.refs_1_
  20.7 0.8 %collective-permute-start.11 = (f32[256,128]{1,0:T(8,128)S(1)}, f32[256,128]{1,0:T(8,128)S(1)}, u32[]{:S(2)}, u32[]{:S(2)}) collective-permute-start(f32[256,128]{1,0:T(8,128)S(1)} %get-tuple-element.26), channel_id=1, source_target_pairs={{0,2},{1,3},{2,0},{3,1},{4,6},{5,7},{6,4},{7,5},{8,10},{9,11},{10,... | collective-permute-start | bytes 393224 | tf_op jit(solution)/shard_map/reduce/ppermute | solution.py:216
  21.5 0.2 collective-permute-start.10
  21.7 0.3 collective-permute-done.8.refs_3_
  22.0 0.0 collective-permute-done.7.refs_1_
  22.0 2.4 %forward.1 = (f32[256,128]{1,0:T(8,128)S(1)}, f32[256,128]{1,0:T(8,128)S(1)}, f32[256,128]{1,0:T(8,128)S(1)}, f32[256,128]{1,0:T(8,128)S(1)}) custom-call(f32[256,128]{1,0:T(8,128)S(1)} %get-tuple-element.22._.refs_0_, f32[3,256,128]{2,1,0:T(8,128)S(1)} %gather.4._.refs_0_, f32[3,256,128]{2,1,0:T(8,128)S(1)} %collective-permute-done.7.refs_1_, ...), custom_call_target="tpu_custom_call" | custom-call | bytes 1024 | tf_op jit(solution)/shard_map/forward/pallas_call | solution.py:229
  24.4 0.6 %collective-permute-start.9 = (f32[256,128]{1,0:T(8,128)S(1)}, f32[256,128]{1,0:T(8,128)S(1)}, u32[]{:S(2)}, u32[]{:S(2)}) collective-permute-start(f32[256,128]{1,0:T(8,128)S(1)} %get-tuple-element.24), channel_id=1, source_target_pairs={{0,8},{8,0},{16,24},{24,16},{1,9},{9,1},{17,25},{25,17},{2,10},{10... | collective-permute-start | bytes 393224 | tf_op jit(solution)/shard_map/reduce/ppermute | solution.py:216
  25.0 1.6 %collective-permute-done.11.refs_1_ = f32[256,128]{1,0:T(8,128)S(1)} collective-permute-done((f32[256,128]{1,0:T(8,128)S(1)}, f32[256,128]{1,0:T(8,128)S(1)}, u32[]{:S(2)}, u32[]{:S(2)}) %collective-permute-start.11) | collective-permute-done | bytes 131104 | tf_op jit(solution)/shard_map/reduce/ppermute | solution.py:216
  26.6 0.1 collective-permute-start.12
  26.7 1.9 %collective-permute-start.13 = (f32[256,128]{1,0:T(8,128)S(1)}, f32[256,128]{1,0:T(8,128)S(1)}, u32[]{:S(2)}, u32[]{:S(2)}) collective-permute-start(f32[256,128]{1,0:T(8,128)S(1)} %get-tuple-element.27), channel_id=1, source_target_pairs={{0,16},{8,24},{16,0},{24,8},{1,17},{9,25},{17,1},{25,9},{2,18},{10... | collective-permute-start | bytes 393224 | tf_op jit(solution)/shard_map/reduce/ppermute | solution.py:216
  28.6 0.7 %collective-permute-start.14 = (f32[256,128]{1,0:T(8,128)S(1)}, f32[256,128]{1,0:T(8,128)S(1)}, u32[]{:S(2)}, u32[]{:S(2)}) collective-permute-start(f32[256,128]{1,0:T(8,128)S(1)} %get-tuple-element.28), channel_id=1, source_target_pairs={{0,24},{8,16},{16,8},{24,0},{1,25},{9,17},{17,9},{25,1},{2,26},{10... | collective-permute-start | bytes 393224 | tf_op jit(solution)/shard_map/reduce/ppermute | solution.py:216
  29.3 0.0 collective-permute-done.10.refs_1_
  29.4 1.7 %collective-permute-start.15 = (f32[256,128]{1,0:T(8,128)S(1)}, f32[256,128]{1,0:T(8,128)S(1)}, u32[]{:S(2)}, u32[]{:S(2)}) collective-permute-start(f32[256,128]{1,0:T(8,128)S(1)} %get-tuple-element.31), channel_id=1, source_target_pairs={{0,2},{1,3},{2,0},{3,1},{4,6},{5,7},{6,4},{7,5},{8,10},{9,11},{10,... | collective-permute-start | bytes 393224 | tf_op jit(solution)/shard_map/reduce/ppermute | solution.py:216
  31.1 0.0 collective-permute-done.9.refs_1_
  31.1 4.5 %collective-permute-done.12.refs_1_ = f32[256,128]{1,0:T(8,128)S(1)} collective-permute-done((f32[256,128]{1,0:T(8,128)S(1)}, f32[256,128]{1,0:T(8,128)S(1)}, u32[]{:S(2)}, u32[]{:S(2)}) %collective-permute-start.12) | collective-permute-done | bytes 131104 | tf_op jit(solution)/shard_map/reduce/ppermute | solution.py:216
  35.6 0.0 collective-permute-done.13.refs_1_
  35.7 0.0 collective-permute-done.14.refs_2_
  35.7 1.1 %collective-permute-done.15.refs_1_ = f32[256,128]{1,0:T(8,128)S(1)} collective-permute-done((f32[256,128]{1,0:T(8,128)S(1)}, f32[256,128]{1,0:T(8,128)S(1)}, u32[]{:S(2)}, u32[]{:S(2)}) %collective-permute-start.15) | collective-permute-done | bytes 131104 | tf_op jit(solution)/shard_map/reduce/ppermute | solution.py:216
  36.8 0.7 %reduce.11 = (f32[256,128]{1,0:T(8,128)}, f32[256,128]{1,0:T(8,128)}) custom-call(f32[256,128]{1,0:T(8,128)S(1)} %reduce.10.row_ref, f32[256,128]{1,0:T(8,128)S(1)} %get-tuple-element.29.row_factor_ref, f32[256,128]{1,0:T(8,128)S(1)} %get-tuple-element.30.col_factor_ref, f32[256,128]{1,0:T(8,128)S(1)} %reduce.9._.refs_0_, ...), custom_call_target="tpu_custom_call" | custom-call | bytes 1024 | tf_op jit(solution)/shard_map/reduce/pallas_call | solution.py:229
  (9 shorter events, 0.2 us)
Async XLA Ops:
  1.8 13.7 %collective-permute-start = (f32[256,128]{1,0:T(8,128)S(1)}, f32[256,128]{1,0:T(8,128)S(1)}, u32[]{:S(2)}, u32[]{:S(2)}) collective-permute-start(f32[256,128]{1,0:T(8,128)S(1)} %get-tuple-element.19.refs_0_), channel_id=1, source_target_pairs={{0,4},{1,5},{2,6},{3,7},{4,0},{5,1},{6,2},{7,3},{8,12},{9,13},{10,... | collective-permute-start | bytes 393224 | tf_op jit(solution)/shard_map/gather/ppermute | solution.py:216
  5.9 10.1 %collective-permute-start.3 = (f32[256,128]{1,0:T(8,128)S(1)}, f32[256,128]{1,0:T(8,128)S(1)}, u32[]{:S(2)}, u32[]{:S(2)}) collective-permute-start(f32[256,128]{1,0:T(8,128)S(1)} %get-tuple-element.20.refs_0_), channel_id=1, source_target_pairs={{0,24},{8,16},{16,8},{24,0},{1,25},{9,17},{17,9},{25,1},{2,26},{10... | collective-permute-start | bytes 393224 | tf_op jit(solution)/shard_map/gather/ppermute | solution.py:216
  8.3 7.7 %collective-permute-start.2 = (f32[256,128]{1,0:T(8,128)S(1)}, f32[256,128]{1,0:T(8,128)S(1)}, u32[]{:S(2)}, u32[]{:S(2)}) collective-permute-start(f32[256,128]{1,0:T(8,128)S(1)} %get-tuple-element.20.refs_0_), channel_id=1, source_target_pairs={{0,16},{8,24},{16,0},{24,8},{1,17},{9,25},{17,1},{25,9},{2,18},{10... | collective-permute-start | bytes 393224 | tf_op jit(solution)/shard_map/gather/ppermute | solution.py:216
  8.9 7.2 %collective-permute-start.1 = (f32[256,128]{1,0:T(8,128)S(1)}, f32[256,128]{1,0:T(8,128)S(1)}, u32[]{:S(2)}, u32[]{:S(2)}) collective-permute-start(f32[256,128]{1,0:T(8,128)S(1)} %get-tuple-element.20.refs_0_), channel_id=1, source_target_pairs={{0,8},{8,0},{16,24},{24,16},{1,9},{9,1},{17,25},{25,17},{2,10},{10... | collective-permute-start | bytes 393224 | tf_op jit(solution)/shard_map/gather/ppermute | solution.py:216
  9.4 6.9 %collective-permute-start.4 = (f32[256,128]{1,0:T(8,128)S(1)}, f32[256,128]{1,0:T(8,128)S(1)}, u32[]{:S(2)}, u32[]{:S(2)}) collective-permute-start(f32[256,128]{1,0:T(8,128)S(1)} %get-tuple-element.19.refs_0_), channel_id=1, source_target_pairs={{0,2},{1,3},{2,0},{3,1},{4,6},{5,7},{6,4},{7,5},{8,10},{9,11},{10,... | collective-permute-start | bytes 393224 | tf_op jit(solution)/shard_map/gather/ppermute | solution.py:216
  15.5 5.0 %collective-permute-start.5 = (f32[256,128]{1,0:T(8,128)S(1)}, f32[256,128]{1,0:T(8,128)S(1)}, u32[]{:S(2)}, u32[]{:S(2)}) collective-permute-start(f32[256,128]{1,0:T(8,128)S(1)} %gather.3._.refs_2_), channel_id=1, source_target_pairs={{0,2},{1,3},{2,0},{3,1},{4,6},{5,7},{6,4},{7,5},{8,10},{9,11},{10,... | collective-permute-start | bytes 393224 | tf_op jit(solution)/shard_map/gather/ppermute | solution.py:216
  16.3 5.7 %collective-permute-start.7 = (f32[3,256,128]{2,1,0:T(8,128)S(1)}, f32[3,256,128]{2,1,0:T(8,128)S(1)}, u32[]{:S(2)}, u32[]{:S(2)}) collective-permute-start(f32[3,256,128]{2,1,0:T(8,128)S(1)} %gather.4._.refs_0_), channel_id=1, source_target_pairs={{0,1},{1,0},{2,3},{3,2},{4,5},{5,4},{6,7},{7,6},{8,9},{9,8},{10,11... | collective-permute-start | bytes 1179656 | tf_op jit(solution)/shard_map/gather/ppermute | solution.py:216
  17.1 3.6 %collective-permute-start.6 = (f32[2,256,128]{2,1,0:T(8,128)S(1)}, f32[2,256,128]{2,1,0:T(8,128)S(1)}, u32[]{:S(2)}, u32[]{:S(2)}) collective-permute-start(f32[2,256,128]{2,1,0:T(8,128)S(1)} %backward.5._), channel_id=1, source_target_pairs={{0,1},{1,0},{2,3},{3,2},{4,5},{5,4},{6,7},{7,6},{8,9},{9,8},{10,11... | collective-permute-start | bytes 786440 | tf_op jit(solution)/shard_map/backward/ppermute | solution.py:216
  20.5 1.4 %collective-permute-start.8 = (f32[1,256,128]{2,1,0:T(8,128)S(1)}, f32[1,256,128]{2,1,0:T(8,128)S(1)}, u32[]{:S(2)}, u32[]{:S(2)}) collective-permute-start(f32[1,256,128]{2,1,0:T(8,128)S(1)} %gather.5._.refs_2_), channel_id=1, source_target_pairs={{0,1},{1,0},{2,3},{3,2},{4,5},{5,4},{6,7},{7,6},{8,9},{9,8},{10,11... | collective-permute-start | bytes 393224 | tf_op jit(solution)/shard_map/gather/ppermute | solution.py:216
  20.7 6.0 %collective-permute-start.11 = (f32[256,128]{1,0:T(8,128)S(1)}, f32[256,128]{1,0:T(8,128)S(1)}, u32[]{:S(2)}, u32[]{:S(2)}) collective-permute-start(f32[256,128]{1,0:T(8,128)S(1)} %get-tuple-element.26), channel_id=1, source_target_pairs={{0,2},{1,3},{2,0},{3,1},{4,6},{5,7},{6,4},{7,5},{8,10},{9,11},{10,... | collective-permute-start | bytes 393224 | tf_op jit(solution)/shard_map/reduce/ppermute | solution.py:216
  21.5 7.8 %collective-permute-start.10 = (f32[2,256,128]{2,1,0:T(8,128)S(1)}, f32[2,256,128]{2,1,0:T(8,128)S(1)}, u32[]{:S(2)}, u32[]{:S(2)}) collective-permute-start(f32[2,256,128]{2,1,0:T(8,128)S(1)} %backward.7._), channel_id=1, source_target_pairs={{0,1},{1,0},{2,3},{3,2},{4,5},{5,4},{6,7},{7,6},{8,9},{9,8},{10,11... | collective-permute-start | bytes 786440 | tf_op jit(solution)/shard_map/reduce/ppermute | solution.py:216
  24.4 6.7 %collective-permute-start.9 = (f32[256,128]{1,0:T(8,128)S(1)}, f32[256,128]{1,0:T(8,128)S(1)}, u32[]{:S(2)}, u32[]{:S(2)}) collective-permute-start(f32[256,128]{1,0:T(8,128)S(1)} %get-tuple-element.24), channel_id=1, source_target_pairs={{0,8},{8,0},{16,24},{24,16},{1,9},{9,1},{17,25},{25,17},{2,10},{10... | collective-permute-start | bytes 393224 | tf_op jit(solution)/shard_map/reduce/ppermute | solution.py:216
  26.6 9.0 %collective-permute-start.12 = (f32[256,128]{1,0:T(8,128)S(1)}, f32[256,128]{1,0:T(8,128)S(1)}, u32[]{:S(2)}, u32[]{:S(2)}) collective-permute-start(f32[256,128]{1,0:T(8,128)S(1)} %reduce.8), channel_id=1, source_target_pairs={{0,4},{1,5},{2,6},{3,7},{4,0},{5,1},{6,2},{7,3},{8,12},{9,13},{10,... | collective-permute-start | bytes 393224 | tf_op jit(solution)/shard_map/reduce/ppermute | solution.py:216
  26.7 8.9 %collective-permute-start.13 = (f32[256,128]{1,0:T(8,128)S(1)}, f32[256,128]{1,0:T(8,128)S(1)}, u32[]{:S(2)}, u32[]{:S(2)}) collective-permute-start(f32[256,128]{1,0:T(8,128)S(1)} %get-tuple-element.27), channel_id=1, source_target_pairs={{0,16},{8,24},{16,0},{24,8},{1,17},{9,25},{17,1},{25,9},{2,18},{10... | collective-permute-start | bytes 393224 | tf_op jit(solution)/shard_map/reduce/ppermute | solution.py:216
  28.6 7.1 %collective-permute-start.14 = (f32[256,128]{1,0:T(8,128)S(1)}, f32[256,128]{1,0:T(8,128)S(1)}, u32[]{:S(2)}, u32[]{:S(2)}) collective-permute-start(f32[256,128]{1,0:T(8,128)S(1)} %get-tuple-element.28), channel_id=1, source_target_pairs={{0,24},{8,16},{16,8},{24,0},{1,25},{9,17},{17,9},{25,1},{2,26},{10... | collective-permute-start | bytes 393224 | tf_op jit(solution)/shard_map/reduce/ppermute | solution.py:216
  29.4 7.5 %collective-permute-start.15 = (f32[256,128]{1,0:T(8,128)S(1)}, f32[256,128]{1,0:T(8,128)S(1)}, u32[]{:S(2)}, u32[]{:S(2)}) collective-permute-start(f32[256,128]{1,0:T(8,128)S(1)} %get-tuple-element.31), channel_id=1, source_target_pairs={{0,2},{1,3},{2,0},{3,1},{4,6},{5,7},{6,4},{7,5},{8,10},{9,11},{10,... | collective-permute-start | bytes 393224 | tf_op jit(solution)/shard_map/reduce/ppermute | solution.py:216

commit v15 on v13

--- a/solution.py
+++ b/solution.py
@@ -329,11 +329,14 @@
         with jax.named_scope("gather"):
             passed, late = gathered(high)
         with jax.named_scope("flip"):
+            after = passed
+            for at in range(1, n_row - 1):
+                after = grads[at] = call(pass_kernel, block, [grads[at]], after=after)
             flipped = call(
                 functools.partial(flip_kernel, tile),
                 jax.ShapeDtypeStruct((2 * width, n_rows), BF16),
                 grads,
-                after=passed,
+                after=after,
             )
         with jax.named_scope("gather"):
             early = stacked(passed, flipped)

time: 37.3 us -> 37.1 us (level)
  starting transfers between devices: 17.5 us -> 18.8 us
  Pallas kernels: 11.3 us -> 10.3 us
  waiting for transfers between devices: 6.96 us -> 6.41 us
    ppermute x16, starting transfers between devices: 17.5 us -> 18.8 us  [swap(): lax.ppermute(x, axis, [(at, at ^ mask) for at in range(lax.axis_size(axis...]
    pallas_call x18 -> x20, Pallas kernels: 11.3 us -> 10.3 us  [call(): pl.pallas_call(body, out_shape=out_shape, in_specs=specs, out_specs=tuple...]
    ppermute x16, waiting for transfers between devices: 6.96 us -> 6.41 us  [swap(): lax.ppermute(x, axis, [(at, at ^ mask) for at in range(lax.axis_size(axis...]
  transfers between devices with their start and end apart: 16 -> 16, of which waited for: 3 -> 5; matrix products, arithmetic and copies ran while one was open for 0% -> 0% of each run, Pallas kernels for 25% -> 23%
where the time goes in v15:
time: 37.1 us; the launch traced here: 37 us
  starting transfers between devices  18.8 us (51%)
  Pallas kernels  10.3 us (28%)
  waiting for transfers between devices  6.41 us (17%)
  between operations  1.47 us (4%)
    ppermute x16, starting transfers between devices, swap(): lax.ppermute(x, axis, [(at, at ^ mask) for at in range(lax.axis_size(axis...  18.8 us
    pallas_call x20, Pallas kernels, call(): pl.pallas_call(body, out_shape=out_shape, in_specs=specs, out_specs=tuple...  10.3 us
    ppermute x16, waiting for transfers between devices, swap(): lax.ppermute(x, axis, [(at, at ^ mask) for at in range(lax.axis_size(axis...  6.41 us
  transfers between devices with their start and end apart: 16, of which 5 were waited for; matrix products, arithmetic and copies ran while one was open for 0% of the time, Pallas kernels for 23%

profile of v15, /device:TPU:0, one launch (start us, length us, event | category | flops | bytes accessed | tf_op | source)
XLA Modules:
  0.0 37.0 jit_solution(10308758463281954277)
XLA Ops:
  0.6 1.2 %scale.1 = (f32[256,128]{1,0:T(8,128)S(1)}, f32[256,128]{1,0:T(8,128)S(1)}, f32[256,128]{1,0:T(8,128)S(1)}, f32[256,128]{1,0:T(8,128)S(1)}, s32[2,128]{1,0:T(2,128)S(1)}) custom-call(f32[256,128]{1,0:T(8,128)} %refs_0_.1, f32[256,128]{1,0:T(8,128)} %refs_1_.1, s32[2,128]{1,0:T(2,128)} %bitcast.4, s32[2,128]{1,0:T(2,128)} %bitcast.5, s32[2,1,1,128]{3,2,1,0:T(1,128)} %refs_4_.1), custom_call_target="tpu_custom_call" | custom-call | bytes 1024 | tf_op jit(solution)/shard_map/scale/pallas_call | solution.py:229
  1.8 4.1 %collective-permute-start = (f32[256,128]{1,0:T(8,128)S(1)}, f32[256,128]{1,0:T(8,128)S(1)}, u32[]{:S(2)}, u32[]{:S(2)}) collective-permute-start(f32[256,128]{1,0:T(8,128)S(1)} %get-tuple-element.19.refs_0_), channel_id=1, source_target_pairs={{0,4},{1,5},{2,6},{3,7},{4,0},{5,1},{6,2},{7,3},{8,12},{9,13},{10,... | collective-permute-start | bytes 393224 | tf_op jit(solution)/shard_map/gather/ppermute | solution.py:216
  5.9 1.5 %collective-permute-start.1 = (f32[256,128]{1,0:T(8,128)S(1)}, f32[256,128]{1,0:T(8,128)S(1)}, u32[]{:S(2)}, u32[]{:S(2)}) collective-permute-start(f32[256,128]{1,0:T(8,128)S(1)} %get-tuple-element.20.refs_0_), channel_id=1, source_target_pairs={{0,8},{8,0},{16,24},{24,16},{1,9},{9,1},{17,25},{25,17},{2,10},{10... | collective-permute-start | bytes 393224 | tf_op jit(solution)/shard_map/gather/ppermute | solution.py:216
  7.4 1.5 %collective-permute-start.2 = (f32[256,128]{1,0:T(8,128)S(1)}, f32[256,128]{1,0:T(8,128)S(1)}, u32[]{:S(2)}, u32[]{:S(2)}) collective-permute-start(f32[256,128]{1,0:T(8,128)S(1)} %get-tuple-element.20.refs_0_), channel_id=1, source_target_pairs={{0,16},{8,24},{16,0},{24,8},{1,17},{9,25},{17,1},{25,9},{2,18},{10... | collective-permute-start | bytes 393224 | tf_op jit(solution)/shard_map/gather/ppermute | solution.py:216
  8.9 0.5 %collective-permute-start.3 = (f32[256,128]{1,0:T(8,128)S(1)}, f32[256,128]{1,0:T(8,128)S(1)}, u32[]{:S(2)}, u32[]{:S(2)}) collective-permute-start(f32[256,128]{1,0:T(8,128)S(1)} %get-tuple-element.20.refs_0_), channel_id=1, source_target_pairs={{0,24},{8,16},{16,8},{24,0},{1,25},{9,17},{17,9},{25,1},{2,26},{10... | collective-permute-start | bytes 393224 | tf_op jit(solution)/shard_map/gather/ppermute | solution.py:216
  9.4 1.6 %collective-permute-start.4 = (f32[256,128]{1,0:T(8,128)S(1)}, f32[256,128]{1,0:T(8,128)S(1)}, u32[]{:S(2)}, u32[]{:S(2)}) collective-permute-start(f32[256,128]{1,0:T(8,128)S(1)} %get-tuple-element.19.refs_0_), channel_id=1, source_target_pairs={{0,2},{1,3},{2,0},{3,1},{4,6},{5,7},{6,4},{7,5},{8,10},{9,11},{10,... | collective-permute-start | bytes 393224 | tf_op jit(solution)/shard_map/gather/ppermute | solution.py:216
  11.6 2.9 %split.1 = (bf16[1024,2048]{1,0:T(8,128)(2,1)S(1)}, bf16[1024,2048]{1,0:T(8,128)(2,1)S(1)}) custom-call(s32[1,1]{1,0:T(1,128)S(6)} %copy.9.count_ref, s32[2,128]{1,0:T(2,128)S(1)} %get-tuple-element.17.plan_ref, f32[128,128,128]{2,1,0:T(8,128)} %bitcast.3), custom_call_target="tpu_custom_call" | custom-call | bytes 1024 | tf_op jit(solution)/shard_map/split/pallas_call | solution.py:229
  14.5 0.0 collective-permute-done.refs_0_
  14.6 0.5 %collective-permute-start.5 = (f32[256,128]{1,0:T(8,128)S(1)}, f32[256,128]{1,0:T(8,128)S(1)}, u32[]{:S(2)}, u32[]{:S(2)}) collective-permute-start(f32[256,128]{1,0:T(8,128)S(1)} %gather.3._.refs_2_), channel_id=1, source_target_pairs={{0,2},{1,3},{2,0},{3,1},{4,6},{5,7},{6,4},{7,5},{8,10},{9,11},{10,... | collective-permute-start | bytes 393224 | tf_op jit(solution)/shard_map/gather/ppermute | solution.py:216
  15.1 0.0 collective-permute-done.1.refs_0_
  15.1 0.1 collective-permute-done.2.refs_0_
  15.2 0.0 collective-permute-done.3.refs_3_
  15.2 0.2 flip.5._.refs_0_
  15.4 0.0 collective-permute-done.4.refs_1_
  15.5 0.1 collective-permute-start.7
  15.5 0.7 %backward.5._ = f32[2,256,128]{2,1,0:T(8,128)S(1)} custom-call(f32[3,256,128]{2,1,0:T(8,128)S(1)} %gather.4._.refs_0_, bf16[256,1024]{1,0:T(8,128)(2,1)S(1)} %flip.5._.refs_0_, bf16[1024,2048]{1,0:T(8,128)(2,1)S(1)} %get-tuple-element.18._.refs_1_.refs_4_, bf16[1024,2048]{1,0:T(8,128)(2,1)S(1)} %get-tuple-element.21.refs_2_.refs_5_), custom_call_target="tpu_custom_call" | custom-call | bytes 1024 | tf_op jit(solution)/shard_map/backward/pallas_call | solution.py:229
  16.2 0.6 %collective-permute-start.6 = (f32[2,256,128]{2,1,0:T(8,128)S(1)}, f32[2,256,128]{2,1,0:T(8,128)S(1)}, u32[]{:S(2)}, u32[]{:S(2)}) collective-permute-start(f32[2,256,128]{2,1,0:T(8,128)S(1)} %backward.5._), channel_id=1, source_target_pairs={{0,1},{1,0},{2,3},{3,2},{4,5},{5,4},{6,7},{7,6},{8,9},{9,8},{10,11... | collective-permute-start | bytes 786440 | tf_op jit(solution)/shard_map/backward/ppermute | solution.py:216
  16.8 0.7 %backward.6._.refs_0_ = f32[2,256,128]{2,1,0:T(8,128)S(1)} custom-call(f32[2,256,128]{2,1,0:T(8,128)S(1)} %backward.5._, bf16[256,1024]{1,0:T(8,128)(2,1)S(1)} %flip.5._.refs_0_, bf16[1024,2048]{1,0:T(8,128)(2,1)S(1)} %get-tuple-element.18._.refs_1_.refs_4_, bf16[1024,2048]{1,0:T(8,128)(2,1)S(1)} %get-tuple-element.21.refs_2_.refs_5_), custom_call_target="tpu_custom_call" | custom-call | bytes 1024 | tf_op jit(solution)/shard_map/backward/pallas_call | solution.py:229
  17.5 0.7 %backward.7._ = f32[2,256,128]{2,1,0:T(8,128)S(1)} custom-call(f32[2,256,128]{2,1,0:T(8,128)S(1)} %backward.6._.refs_0_, bf16[256,1024]{1,0:T(8,128)(2,1)S(1)} %flip.5._.refs_0_, bf16[1024,2048]{1,0:T(8,128)(2,1)S(1)} %get-tuple-element.18._.refs_1_.refs_4_, bf16[1024,2048]{1,0:T(8,128)(2,1)S(1)} %get-tuple-element.21.refs_2_.refs_5_), custom_call_target="tpu_custom_call" | custom-call | bytes 1024 | tf_op jit(solution)/shard_map/backward/pallas_call | solution.py:229
  18.2 0.7 %backward.8._.refs_0_ = f32[2,256,128]{2,1,0:T(8,128)S(1)} custom-call(f32[2,256,128]{2,1,0:T(8,128)S(1)} %backward.7._, bf16[256,1024]{1,0:T(8,128)(2,1)S(1)} %flip.5._.refs_0_, bf16[1024,2048]{1,0:T(8,128)(2,1)S(1)} %get-tuple-element.18._.refs_1_.refs_4_, bf16[1024,2048]{1,0:T(8,128)(2,1)S(1)} %get-tuple-element.21.refs_2_.refs_5_), custom_call_target="tpu_custom_call" | custom-call | bytes 1024 | tf_op jit(solution)/shard_map/backward/pallas_call | solution.py:229
  18.9 0.1 collective-permute-start.11
  18.9 0.7 %collective-permute-done.5.refs_0_ = f32[256,128]{1,0:T(8,128)S(1)} collective-permute-done((f32[256,128]{1,0:T(8,128)S(1)}, f32[256,128]{1,0:T(8,128)S(1)}, u32[]{:S(2)}, u32[]{:S(2)}) %collective-permute-start.5) | collective-permute-done | bytes 131104 | tf_op jit(solution)/shard_map/gather/ppermute | solution.py:216
  19.6 0.1 collective-permute-start.8
  19.7 0.0 collective-permute-done.6.refs_1_
  19.7 1.5 %collective-permute-start.12 = (f32[256,128]{1,0:T(8,128)S(1)}, f32[256,128]{1,0:T(8,128)S(1)}, u32[]{:S(2)}, u32[]{:S(2)}) collective-permute-start(f32[256,128]{1,0:T(8,128)S(1)} %get-tuple-element.27), channel_id=1, source_target_pairs={{0,2},{1,3},{2,0},{3,1},{4,6},{5,7},{6,4},{7,5},{8,10},{9,11},{10,... | collective-permute-start | bytes 393224 | tf_op jit(solution)/shard_map/reduce/ppermute | solution.py:216
  21.2 0.0 collective-permute-done.8.refs_3_
  21.2 0.0 collective-permute-done.7.refs_1_
  21.2 2.4 %forward.1 = (f32[256,128]{1,0:T(8,128)S(1)}, f32[256,128]{1,0:T(8,128)S(1)}, f32[256,128]{1,0:T(8,128)S(1)}, f32[256,128]{1,0:T(8,128)S(1)}) custom-call(f32[256,128]{1,0:T(8,128)S(1)} %get-tuple-element.22._.refs_0_, f32[3,256,128]{2,1,0:T(8,128)S(1)} %gather.4._.refs_0_, f32[3,256,128]{2,1,0:T(8,128)S(1)} %collective-permute-done.7.refs_1_, ...), custom_call_target="tpu_custom_call" | custom-call | bytes 1024 | tf_op jit(solution)/shard_map/forward/pallas_call | solution.py:229
  23.6 1.9 %collective-permute-start.9 = (f32[256,128]{1,0:T(8,128)S(1)}, f32[256,128]{1,0:T(8,128)S(1)}, u32[]{:S(2)}, u32[]{:S(2)}) collective-permute-start(f32[256,128]{1,0:T(8,128)S(1)} %get-tuple-element.24), channel_id=1, source_target_pairs={{0,8},{8,0},{16,24},{24,16},{1,9},{9,1},{17,25},{25,17},{2,10},{10... | collective-permute-start | bytes 393224 | tf_op jit(solution)/shard_map/reduce/ppermute | solution.py:216
  25.5 1.1 %collective-permute-start.10 = (f32[256,128]{1,0:T(8,128)S(1)}, f32[256,128]{1,0:T(8,128)S(1)}, u32[]{:S(2)}, u32[]{:S(2)}) collective-permute-start(f32[256,128]{1,0:T(8,128)S(1)} %get-tuple-element.25), channel_id=1, source_target_pairs={{0,16},{8,24},{16,0},{24,8},{1,17},{9,25},{17,1},{25,9},{2,18},{10... | collective-permute-start | bytes 393224 | tf_op jit(solution)/shard_map/reduce/ppermute | solution.py:216
  26.6 0.0 collective-permute-done.12.refs_1_
  26.7 1.3 %collective-permute-start.13 = (f32[256,128]{1,0:T(8,128)S(1)}, f32[256,128]{1,0:T(8,128)S(1)}, u32[]{:S(2)}, u32[]{:S(2)}) collective-permute-start(f32[256,128]{1,0:T(8,128)S(1)} %reduce.8), channel_id=1, source_target_pairs={{0,4},{1,5},{2,6},{3,7},{4,0},{5,1},{6,2},{7,3},{8,12},{9,13},{10,... | collective-permute-start | bytes 393224 | tf_op jit(solution)/shard_map/reduce/ppermute | solution.py:216
  28.0 1.5 %collective-permute-start.14 = (f32[256,128]{1,0:T(8,128)S(1)}, f32[256,128]{1,0:T(8,128)S(1)}, u32[]{:S(2)}, u32[]{:S(2)}) collective-permute-start(f32[256,128]{1,0:T(8,128)S(1)} %get-tuple-element.28), channel_id=1, source_target_pairs={{0,24},{8,16},{16,8},{24,0},{1,25},{9,17},{17,9},{25,1},{2,26},{10... | collective-permute-start | bytes 393224 | tf_op jit(solution)/shard_map/reduce/ppermute | solution.py:216
  29.5 0.0 collective-permute-done.11.refs_1_
  29.5 1.0 %collective-permute-start.15 = (f32[256,128]{1,0:T(8,128)S(1)}, f32[256,128]{1,0:T(8,128)S(1)}, u32[]{:S(2)}, u32[]{:S(2)}) collective-permute-start(f32[256,128]{1,0:T(8,128)S(1)} %get-tuple-element.31), channel_id=1, source_target_pairs={{0,2},{1,3},{2,0},{3,1},{4,6},{5,7},{6,4},{7,5},{8,10},{9,11},{10,... | collective-permute-start | bytes 393224 | tf_op jit(solution)/shard_map/reduce/ppermute | solution.py:216
  30.6 0.0 collective-permute-done.9.refs_1_
  30.6 1.7 %collective-permute-done.10.refs_2_ = f32[256,128]{1,0:T(8,128)S(1)} collective-permute-done((f32[256,128]{1,0:T(8,128)S(1)}, f32[256,128]{1,0:T(8,128)S(1)}, u32[]{:S(2)}, u32[]{:S(2)}) %collective-permute-start.10) | collective-permute-done | bytes 131104 | tf_op jit(solution)/shard_map/reduce/ppermute | solution.py:216
  32.3 3.1 %collective-permute-done.13.refs_1_ = f32[256,128]{1,0:T(8,128)S(1)} collective-permute-done((f32[256,128]{1,0:T(8,128)S(1)}, f32[256,128]{1,0:T(8,128)S(1)}, u32[]{:S(2)}, u32[]{:S(2)}) %collective-permute-start.13) | collective-permute-done | bytes 131104 | tf_op jit(solution)/shard_map/reduce/ppermute | solution.py:216
  35.4 0.0 collective-permute-done.14.refs_1_
  35.5 0.8 %collective-permute-done.15.refs_1_ = f32[256,128]{1,0:T(8,128)S(1)} collective-permute-done((f32[256,128]{1,0:T(8,128)S(1)}, f32[256,128]{1,0:T(8,128)S(1)}, u32[]{:S(2)}, u32[]{:S(2)}) %collective-permute-start.15) | collective-permute-done | bytes 131104 | tf_op jit(solution)/shard_map/reduce/ppermute | solution.py:216
  36.3 0.7 %reduce.11 = (f32[256,128]{1,0:T(8,128)}, f32[256,128]{1,0:T(8,128)}) custom-call(f32[256,128]{1,0:T(8,128)S(1)} %reduce.10.row_ref, f32[256,128]{1,0:T(8,128)S(1)} %get-tuple-element.29.row_factor_ref, f32[256,128]{1,0:T(8,128)S(1)} %get-tuple-element.30.col_factor_ref, f32[256,128]{1,0:T(8,128)S(1)} %reduce.9._.refs_0_, ...), custom_call_target="tpu_custom_call" | custom-call | bytes 1024 | tf_op jit(solution)/shard_map/reduce/pallas_call | solution.py:229
  (11 shorter events, 0.2 us)
Async XLA Ops:
  1.8 12.7 %collective-permute-start = (f32[256,128]{1,0:T(8,128)S(1)}, f32[256,128]{1,0:T(8,128)S(1)}, u32[]{:S(2)}, u32[]{:S(2)}) collective-permute-start(f32[256,128]{1,0:T(8,128)S(1)} %get-tuple-element.19.refs_0_), channel_id=1, source_target_pairs={{0,4},{1,5},{2,6},{3,7},{4,0},{5,1},{6,2},{7,3},{8,12},{9,13},{10,... | collective-permute-start | bytes 393224 | tf_op jit(solution)/shard_map/gather/ppermute | solution.py:216
  5.9 9.2 %collective-permute-start.1 = (f32[256,128]{1,0:T(8,128)S(1)}, f32[256,128]{1,0:T(8,128)S(1)}, u32[]{:S(2)}, u32[]{:S(2)}) collective-permute-start(f32[256,128]{1,0:T(8,128)S(1)} %get-tuple-element.20.refs_0_), channel_id=1, source_target_pairs={{0,8},{8,0},{16,24},{24,16},{1,9},{9,1},{17,25},{25,17},{2,10},{10... | collective-permute-start | bytes 393224 | tf_op jit(solution)/shard_map/gather/ppermute | solution.py:216
  7.4 7.8 %collective-permute-start.2 = (f32[256,128]{1,0:T(8,128)S(1)}, f32[256,128]{1,0:T(8,128)S(1)}, u32[]{:S(2)}, u32[]{:S(2)}) collective-permute-start(f32[256,128]{1,0:T(8,128)S(1)} %get-tuple-element.20.refs_0_), channel_id=1, source_target_pairs={{0,16},{8,24},{16,0},{24,8},{1,17},{9,25},{17,1},{25,9},{2,18},{10... | collective-permute-start | bytes 393224 | tf_op jit(solution)/shard_map/gather/ppermute | solution.py:216
  8.9 6.3 %collective-permute-start.3 = (f32[256,128]{1,0:T(8,128)S(1)}, f32[256,128]{1,0:T(8,128)S(1)}, u32[]{:S(2)}, u32[]{:S(2)}) collective-permute-start(f32[256,128]{1,0:T(8,128)S(1)} %get-tuple-element.20.refs_0_), channel_id=1, source_target_pairs={{0,24},{8,16},{16,8},{24,0},{1,25},{9,17},{17,9},{25,1},{2,26},{10... | collective-permute-start | bytes 393224 | tf_op jit(solution)/shard_map/gather/ppermute | solution.py:216
  9.4 6.0 %collective-permute-start.4 = (f32[256,128]{1,0:T(8,128)S(1)}, f32[256,128]{1,0:T(8,128)S(1)}, u32[]{:S(2)}, u32[]{:S(2)}) collective-permute-start(f32[256,128]{1,0:T(8,128)S(1)} %get-tuple-element.19.refs_0_), channel_id=1, source_target_pairs={{0,2},{1,3},{2,0},{3,1},{4,6},{5,7},{6,4},{7,5},{8,10},{9,11},{10,... | collective-permute-start | bytes 393224 | tf_op jit(solution)/shard_map/gather/ppermute | solution.py:216
  14.6 5.0 %collective-permute-start.5 = (f32[256,128]{1,0:T(8,128)S(1)}, f32[256,128]{1,0:T(8,128)S(1)}, u32[]{:S(2)}, u32[]{:S(2)}) collective-permute-start(f32[256,128]{1,0:T(8,128)S(1)} %gather.3._.refs_2_), channel_id=1, source_target_pairs={{0,2},{1,3},{2,0},{3,1},{4,6},{5,7},{6,4},{7,5},{8,10},{9,11},{10,... | collective-permute-start | bytes 393224 | tf_op jit(solution)/shard_map/gather/ppermute | solution.py:216
  15.5 5.7 %collective-permute-start.7 = (f32[3,256,128]{2,1,0:T(8,128)S(1)}, f32[3,256,128]{2,1,0:T(8,128)S(1)}, u32[]{:S(2)}, u32[]{:S(2)}) collective-permute-start(f32[3,256,128]{2,1,0:T(8,128)S(1)} %gather.4._.refs_0_), channel_id=1, source_target_pairs={{0,1},{1,0},{2,3},{3,2},{4,5},{5,4},{6,7},{7,6},{8,9},{9,8},{10,11... | collective-permute-start | bytes 1179656 | tf_op jit(solution)/shard_map/gather/ppermute | solution.py:216
  16.2 3.5 %collective-permute-start.6 = (f32[2,256,128]{2,1,0:T(8,128)S(1)}, f32[2,256,128]{2,1,0:T(8,128)S(1)}, u32[]{:S(2)}, u32[]{:S(2)}) collective-permute-start(f32[2,256,128]{2,1,0:T(8,128)S(1)} %backward.5._), channel_id=1, source_target_pairs={{0,1},{1,0},{2,3},{3,2},{4,5},{5,4},{6,7},{7,6},{8,9},{9,8},{10,11... | collective-permute-start | bytes 786440 | tf_op jit(solution)/shard_map/backward/ppermute | solution.py:216
  18.9 10.6 %collective-permute-start.11 = (f32[2,256,128]{2,1,0:T(8,128)S(1)}, f32[2,256,128]{2,1,0:T(8,128)S(1)}, u32[]{:S(2)}, u32[]{:S(2)}) collective-permute-start(f32[2,256,128]{2,1,0:T(8,128)S(1)} %backward.7._), channel_id=1, source_target_pairs={{0,1},{1,0},{2,3},{3,2},{4,5},{5,4},{6,7},{7,6},{8,9},{9,8},{10,11... | collective-permute-start | bytes 786440 | tf_op jit(solution)/shard_map/reduce/ppermute | solution.py:216
  19.6 1.6 %collective-permute-start.8 = (f32[1,256,128]{2,1,0:T(8,128)S(1)}, f32[1,256,128]{2,1,0:T(8,128)S(1)}, u32[]{:S(2)}, u32[]{:S(2)}) collective-permute-start(f32[1,256,128]{2,1,0:T(8,128)S(1)} %gather.5._.refs_2_), channel_id=1, source_target_pairs={{0,1},{1,0},{2,3},{3,2},{4,5},{5,4},{6,7},{7,6},{8,9},{9,8},{10,11... | collective-permute-start | bytes 393224 | tf_op jit(solution)/shard_map/gather/ppermute | solution.py:216
  19.7 6.9 %collective-permute-start.12 = (f32[256,128]{1,0:T(8,128)S(1)}, f32[256,128]{1,0:T(8,128)S(1)}, u32[]{:S(2)}, u32[]{:S(2)}) collective-permute-start(f32[256,128]{1,0:T(8,128)S(1)} %get-tuple-element.27), channel_id=1, source_target_pairs={{0,2},{1,3},{2,0},{3,1},{4,6},{5,7},{6,4},{7,5},{8,10},{9,11},{10,... | collective-permute-start | bytes 393224 | tf_op jit(solution)/shard_map/reduce/ppermute | solution.py:216
  23.6 7.0 %collective-permute-start.9 = (f32[256,128]{1,0:T(8,128)S(1)}, f32[256,128]{1,0:T(8,128)S(1)}, u32[]{:S(2)}, u32[]{:S(2)}) collective-permute-start(f32[256,128]{1,0:T(8,128)S(1)} %get-tuple-element.24), channel_id=1, source_target_pairs={{0,8},{8,0},{16,24},{24,16},{1,9},{9,1},{17,25},{25,17},{2,10},{10... | collective-permute-start | bytes 393224 | tf_op jit(solution)/shard_map/reduce/ppermute | solution.py:216
  25.5 6.7 %collective-permute-start.10 = (f32[256,128]{1,0:T(8,128)S(1)}, f32[256,128]{1,0:T(8,128)S(1)}, u32[]{:S(2)}, u32[]{:S(2)}) collective-permute-start(f32[256,128]{1,0:T(8,128)S(1)} %get-tuple-element.25), channel_id=1, source_target_pairs={{0,16},{8,24},{16,0},{24,8},{1,17},{9,25},{17,1},{25,9},{2,18},{10... | collective-permute-start | bytes 393224 | tf_op jit(solution)/shard_map/reduce/ppermute | solution.py:216
  26.7 8.8 %collective-permute-start.13 = (f32[256,128]{1,0:T(8,128)S(1)}, f32[256,128]{1,0:T(8,128)S(1)}, u32[]{:S(2)}, u32[]{:S(2)}) collective-permute-start(f32[256,128]{1,0:T(8,128)S(1)} %reduce.8), channel_id=1, source_target_pairs={{0,4},{1,5},{2,6},{3,7},{4,0},{5,1},{6,2},{7,3},{8,12},{9,13},{10,... | collective-permute-start | bytes 393224 | tf_op jit(solution)/shard_map/reduce/ppermute | solution.py:216
  28.0 7.4 %collective-permute-start.14 = (f32[256,128]{1,0:T(8,128)S(1)}, f32[256,128]{1,0:T(8,128)S(1)}, u32[]{:S(2)}, u32[]{:S(2)}) collective-permute-start(f32[256,128]{1,0:T(8,128)S(1)} %get-tuple-element.28), channel_id=1, source_target_pairs={{0,24},{8,16},{16,8},{24,0},{1,25},{9,17},{17,9},{25,1},{2,26},{10... | collective-permute-start | bytes 393224 | tf_op jit(solution)/shard_map/reduce/ppermute | solution.py:216
  29.5 6.8 %collective-permute-start.15 = (f32[256,128]{1,0:T(8,128)S(1)}, f32[256,128]{1,0:T(8,128)S(1)}, u32[]{:S(2)}, u32[]{:S(2)}) collective-permute-start(f32[256,128]{1,0:T(8,128)S(1)} %get-tuple-element.31), channel_id=1, source_target_pairs={{0,2},{1,3},{2,0},{3,1},{4,6},{5,7},{6,4},{7,5},{8,10},{9,11},{10,... | collective-permute-start | bytes 393224 | tf_op jit(solution)/shard_map/reduce/ppermute | solution.py:216

commit v16 on v15

--- a/solution.py
+++ b/solution.py
@@ -425,10 +425,9 @@
 
     with jax.named_scope("reduce"):
         mine, *grad_parts = halved(close_sums, after)
-        first = [swap(forwards[k], "row", k) for k in range(1, n_row - 1)]
-        row_sum = call(sum_kernel, block, [forwards[0], *first])
-        mine = total([mine, swap(crossing, "col", 2 * half)], row_sum)
-        row_sum = call(sum_kernel, block, [row_sum, swap(forwards[-1], "row", n_row - 1)], after=mine)
+        mine = total([mine, swap(crossing, "col", 2 * half)], None, 2 * 10**9)
+        row_parts = [forwards[0]] + [swap(forwards[k], "row", k) for k in range(1, n_row)]
+        row_sum = call(sum_kernel, block, row_parts, after=mine)
         return call(
             finish_kernel, (block, block), (row_sum, row_factor, col_factor, mine, *grad_parts), mebibytes=4
         )

time: 37.1 us -> 37.5 us (1.011); the launches traced: 37 us -> 37.9 us
  starting transfers between devices: 18.8 us -> 16.4 us
  waiting for transfers between devices: 6.41 us -> 8.72 us
  Pallas kernels: 10.3 us -> 11.3 us
    ppermute x16, starting transfers between devices: 18.8 us -> 16.4 us  [swap(): lax.ppermute(x, axis, [(at, at ^ mask) for at in range(lax.axis_size(axis...]
    ppermute x16, waiting for transfers between devices: 6.41 us -> 8.72 us  [swap(): lax.ppermute(x, axis, [(at, at ^ mask) for at in range(lax.axis_size(axis...]
    pallas_call x20 -> x19, Pallas kernels: 10.3 us -> 11.3 us  [call(): pl.pallas_call(body, out_shape=out_shape, in_specs=specs, out_specs=tuple...]
  transfers between devices with their start and end apart: 16 -> 16, of which waited for: 5 -> 6; matrix products, arithmetic and copies ran while one was open for 0% -> 0% of each run, Pallas kernels for 23% -> 25%
where the time goes in v16:
time: 37.5 us; the launch traced here: 37.9 us
  starting transfers between devices  16.4 us (44%)
  Pallas kernels  11.3 us (30%)
  waiting for transfers between devices  8.72 us (23%)
  between operations  1.49 us (4%)
    ppermute x16, starting transfers between devices, swap(): lax.ppermute(x, axis, [(at, at ^ mask) for at in range(lax.axis_size(axis...  16.4 us
    pallas_call x19, Pallas kernels, call(): pl.pallas_call(body, out_shape=out_shape, in_specs=specs, out_specs=tuple...  11.3 us
    ppermute x16, waiting for transfers between devices, swap(): lax.ppermute(x, axis, [(at, at ^ mask) for at in range(lax.axis_size(axis...  8.72 us
  transfers between devices with their start and end apart: 16, of which 6 were waited for; matrix products, arithmetic and copies ran while one was open for 0% of the time, Pallas kernels for 25%

profile of v16, /device:TPU:0, one launch (start us, length us, event | category | flops | bytes accessed | tf_op | source)
XLA Modules:
  0.0 37.9 jit_solution(17168216466078652969)
XLA Ops:
  0.6 1.2 %scale.1 = (f32[256,128]{1,0:T(8,128)S(1)}, f32[256,128]{1,0:T(8,128)S(1)}, f32[256,128]{1,0:T(8,128)S(1)}, f32[256,128]{1,0:T(8,128)S(1)}, s32[2,128]{1,0:T(2,128)S(1)}) custom-call(f32[256,128]{1,0:T(8,128)} %refs_0_.1, f32[256,128]{1,0:T(8,128)} %refs_1_.1, s32[2,128]{1,0:T(2,128)} %bitcast.4, s32[2,128]{1,0:T(2,128)} %bitcast.5, s32[2,1,1,128]{3,2,1,0:T(1,128)} %refs_4_.1), custom_call_target="tpu_custom_call" | custom-call | bytes 1024 | tf_op jit(solution)/shard_map/scale/pallas_call | solution.py:229
  1.8 4.1 %collective-permute-start = (f32[256,128]{1,0:T(8,128)S(1)}, f32[256,128]{1,0:T(8,128)S(1)}, u32[]{:S(2)}, u32[]{:S(2)}) collective-permute-start(f32[256,128]{1,0:T(8,128)S(1)} %get-tuple-element.19.refs_0_), channel_id=1, source_target_pairs={{0,4},{1,5},{2,6},{3,7},{4,0},{5,1},{6,2},{7,3},{8,12},{9,13},{10,... | collective-permute-start | bytes 393224 | tf_op jit(solution)/shard_map/gather/ppermute | solution.py:216
  5.9 1.5 %collective-permute-start.1 = (f32[256,128]{1,0:T(8,128)S(1)}, f32[256,128]{1,0:T(8,128)S(1)}, u32[]{:S(2)}, u32[]{:S(2)}) collective-permute-start(f32[256,128]{1,0:T(8,128)S(1)} %get-tuple-element.20.refs_0_), channel_id=1, source_target_pairs={{0,8},{8,0},{16,24},{24,16},{1,9},{9,1},{17,25},{25,17},{2,10},{10... | collective-permute-start | bytes 393224 | tf_op jit(solution)/shard_map/gather/ppermute | solution.py:216
  7.4 1.5 %collective-permute-start.2 = (f32[256,128]{1,0:T(8,128)S(1)}, f32[256,128]{1,0:T(8,128)S(1)}, u32[]{:S(2)}, u32[]{:S(2)}) collective-permute-start(f32[256,128]{1,0:T(8,128)S(1)} %get-tuple-element.20.refs_0_), channel_id=1, source_target_pairs={{0,16},{8,24},{16,0},{24,8},{1,17},{9,25},{17,1},{25,9},{2,18},{10... | collective-permute-start | bytes 393224 | tf_op jit(solution)/shard_map/gather/ppermute | solution.py:216
  8.9 0.5 %collective-permute-start.3 = (f32[256,128]{1,0:T(8,128)S(1)}, f32[256,128]{1,0:T(8,128)S(1)}, u32[]{:S(2)}, u32[]{:S(2)}) collective-permute-start(f32[256,128]{1,0:T(8,128)S(1)} %get-tuple-element.20.refs_0_), channel_id=1, source_target_pairs={{0,24},{8,16},{16,8},{24,0},{1,25},{9,17},{17,9},{25,1},{2,26},{10... | collective-permute-start | bytes 393224 | tf_op jit(solution)/shard_map/gather/ppermute | solution.py:216
  9.4 1.6 %collective-permute-start.4 = (f32[256,128]{1,0:T(8,128)S(1)}, f32[256,128]{1,0:T(8,128)S(1)}, u32[]{:S(2)}, u32[]{:S(2)}) collective-permute-start(f32[256,128]{1,0:T(8,128)S(1)} %get-tuple-element.19.refs_0_), channel_id=1, source_target_pairs={{0,2},{1,3},{2,0},{3,1},{4,6},{5,7},{6,4},{7,5},{8,10},{9,11},{10,... | collective-permute-start | bytes 393224 | tf_op jit(solution)/shard_map/gather/ppermute | solution.py:216
  11.6 3.8 %split.1 = (bf16[1024,2048]{1,0:T(8,128)(2,1)S(1)}, bf16[1024,2048]{1,0:T(8,128)(2,1)S(1)}) custom-call(s32[1,1]{1,0:T(1,128)S(6)} %copy.9.count_ref, s32[2,128]{1,0:T(2,128)S(1)} %get-tuple-element.17.plan_ref, f32[128,128,128]{2,1,0:T(8,128)} %bitcast.3), custom_call_target="tpu_custom_call" | custom-call | bytes 1024 | tf_op jit(solution)/shard_map/split/pallas_call | solution.py:229
  15.5 0.0 collective-permute-done.refs_0_
  15.5 0.5 %collective-permute-start.5 = (f32[256,128]{1,0:T(8,128)S(1)}, f32[256,128]{1,0:T(8,128)S(1)}, u32[]{:S(2)}, u32[]{:S(2)}) collective-permute-start(f32[256,128]{1,0:T(8,128)S(1)} %gather.3._.refs_2_), channel_id=1, source_target_pairs={{0,2},{1,3},{2,0},{3,1},{4,6},{5,7},{6,4},{7,5},{8,10},{9,11},{10,... | collective-permute-start | bytes 393224 | tf_op jit(solution)/shard_map/gather/ppermute | solution.py:216
  16.0 0.0 collective-permute-done.1.refs_0_
  16.0 0.0 collective-permute-done.2.refs_0_
  16.1 0.0 collective-permute-done.3.refs_3_
  16.1 0.2 flip.5._.refs_0_
  16.3 0.0 collective-permute-done.4.refs_1_
  16.3 0.1 collective-permute-start.7
  16.4 0.7 %backward.5._ = f32[2,256,128]{2,1,0:T(8,128)S(1)} custom-call(f32[3,256,128]{2,1,0:T(8,128)S(1)} %gather.4._.refs_0_, bf16[256,1024]{1,0:T(8,128)(2,1)S(1)} %flip.5._.refs_0_, bf16[1024,2048]{1,0:T(8,128)(2,1)S(1)} %get-tuple-element.18._.refs_1_.refs_4_, bf16[1024,2048]{1,0:T(8,128)(2,1)S(1)} %get-tuple-element.21.refs_2_.refs_5_), custom_call_target="tpu_custom_call" | custom-call | bytes 1024 | tf_op jit(solution)/shard_map/backward/pallas_call | solution.py:229
  17.1 0.6 %collective-permute-start.6 = (f32[2,256,128]{2,1,0:T(8,128)S(1)}, f32[2,256,128]{2,1,0:T(8,128)S(1)}, u32[]{:S(2)}, u32[]{:S(2)}) collective-permute-start(f32[2,256,128]{2,1,0:T(8,128)S(1)} %backward.5._), channel_id=1, source_target_pairs={{0,1},{1,0},{2,3},{3,2},{4,5},{5,4},{6,7},{7,6},{8,9},{9,8},{10,11... | collective-permute-start | bytes 786440 | tf_op jit(solution)/shard_map/backward/ppermute | solution.py:216
  17.7 0.7 %backward.6._.refs_0_ = f32[2,256,128]{2,1,0:T(8,128)S(1)} custom-call(f32[2,256,128]{2,1,0:T(8,128)S(1)} %backward.5._, bf16[256,1024]{1,0:T(8,128)(2,1)S(1)} %flip.5._.refs_0_, bf16[1024,2048]{1,0:T(8,128)(2,1)S(1)} %get-tuple-element.18._.refs_1_.refs_4_, bf16[1024,2048]{1,0:T(8,128)(2,1)S(1)} %get-tuple-element.21.refs_2_.refs_5_), custom_call_target="tpu_custom_call" | custom-call | bytes 1024 | tf_op jit(solution)/shard_map/backward/pallas_call | solution.py:229
  18.4 0.7 %backward.7._ = f32[2,256,128]{2,1,0:T(8,128)S(1)} custom-call(f32[2,256,128]{2,1,0:T(8,128)S(1)} %backward.6._.refs_0_, bf16[256,1024]{1,0:T(8,128)(2,1)S(1)} %flip.5._.refs_0_, bf16[1024,2048]{1,0:T(8,128)(2,1)S(1)} %get-tuple-element.18._.refs_1_.refs_4_, bf16[1024,2048]{1,0:T(8,128)(2,1)S(1)} %get-tuple-element.21.refs_2_.refs_5_), custom_call_target="tpu_custom_call" | custom-call | bytes 1024 | tf_op jit(solution)/shard_map/backward/pallas_call | solution.py:229
  19.0 0.7 %backward.8._.refs_0_ = f32[2,256,128]{2,1,0:T(8,128)S(1)} custom-call(f32[2,256,128]{2,1,0:T(8,128)S(1)} %backward.7._, bf16[256,1024]{1,0:T(8,128)(2,1)S(1)} %flip.5._.refs_0_, bf16[1024,2048]{1,0:T(8,128)(2,1)S(1)} %get-tuple-element.18._.refs_1_.refs_4_, bf16[1024,2048]{1,0:T(8,128)(2,1)S(1)} %get-tuple-element.21.refs_2_.refs_5_), custom_call_target="tpu_custom_call" | custom-call | bytes 1024 | tf_op jit(solution)/shard_map/backward/pallas_call | solution.py:229
  19.7 0.8 %collective-permute-done.5.refs_0_ = f32[256,128]{1,0:T(8,128)S(1)} collective-permute-done((f32[256,128]{1,0:T(8,128)S(1)}, f32[256,128]{1,0:T(8,128)S(1)}, u32[]{:S(2)}, u32[]{:S(2)}) %collective-permute-start.5) | collective-permute-done | bytes 131104 | tf_op jit(solution)/shard_map/gather/ppermute | solution.py:216
  20.5 0.1 collective-permute-start.8
  20.6 0.0 collective-permute-done.6.refs_1_
  20.7 0.9 %collective-permute-start.10 = (f32[256,128]{1,0:T(8,128)S(1)}, f32[256,128]{1,0:T(8,128)S(1)}, u32[]{:S(2)}, u32[]{:S(2)}) collective-permute-start(f32[256,128]{1,0:T(8,128)S(1)} %get-tuple-element.25), channel_id=1, source_target_pairs={{0,2},{1,3},{2,0},{3,1},{4,6},{5,7},{6,4},{7,5},{8,10},{9,11},{10,... | collective-permute-start | bytes 393224 | tf_op jit(solution)/shard_map/reduce/ppermute | solution.py:216
  21.5 0.2 collective-permute-start.9
  21.7 0.2 collective-permute-done.8.refs_3_
  22.0 0.0 collective-permute-done.7.refs_1_
  22.0 2.4 %forward.1 = (f32[256,128]{1,0:T(8,128)S(1)}, f32[256,128]{1,0:T(8,128)S(1)}, f32[256,128]{1,0:T(8,128)S(1)}, f32[256,128]{1,0:T(8,128)S(1)}) custom-call(f32[256,128]{1,0:T(8,128)S(1)} %get-tuple-element.22._.refs_0_, f32[3,256,128]{2,1,0:T(8,128)S(1)} %gather.4._.refs_0_, f32[3,256,128]{2,1,0:T(8,128)S(1)} %collective-permute-done.7.refs_1_, ...), custom_call_target="tpu_custom_call" | custom-call | bytes 1024 | tf_op jit(solution)/shard_map/forward/pallas_call | solution.py:229
  24.4 2.3 %collective-permute-done.10.refs_1_ = f32[256,128]{1,0:T(8,128)S(1)} collective-permute-done((f32[256,128]{1,0:T(8,128)S(1)}, f32[256,128]{1,0:T(8,128)S(1)}, u32[]{:S(2)}, u32[]{:S(2)}) %collective-permute-start.10) | collective-permute-done | bytes 131104 | tf_op jit(solution)/shard_map/reduce/ppermute | solution.py:216
  26.6 0.1 collective-permute-start.11
  26.7 1.2 %collective-permute-start.12 = (f32[256,128]{1,0:T(8,128)S(1)}, f32[256,128]{1,0:T(8,128)S(1)}, u32[]{:S(2)}, u32[]{:S(2)}) collective-permute-start(f32[256,128]{1,0:T(8,128)S(1)} %get-tuple-element.26), channel_id=1, source_target_pairs={{0,8},{8,0},{16,24},{24,16},{1,9},{9,1},{17,25},{25,17},{2,10},{10... | collective-permute-start | bytes 393224 | tf_op jit(solution)/shard_map/reduce/ppermute | solution.py:216
  27.9 1.5 %collective-permute-start.13 = (f32[256,128]{1,0:T(8,128)S(1)}, f32[256,128]{1,0:T(8,128)S(1)}, u32[]{:S(2)}, u32[]{:S(2)}) collective-permute-start(f32[256,128]{1,0:T(8,128)S(1)} %get-tuple-element.27), channel_id=1, source_target_pairs={{0,16},{8,24},{16,0},{24,8},{1,17},{9,25},{17,1},{25,9},{2,18},{10... | collective-permute-start | bytes 393224 | tf_op jit(solution)/shard_map/reduce/ppermute | solution.py:216
  29.4 0.9 %collective-permute-start.14 = (f32[256,128]{1,0:T(8,128)S(1)}, f32[256,128]{1,0:T(8,128)S(1)}, u32[]{:S(2)}, u32[]{:S(2)}) collective-permute-start(f32[256,128]{1,0:T(8,128)S(1)} %get-tuple-element.28), channel_id=1, source_target_pairs={{0,24},{8,16},{16,8},{24,0},{1,25},{9,17},{17,9},{25,1},{2,26},{10... | collective-permute-start | bytes 393224 | tf_op jit(solution)/shard_map/reduce/ppermute | solution.py:216
  30.3 0.0 collective-permute-done.9.refs_1_
  30.3 1.3 %collective-permute-start.15 = (f32[256,128]{1,0:T(8,128)S(1)}, f32[256,128]{1,0:T(8,128)S(1)}, u32[]{:S(2)}, u32[]{:S(2)}) collective-permute-start(f32[256,128]{1,0:T(8,128)S(1)} %get-tuple-element.31), channel_id=1, source_target_pairs={{0,2},{1,3},{2,0},{3,1},{4,6},{5,7},{6,4},{7,5},{8,10},{9,11},{10,... | collective-permute-start | bytes 393224 | tf_op jit(solution)/shard_map/reduce/ppermute | solution.py:216
  31.6 4.0 %collective-permute-done.11.y_ref = f32[256,128]{1,0:T(8,128)S(1)} collective-permute-done((f32[256,128]{1,0:T(8,128)S(1)}, f32[256,128]{1,0:T(8,128)S(1)}, u32[]{:S(2)}, u32[]{:S(2)}) %collective-permute-start.11) | collective-permute-done | bytes 131104 | tf_op jit(solution)/shard_map/reduce/ppermute | solution.py:216
  35.7 0.0 collective-permute-done.12.refs_1_
  35.7 0.0 collective-permute-done.13.refs_2_
  35.7 0.1 collective-permute-done.14.refs_3_
  35.8 1.3 %collective-permute-done.15.refs_1_ = f32[256,128]{1,0:T(8,128)S(1)} collective-permute-done((f32[256,128]{1,0:T(8,128)S(1)}, f32[256,128]{1,0:T(8,128)S(1)}, u32[]{:S(2)}, u32[]{:S(2)}) %collective-permute-start.15) | collective-permute-done | bytes 131104 | tf_op jit(solution)/shard_map/reduce/ppermute | solution.py:216
  37.1 0.7 %reduce.9 = (f32[256,128]{1,0:T(8,128)}, f32[256,128]{1,0:T(8,128)}) custom-call(f32[256,128]{1,0:T(8,128)S(1)} %reduce.8.row_ref, f32[256,128]{1,0:T(8,128)S(1)} %get-tuple-element.29.row_factor_ref, f32[256,128]{1,0:T(8,128)S(1)} %get-tuple-element.30.col_factor_ref, f32[256,128]{1,0:T(8,128)S(1)} %reduce.7._.refs_0_, ...), custom_call_target="tpu_custom_call" | custom-call | bytes 1024 | tf_op jit(solution)/shard_map/reduce/pallas_call | solution.py:229
  (10 shorter events, 0.2 us)
Async XLA Ops:
  1.8 13.7 %collective-permute-start = (f32[256,128]{1,0:T(8,128)S(1)}, f32[256,128]{1,0:T(8,128)S(1)}, u32[]{:S(2)}, u32[]{:S(2)}) collective-permute-start(f32[256,128]{1,0:T(8,128)S(1)} %get-tuple-element.19.refs_0_), channel_id=1, source_target_pairs={{0,4},{1,5},{2,6},{3,7},{4,0},{5,1},{6,2},{7,3},{8,12},{9,13},{10,... | collective-permute-start | bytes 393224 | tf_op jit(solution)/shard_map/gather/ppermute | solution.py:216
  5.9 10.1 %collective-permute-start.1 = (f32[256,128]{1,0:T(8,128)S(1)}, f32[256,128]{1,0:T(8,128)S(1)}, u32[]{:S(2)}, u32[]{:S(2)}) collective-permute-start(f32[256,128]{1,0:T(8,128)S(1)} %get-tuple-element.20.refs_0_), channel_id=1, source_target_pairs={{0,8},{8,0},{16,24},{24,16},{1,9},{9,1},{17,25},{25,17},{2,10},{10... | collective-permute-start | bytes 393224 | tf_op jit(solution)/shard_map/gather/ppermute | solution.py:216
  7.4 8.7 %collective-permute-start.2 = (f32[256,128]{1,0:T(8,128)S(1)}, f32[256,128]{1,0:T(8,128)S(1)}, u32[]{:S(2)}, u32[]{:S(2)}) collective-permute-start(f32[256,128]{1,0:T(8,128)S(1)} %get-tuple-element.20.refs_0_), channel_id=1, source_target_pairs={{0,16},{8,24},{16,0},{24,8},{1,17},{9,25},{17,1},{25,9},{2,18},{10... | collective-permute-start | bytes 393224 | tf_op jit(solution)/shard_map/gather/ppermute | solution.py:216
  8.9 7.2 %collective-permute-start.3 = (f32[256,128]{1,0:T(8,128)S(1)}, f32[256,128]{1,0:T(8,128)S(1)}, u32[]{:S(2)}, u32[]{:S(2)}) collective-permute-start(f32[256,128]{1,0:T(8,128)S(1)} %get-tuple-element.20.refs_0_), channel_id=1, source_target_pairs={{0,24},{8,16},{16,8},{24,0},{1,25},{9,17},{17,9},{25,1},{2,26},{10... | collective-permute-start | bytes 393224 | tf_op jit(solution)/shard_map/gather/ppermute | solution.py:216
  9.4 6.9 %collective-permute-start.4 = (f32[256,128]{1,0:T(8,128)S(1)}, f32[256,128]{1,0:T(8,128)S(1)}, u32[]{:S(2)}, u32[]{:S(2)}) collective-permute-start(f32[256,128]{1,0:T(8,128)S(1)} %get-tuple-element.19.refs_0_), channel_id=1, source_target_pairs={{0,2},{1,3},{2,0},{3,1},{4,6},{5,7},{6,4},{7,5},{8,10},{9,11},{10,... | collective-permute-start | bytes 393224 | tf_op jit(solution)/shard_map/gather/ppermute | solution.py:216
  15.5 5.0 %collective-permute-start.5 = (f32[256,128]{1,0:T(8,128)S(1)}, f32[256,128]{1,0:T(8,128)S(1)}, u32[]{:S(2)}, u32[]{:S(2)}) collective-permute-start(f32[256,128]{1,0:T(8,128)S(1)} %gather.3._.refs_2_), channel_id=1, source_target_pairs={{0,2},{1,3},{2,0},{3,1},{4,6},{5,7},{6,4},{7,5},{8,10},{9,11},{10,... | collective-permute-start | bytes 393224 | tf_op jit(solution)/shard_map/gather/ppermute | solution.py:216
  16.3 5.6 %collective-permute-start.7 = (f32[3,256,128]{2,1,0:T(8,128)S(1)}, f32[3,256,128]{2,1,0:T(8,128)S(1)}, u32[]{:S(2)}, u32[]{:S(2)}) collective-permute-start(f32[3,256,128]{2,1,0:T(8,128)S(1)} %gather.4._.refs_0_), channel_id=1, source_target_pairs={{0,1},{1,0},{2,3},{3,2},{4,5},{5,4},{6,7},{7,6},{8,9},{9,8},{10,11... | collective-permute-start | bytes 1179656 | tf_op jit(solution)/shard_map/gather/ppermute | solution.py:216
  17.1 3.5 %collective-permute-start.6 = (f32[2,256,128]{2,1,0:T(8,128)S(1)}, f32[2,256,128]{2,1,0:T(8,128)S(1)}, u32[]{:S(2)}, u32[]{:S(2)}) collective-permute-start(f32[2,256,128]{2,1,0:T(8,128)S(1)} %backward.5._), channel_id=1, source_target_pairs={{0,1},{1,0},{2,3},{3,2},{4,5},{5,4},{6,7},{7,6},{8,9},{9,8},{10,11... | collective-permute-start | bytes 786440 | tf_op jit(solution)/shard_map/backward/ppermute | solution.py:216
  20.5 1.4 %collective-permute-start.8 = (f32[1,256,128]{2,1,0:T(8,128)S(1)}, f32[1,256,128]{2,1,0:T(8,128)S(1)}, u32[]{:S(2)}, u32[]{:S(2)}) collective-permute-start(f32[1,256,128]{2,1,0:T(8,128)S(1)} %gather.5._.refs_2_), channel_id=1, source_target_pairs={{0,1},{1,0},{2,3},{3,2},{4,5},{5,4},{6,7},{7,6},{8,9},{9,8},{10,11... | collective-permute-start | bytes 393224 | tf_op jit(solution)/shard_map/gather/ppermute | solution.py:216
  20.7 6.0 %collective-permute-start.10 = (f32[256,128]{1,0:T(8,128)S(1)}, f32[256,128]{1,0:T(8,128)S(1)}, u32[]{:S(2)}, u32[]{:S(2)}) collective-permute-start(f32[256,128]{1,0:T(8,128)S(1)} %get-tuple-element.25), channel_id=1, source_target_pairs={{0,2},{1,3},{2,0},{3,1},{4,6},{5,7},{6,4},{7,5},{8,10},{9,11},{10,... | collective-permute-start | bytes 393224 | tf_op jit(solution)/shard_map/reduce/ppermute | solution.py:216
  21.5 8.7 %collective-permute-start.9 = (f32[2,256,128]{2,1,0:T(8,128)S(1)}, f32[2,256,128]{2,1,0:T(8,128)S(1)}, u32[]{:S(2)}, u32[]{:S(2)}) collective-permute-start(f32[2,256,128]{2,1,0:T(8,128)S(1)} %backward.7._), channel_id=1, source_target_pairs={{0,1},{1,0},{2,3},{3,2},{4,5},{5,4},{6,7},{7,6},{8,9},{9,8},{10,11... | collective-permute-start | bytes 786440 | tf_op jit(solution)/shard_map/reduce/ppermute | solution.py:216
  26.6 9.0 %collective-permute-start.11 = (f32[256,128]{1,0:T(8,128)S(1)}, f32[256,128]{1,0:T(8,128)S(1)}, u32[]{:S(2)}, u32[]{:S(2)}) collective-permute-start(f32[256,128]{1,0:T(8,128)S(1)} %reduce.6), channel_id=1, source_target_pairs={{0,4},{1,5},{2,6},{3,7},{4,0},{5,1},{6,2},{7,3},{8,12},{9,13},{10,... | collective-permute-start | bytes 393224 | tf_op jit(solution)/shard_map/reduce/ppermute | solution.py:216
  26.7 8.9 %collective-permute-start.12 = (f32[256,128]{1,0:T(8,128)S(1)}, f32[256,128]{1,0:T(8,128)S(1)}, u32[]{:S(2)}, u32[]{:S(2)}) collective-permute-start(f32[256,128]{1,0:T(8,128)S(1)} %get-tuple-element.26), channel_id=1, source_target_pairs={{0,8},{8,0},{16,24},{24,16},{1,9},{9,1},{17,25},{25,17},{2,10},{10... | collective-permute-start | bytes 393224 | tf_op jit(solution)/shard_map/reduce/ppermute | solution.py:216
  27.9 7.8 %collective-permute-start.13 = (f32[256,128]{1,0:T(8,128)S(1)}, f32[256,128]{1,0:T(8,128)S(1)}, u32[]{:S(2)}, u32[]{:S(2)}) collective-permute-start(f32[256,128]{1,0:T(8,128)S(1)} %get-tuple-element.27), channel_id=1, source_target_pairs={{0,16},{8,24},{16,0},{24,8},{1,17},{9,25},{17,1},{25,9},{2,18},{10... | collective-permute-start | bytes 393224 | tf_op jit(solution)/shard_map/reduce/ppermute | solution.py:216
  29.4 6.4 %collective-permute-start.14 = (f32[256,128]{1,0:T(8,128)S(1)}, f32[256,128]{1,0:T(8,128)S(1)}, u32[]{:S(2)}, u32[]{:S(2)}) collective-permute-start(f32[256,128]{1,0:T(8,128)S(1)} %get-tuple-element.28), channel_id=1, source_target_pairs={{0,24},{8,16},{16,8},{24,0},{1,25},{9,17},{17,9},{25,1},{2,26},{10... | collective-permute-start | bytes 393224 | tf_op jit(solution)/shard_map/reduce/ppermute | solution.py:216
  30.3 6.8 %collective-permute-start.15 = (f32[256,128]{1,0:T(8,128)S(1)}, f32[256,128]{1,0:T(8,128)S(1)}, u32[]{:S(2)}, u32[]{:S(2)}) collective-permute-start(f32[256,128]{1,0:T(8,128)S(1)} %get-tuple-element.31), channel_id=1, source_target_pairs={{0,2},{1,3},{2,0},{3,1},{4,6},{5,7},{6,4},{7,5},{8,10},{9,11},{10,... | collective-permute-start | bytes 393224 | tf_op jit(solution)/shard_map/reduce/ppermute | solution.py:216
